TPU v7x, 32 devices: a whole 2x2x4 slice. The times are simulated.
32 devices in a mesh: seq: 4 (over z), exp: 8 (over y, x, core).
Axes of the slice: x: 2, y: 2, z: 4, core: 2. Of those that a mesh axis runs over, the one named last changes fastest.
Arguments:
- inputs: bfloat16 [8, 512, 4096], P('exp', 'seq'), may hold values from -6 to 6
- b_proj: bfloat16 [8, 512, 128], P('exp', 'seq'), may hold values from -0.046875 to 0.046875
- c_proj: bfloat16 [8, 512, 128], P('exp', 'seq'), may hold values from -6 to 6
- log_decay: float32 [8, 32, 512], P('exp', None, 'seq'), may hold values from -1.1 to 0, as said below
- doc_lengths: int32 [8, 6], P('exp'), may hold values from 1 to 256, 512 in all within a row
- expert_ids: int32 [8, 512, 2], P('exp', 'seq'), may hold values from 0 to 7, all different within a row; in each aligned block of 128 rows (0 to 127, 128 to 255, ..., all dimensions but the last counted through in order) at most 48 rows name the same one
- gate_weights: float32 [8, 512, 2], P('exp', 'seq'), may hold values from 0.2 to 1
- w_up: bfloat16 [8, 4096, 1024], P('exp'), may hold values from -0.09375 to 0.09375
- w_down: bfloat16 [8, 1024, 4096], P('exp'), may hold values from -0.1875 to 0.1875
- cotangent: bfloat16 [8, 512, 4096], P('exp', 'seq'), may hold values from -6 to 6
Outputs:
- output: bfloat16 [8, 512, 4096], P('exp', 'seq')
- input_grad: bfloat16 [8, 512, 4096], P('exp', 'seq')
Inputs may be any that keep to these rules, and one draw needn't show every extreme that they name: `log_decay`: log of a decay factor, below zero. `doc_lengths`: each sequence's document lengths sum to 512. `expert_ids`: two different experts a position; among the 128 positions of one device no expert is named more than 48 times, a bound that some block reaches.
All inputs are finite; a program needn't handle non-finite values.
Results may differ from a plain program's by a relative error of at most 0.013.
Values may be sent and summed in bfloat16 or wider, within the bound.
No kernel may reach another device: no remote copies, remote signals or barrier semaphores. Data moves between devices by JAX's collectives and lax.ppermute only.
A program may use at most 128 MiB of HBM per device.

v0:
```python
import jax
import jax.numpy as jnp
from jax import lax
from jax.sharding import PartitionSpec as P

BLOCK = 128


EPSILON = 1e-06
HIGHEST_PREC = lax.Precision.HIGHEST


def carried_in(x, axis, combine, identity, reverse):
    length, index = (lax.axis_size(axis), lax.axis_index(axis))
    everything = jax.tree.map(
        lambda part, kind: lax.all_gather(part.astype(kind), axis),
        x,
        jax.tree.map(lambda a: jnp.bfloat16 if a.dtype == jnp.float32 else a.dtype, x),
    )
    start = jax.tree.map(
        lambda part, zero: jnp.broadcast_to(jnp.asarray(zero, part.dtype), part.shape), x, identity
    )

    def hop(k, before):
        at = length - 1 - k if reverse else k
        reached = at > index if reverse else at < index
        new = combine(
            before, jax.tree.map(lambda part, own: part[at].astype(own.dtype), everything, x)
        )
        return jax.tree.map(lambda a, b: jnp.where(reached, a, b), new, before)

    return lax.fori_loop(0, length, hop, start)


def combine(earlier, later):
    return (earlier[0] * later[0], later[0][:, None, None] * earlier[1] + later[1])


def doc_index(starts, element_offsets):
    return jnp.sum((starts[None, :] <= element_offsets[:, None]).astype(jnp.int32), axis=1) - 1


def block_terms(x_blocks, b_blocks, c_blocks, log_blocks, doc_of, doc_before):
    span_len = log_blocks.shape[2]
    cumulative = jnp.cumsum(log_blocks, axis=2)
    lower = jnp.arange(span_len)[:, None] >= jnp.arange(span_len)[None, :]
    same_doc = (doc_of[:, :, None] == doc_of[:, None, :]) & lower[None]
    spread = cumulative[:, :, :, None] - cumulative[:, :, None, :]
    decay_pairs = jnp.where(same_doc[:, None], jnp.exp(jnp.minimum(spread, 0.0)), 0.0)
    scores = jnp.einsum("ktn,ksn->kts", c_blocks, b_blocks, preferred_element_type=jnp.float32)
    mixing = (decay_pairs * scores[:, None]).astype(jnp.bfloat16)
    opened = (doc_of == doc_before[:, None]).astype(jnp.float32)
    tail_mask = (doc_of == doc_of[:, -1:]).astype(jnp.float32)
    last_cum = cumulative[:, :, -1:]
    c_weighted = (
        opened[:, None, :, None]
        * jnp.exp(cumulative)[..., None]
        * c_blocks[:, None].astype(jnp.float32)
    ).astype(jnp.bfloat16)
    b_weighted = (
        tail_mask[:, None, :, None]
        * jnp.exp(last_cum - cumulative)[..., None]
        * b_blocks[:, None].astype(jnp.float32)
    ).astype(jnp.bfloat16)
    retained = opened[:, -1:] * jnp.exp(last_cum[:, :, 0])
    local_state = jnp.einsum(
        "kshp,khsn->khpn", x_blocks, b_weighted, preferred_element_type=jnp.float32
    )
    return (mixing, c_weighted, b_weighted, retained, local_state)


def local_prefix(decays, states, backward):
    initial = (jnp.ones(decays.shape[1:], jnp.float32), jnp.zeros(states.shape[1:], jnp.float32))

    def advance(accumulated, element):
        return (combine(accumulated, element), accumulated)

    return lax.scan(advance, initial, (decays, states), reverse=backward)


def pass_states(overall, backward):
    identity = (jnp.ones_like(overall[0]), jnp.zeros_like(overall[1]))
    return carried_in(overall, "seq", combine, identity, backward)


def expert_forward(rows_in, expert_up, expert_down):
    pre_act = jnp.dot(rows_in, expert_up, preferred_element_type=jnp.float32)
    gate_sig = jax.nn.sigmoid(pre_act)
    activated = (pre_act * gate_sig).astype(jnp.bfloat16)
    expert_out = jnp.dot(activated, expert_down, preferred_element_type=jnp.float32).astype(
        jnp.bfloat16
    )
    return (expert_out, pre_act, gate_sig)


def expert_backward(pre_act, gate_sig, rows_grad, expert_up, expert_down):
    back_hidden = lax.dot_general(
        rows_grad, expert_down, (((1,), (1,)), ((), ())), preferred_element_type=jnp.float32
    )
    pre_grad = (back_hidden * gate_sig * (1.0 + pre_act * (1.0 - gate_sig))).astype(jnp.bfloat16)
    return lax.dot_general(
        pre_grad, expert_up, (((1,), (1,)), ((), ())), preferred_element_type=jnp.float32
    ).astype(jnp.bfloat16)


def expert_rows(rows_in, rows_grad, expert_up, expert_down):
    expert_out, pre_act, gate_sig = expert_forward(rows_in, expert_up, expert_down)
    return (expert_out, expert_backward(pre_act, gate_sig, rows_grad, expert_up, expert_down))


def send_back(expert_out, expert_grad):
    return (
        lax.all_to_all(expert_out, "exp", split_axis=0, concat_axis=0, tiled=True),
        lax.all_to_all(expert_grad, "exp", split_axis=0, concat_axis=0, tiled=True),
    )


def on_device(
    inputs,
    b_proj,
    c_proj,
    log_decay,
    doc_lengths,
    expert_ids,
    gate_weights,
    w_up,
    w_down,
    cotangent,
):
    tokens_here = inputs.shape[1]
    feature_count = inputs.shape[2]
    head_count = log_decay.shape[1]
    head_size = feature_count // head_count
    state_size = b_proj.shape[2]
    block_count = tokens_here // BLOCK
    expert_count = lax.axis_size("exp")
    capacity = 3 * tokens_here // expert_count
    lengths_here = doc_lengths[0]
    starts = jnp.cumsum(lengths_here) - lengths_here
    first_pos = lax.axis_index("seq") * tokens_here
    doc_of = doc_index(starts, first_pos + jnp.arange(tokens_here, dtype=jnp.int32)).reshape(
        block_count, BLOCK
    )
    doc_before = doc_index(starts, first_pos + jnp.arange(block_count, dtype=jnp.int32) * BLOCK - 1)
    x_blocks = inputs[0].reshape(block_count, BLOCK, head_count, head_size)
    log_blocks = log_decay[0].reshape(head_count, block_count, BLOCK).transpose(1, 0, 2)
    mixing, c_weighted, b_weighted, retained, local_state = block_terms(
        x_blocks,
        b_proj[0].reshape(block_count, BLOCK, state_size),
        c_proj[0].reshape(block_count, BLOCK, state_size),
        log_blocks,
        doc_of,
        doc_before,
    )
    overall, before = local_prefix(retained, local_state, False)
    arriving = pass_states(overall, False)
    state_in = before[0][:, :, None, None] * arriving[1][None] + before[1]
    inner = jnp.einsum("khts,kshp->kthp", mixing, x_blocks, preferred_element_type=jnp.float32)
    carried = jnp.einsum(
        "khpn,khtn->kthp", state_in, c_weighted.astype(jnp.float32), precision=HIGHEST_PREC
    )
    resid = (inner + carried).astype(jnp.bfloat16).reshape(tokens_here, feature_count)
    resid_rows = resid.astype(jnp.float32)
    scale_rows = lax.rsqrt(jnp.mean(resid_rows * resid_rows, axis=1, keepdims=True) + EPSILON)
    normed = resid_rows * scale_rows
    mixed_in = normed.astype(jnp.bfloat16)
    expert_flat = expert_ids[0].reshape(-1)
    one_hot = (expert_flat[:, None] == jnp.arange(expert_count, dtype=jnp.int32)[None, :]).astype(
        jnp.int32
    )
    slot_rank = jnp.sum((jnp.cumsum(one_hot, axis=0) - one_hot) * one_hot, axis=1)
    slot_of = expert_flat * capacity + slot_rank
    slot_owner = (
        jnp.full((expert_count * capacity,), tokens_here, jnp.int32)
        .at[slot_of]
        .set(jnp.arange(2 * tokens_here, dtype=jnp.int32) // 2)
    )
    pad_rows = jnp.zeros((1, feature_count), jnp.bfloat16)
    sent_in = jnp.concatenate([mixed_in, pad_rows])[slot_owner].reshape(
        expert_count, capacity, feature_count
    )
    sent_grad = jnp.concatenate([cotangent[0], pad_rows])[slot_owner].reshape(
        expert_count, capacity, feature_count
    )
    expert_up = w_up[0]
    expert_down = w_down[0]
    total_rows = expert_count * capacity
    got_in = lax.all_to_all(sent_in, "exp", split_axis=0, concat_axis=0, tiled=True)
    got_grad = lax.all_to_all(sent_grad, "exp", split_axis=0, concat_axis=0, tiled=True)
    slot_count = got_in.shape[1]
    expert_out, expert_grad = expert_rows(
        got_in.reshape(-1, feature_count),
        got_grad.reshape(-1, feature_count),
        expert_up,
        expert_down,
    )
    back_out, back_grad = send_back(
        expert_out.reshape(expert_count, slot_count, feature_count),
        expert_grad.reshape(expert_count, slot_count, feature_count),
    )
    got_out = back_out.reshape(total_rows, feature_count)[slot_of].reshape(
        tokens_here, 2, feature_count
    )
    got_back = back_grad.reshape(total_rows, feature_count)[slot_of].reshape(
        tokens_here, 2, feature_count
    )
    pair_weights = gate_weights[0][:, :, None]
    moe_rows = jnp.sum(pair_weights * got_out.astype(jnp.float32), axis=1)
    dmixed = jnp.sum(pair_weights * got_back.astype(jnp.float32), axis=1)
    output = (resid_rows + moe_rows).astype(jnp.bfloat16)
    dresid = (
        cotangent[0].astype(jnp.float32)
        + scale_rows * (dmixed - normed * jnp.mean(dmixed * normed, axis=1, keepdims=True))
    ).astype(jnp.bfloat16)
    grad_blocks = dresid.reshape(block_count, BLOCK, head_count, head_size)
    sources = jnp.einsum(
        "kthp,khtn->khpn", grad_blocks, c_weighted, preferred_element_type=jnp.float32
    )
    overall_back, after_local = local_prefix(retained, sources, True)
    arriving_back = pass_states(overall_back, True)
    state_after = after_local[0][:, :, None, None] * arriving_back[1][None] + after_local[1]
    inner_back = jnp.einsum(
        "khts,kthp->kshp", mixing, grad_blocks, preferred_element_type=jnp.float32
    )
    carried_back = jnp.einsum(
        "khpn,khsn->kshp", state_after, b_weighted.astype(jnp.float32), precision=HIGHEST_PREC
    )
    input_grad = (
        (inner_back + carried_back).astype(jnp.bfloat16).reshape(tokens_here, feature_count)
    )
    return (output[None], input_grad[None])


def solution(mesh):
    placed = (
        P("exp", "seq", None),
        P("exp", "seq", None),
        P("exp", "seq", None),
        P("exp", None, "seq"),
        P("exp", None),
        P("exp", "seq", None),
        P("exp", "seq", None),
        P("exp", None, None),
        P("exp", None, None),
        P("exp", "seq", None),
    )
    return jax.shard_map(
        on_device,
        mesh=mesh,
        in_specs=placed,
        out_specs=(P("exp", "seq", None), P("exp", "seq", None)),
        check_vma=False,
    )
```

profile of v0, /device:TPU:0, one launch (start us, length us, event | category | flops | bytes accessed | tf_op | source)
XLA Modules:
  0.0 441.0 jit_solution(11941902683706142964)
XLA Ops:
  19.3 12.6 %all-gather = bf16[4,32,1]{1,2,0:T(2,128)(2,1)S(1)} all-gather(bf16[1,32,1]{1,2,0:T(2,128)(2,1)S(1)} %multiply_convert_fusion.15), channel_id=2, replica_groups=mesh['seq'=4,'exp'=8] {'seq'}, dimensions={0}, use_global_device_ids=true | all-gather | bytes 320 | tf_op jit(solution)/shard_map/all_gather | solution.py:16
  37.6 64.9 %all-gather.6.cloned.1.call-done = bf16[128,128,128]{2,1,0:T(8,128)(2,1)} async-done(((bf16[32,128,128]{2,1,0:T(8,128)(2,1)}), bf16[128,128,128]{2,1,0:T(8,128)(2,1)}) %all-gather.6.cloned.1.call-update) | async-done | bytes 4194320 | tf_op jit(solution)/shard_map/all_gather | solution.py:16
  102.5 9.0 %while.20 = (s32[]{:T(128)}, f32[32,128,128]{2,1,0:T(8,128)S(1)}, s32[]{:T(128)}, bf16[4,32]{1,0:T(4,128)(2,1)S(1)}, bf16[4,32,128,128]{3,2,1,0:T(8,128)(2,1)}, /*index=5*/s32[]{:T(128)}, s32[]{:T(128)}) while((s32[]{:T(128)}, f32[32,128,128]{2,1,0:T(8,128)S(1)}, s32[]{:T(128)}, bf16[4,32]{1,0:T(4,128)(2,1)S(1)}, ...), condition=%wide.region_5.6_spmd.clone, body=%wide.region_4.5_spmd.clone.sunk | while | flops 2621476 | bytes 5243305 | solution.py:32
  111.5 4.8 %fusion.53 = (f32[1,128,32,128]{1,3,2,0:T(8,128)}, bf16[1,128,32,128]{1,3,2,0:T(8,128)(2,1)S(1)}) fusion(f32[32,128,128]{2,1,0:T(8,128)S(1)} %get-tuple-element.270, f32[128,128]{1,0:T(8,128)S(1)} %bitcast_convert_fusion.3, f32[32,128]{1,0:T(8,128)S(1)} %get-tuple-element.350, f32[32,128,128]{1,2,0:T(8,128)} %fusion.32), kind=kOutput, calls=%fused_computation.102 | convolution fusion | flops 807927808 | bytes 7421952 | tf_op jit(solution)/shard_map/khpn,khtn->kthp/dot_general | solution.py:159
  119.5 4.1 gather_fusion
  123.7 4.6 %all-to-all-start = ((bf16[8,48,4096]{2,1,0:T(8,128)(2,1)}), bf16[8,48,4096]{2,1,0:T(8,128)(2,1)}, u32[]{:S(2)}, u32[]{:S(2)}) async-start(bf16[8,48,4096]{2,1,0:T(8,128)(2,1)} %bitcast.133), calls=%async_computation | async-start | bytes 6291456 | tf_op jit(solution)/shard_map/all_to_all | solution.py:188
  128.4 4.1 gather_fusion.2
  132.4 33.7 %all-to-all-done = bf16[8,48,4096]{2,1,0:T(8,128)(2,1)} async-done(((bf16[8,48,4096]{2,1,0:T(8,128)(2,1)}), bf16[8,48,4096]{2,1,0:T(8,128)(2,1)}, u32[]{:S(2)}, u32[]{:S(2)}) %all-to-all-start) | async-done | bytes 3145760 | tf_op jit(solution)/shard_map/all_to_all | solution.py:188
  166.1 3.8 all-to-all-start.2
  170.0 9.0 %fusion.8 = f32[384,1024]{1,0:T(8,128)} fusion(bf16[384,4096]{1,0:T(8,128)(2,1)} %bitcast.23, bf16[1,4096,1024]{2,1,0:T(8,128)(2,1)} %param.21), kind=kOutput, calls=%fused_computation.17 | convolution fusion | flops 3221225472 | bytes 13107200 | tf_op jit(solution)/shard_map/dot_general | solution.py:87
  178.9 28.6 %all-to-all-done.2 = bf16[8,48,4096]{2,1,0:T(8,128)(2,1)S(1)} async-done(((bf16[8,48,4096]{2,1,0:T(8,128)(2,1)}), bf16[8,48,4096]{2,1,0:T(8,128)(2,1)S(1)}, u32[]{:S(2)}, u32[]{:S(2)}) %all-to-all-start.2) | async-done | bytes 3145760 | tf_op jit(solution)/shard_map/all_to_all | solution.py:189
  207.6 18.5 %fusion.10 = bf16[384,4096]{1,0:T(8,128)(2,1)} fusion(bf16[1,4096,1024]{2,1,0:T(8,128)(2,1)} %param.21, f32[384,1024]{1,0:T(8,128)} %fusion.8, bf16[384,4096]{1,0:T(8,128)(2,1)S(1)} %bitcast.140, bf16[1,1024,4096]{2,1,0:T(8,128)(2,1)} %param.22), kind=kOutput, calls=%fused_computation.19 | convolution fusion | flops 6447562752 | bytes 24641536 | tf_op jit(solution)/shard_map/dot_general | solution.py:101
  226.1 3.6 all-to-all-start.3
  229.7 9.0 %fusion.13 = bf16[384,4096]{1,0:T(8,128)(2,1)} fusion(bf16[1,1024,4096]{2,1,0:T(8,128)(2,1)} %param.22, f32[384,1024]{1,0:T(8,128)} %fusion.8), kind=kOutput, calls=%fused_computation.20 | convolution fusion | flops 3224764416 | bytes 13107200 | tf_op jit(solution)/shard_map/dot_general | solution.py:90
  238.7 28.8 %all-to-all-done.3 = bf16[8,48,4096]{2,1,0:T(8,128)(2,1)S(1)} async-done(((bf16[8,48,4096]{2,1,0:T(8,128)(2,1)}), bf16[8,48,4096]{2,1,0:T(8,128)(2,1)S(1)}, u32[]{:S(2)}, u32[]{:S(2)}) %all-to-all-start.3) | async-done | bytes 3145760 | tf_op jit(solution)/shard_map/all_to_all | solution.py:114
  267.5 4.4 %all-to-all-start.1 = ((bf16[8,48,4096]{2,1,0:T(8,128)(2,1)}), bf16[8,48,4096]{2,1,0:T(8,128)(2,1)}, u32[]{:S(2)}, u32[]{:S(2)}) async-start(bf16[8,48,4096]{2,1,0:T(8,128)(2,1)} %bitcast.139), calls=%async_computation.1 | async-start | bytes 6291456 | tf_op jit(solution)/shard_map/all_to_all | solution.py:113
  278.1 5.4 %reshape.539 = f32[128,2,4096]{2,1,0:T(2,128)} reshape(bf16[256,4096]{1,0:T(8,128)(2,1)} %gather_fusion.3) | data formatting | bytes 6291456 | tf_op jit(solution)/shard_map/convert_element_type | solution.py:209
  283.6 26.3 %all-to-all-done.1 = bf16[8,48,4096]{2,1,0:T(8,128)(2,1)} async-done(((bf16[8,48,4096]{2,1,0:T(8,128)(2,1)}), bf16[8,48,4096]{2,1,0:T(8,128)(2,1)}, u32[]{:S(2)}, u32[]{:S(2)}) %all-to-all-start.1) | async-done | bytes 3145760 | tf_op jit(solution)/shard_map/all_to_all | solution.py:113
  309.9 6.2 %gather_fusion.1 = bf16[256,4096]{1,0:T(8,128)(2,1)S(1)} fusion(bf16[384,4096]{1,0:T(8,128)(2,1)} %bitcast.27, s32[1024]{0:T(1024)S(1)} %pad_clamp_fusion), kind=kCustom, calls=%fused_computation.1 | custom fusion | bytes 4195328 | tf_op jit(solution)/shard_map/gather | solution.py:201
  316.0 4.0 reshape.537
  320.0 15.3 %multiply_reduce_fusion = (f32[128,4096]{1,0:T(8,128)}, f32[128,4096]{1,0:T(8,128)}) fusion(f32[128,2,4096]{2,1,0:T(2,128)} %reshape.539, f32[128,2]{1,0:T(8,128)S(1)} %copy.66, f32[128,2,4096]{2,1,0:T(2,128)} %reshape.537), kind=kLoop, calls=%fused_computation.21 | loop fusion | flops 3145728 | bytes 12583936 | tf_op jit(solution)/shard_map/reduce_sum | solution.py:209
  350.1 69.9 %all-gather.8.cloned.1.call-done = bf16[128,128,128]{2,1,0:T(8,128)(2,1)} async-done(((bf16[32,128,128]{2,1,0:T(8,128)(2,1)}), bf16[128,128,128]{2,1,0:T(8,128)(2,1)}) %all-gather.8.cloned.1.call-update) | async-done | bytes 4194320 | tf_op jit(solution)/shard_map/all_gather | solution.py:16
  420.0 9.0 %while.21 = (s32[]{:T(128)}, f32[32,128,128]{2,1,0:T(8,128)S(1)}, s32[]{:T(128)}, bf16[4,32]{1,0:T(4,128)(2,1)S(1)}, bf16[4,32,128,128]{3,2,1,0:T(8,128)(2,1)}, ...) while((s32[]{:T(128)}, f32[32,128,128]{2,1,0:T(8,128)S(1)}, s32[]{:T(128)}, ...), condition=%wide.region_15.16_spmd.clone, body=%wide.region_14.15_spmd.clone.sunk | while | flops 2621480 | bytes 5243367 | solution.py:32
  429.0 3.8 fusion.16
  (106 shorter events, 59.6 us)
Async XLA Ops:
  7.2 8.1 %copy-start.8 = (bf16[1,128,128]{2,1,0:T(8,128)(2,1)S(1)}, bf16[1,128,128]{2,1,0:T(8,128)(2,1)}, u32[]{:S(2)}) copy-start(bf16[1,128,128]{2,1,0:T(8,128)(2,1)} %param.15) | copy-start | bytes 98308
  7.2 95.3 %all-gather.6.cloned.1.call-start = ((), (), s32[]{:S(2)}) async-start(), calls=%async_computation.4 | async-start | bytes 5242880 | tf_op jit(solution)/shard_map/all_gather | solution.py:16
  17.5 1.4 copy-start.10
  17.5 17.1 %copy-start.9 = (bf16[1,128,128]{2,1,0:T(8,128)(2,1)S(1)}, bf16[1,128,128]{2,1,0:T(8,128)(2,1)}, u32[]{:S(2)}) copy-start(bf16[1,128,128]{2,1,0:T(8,128)(2,1)} %param.16) | copy-start | bytes 98308
  116.3 2.3 copy-start
  123.7 4.6 %copy-start.5 = (bf16[1,128,4096]{2,1,0:T(8,128)(2,1)S(1)}, bf16[1,128,4096]{2,1,0:T(8,128)(2,1)}, u32[]{:S(2)}) copy-start(bf16[1,128,4096]{2,1,0:T(8,128)(2,1)} %param.23) | copy-start | bytes 3145732
  123.7 42.5 %all-to-all-start = ((bf16[8,48,4096]{2,1,0:T(8,128)(2,1)}), bf16[8,48,4096]{2,1,0:T(8,128)(2,1)}, u32[]{:S(2)}, u32[]{:S(2)}) async-start(bf16[8,48,4096]{2,1,0:T(8,128)(2,1)} %bitcast.133), calls=%async_computation | async-start | bytes 6291456 | tf_op jit(solution)/shard_map/all_to_all | solution.py:188
  166.1 41.5 %all-to-all-start.2 = ((bf16[8,48,4096]{2,1,0:T(8,128)(2,1)}), bf16[8,48,4096]{2,1,0:T(8,128)(2,1)S(1)}, u32[]{:S(2)}, u32[]{:S(2)}) async-start(bf16[8,48,4096]{2,1,0:T(8,128)(2,1)} %bitcast.132), calls=%async_computation.2 | async-start | bytes 6291456 | tf_op jit(solution)/shard_map/all_to_all | solution.py:189
  226.1 41.5 %all-to-all-start.3 = ((bf16[8,48,4096]{2,1,0:T(8,128)(2,1)}), bf16[8,48,4096]{2,1,0:T(8,128)(2,1)S(1)}, u32[]{:S(2)}, u32[]{:S(2)}) async-start(bf16[8,48,4096]{2,1,0:T(8,128)(2,1)} %bitcast.141), calls=%async_computation.3 | async-start | bytes 6291456 | tf_op jit(solution)/shard_map/all_to_all | solution.py:114
  267.5 42.3 %all-to-all-start.1 = ((bf16[8,48,4096]{2,1,0:T(8,128)(2,1)}), bf16[8,48,4096]{2,1,0:T(8,128)(2,1)}, u32[]{:S(2)}, u32[]{:S(2)}) async-start(bf16[8,48,4096]{2,1,0:T(8,128)(2,1)} %bitcast.139), calls=%async_computation.1 | async-start | bytes 6291456 | tf_op jit(solution)/shard_map/all_to_all | solution.py:113
  272.0 2.8 copy-start.11
  272.0 148.0 %all-gather.8.cloned.1.call-start = ((), (), s32[]{:S(2)}) async-start(), calls=%async_computation.5 | async-start | bytes 5242880 | tf_op jit(solution)/shard_map/all_gather | solution.py:16
  335.3 2.0 copy-start.1
  337.3 1.6 copy-start.2
  339.5 1.0 copy-start.6
  342.4 3.2 copy-start.7
  345.6 2.2 copy-start.3
  345.6 3.2 copy-start.4
Sparse Core Ops, SparseCore 0:
  19.0 83.4 all-gather.5
  342.5 77.4 all-gather.7
where the time goes:
time: 442 us; the launch traced here: 441 us
  waiting for transfers between devices  252 us (57%)
  matrix products  54.3 us (12%)
  local copies, waits for them, and re-layouts  48.1 us (11%)
  other arithmetic  40.9 us (9%)
  starting transfers between devices  16.8 us (4%)
  between operations  15.7 us (4%)
  blocking collectives  12.6 us (3%)
    all_gather x2, waiting for transfers between devices, carried_in(): lax.all_gather(part.astype(kind), axis)  135 us
    all_to_all x1, waiting for transfers between devices, on_device(): lax.all_to_all(sent_in, 'exp', split_axis=0, concat_axis=0, tiled=True)  33.7 us
    all_to_all x1, waiting for transfers between devices, send_back(): lax.all_to_all(expert_grad, 'exp', split_axis=0, concat_axis=0, tiled=True)  28.8 us
    all_to_all x1, waiting for transfers between devices, on_device(): lax.all_to_all(sent_grad, 'exp', split_axis=0, concat_axis=0, tiled=True)  28.6 us
    all_to_all x1, waiting for transfers between devices, send_back(): lax.all_to_all(expert_out, 'exp', split_axis=0, concat_axis=0, tiled=True)  26.3 us
    dot_general x1, matrix products, expert_backward(): lax.dot_general(pre_grad, expert_up, (((1,), (1,)), ((), ())), preferred_...  18.5 us
    select_n x8, other arithmetic, hop(): return jax.tree.map(lambda a, b: jnp.where(reached, a, b), new, before)  17.7 us
    reduce_sum x1, other arithmetic, on_device(): dmixed = jnp.sum(pair_weights * got_back.astype(jnp.float32), axis=1)  15.3 us
  transfers between devices with their start and end apart: 6, of which 6 were waited for; matrix products, arithmetic and copies ran while one was open for 10% of the time, Pallas kernels for 0%

commit v1 on v0

v1 whole, which is shorter than its diff:
```python
import functools

import jax
import jax.numpy as jnp
from jax import lax
from jax.experimental import pallas as pl
from jax.experimental.pallas import tpu as pltpu
from jax.sharding import PartitionSpec as P

EPSILON = 1e-06
F32 = jnp.float32
BF16 = jnp.bfloat16
HEADS_STEP = 8
VMEM_BYTES = 48 * 1024 * 1024
NT = (((1,), (1,)), ((), ()))


def dot(a, b):
    return jnp.dot(a, b, preferred_element_type=F32)


def dot_nt(a, b):
    return lax.dot_general(a, b, NT, preferred_element_type=F32)


def call(kernel, grid, in_specs, out_specs, out_shape, flops, nbytes, name, scratch=()):
    return pl.pallas_call(
        kernel,
        grid=grid,
        in_specs=in_specs,
        out_specs=out_specs,
        out_shape=out_shape,
        scratch_shapes=scratch,
        name=name,
        cost_estimate=pl.CostEstimate(flops=flops, bytes_accessed=nbytes, transcendentals=0),
        compiler_params=pltpu.CompilerParams(vmem_limit_bytes=VMEM_BYTES),
    )


def whole(shape):
    return pl.BlockSpec(shape, lambda i: (0,) * len(shape))


def columns(rows, width):
    return pl.BlockSpec((rows, width), lambda i: (0, i))


SMEM = pl.BlockSpec(memory_space=pltpu.SMEM)


def documents(meta, rows, size):
    count = meta.shape[0] - 1
    first = meta[count]
    along = first + lax.broadcasted_iota(jnp.int32, (1, size), 1)
    down = first + lax.broadcasted_iota(jnp.int32, (size, 1), 0)
    row = jnp.full((1, size), -1, jnp.int32)
    col = jnp.full((size, 1), -1, jnp.int32)
    before, last, start = jnp.int32(-1), jnp.int32(-1), jnp.int32(0)
    for i in range(count):
        row += (start <= along).astype(jnp.int32)
        col += (start <= down).astype(jnp.int32)
        before += (start <= first - 1).astype(jnp.int32)
        last += (start <= first + size - 1).astype(jnp.int32)
        start = start + meta[i]
    return row, col, before, last


def running(log_ref):
    size = log_ref.shape[1]
    upto = (
        lax.broadcasted_iota(jnp.int32, (size, size), 0)
        <= lax.broadcasted_iota(jnp.int32, (size, size), 1)
    ).astype(F32)
    return jnp.dot(
        log_ref[...], upto, precision=lax.Precision.HIGHEST, preferred_element_type=F32
    )


def head(h, size):
    return slice(h * size, (h + 1) * size)


def local_kernel(meta, log_ref, b_ref, x_ref, state_ref):
    size = log_ref.shape[1]
    cum = running(log_ref)
    row, _, _, last = documents(meta, cum.shape[0], size)
    tail = (row == last).astype(F32)
    weight = tail * jnp.exp(cum[:, size - 1 :] - cum)
    b_t = b_ref[...].astype(F32).T
    p = x_ref.shape[1] // cum.shape[0]
    for h in range(cum.shape[0]):
        b_weighted = (b_t * weight[h : h + 1, :]).astype(BF16)
        state_ref[:, head(h, p)] = dot(b_weighted, x_ref[:, head(h, p)]).astype(BF16)


def pair_mask(meta, size):
    row, col, before, last = documents(meta, size, size)
    later = lax.broadcasted_iota(jnp.int32, (size, size), 0)
    earlier = lax.broadcasted_iota(jnp.int32, (size, size), 1)
    return row, col, before, last, later, earlier


def inner_kernel(meta, log_ref, b_ref, c_ref, x_ref, out_ref):
    size = log_ref.shape[1]
    cum = running(log_ref)
    cum_t = cum.T
    row, col, _, _, down, along = pair_mask(meta, size)
    scores = jnp.where((row == col) & (down >= along), dot_nt(c_ref[...], b_ref[...]), 0.0)
    p = x_ref.shape[1] // cum.shape[0]
    for h in range(cum.shape[0]):
        spread = cum_t[:, h : h + 1] - cum[h : h + 1, :]
        pair = (jnp.exp(jnp.minimum(spread, 0.0)) * scores).astype(BF16)
        out_ref[:, head(h, p)] = dot(pair, x_ref[:, head(h, p)])


def inner_back_kernel(meta, log_ref, b_ref, c_ref, grad_ref, out_ref):
    size = log_ref.shape[1]
    cum = running(log_ref)
    cum_t = cum.T
    row, col, _, _, down, along = pair_mask(meta, size)
    scores = jnp.where((row == col) & (down <= along), dot_nt(b_ref[...], c_ref[...]), 0.0)
    p = grad_ref.shape[1] // cum.shape[0]
    for h in range(cum.shape[0]):
        spread = cum[h : h + 1, :] - cum_t[:, h : h + 1]
        pair = (jnp.exp(jnp.minimum(spread, 0.0)) * scores).astype(BF16)
        out_ref[:, head(h, p)] = dot(pair, grad_ref[:, head(h, p)])


def keep_kernel(meta, log_ref, state_ref, out_ref):
    size = log_ref.shape[1]
    total = jnp.exp(running(log_ref)[:, size - 1 :])
    _, _, before, last = documents(meta, 1, size)
    total = jnp.where(before == last, total, 0.0)
    p = state_ref.shape[1] // total.shape[0]
    for h in range(total.shape[0]):
        out_ref[:, head(h, p)] = (
            state_ref[:, head(h, p)].astype(F32) * total[h : h + 1, :]
        ).astype(BF16)


def resid_kernel(hops, meta, log_ref, c_ref, pick_ref, inner_ref, *refs):
    states, (resid_ref, sent_ref, scale_ref) = refs[:hops], refs[hops:]
    size = log_ref.shape[1]
    features = inner_ref.shape[1] * pl.num_programs(0)
    _, col, before, _ = documents(meta, size, size)
    weight = jnp.where(col == before, jnp.exp(running(log_ref).T), 0.0)
    p = inner_ref.shape[1] // log_ref.shape[0]
    squares = jnp.zeros((size, p), F32)
    for h in range(log_ref.shape[0]):
        carried = dot(c_ref[...], states[0][:, head(h, p)])
        for state in states[1:]:
            carried += dot(c_ref[...], state[:, head(h, p)])
        rows = (inner_ref[:, head(h, p)] + weight[:, h : h + 1] * carried).astype(BF16)
        resid_ref[:, head(h, p)] = rows
        squares += rows.astype(F32) * rows.astype(F32)
    sent_ref[...] = dot(pick_ref[...], resid_ref[...]).astype(BF16)
    squares = jnp.broadcast_to(jnp.sum(squares, axis=1, keepdims=True), scale_ref.shape)
    step = pl.program_id(0)

    @pl.when(step == 0)
    def _():
        scale_ref[...] = squares

    @pl.when(step > 0)
    def _():
        scale_ref[...] += squares

    @pl.when(step == pl.num_programs(0) - 1)
    def _():
        scale_ref[...] = lax.rsqrt(scale_ref[...] / features + EPSILON)


def dresid_kernel(meta, log_ref, c_ref, high_ref, low_ref, scale_ref, cot_ref, got_ref, dresid_ref, source_ref):
    size = log_ref.shape[1]
    row, _, before, _ = documents(meta, size, size)
    weight = jnp.where(row == before, jnp.exp(running(log_ref)), 0.0)
    c_t = c_ref[...].astype(F32).T
    got = got_ref[...]
    moved = dot(high_ref[...], got) + dot(low_ref[...], got)
    dresid_ref[...] = (cot_ref[...].astype(F32) + scale_ref[:, :1] * moved).astype(BF16)
    p = cot_ref.shape[1] // log_ref.shape[0]
    for h in range(log_ref.shape[0]):
        c_weighted = (c_t * weight[h : h + 1, :]).astype(BF16)
        source_ref[:, head(h, p)] = dot(c_weighted, dresid_ref[:, head(h, p)]).astype(BF16)


def grad_kernel(hops, meta, log_ref, b_ref, inner_ref, *refs):
    states, out_ref = refs[:hops], refs[hops]
    size = log_ref.shape[1]
    _, col, _, last = documents(meta, size, size)
    cum = running(log_ref)
    weight = jnp.where(col == last, jnp.exp(cum[:, size - 1 :] - cum).T, 0.0)
    p = inner_ref.shape[1] // log_ref.shape[0]
    for h in range(log_ref.shape[0]):
        carried = dot(b_ref[...], states[0][:, head(h, p)])
        for state in states[1:]:
            carried += dot(b_ref[...], state[:, head(h, p)])
        out_ref[:, head(h, p)] = (inner_ref[:, head(h, p)] + weight[:, h : h + 1] * carried).astype(BF16)


def output_kernel(high_ref, low_ref, resid_ref, got_ref, out_ref):
    got = got_ref[...]
    moved = dot(high_ref[...], got) + dot(low_ref[...], got)
    out_ref[...] = (resid_ref[...].astype(F32) + moved).astype(BF16)


def pick_kernel(experts, capacity, ids_ref, gate_ref, cot_ref, pick_ref, high_ref, low_ref, sent_ref):
    tokens = ids_ref.shape[1]

    @pl.when(pl.program_id(0) == 0)
    def _():
        expert = lax.broadcasted_iota(jnp.int32, (experts, tokens), 0)
        first, second = ids_ref[0:1, :] == expert, ids_ref[1:2, :] == expert
        named = (first | second).astype(F32)
        gate = jnp.where(first, gate_ref[0:1, :], 0.0) + jnp.where(second, gate_ref[1:2, :], 0.0)
        before = (
            lax.broadcasted_iota(jnp.int32, (tokens, tokens), 0)
            < lax.broadcasted_iota(jnp.int32, (tokens, tokens), 1)
        ).astype(BF16)
        rank = jnp.where(named > 0, dot(named.astype(BF16), before), -1.0)
        slot = lax.broadcasted_iota(jnp.int32, (capacity, tokens), 0).astype(F32)
        picks, gates = [], []
        for e in range(experts):
            pick = (rank[e : e + 1, :] == slot).astype(F32)
            picks.append(pick)
            gates.append(pick * gate[e : e + 1, :])
        pick_ref[...] = jnp.concatenate(picks, axis=0).astype(BF16)
        gates = jnp.concatenate(gates, axis=0).T
        high = gates.astype(BF16)
        high_ref[...] = high
        low_ref[...] = (gates - high.astype(F32)).astype(BF16)

    sent_ref[...] = dot(pick_ref[...], cot_ref[...]).astype(BF16)


def back_kernel(rows_ref, down_ref, back_ref):
    part = dot_nt(rows_ref[...], down_ref[...])

    @pl.when(pl.program_id(0) == 0)
    def _():
        back_ref[...] = part

    @pl.when(pl.program_id(0) > 0)
    def _():
        back_ref[...] += part


def up_kernel(rows_ref, up_ref, back_ref, act_ref, pre_grad_ref, along_ref, total, squares):
    step, steps = pl.program_id(0), pl.num_programs(0)
    features = rows_ref.shape[1] * steps
    part = dot(rows_ref[...], up_ref[...])
    rows = rows_ref[...].astype(F32)
    square = jnp.sum(rows * rows, axis=1, keepdims=True)

    @pl.when(step == 0)
    def _():
        total[...] = part
        squares[...] = jnp.broadcast_to(square, squares.shape)

    @pl.when(step > 0)
    def _():
        total[...] += part
        squares[...] += jnp.broadcast_to(square, squares.shape)

    @pl.when(step == steps - 1)
    def _():
        scale = lax.rsqrt(squares[:, :1] / features + EPSILON)
        pre = total[...] * scale
        gate = jax.nn.sigmoid(pre)
        act_ref[...] = (pre * gate).astype(BF16)
        pre_grad = (back_ref[...] * gate * (1.0 + pre * (1.0 - gate))).astype(BF16)
        pre_grad_ref[...] = pre_grad
        along = jnp.sum(pre_grad.astype(F32) * pre, axis=1, keepdims=True)
        along_ref[...] = jnp.broadcast_to(scale * along / features, along_ref.shape)


def expert_grad_kernel(pre_grad_ref, up_ref, rows_ref, along_ref, out_ref):
    out_ref[...] = (
        dot_nt(pre_grad_ref[...], up_ref[...]) - rows_ref[...].astype(F32) * along_ref[:, :1]
    ).astype(BF16)


def expert_out_kernel(act_ref, down_ref, out_ref):
    out_ref[...] = dot(act_ref[...], down_ref[...]).astype(BF16)


def exchange(rows, experts):
    parts = rows.reshape(experts, rows.shape[0] // experts, rows.shape[1])
    return lax.all_to_all(parts, "exp", split_axis=0, concat_axis=0, tiled=True).reshape(rows.shape)


def on_device(inputs, b_proj, c_proj, log_decay, doc_lengths, expert_ids, gate_weights, w_up, w_down, cotangent):
    tokens, features = inputs.shape[1:]
    heads = log_decay.shape[1]
    state = b_proj.shape[2]
    experts, blocks = lax.axis_size("exp"), lax.axis_size("seq")
    hidden = w_up.shape[2]
    capacity = 3 * tokens // experts
    slots = experts * capacity
    steps = heads // HEADS_STEP
    width = features // steps
    hops = max(1, blocks // 2)

    x, b, c, log, cot = inputs[0], b_proj[0], c_proj[0], log_decay[0], cotangent[0]
    up, down = w_up[0], w_down[0]
    meta = jnp.concatenate([doc_lengths[0], (lax.axis_index("seq") * tokens)[None].astype(jnp.int32)])

    log_spec = pl.BlockSpec((HEADS_STEP, tokens), lambda i: (i, 0))
    part, small = columns(tokens, width), whole((tokens, state))
    rows_f32 = jax.ShapeDtypeStruct((tokens, features), F32)
    rows_bf16 = jax.ShapeDtypeStruct((tokens, features), BF16)
    slots_bf16 = jax.ShapeDtypeStruct((slots, features), BF16)
    unit = tokens * features
    head_flops = 2 * tokens * unit

    pick, high, low, sent_cot = call(
        functools.partial(pick_kernel, experts, capacity),
        (steps,),
        [whole((2, tokens)), whole((2, tokens)), part],
        [whole((slots, tokens)), whole((tokens, slots)), whole((tokens, slots)), columns(slots, width)],
        [
            jax.ShapeDtypeStruct((slots, tokens), BF16),
            jax.ShapeDtypeStruct((tokens, slots), BF16),
            jax.ShapeDtypeStruct((tokens, slots), BF16),
            slots_bf16,
        ],
        2 * slots * unit,
        2 * (unit + slots * features),
        "pick_rows",
    )(expert_ids[0].T, gate_weights[0].T, cot)
    got_cot = exchange(sent_cot, experts)

    local = call(
        local_kernel, (steps,), [SMEM, log_spec, small, part], part, rows_bf16, head_flops, 4 * unit, "local_states"
    )(meta, log, b, x)

    keep = call(keep_kernel, (steps,), [SMEM, log_spec, part], part, rows_bf16, unit, 4 * unit, "keep_states")

    def passed(states, step):
        pairs = [(i, i + step) for i in range(blocks) if 0 <= i + step < blocks]
        arrived = [lax.ppermute(states, "seq", pairs)]
        for _ in range(hops - 1):
            arrived.append(lax.ppermute(keep(meta, log, arrived[-1]), "seq", pairs))
        return arrived

    states_in = passed(local, 1)
    inner = call(
        inner_kernel, (steps,), [SMEM, log_spec, small, small, part], part, rows_f32, 2 * head_flops, 6 * unit, "inner"
    )(meta, log, b, c, x)

    resid, sent_in, scale = call(
        functools.partial(resid_kernel, hops),
        (steps,),
        [SMEM, log_spec, small, whole((slots, tokens)), part] + [part] * hops,
        [part, columns(slots, width), whole((tokens, 128))],
        [rows_bf16, slots_bf16, jax.ShapeDtypeStruct((tokens, 128), F32)],
        hops * head_flops + 2 * slots * unit,
        (4 + 2 * hops + 2) * unit + 2 * slots * features,
        "resid",
    )(meta, log, c, pick, inner, *states_in)
    got_in = exchange(sent_in, experts)

    expert_flops = 2 * slots * features * hidden
    expert_bytes = 2 * features * (hidden + slots)
    chunk = features // 4
    slots_hidden = whole((slots, hidden))
    back = call(
        back_kernel,
        (4,),
        [columns(slots, chunk), columns(hidden, chunk)],
        slots_hidden,
        jax.ShapeDtypeStruct((slots, hidden), F32),
        expert_flops,
        expert_bytes,
        "back",
    )(got_cot, down)
    act, pre_grad, along = call(
        up_kernel,
        (4,),
        [columns(slots, chunk), pl.BlockSpec((chunk, hidden), lambda i: (i, 0)), slots_hidden],
        [slots_hidden, slots_hidden, whole((slots, 128))],
        [
            jax.ShapeDtypeStruct((slots, hidden), BF16),
            jax.ShapeDtypeStruct((slots, hidden), BF16),
            jax.ShapeDtypeStruct((slots, 128), F32),
        ],
        expert_flops,
        expert_bytes,
        "up",
        [pltpu.VMEM((slots, hidden), F32), pltpu.VMEM((slots, 128), F32)],
    )(got_in, up, back)
    expert_grad = call(
        expert_grad_kernel,
        (4,),
        [
            slots_hidden,
            pl.BlockSpec((chunk, hidden), lambda i: (i, 0)),
            columns(slots, chunk),
            whole((slots, 128)),
        ],
        columns(slots, chunk),
        slots_bf16,
        expert_flops,
        expert_bytes,
        "expert_grad",
    )(pre_grad, up, got_in, along)
    got_grad = exchange(expert_grad, experts)
    expert_out = call(
        expert_out_kernel,
        (4,),
        [slots_hidden, columns(hidden, chunk)],
        columns(slots, chunk),
        slots_bf16,
        expert_flops,
        expert_bytes,
        "expert_out",
    )(act, down)
    got_out = exchange(expert_out, experts)

    weights = [whole((tokens, slots))] * 2
    dresid, sources = call(
        dresid_kernel,
        (steps,),
        [SMEM, log_spec, small] + weights + [whole((tokens, 128)), part, columns(slots, width)],
        [part, part],
        [rows_bf16, rows_bf16],
        head_flops + 4 * slots * unit,
        6 * unit + 2 * slots * features,
        "dresid",
    )(meta, log, c, high, low, scale, cot, got_grad)
    states_after = passed(sources, -1)
    inner_back = call(
        inner_back_kernel,
        (steps,),
        [SMEM, log_spec, small, small, part],
        part,
        rows_f32,
        2 * head_flops,
        6 * unit,
        "inner_back",
    )(meta, log, b, c, dresid)
    input_grad = call(
        functools.partial(grad_kernel, hops),
        (steps,),
        [SMEM, log_spec, small, part] + [part] * hops,
        part,
        rows_bf16,
        hops * head_flops,
        (6 + 2 * hops) * unit,
        "input_grad",
    )(meta, log, b, inner_back, *states_after)
    output = call(
        output_kernel,
        (steps,),
        weights + [part, columns(slots, width)],
        part,
        rows_bf16,
        4 * slots * unit,
        4 * unit + 2 * slots * features,
        "output",
    )(high, low, resid, got_out)
    return (output[None], input_grad[None])


def solution(mesh):
    placed = (
        P("exp", "seq", None),
        P("exp", "seq", None),
        P("exp", "seq", None),
        P("exp", None, "seq"),
        P("exp", None),
        P("exp", "seq", None),
        P("exp", "seq", None),
        P("exp", None, None),
        P("exp", None, None),
        P("exp", "seq", None),
    )
    return jax.shard_map(
        on_device,
        mesh=mesh,
        in_specs=placed,
        out_specs=(P("exp", "seq", None), P("exp", "seq", None)),
        check_vma=False,
    )
```

time: 442 us -> 255 us (0.58)
  waiting for transfers between devices: 252 us -> 144 us
  Pallas kernels: 0 us -> 65.2 us
  matrix products: 54.3 us -> 0 us
  other arithmetic: 40.9 us -> 0.08 us
  local copies, waits for them, and re-layouts: 48.1 us -> 15.2 us
  between operations: 15.7 us -> 0.87 us
  blocking collectives: 12.6 us -> 0 us
  starting transfers between devices: 16.8 us -> 28.6 us
    all_gather x2 -> x0, waiting for transfers between devices: 135 us -> none  [carried_in(): lax.all_gather(part.astype(kind), axis)]
    ppermute x0 -> x4, waiting for transfers between devices: none -> 84.8 us  [the longest x2 49.8 us: passed(): arrived = [lax.ppermute(states, 'seq', pairs)]]
    pallas_call x0 -> x14, Pallas kernels: none -> 65.2 us  [the longest x1 8.21 us: on_device(): call(up_kernel, (4,), [columns(slots, chunk), pl.BlockSpec((chunk, hidden...]
    all_to_all x4, waiting for transfers between devices: 117 us -> 59.6 us  [exchange(): lax.all_to_all(parts, 'exp', split_axis=0, concat_axis=0, tiled=True)]
    dot_general x10 -> x0, matrix products: 54.3 us -> none  [the longest x1 18.5 us: expert_backward(): lax.dot_general(pre_grad, expert_up, (((1,), (1,)), ((), ())), preferred_...]
    convert_element_type x6 -> x0, local copies, waits for them, and re-layouts: 18.8 us -> none  [the longest x2 5.51 us: on_device(): resid_rows = resid.astype(jnp.float32)]
    reduce_sum x6 -> x0, other arithmetic: 17.9 us -> none  [the longest x1 15.3 us: on_device(): dmixed = jnp.sum(pair_weights * got_back.astype(jnp.float32), axis=1)]
    select_n x11 -> x0, other arithmetic: 17.7 us -> none  [the longest x8 17.7 us: hop(): return jax.tree.map(lambda a, b: jnp.where(reached, a, b), new, before)]
  transfers between devices with their start and end apart: 6 -> 8, of which waited for: 6 -> 6; matrix products, arithmetic and copies ran while one was open for 10% -> 0% of each run, Pallas kernels for 0% -> 17%
where the time goes in v1:
time: 255 us; the launch traced here: 254 us
  waiting for transfers between devices  144 us (56%)
  Pallas kernels  65.2 us (26%)
  starting transfers between devices  28.6 us (11%)
  local copies, waits for them, and re-layouts  15.2 us (6%)
    all_to_all x4, waiting for transfers between devices, exchange(): lax.all_to_all(parts, 'exp', split_axis=0, concat_axis=0, tiled=True)  59.6 us
    ppermute x2, waiting for transfers between devices, passed(): arrived = [lax.ppermute(states, 'seq', pairs)]  49.8 us
    ppermute x2, waiting for transfers between devices, passed(): arrived.append(lax.ppermute(keep(meta, log, arrived[-1]), 'seq', pairs))  35 us
    all_to_all x4, starting transfers between devices, exchange(): lax.all_to_all(parts, 'exp', split_axis=0, concat_axis=0, tiled=True)  18 us
    unnamed x44, local copies, waits for them, and re-layouts  15.2 us
    pallas_call x1, Pallas kernels, on_device(): call(up_kernel, (4,), [columns(slots, chunk), pl.BlockSpec((chunk, hidden...  8.21 us
    pallas_call x1, Pallas kernels, on_device(): call(expert_grad_kernel, (4,), [slots_hidden, pl.BlockSpec((chunk, hidden...  8.08 us
    pallas_call x1, Pallas kernels, on_device(): call(back_kernel, (4,), [columns(slots, chunk), columns(hidden, chunk)],...  6.94 us
  transfers between devices with their start and end apart: 8, of which 6 were waited for; matrix products, arithmetic and copies ran while one was open for 0% of the time, Pallas kernels for 17%

profile of v1, /device:TPU:0, one launch (start us, length us, event | category | flops | bytes accessed | tf_op | source)
XLA Modules:
  0.0 254.3 jit_solution(15799619104585891783)
XLA Ops:
  6.9 5.3 %all-to-all-start.1 = ((bf16[8,48,4096]{2,1,0:T(8,128)(2,1)}), bf16[8,48,4096]{2,1,0:T(8,128)(2,1)S(1)}, u32[]{:S(2)}, u32[]{:S(2)}) async-start(bf16[8,48,4096]{2,1,0:T(8,128)(2,1)} %bitcast.30), calls=%async_computation.1 | async-start | bytes 6291456 | tf_op jit(solution)/shard_map/all_to_all | solution.py:289
  13.5 3.0 %local_states.1 = bf16[128,4096]{1,0:T(8,128)(2,1)S(1)} custom-call(s32[7]{0:T(128)S(1)} %pad_add_fusion.meta, f32[32,128]{1,0:T(8,128)S(1)} %bitcast.31, bf16[128,128]{1,0:T(8,128)(2,1)S(1)} %bitcast.45, bf16[128,4096]{1,0:T(8,128)(2,1)S(1)} %bitcast.28), custom_call_target="tpu_custom_call" | custom-call | flops 134217728 | bytes 2097152 | tf_op jit(solution)/shard_map/local_states/pallas_call | solution.py:333
  16.5 3.5 %collective-permute-start = (bf16[128,4096]{1,0:T(8,128)(2,1)S(1)}, bf16[128,4096]{1,0:T(8,128)(2,1)S(1)}, u32[]{:S(2)}, u32[]{:S(2)}) collective-permute-start(bf16[128,4096]{1,0:T(8,128)(2,1)S(1)} %local_states.1), channel_id=1, source_target_pairs={{0,8},{8,16},{16,24},{1,9},{9,17},{17,25},{2,10},{10,18},{18,26},{... | collective-permute-start | bytes 3145736 | tf_op jit(solution)/shard_map/ppermute | solution.py:341
  20.0 23.0 %collective-permute-done.state_ref.refs_0_ = bf16[128,4096]{1,0:T(8,128)(2,1)S(1)} collective-permute-done((bf16[128,4096]{1,0:T(8,128)(2,1)S(1)}, bf16[128,4096]{1,0:T(8,128)(2,1)S(1)}, u32[]{:S(2)}, u32[]{:S(2)}) %collective-permute-start) | collective-permute-done | bytes 1048608 | tf_op jit(solution)/shard_map/ppermute | solution.py:341
  45.2 4.5 %collective-permute-start.1 = (bf16[128,4096]{1,0:T(8,128)(2,1)S(1)}, bf16[128,4096]{1,0:T(8,128)(2,1)S(1)}, u32[]{:S(2)}, u32[]{:S(2)}) collective-permute-start(bf16[128,4096]{1,0:T(8,128)(2,1)S(1)} %keep_states.2), channel_id=1, source_target_pairs={{0,8},{8,16},{16,24},{1,9},{9,17},{17,25},{2,10},{10,18},{18,26},{... | collective-permute-start | bytes 3145736 | tf_op jit(solution)/shard_map/ppermute | solution.py:343
  49.7 3.6 %inner.1.inner_ref = f32[128,4096]{1,0:T(8,128)S(1)} custom-call(s32[7]{0:T(128)S(1)} %pad_add_fusion.meta, f32[32,128]{1,0:T(8,128)S(1)} %bitcast.33, bf16[128,128]{1,0:T(8,128)(2,1)S(1)} %bitcast.46, bf16[128,128]{1,0:T(8,128)(2,1)S(1)} %bitcast.41, bf16[128,4096]{1,0:T(8,128)(2,1)S(1)} %bitcast.29), custom_call_target="tpu_custom_call" | custom-call | flops 268435456 | bytes 3145728 | tf_op jit(solution)/shard_map/inner/pallas_call | solution.py:347
  53.3 18.6 %collective-permute-done.1.refs_1_ = bf16[128,4096]{1,0:T(8,128)(2,1)S(1)} collective-permute-done((bf16[128,4096]{1,0:T(8,128)(2,1)S(1)}, bf16[128,4096]{1,0:T(8,128)(2,1)S(1)}, u32[]{:S(2)}, u32[]{:S(2)}) %collective-permute-start.1) | collective-permute-done | bytes 1048608 | tf_op jit(solution)/shard_map/ppermute | solution.py:343
  71.9 5.5 %resid.1 = (bf16[128,4096]{1,0:T(8,128)(2,1)S(1)}, bf16[384,4096]{1,0:T(8,128)(2,1)}, f32[128,128]{1,0:T(8,128)S(1)}) custom-call(s32[7]{0:T(128)S(1)} %pad_add_fusion.meta, f32[32,128]{1,0:T(8,128)S(1)} %bitcast.34, bf16[128,128]{1,0:T(8,128)(2,1)S(1)} %bitcast.42, bf16[384,128]{1,0:T(8,128)(2,1)S(1)} %get-tuple-element.16.pick_ref, ...), custom_call_target="tpu_custom_call" | custom-call | flops 671088640 | bytes 8388608 | tf_op jit(solution)/shard_map/resid/pallas_call | solution.py:351
  79.0 4.4 %all-to-all-start = ((bf16[8,48,4096]{2,1,0:T(8,128)(2,1)}), bf16[8,48,4096]{2,1,0:T(8,128)(2,1)}, u32[]{:S(2)}, u32[]{:S(2)}) async-start(bf16[8,48,4096]{2,1,0:T(8,128)(2,1)} %bitcast.55), calls=%async_computation | async-start | bytes 6291456 | tf_op jit(solution)/shard_map/all_to_all | solution.py:289
  83.4 6.9 %back.1.back_ref = f32[384,1024]{1,0:T(8,128)S(1)} custom-call(bf16[384,4096]{1,0:T(8,128)(2,1)S(1)} %bitcast.25, bf16[1024,4096]{1,0:T(8,128)(2,1)} %bitcast.53), custom_call_target="tpu_custom_call" | custom-call | flops 3221225472 | bytes 11534336 | tf_op jit(solution)/shard_map/back/pallas_call | solution.py:367
  91.5 29.8 %all-to-all-done = bf16[8,48,4096]{2,1,0:T(8,128)(2,1)} async-done(((bf16[8,48,4096]{2,1,0:T(8,128)(2,1)}), bf16[8,48,4096]{2,1,0:T(8,128)(2,1)}, u32[]{:S(2)}, u32[]{:S(2)}) %all-to-all-start) | async-done | bytes 3145760 | tf_op jit(solution)/shard_map/all_to_all | solution.py:289
  122.7 8.2 %up.1 = (bf16[384,1024]{1,0:T(8,128)(2,1)S(1)}, bf16[384,1024]{1,0:T(8,128)(2,1)S(1)}, f32[384,128]{1,0:T(8,128)S(1)}) custom-call(bf16[384,4096]{1,0:T(8,128)(2,1)} %bitcast.12.rows_ref, bf16[4096,1024]{1,0:T(8,128)(2,1)} %bitcast.51, f32[384,1024]{1,0:T(8,128)S(1)} %copy-done.4), custom_call_target="tpu_custom_call" | custom-call | flops 3221225472 | bytes 11534336 | tf_op jit(solution)/shard_map/up/pallas_call | solution.py:377
  130.9 8.1 %expert_grad.1 = bf16[384,4096]{1,0:T(8,128)(2,1)} custom-call(bf16[384,1024]{1,0:T(8,128)(2,1)S(1)} %get-tuple-element.22.pre_grad_ref, bf16[4096,1024]{1,0:T(8,128)(2,1)} %bitcast.52, bf16[384,4096]{1,0:T(8,128)(2,1)} %bitcast.12.rows_ref, f32[384,128]{1,0:T(8,128)S(1)} %get-tuple-element.23.along_ref), custom_call_target="tpu_custom_call" | custom-call | flops 3221225472 | bytes 11534336 | tf_op jit(solution)/shard_map/expert_grad/pallas_call | solution.py:392
  139.0 4.5 %all-to-all-start.3 = ((bf16[8,48,4096]{2,1,0:T(8,128)(2,1)}), bf16[8,48,4096]{2,1,0:T(8,128)(2,1)}, u32[]{:S(2)}, u32[]{:S(2)}) async-start(bf16[8,48,4096]{2,1,0:T(8,128)(2,1)} %bitcast.20), calls=%async_computation.3 | async-start | bytes 6291456 | tf_op jit(solution)/shard_map/all_to_all | solution.py:289
  143.5 6.5 %expert_out.1 = bf16[384,4096]{1,0:T(8,128)(2,1)S(1)} custom-call(bf16[384,1024]{1,0:T(8,128)(2,1)S(1)} %get-tuple-element.20.act_ref, bf16[1024,4096]{1,0:T(8,128)(2,1)} %bitcast.54), custom_call_target="tpu_custom_call" | custom-call | flops 3221225472 | bytes 11534336 | tf_op jit(solution)/shard_map/expert_out/pallas_call | solution.py:408
  151.6 29.8 %all-to-all-done.3 = bf16[8,48,4096]{2,1,0:T(8,128)(2,1)} async-done(((bf16[8,48,4096]{2,1,0:T(8,128)(2,1)}), bf16[8,48,4096]{2,1,0:T(8,128)(2,1)}, u32[]{:S(2)}, u32[]{:S(2)}) %all-to-all-start.3) | async-done | bytes 3145760 | tf_op jit(solution)/shard_map/all_to_all | solution.py:289
  181.4 3.8 %all-to-all-start.2 = ((bf16[8,48,4096]{2,1,0:T(8,128)(2,1)}), bf16[8,48,4096]{2,1,0:T(8,128)(2,1)S(1)}, u32[]{:S(2)}, u32[]{:S(2)}) async-start(bf16[8,48,4096]{2,1,0:T(8,128)(2,1)} %bitcast.27), calls=%async_computation.2 | async-start | bytes 6291456 | tf_op jit(solution)/shard_map/all_to_all | solution.py:289
  186.4 4.7 %dresid.1 = (bf16[128,4096]{1,0:T(8,128)(2,1)S(1)}, bf16[128,4096]{1,0:T(8,128)(2,1)S(1)}) custom-call(s32[7]{0:T(128)S(1)} %pad_add_fusion.meta, f32[32,128]{1,0:T(8,128)S(1)} %bitcast.35, bf16[128,128]{1,0:T(8,128)(2,1)S(1)} %bitcast.43, bf16[128,384]{1,0:T(8,128)(2,1)S(1)} %get-tuple-element.14.high_ref, bf16[128,384]{1,0:T(8,128)(2,1)S(1)} %get-tuple-element.15.low_ref, ...), custom_call_target="tpu_custom_call" | custom-call | flops 939524096 | bytes 6291456 | tf_op jit(solution)/shard_map/dresid/pallas_call | solution.py:421
  192.4 26.8 %collective-permute-done.2.state_ref.refs_0_ = bf16[128,4096]{1,0:T(8,128)(2,1)S(1)} collective-permute-done((bf16[128,4096]{1,0:T(8,128)(2,1)S(1)}, bf16[128,4096]{1,0:T(8,128)(2,1)S(1)}, u32[]{:S(2)}, u32[]{:S(2)}) %collective-permute-start.2) | collective-permute-done | bytes 1048608 | tf_op jit(solution)/shard_map/ppermute | solution.py:341
  219.2 3.2 %keep_states.3 = bf16[128,4096]{1,0:T(8,128)(2,1)} custom-call(s32[7]{0:T(128)S(1)} %pad_add_fusion.meta, f32[32,128]{1,0:T(8,128)S(1)} %bitcast.36, bf16[128,4096]{1,0:T(8,128)(2,1)S(1)} %collective-permute-done.2.state_ref.refs_0_), custom_call_target="tpu_custom_call" | custom-call | flops 524288 | bytes 2097152 | tf_op jit(solution)/shard_map/keep_states/pallas_call | solution.py:343
  223.7 3.6 %inner_back.1.inner_ref = f32[128,4096]{1,0:T(8,128)S(1)} custom-call(s32[7]{0:T(128)S(1)} %pad_add_fusion.meta, f32[32,128]{1,0:T(8,128)S(1)} %bitcast.37, bf16[128,128]{1,0:T(8,128)(2,1)S(1)} %bitcast.47, bf16[128,128]{1,0:T(8,128)(2,1)S(1)} %bitcast.44, bf16[128,4096]{1,0:T(8,128)(2,1)S(1)} %get-tuple-element.24.grad_ref), custom_call_target="tpu_custom_call" | custom-call | flops 268435456 | bytes 3145728 | tf_op jit(solution)/shard_map/inner_back/pallas_call | solution.py:432
  230.0 3.0 %output.1 = bf16[128,4096]{1,0:T(8,128)(2,1)} custom-call(bf16[128,384]{1,0:T(8,128)(2,1)S(1)} %get-tuple-element.14.high_ref, bf16[128,384]{1,0:T(8,128)(2,1)S(1)} %get-tuple-element.15.low_ref, bf16[128,4096]{1,0:T(8,128)(2,1)S(1)} %copy-done.14, bf16[384,4096]{1,0:T(8,128)(2,1)S(1)} %bitcast.26), custom_call_target="tpu_custom_call" | custom-call | flops 805306368 | bytes 5242880 | tf_op jit(solution)/shard_map/output/pallas_call | solution.py:452
  233.0 16.4 %collective-permute-done.3.refs_1_ = bf16[128,4096]{1,0:T(8,128)(2,1)} collective-permute-done((bf16[128,4096]{1,0:T(8,128)(2,1)}, bf16[128,4096]{1,0:T(8,128)(2,1)}, u32[]{:S(2)}, u32[]{:S(2)}) %collective-permute-start.3) | collective-permute-done | bytes 1048608 | tf_op jit(solution)/shard_map/ppermute | solution.py:343
  249.4 4.9 %input_grad.1 = bf16[128,4096]{1,0:T(8,128)(2,1)} custom-call(s32[7]{0:T(128)S(1)} %pad_add_fusion.meta, f32[32,128]{1,0:T(8,128)S(1)} %bitcast.38, bf16[128,128]{1,0:T(8,128)(2,1)S(1)} %bitcast.48, f32[128,4096]{1,0:T(8,128)S(1)} %copy-done.2, bf16[128,4096]{1,0:T(8,128)(2,1)S(1)} %copy-done.8, bf16[128,4096]{1,0:T(8,128)(2,1)} %collective-permute-done.3.refs_1_), custom_call_target="tpu_custom_call" | custom-call | flops 268435456 | bytes 5242880 | tf_op jit(solution)/shard_map/input_grad/pallas_call | solution.py:442
  (51 shorter events, 22.0 us)
Async XLA Ops:
  0.6 1.2 copy-start.11
  5.2 1.6 copy-start.9
  6.8 5.3 %copy-start.21 = (s32[1,6]{1,0:T(1,128)S(1)}, s32[1,6]{1,0:T(1,128)}, u32[]{:S(2)}) copy-start(s32[1,6]{1,0:T(1,128)} %param.14) | copy-start | bytes 76
  6.8 5.4 %copy-start.10 = (f32[1,32,128]{2,1,0:T(8,128)S(1)}, f32[1,32,128]{2,1,0:T(8,128)}, u32[]{:S(2)}) copy-start(f32[1,32,128]{2,1,0:T(8,128)} %param.13) | copy-start | bytes 49156
  6.8 5.4 %copy-start.16 = (bf16[1,128,128]{2,1,0:T(8,128)(2,1)S(1)}, bf16[1,128,128]{2,1,0:T(8,128)(2,1)}, u32[]{:S(2)}) copy-start(bf16[1,128,128]{2,1,0:T(8,128)(2,1)} %param.11) | copy-start | bytes 98308
  6.8 42.8 %copy-start.15 = (bf16[1,128,128]{2,1,0:T(8,128)(2,1)S(1)}, bf16[1,128,128]{2,1,0:T(8,128)(2,1)}, u32[]{:S(2)}) copy-start(bf16[1,128,128]{2,1,0:T(8,128)(2,1)} %param.12) | copy-start | bytes 98308
  6.9 72.1 %all-to-all-start.1 = ((bf16[8,48,4096]{2,1,0:T(8,128)(2,1)}), bf16[8,48,4096]{2,1,0:T(8,128)(2,1)S(1)}, u32[]{:S(2)}, u32[]{:S(2)}) async-start(bf16[8,48,4096]{2,1,0:T(8,128)(2,1)} %bitcast.30), calls=%async_computation.1 | async-start | bytes 6291456 | tf_op jit(solution)/shard_map/all_to_all | solution.py:289
  13.5 36.2 %copy-start.6 = (bf16[1,128,4096]{2,1,0:T(8,128)(2,1)S(1)}, bf16[1,128,4096]{2,1,0:T(8,128)(2,1)}, u32[]{:S(2)}) copy-start(bf16[1,128,4096]{2,1,0:T(8,128)(2,1)} %param.10) | copy-start | bytes 3145732
  16.5 26.6 %collective-permute-start = (bf16[128,4096]{1,0:T(8,128)(2,1)S(1)}, bf16[128,4096]{1,0:T(8,128)(2,1)S(1)}, u32[]{:S(2)}, u32[]{:S(2)}) collective-permute-start(bf16[128,4096]{1,0:T(8,128)(2,1)S(1)} %local_states.1), channel_id=1, source_target_pairs={{0,8},{8,16},{16,24},{1,9},{9,17},{17,25},{2,10},{10,18},{18,26},{... | collective-permute-start | bytes 3145736 | tf_op jit(solution)/shard_map/ppermute | solution.py:341
  45.2 26.7 %collective-permute-start.1 = (bf16[128,4096]{1,0:T(8,128)(2,1)S(1)}, bf16[128,4096]{1,0:T(8,128)(2,1)S(1)}, u32[]{:S(2)}, u32[]{:S(2)}) collective-permute-start(bf16[128,4096]{1,0:T(8,128)(2,1)S(1)} %keep_states.2), channel_id=1, source_target_pairs={{0,8},{8,16},{16,24},{1,9},{9,17},{17,25},{2,10},{10,18},{18,26},{... | collective-permute-start | bytes 3145736 | tf_op jit(solution)/shard_map/ppermute | solution.py:343
  79.0 42.3 %all-to-all-start = ((bf16[8,48,4096]{2,1,0:T(8,128)(2,1)}), bf16[8,48,4096]{2,1,0:T(8,128)(2,1)}, u32[]{:S(2)}, u32[]{:S(2)}) async-start(bf16[8,48,4096]{2,1,0:T(8,128)(2,1)} %bitcast.55), calls=%async_computation | async-start | bytes 6291456 | tf_op jit(solution)/shard_map/all_to_all | solution.py:289
  121.3 1.4 copy-start.4
  139.0 42.4 %all-to-all-start.3 = ((bf16[8,48,4096]{2,1,0:T(8,128)(2,1)}), bf16[8,48,4096]{2,1,0:T(8,128)(2,1)}, u32[]{:S(2)}, u32[]{:S(2)}) async-start(bf16[8,48,4096]{2,1,0:T(8,128)(2,1)} %bitcast.20), calls=%async_computation.3 | async-start | bytes 6291456 | tf_op jit(solution)/shard_map/all_to_all | solution.py:289
  149.9 1.6 copy-start
  181.4 3.8 %copy-start.18 = (f32[128,128]{1,0:T(8,128)S(1)}, f32[128,128]{1,0:T(8,128)}, u32[]{:S(2)}) copy-start(f32[128,128]{1,0:T(8,128)} %copy-done.17) | copy-start | bytes 196612
  181.4 47.3 %all-to-all-start.2 = ((bf16[8,48,4096]{2,1,0:T(8,128)(2,1)}), bf16[8,48,4096]{2,1,0:T(8,128)(2,1)S(1)}, u32[]{:S(2)}, u32[]{:S(2)}) async-start(bf16[8,48,4096]{2,1,0:T(8,128)(2,1)} %bitcast.27), calls=%async_computation.2 | async-start | bytes 6291456 | tf_op jit(solution)/shard_map/all_to_all | solution.py:289
  185.2 1.2 copy-start.12
  191.1 28.1 %collective-permute-start.2 = (bf16[128,4096]{1,0:T(8,128)(2,1)S(1)}, bf16[128,4096]{1,0:T(8,128)(2,1)S(1)}, u32[]{:S(2)}, u32[]{:S(2)}) collective-permute-start(bf16[128,4096]{1,0:T(8,128)(2,1)S(1)} %get-tuple-element.25), channel_id=1, source_target_pairs={{8,0},{16,8},{24,16},{9,1},{17,9},{25,17},{10,2},{18,10},{26,18},{... | collective-permute-start | bytes 3145736 | tf_op jit(solution)/shard_map/ppermute | solution.py:341
  219.2 4.5 %copy-start.7 = (bf16[128,4096]{1,0:T(8,128)(2,1)}, bf16[128,4096]{1,0:T(8,128)(2,1)S(1)}, u32[]{:S(2)}) copy-start(bf16[128,4096]{1,0:T(8,128)(2,1)S(1)} %collective-permute-done.2.state_ref.refs_0_) | copy-start | bytes 3145732
  222.4 27.1 %collective-permute-start.3 = (bf16[128,4096]{1,0:T(8,128)(2,1)}, bf16[128,4096]{1,0:T(8,128)(2,1)}, u32[]{:S(2)}, u32[]{:S(2)}) collective-permute-start(bf16[128,4096]{1,0:T(8,128)(2,1)} %keep_states.3), channel_id=1, source_target_pairs={{8,0},{16,8},{24,16},{9,1},{17,9},{25,17},{10,2},{18,10},{26,18},{... | collective-permute-start | bytes 3145736 | tf_op jit(solution)/shard_map/ppermute | solution.py:343
  227.3 1.3 copy-start.1
  228.6 20.8 %copy-start.2 = (f32[128,4096]{1,0:T(8,128)S(1)}, f32[128,4096]{1,0:T(8,128)}, u32[]{:S(2)}) copy-start(f32[128,4096]{1,0:T(8,128)} %copy-done.1) | copy-start | bytes 6291460
  228.6 20.8 %copy-start.8 = (bf16[128,4096]{1,0:T(8,128)(2,1)S(1)}, bf16[128,4096]{1,0:T(8,128)(2,1)}, u32[]{:S(2)}) copy-start(bf16[128,4096]{1,0:T(8,128)(2,1)} %copy-done.7) | copy-start | bytes 3145732
  228.6 1.4 copy-start.14
  (6 other events, 5.3 us)

commit v2 on v1

v2 whole, which is shorter than its diff:
```python
import functools

import jax
import jax.numpy as jnp
from jax import lax
from jax.experimental import pallas as pl
from jax.experimental.pallas import tpu as pltpu
from jax.sharding import PartitionSpec as P

EPSILON = 1e-06
F32 = jnp.float32
BF16 = jnp.bfloat16
CHUNKS = 2
VMEM_BYTES = 32 * 1024 * 1024
NT = (((1,), (1,)), ((), ()))


def dot(a, b):
    return jnp.dot(a, b, preferred_element_type=F32)


def dot_nt(a, b):
    return lax.dot_general(a, b, NT, preferred_element_type=F32)


def call(kernel, grid, in_specs, out_specs, out_shape, flops, nbytes, name, scratch=()):
    return pl.pallas_call(
        kernel,
        grid=grid,
        in_specs=in_specs,
        out_specs=out_specs,
        out_shape=out_shape,
        scratch_shapes=scratch,
        name=name,
        cost_estimate=pl.CostEstimate(flops=flops, bytes_accessed=nbytes, transcendentals=0),
        compiler_params=pltpu.CompilerParams(vmem_limit_bytes=VMEM_BYTES),
    )


def whole(shape):
    return pl.BlockSpec(shape, lambda i: (0,) * len(shape))


def columns(rows, width):
    return pl.BlockSpec((rows, width), lambda i: (0, i))


SMEM = pl.BlockSpec(memory_space=pltpu.SMEM)


def documents(meta, rows, size):
    count = meta.shape[0] - 1
    first = meta[count]
    along = first + lax.broadcasted_iota(jnp.int32, (1, size), 1)
    down = first + lax.broadcasted_iota(jnp.int32, (size, 1), 0)
    row = jnp.full((1, size), -1, jnp.int32)
    col = jnp.full((size, 1), -1, jnp.int32)
    before, last, start = jnp.int32(-1), jnp.int32(-1), jnp.int32(0)
    for i in range(count):
        row += (start <= along).astype(jnp.int32)
        col += (start <= down).astype(jnp.int32)
        before += (start <= first - 1).astype(jnp.int32)
        last += (start <= first + size - 1).astype(jnp.int32)
        start = start + meta[i]
    return row, col, before, last


def running(log_ref):
    size = log_ref.shape[1]
    upto = (
        lax.broadcasted_iota(jnp.int32, (size, size), 0)
        <= lax.broadcasted_iota(jnp.int32, (size, size), 1)
    ).astype(F32)
    return jnp.dot(
        log_ref[...], upto, precision=lax.Precision.HIGHEST, preferred_element_type=F32
    )


def head(h, size):
    return slice(h * size, (h + 1) * size)


def local_kernel(meta, log_ref, b_ref, x_ref, state_ref):
    size = log_ref.shape[1]
    cum = running(log_ref)
    row, _, _, last = documents(meta, cum.shape[0], size)
    tail = (row == last).astype(F32)
    weight = tail * jnp.exp(cum[:, size - 1 :] - cum)
    b_t = b_ref[...].astype(F32).T
    p = x_ref.shape[1] // cum.shape[0]
    for h in range(cum.shape[0]):
        b_weighted = (b_t * weight[h : h + 1, :]).astype(BF16)
        state_ref[:, head(h, p)] = dot(b_weighted, x_ref[:, head(h, p)]).astype(BF16)


def pair_mask(meta, size):
    row, col, before, last = documents(meta, size, size)
    later = lax.broadcasted_iota(jnp.int32, (size, size), 0)
    earlier = lax.broadcasted_iota(jnp.int32, (size, size), 1)
    return row, col, before, last, later, earlier


def inner_kernel(meta, log_ref, b_ref, c_ref, x_ref, out_ref):
    size = log_ref.shape[1]
    cum = running(log_ref)
    cum_t = cum.T
    row, col, _, _, down, along = pair_mask(meta, size)
    scores = jnp.where((row == col) & (down >= along), dot_nt(c_ref[...], b_ref[...]), 0.0)
    p = x_ref.shape[1] // cum.shape[0]
    for h in range(cum.shape[0]):
        spread = cum_t[:, h : h + 1] - cum[h : h + 1, :]
        pair = (jnp.exp(jnp.minimum(spread, 0.0)) * scores).astype(BF16)
        out_ref[:, head(h, p)] = dot(pair, x_ref[:, head(h, p)])


def inner_back_kernel(meta, log_ref, b_ref, c_ref, grad_ref, out_ref):
    size = log_ref.shape[1]
    cum = running(log_ref)
    cum_t = cum.T
    row, col, _, _, down, along = pair_mask(meta, size)
    scores = jnp.where((row == col) & (down <= along), dot_nt(b_ref[...], c_ref[...]), 0.0)
    p = grad_ref.shape[1] // cum.shape[0]
    for h in range(cum.shape[0]):
        spread = cum[h : h + 1, :] - cum_t[:, h : h + 1]
        pair = (jnp.exp(jnp.minimum(spread, 0.0)) * scores).astype(BF16)
        out_ref[:, head(h, p)] = dot(pair, grad_ref[:, head(h, p)])


def keep_kernel(meta, log_ref, state_ref, out_ref):
    size = log_ref.shape[1]
    total = jnp.exp(running(log_ref)[:, size - 1 :])
    _, _, before, last = documents(meta, 1, size)
    total = jnp.where(before == last, total, 0.0)
    p = state_ref.shape[1] // total.shape[0]
    for h in range(total.shape[0]):
        out_ref[:, head(h, p)] = (
            state_ref[:, head(h, p)].astype(F32) * total[h : h + 1, :]
        ).astype(BF16)


def resid_kernel(hops, meta, log_ref, c_ref, inner_ref, *refs):
    states, (resid_ref, squares_ref) = refs[:hops], refs[hops:]
    size = log_ref.shape[1]
    _, col, before, _ = documents(meta, size, size)
    weight = jnp.where(col == before, jnp.exp(running(log_ref).T), 0.0)
    p = inner_ref.shape[1] // log_ref.shape[0]
    squares = jnp.zeros((size, p), F32)
    for h in range(log_ref.shape[0]):
        carried = dot(c_ref[...], states[0][:, head(h, p)])
        for state in states[1:]:
            carried += dot(c_ref[...], state[:, head(h, p)])
        rows = (inner_ref[:, head(h, p)] + weight[:, h : h + 1] * carried).astype(BF16)
        resid_ref[:, head(h, p)] = rows
        squares += rows.astype(F32) * rows.astype(F32)
    squares_ref[...] = jnp.broadcast_to(jnp.sum(squares, axis=1, keepdims=True), squares_ref.shape)


def combined(weights_ref, pieces):
    total = dot(weights_ref[0], pieces[0][...])
    for i, piece in enumerate(pieces[1:]):
        total += dot(weights_ref[i + 1], piece[...])
    return total


def relay_kernel(weights_ref, *refs):
    pieces, out_ref = refs[:-1], refs[-1]
    out_ref[...] = combined(weights_ref, pieces).astype(BF16)


def dresid_kernel(chunks, features, meta, log_ref, c_ref, weights_ref, cot_ref, *refs):
    squares, refs = refs[:chunks], refs[chunks:]
    moved_refs, (dresid_ref, source_ref) = refs[:-2], refs[-2:]
    size = log_ref.shape[1]
    row, _, before, _ = documents(meta, size, size)
    weight = jnp.where(row == before, jnp.exp(running(log_ref)), 0.0)
    c_t = c_ref[...].astype(F32).T
    total = squares[0][...]
    for part in squares[1:]:
        total = total + part[...]
    scale = lax.rsqrt(total[:, :1] / features + EPSILON)
    count = weights_ref.shape[0]
    moved = combined(weights_ref, moved_refs[:count])
    for arrived in moved_refs[count:]:
        moved += arrived[...].astype(F32)
    dresid_ref[...] = (cot_ref[...].astype(F32) + scale * moved).astype(BF16)
    p = cot_ref.shape[1] // log_ref.shape[0]
    for h in range(log_ref.shape[0]):
        c_weighted = (c_t * weight[h : h + 1, :]).astype(BF16)
        source_ref[:, head(h, p)] = dot(c_weighted, dresid_ref[:, head(h, p)]).astype(BF16)


def grad_kernel(hops, meta, log_ref, b_ref, inner_ref, *refs):
    states, out_ref = refs[:hops], refs[-1]
    size = log_ref.shape[1]
    _, col, _, last = documents(meta, size, size)
    cum = running(log_ref)
    weight = jnp.where(col == last, jnp.exp(cum[:, size - 1 :] - cum).T, 0.0)
    p = inner_ref.shape[1] // log_ref.shape[0]
    for h in range(log_ref.shape[0]):
        carried = dot(b_ref[...], states[0][:, head(h, p)])
        for state in states[1:]:
            carried += dot(b_ref[...], state[:, head(h, p)])
        out_ref[:, head(h, p)] = (inner_ref[:, head(h, p)] + weight[:, h : h + 1] * carried).astype(BF16)


def output_kernel(weights_ref, resid_ref, *refs):
    out_ref = refs[-1]
    count = weights_ref.shape[0]
    moved = combined(weights_ref, refs[:count])
    for arrived in refs[count : len(refs) - 1]:
        if arrived.shape == out_ref.shape:
            moved += arrived[...].astype(F32)
    out_ref[...] = (resid_ref[...].astype(F32) + moved).astype(BF16)


def picks_of(table, me, experts, capacity):
    tokens = table.shape[1]
    offset = lax.broadcasted_iota(jnp.int32, (experts, tokens), 0)
    first = (table[0:1, :].astype(jnp.int32) ^ me) == offset
    second = (table[1:2, :].astype(jnp.int32) ^ me) == offset
    named = (first | second).astype(F32)
    gate = jnp.where(first, table[2:3, :], 0.0) + jnp.where(second, table[3:4, :], 0.0)
    before = (
        lax.broadcasted_iota(jnp.int32, (tokens, tokens), 0)
        < lax.broadcasted_iota(jnp.int32, (tokens, tokens), 1)
    ).astype(BF16)
    rank = jnp.where(named > 0, dot(named.astype(BF16), before), -1.0)
    slot = lax.broadcasted_iota(jnp.int32, (capacity, tokens), 0).astype(F32)
    picks = [(rank[e : e + 1, :] == slot).astype(F32) for e in range(experts)]
    return picks, [pick * gate[e : e + 1, :] for e, pick in enumerate(picks)]


def direct_pick_kernel(experts, capacity, table_ref, pick_ref, weights_ref):
    picks, gated = picks_of(table_ref[...], 0, experts, capacity)
    pick_ref[...] = jnp.concatenate(picks, axis=0).astype(BF16)
    weights_ref[0] = jnp.concatenate(gated, axis=0).T.astype(BF16)


def relay_pick_kernel(experts, capacity, kinds, me_ref, own_ref, *refs):
    tables, outs = refs[: len(kinds)], refs[len(kinds) :]
    me = me_ref[0]
    picks, gated = picks_of(own_ref[...], me, experts, capacity)
    none = jnp.zeros_like(picks[0])
    for (_, offsets), table_ref, (pick_ref, own_weights_ref, relay_weights_ref) in zip(
        kinds, tables, (outs[:3], outs[3:])
    ):
        other_picks, other_gated = picks_of(table_ref[...], me, experts, capacity)
        for i, o in enumerate(offsets):
            pick_ref[i, 0] = picks[o].astype(BF16)
            pick_ref[i, 1] = other_picks[o].astype(BF16)
            own_weights_ref[i] = jnp.concatenate([gated[o], none], axis=0).T.astype(BF16)
            relay_weights_ref[i] = jnp.concatenate([none, other_gated[o]], axis=0).T.astype(BF16)


def gather_kernel(pick_ref, own_ref, other_ref, *outs):
    capacity = pick_ref.shape[2]
    for i, out in enumerate(outs):
        out[:capacity, :] = dot(pick_ref[i, 0], own_ref[...]).astype(BF16)
        out[capacity:, :] = dot(pick_ref[i, 1], other_ref[...]).astype(BF16)


def direct_gather_kernel(pick_ref, own_ref, out_ref):
    out_ref[...] = dot(pick_ref[...], own_ref[...]).astype(BF16)


def assemble(plan, pieces, rows):
    for piece, at, to, count in plan:
        rows[to : to + count, :] = pieces[piece][at : at + count, :]


def back_kernel(plans, *refs):
    counts = [max(b[0] for b in plan) + 1 for plan in plans]
    pieces, (down_ref, back_ref, rows) = refs[: sum(counts)], refs[sum(counts) :]
    step, each = pl.program_id(0), pl.num_programs(0) // len(plans)
    for k, plan in enumerate(plans):
        mine = pieces[sum(counts[:k]) : sum(counts[: k + 1])]

        @pl.when(step // each == k)
        def _(plan=plan, mine=mine):
            assemble(plan, mine, rows)

    part = dot_nt(rows[...], down_ref[...])

    @pl.when(step == 0)
    def _():
        back_ref[...] = part

    @pl.when(step > 0)
    def _():
        back_ref[...] += part


def up_first_kernel(plan, *refs):
    pieces, (up_ref, total_ref, squares_ref, rows) = refs[:-4], refs[-4:]
    assemble(plan, pieces, rows)
    part = dot(rows[...], up_ref[...])
    values = rows[...].astype(F32)
    square = jnp.broadcast_to(jnp.sum(values * values, axis=1, keepdims=True), squares_ref.shape)

    @pl.when(pl.program_id(0) == 0)
    def _():
        total_ref[...] = part
        squares_ref[...] = square

    @pl.when(pl.program_id(0) > 0)
    def _():
        total_ref[...] += part
        squares_ref[...] += square


def up_last_kernel(plan, features, *refs):
    count = max(b[0] for b in plan) + 1
    pieces = refs[:count]
    up_ref, before_ref, before_squares_ref, back_ref, act_ref, pre_grad_ref, along_ref, total, squares, rows = refs[count:]
    step, steps = pl.program_id(0), pl.num_programs(0)
    assemble(plan, pieces, rows)
    part = dot(rows[...], up_ref[...])
    values = rows[...].astype(F32)
    square = jnp.broadcast_to(jnp.sum(values * values, axis=1, keepdims=True), squares.shape)

    @pl.when(step == 0)
    def _():
        total[...] = before_ref[...] + part
        squares[...] = before_squares_ref[...] + square

    @pl.when(step > 0)
    def _():
        total[...] += part
        squares[...] += square

    @pl.when(step == steps - 1)
    def _():
        scale = lax.rsqrt(squares[:, :1] / features + EPSILON)
        pre = total[...] * scale
        gate = jax.nn.sigmoid(pre)
        act_ref[...] = (pre * gate).astype(BF16)
        pre_grad = (back_ref[...] * gate * (1.0 + pre * (1.0 - gate))).astype(BF16)
        pre_grad_ref[...] = pre_grad
        along = jnp.sum(pre_grad.astype(F32) * pre, axis=1, keepdims=True)
        along_ref[...] = jnp.broadcast_to(scale * along / features, along_ref.shape)


def expert_grad_kernel(plan, pre_grad_ref, up_ref, along_ref, *refs):
    count = len(refs) // 2
    total = dot_nt(pre_grad_ref[...], up_ref[...])
    for piece, at, to, size in plan:
        rows = refs[piece][at : at + size, :].astype(F32)
        refs[count + piece][at : at + size, :] = (
            total[to : to + size, :] - rows * along_ref[to : to + size, :1]
        ).astype(BF16)


def expert_out_kernel(plan, act_ref, down_ref, *outs):
    total = dot(act_ref[...], down_ref[...])
    for piece, at, to, size in plan:
        outs[piece][at : at + size, :] = total[to : to + size, :].astype(BF16)


def on_device(inputs, b_proj, c_proj, log_decay, doc_lengths, expert_ids, gate_weights, w_up, w_down, cotangent):
    tokens, features = inputs.shape[1:]
    heads = log_decay.shape[1]
    state = b_proj.shape[2]
    experts, blocks = lax.axis_size("exp"), lax.axis_size("seq")
    hidden = w_up.shape[2]
    capacity = 3 * tokens // experts
    slots = experts * capacity
    width = features // CHUNKS
    hops = max(1, blocks // 2)
    relayed = experts == 8
    kinds = ((2, (0, 1, 4, 5)), (4, (0, 1, 2, 3)))

    x, b, c, log, cot = inputs[0], b_proj[0], c_proj[0], log_decay[0], cotangent[0]
    up, down = w_up[0], w_down[0]
    meta = jnp.concatenate([doc_lengths[0], (lax.axis_index("seq") * tokens)[None].astype(jnp.int32)])

    def log_spec(k):
        return pl.BlockSpec((heads // CHUNKS, tokens), lambda i: (k, 0))

    def chunk(k, rows=tokens):
        return pl.BlockSpec((rows, width), lambda i: (0, k))

    def shape(rows, columns, kind=BF16):
        return jax.ShapeDtypeStruct((rows, columns), kind)

    small, part = whole((tokens, state)), whole((tokens, width))
    unit = tokens * width
    head_flops = 2 * tokens * unit

    def offset(a, k):
        return lax.ppermute(a, "exp", [(i, i ^ k) for i in range(experts)])

    def passed(states, step, k):
        pairs = [(i, i + step) for i in range(blocks) if 0 <= i + step < blocks]
        arrived = [lax.ppermute(states, "seq", pairs)]
        for _ in range(hops - 1):
            kept = call(
                keep_kernel, (1,), [SMEM, log_spec(k), part], part, shape(tokens, width), unit, 4 * unit, "keep_states"
            )(meta, log, arrived[-1])
            arrived.append(lax.ppermute(kept, "seq", pairs))
        return arrived

    states_in, local = [], None
    for k in range(CHUNKS):
        local = call(
            local_kernel,
            (1,),
            [SMEM, log_spec(k), small, chunk(k)],
            part,
            shape(tokens, width),
            head_flops,
            4 * unit,
            "local_states",
        )(meta, log, b, x)
        states_in.append(passed(local, 1, k))

    table = jnp.concatenate([expert_ids[0].T.astype(F32), gate_weights[0].T], axis=0)
    table, cot, _ = lax.optimization_barrier((table, cot, local))
    if relayed:
        plans = [
            [
                block
                for i, o in enumerate(offsets)
                for block in ((i, 0, o * capacity, capacity), (i, capacity, (o ^ by) * capacity, capacity))
            ]
            for by, offsets in kinds
        ]
        pieces_of = [[2 * capacity] * 4] * 2
        pick_shape = (4, 2, capacity, tokens)
        weight_shape = (4, tokens, 2 * capacity)
        outs = [pick_shape, weight_shape, weight_shape] * 2
        me = lax.axis_index("exp").astype(jnp.int32)[None]
        found = call(
            functools.partial(relay_pick_kernel, experts, capacity, kinds),
            (1,),
            [SMEM] + [whole((4, tokens))] * 3,
            [whole(s) for s in outs],
            [jax.ShapeDtypeStruct(s, BF16) for s in outs],
            6 * experts * tokens * tokens,
            4 * slots * tokens,
            "pick_rows",
        )(me, table, *[offset(table, by) for by, _ in kinds])
        picks, own_weights, relay_weights = found[0::3], found[1::3], found[2::3]
    else:
        plans = [[(0, 0, 0, slots)]] * 2
        pieces_of = [[slots]] * 2
        pick, weights = call(
            functools.partial(direct_pick_kernel, experts, capacity),
            (1,),
            [whole((4, tokens))],
            [whole((slots, tokens)), whole((1, tokens, slots))],
            [shape(slots, tokens), jax.ShapeDtypeStruct((1, tokens, slots), BF16)],
            2 * experts * tokens * tokens,
            4 * slots * tokens,
            "pick_rows",
        )(table)
        picks, own_weights = [pick] * 2, [weights] * 2

    def piece_specs(kind):
        return [whole((rows, width)) for rows in pieces_of[kind]]

    def piece_shapes(kind):
        return [shape(rows, width) for rows in pieces_of[kind]]

    def switch(pieces):
        parts = pieces[0].reshape(experts, capacity, width)
        return [lax.all_to_all(parts, "exp", split_axis=0, concat_axis=0, tiled=True).reshape(slots, width)]

    def to_experts(rows, k, spec):
        kind = k % 2
        cost = (2 * slots * unit, 2 * (unit + slots * width))
        if not relayed:
            sent = call(
                direct_gather_kernel, (1,), [whole((slots, tokens)), spec], piece_specs(kind), piece_shapes(kind), *cost, "gather"
            )(picks[kind], rows)
            return switch(sent)
        by, offsets = kinds[kind]
        chunk_rows = rows if rows.shape[1] == width else rows[:, k * width : (k + 1) * width]
        other = offset(chunk_rows, by)
        sent = call(
            gather_kernel,
            (1,),
            [whole(picks[kind].shape), part, part],
            piece_specs(kind),
            piece_shapes(kind),
            *cost,
            "gather",
        )(picks[kind], chunk_rows, other)
        return [piece if o == 0 else offset(piece, o) for piece, o in zip(sent, offsets)]

    def to_positions(pieces, k):
        kind = k % 2
        if not relayed:
            return switch(pieces)
        by, offsets = kinds[kind]
        pieces = [piece if o == 0 else offset(piece, o) for piece, o in zip(pieces, offsets)]
        relay = call(
            relay_kernel,
            (1,),
            [whole(relay_weights[kind].shape)] + piece_specs(kind),
            part,
            shape(tokens, width),
            2 * slots * unit,
            2 * (unit + slots * width),
            "relay",
        )(relay_weights[kind], *pieces)
        return pieces + [offset(relay, by)]

    def moved_specs(kind):
        return piece_specs(kind) + ([part] if relayed else [])

    got_cot = [to_experts(cot, k, chunk(k)) for k in range(CHUNKS)]

    inner = call(
        inner_kernel,
        (CHUNKS,),
        [SMEM, pl.BlockSpec((heads // CHUNKS, tokens), lambda i: (i, 0)), small, small, columns(tokens, width)],
        columns(tokens, width),
        shape(tokens, features, F32),
        2 * CHUNKS * head_flops,
        6 * CHUNKS * unit,
        "inner",
    )(meta, log, b, c, x)

    resid, squares, got_in = [], [], []
    for k in range(CHUNKS):
        rows, square = call(
            functools.partial(resid_kernel, hops),
            (1,),
            [SMEM, log_spec(k), small, chunk(k)] + [part] * hops,
            [part, whole((tokens, 128))],
            [shape(tokens, width), shape(tokens, 128, F32)],
            hops * head_flops,
            (6 + 2 * hops) * unit,
            "resid",
        )(meta, log, c, inner, *states_in[k])
        resid.append(rows)
        squares.append(square)
        got_in.append(to_experts(rows, k, part))

    each = 2
    step = width // each
    chunk_flops = 2 * slots * width * hidden
    chunk_bytes = 2 * width * (hidden + slots)
    slots_hidden = whole((slots, hidden))

    def step_specs(kind, first=0):
        return [
            pl.BlockSpec((rows, step), lambda i: (0, jnp.clip(i - first, 0, each - 1))) for rows in pieces_of[kind]
        ]

    back = call(
        functools.partial(back_kernel, [plans[k % 2] for k in range(CHUNKS)]),
        (each * CHUNKS,),
        [spec for k in range(CHUNKS) for spec in step_specs(k % 2, each * k)] + [columns(hidden, step)],
        slots_hidden,
        shape(slots, hidden, F32),
        CHUNKS * chunk_flops,
        CHUNKS * chunk_bytes,
        "back",
        [pltpu.VMEM((slots, step), BF16)],
    )(*[piece for pieces in got_cot for piece in pieces], down)

    def up_spec(k):
        return pl.BlockSpec((step, hidden), lambda i: (each * k + i, 0))

    slots_small = whole((slots, 128))
    total, total_squares = call(
        functools.partial(up_first_kernel, plans[0]),
        (each,),
        step_specs(0) + [up_spec(0)],
        [slots_hidden, slots_small],
        [shape(slots, hidden, F32), shape(slots, 128, F32)],
        chunk_flops,
        chunk_bytes,
        "up_first",
        [pltpu.VMEM((slots, step), BF16)],
    )(*got_in[0], up)
    act, pre_grad, along = call(
        functools.partial(up_last_kernel, plans[1], features),
        (each,),
        step_specs(1) + [up_spec(1), slots_hidden, slots_small, slots_hidden],
        [slots_hidden, slots_hidden, slots_small],
        [shape(slots, hidden), shape(slots, hidden), shape(slots, 128, F32)],
        chunk_flops,
        chunk_bytes,
        "up_last",
        [pltpu.VMEM((slots, hidden), F32), pltpu.VMEM((slots, 128), F32), pltpu.VMEM((slots, step), BF16)],
    )(*got_in[1], up, total, total_squares, back)

    got_grad = []
    for k in range(CHUNKS):
        kind = k % 2
        expert_grad = call(
            functools.partial(expert_grad_kernel, plans[kind]),
            (each,),
            [slots_hidden, up_spec(k), slots_small] + step_specs(kind),
            step_specs(kind),
            piece_shapes(kind),
            chunk_flops,
            chunk_bytes,
            "expert_grad",
        )(pre_grad, up, along, *got_in[k])
        got_grad.append(to_positions(expert_grad, k))
    got_out = []
    for k in range(CHUNKS):
        kind = k % 2
        expert_out = call(
            functools.partial(expert_out_kernel, plans[kind]),
            (each,),
            [slots_hidden, pl.BlockSpec((hidden, step), lambda i, k=k: (0, each * k + i))],
            step_specs(kind),
            piece_shapes(kind),
            chunk_flops,
            chunk_bytes,
            "expert_out",
        )(act, down)
        got_out.append(to_positions(expert_out, k))

    def weights_spec(kind):
        return whole(own_weights[kind].shape)

    dresid, states_after = [], []
    for k in range(CHUNKS):
        kind = k % 2
        grad, source = call(
            functools.partial(dresid_kernel, CHUNKS, features),
            (1,),
            [SMEM, log_spec(k), small, weights_spec(kind), chunk(k)]
            + [whole((tokens, 128))] * CHUNKS
            + moved_specs(kind),
            [part, part],
            [shape(tokens, width)] * 2,
            head_flops + 2 * slots * unit,
            6 * unit + 2 * slots * width,
            "dresid",
        )(meta, log, c, own_weights[kind], cotangent[0], *squares, *got_grad[k])
        dresid.append(grad)
        states_after.append(passed(source, -1, k))

    into = chunk
    anywhere = pl.BlockSpec(memory_space=pl.ANY)

    def placed(kernel, k, in_specs, operands, earlier, flops, nbytes, name):
        more = [] if earlier is None else [earlier]
        return pl.pallas_call(
            kernel,
            grid=(1,),
            in_specs=in_specs + [anywhere] * len(more),
            out_specs=into(k),
            out_shape=shape(tokens, features),
            input_output_aliases={len(operands): 0} if more else {},
            name=name,
            cost_estimate=pl.CostEstimate(flops=flops, bytes_accessed=nbytes, transcendentals=0),
            compiler_params=pltpu.CompilerParams(vmem_limit_bytes=VMEM_BYTES),
        )(*operands, *more)

    input_grad = output = None
    for k in range(CHUNKS):
        inner_back = call(
            inner_back_kernel,
            (1,),
            [SMEM, log_spec(k), small, small, part],
            part,
            shape(tokens, width, F32),
            2 * head_flops,
            6 * unit,
            "inner_back",
        )(meta, log, b, c, dresid[k])
        input_grad = placed(
            functools.partial(grad_kernel, hops),
            k,
            [SMEM, log_spec(k), small, part] + [part] * hops,
            [meta, log, b, inner_back, *states_after[k]],
            input_grad,
            hops * head_flops,
            (6 + 2 * hops) * unit,
            "input_grad",
        )
    for k in range(CHUNKS):
        kind = k % 2
        output = placed(
            output_kernel,
            k,
            [weights_spec(kind), part] + moved_specs(kind),
            [own_weights[kind], resid[k], *got_out[k]],
            output,
            2 * slots * unit,
            4 * unit + 2 * slots * width,
            "output",
        )
    return (output[None], input_grad[None])


def solution(mesh):
    placed = (
        P("exp", "seq", None),
        P("exp", "seq", None),
        P("exp", "seq", None),
        P("exp", None, "seq"),
        P("exp", None),
        P("exp", "seq", None),
        P("exp", "seq", None),
        P("exp", None, None),
        P("exp", None, None),
        P("exp", "seq", None),
    )
    return jax.shard_map(
        on_device,
        mesh=mesh,
        in_specs=placed,
        out_specs=(P("exp", "seq", None), P("exp", "seq", None)),
        check_vma=False,
    )
```

time: 255 us -> 229 us (0.90)
  waiting for transfers between devices: 144 us -> 106 us
  starting transfers between devices: 28.6 us -> 52.4 us
  local copies, waits for them, and re-layouts: 15.2 us -> 8.93 us
  Pallas kernels: 65.2 us -> 59 us
    ppermute x2 -> x38, waiting for transfers between devices: 35 us -> 95.3 us  [the longest x34 83.2 us: offset(): return lax.ppermute(a, 'exp', [(i, i ^ k) for i in range(experts)])]
    all_to_all x4 -> x0, waiting for transfers between devices: 59.6 us -> none  [exchange(): lax.all_to_all(parts, 'exp', split_axis=0, concat_axis=0, tiled=True)]
    ppermute x2 -> x4, waiting for transfers between devices: 49.8 us -> 10.8 us  [passed(): arrived = [lax.ppermute(states, 'seq', pairs)]]
    ppermute x2 -> x38, starting transfers between devices: 5.73 us -> 41.4 us  [the longest x34 29 us: offset(): return lax.ppermute(a, 'exp', [(i, i ^ k) for i in range(experts)])]
    all_to_all x4 -> x0, starting transfers between devices: 18 us -> none  [exchange(): lax.all_to_all(parts, 'exp', split_axis=0, concat_axis=0, tiled=True)]
    unnamed x44 -> x54, local copies, waits for them, and re-layouts: 15.2 us -> 7.87 us
    pallas_call x14 -> x33, Pallas kernels: 65.2 us -> 59 us  [the longest x4 8.35 us: placed(): pl.pallas_call(kernel, grid=(1,), in_specs=in_specs + [anywhere] * len(mo...]
    ppermute x2 -> x4, starting transfers between devices: 4.84 us -> 11 us  [passed(): arrived = [lax.ppermute(states, 'seq', pairs)]]
  transfers between devices with their start and end apart: 8 -> 42, of which waited for: 6 -> 23; matrix products, arithmetic and copies ran while one was open for 0% -> 0% of each run, Pallas kernels for 17% -> 22%
where the time goes in v2:
time: 229 us; the launch traced here: 228 us
  waiting for transfers between devices  106 us (46%)
  Pallas kernels  59 us (26%)
  starting transfers between devices  52.4 us (23%)
  local copies, waits for them, and re-layouts  8.93 us (4%)
    ppermute x34, waiting for transfers between devices, offset(): return lax.ppermute(a, 'exp', [(i, i ^ k) for i in range(experts)])  83.2 us
    ppermute x34, starting transfers between devices, offset(): return lax.ppermute(a, 'exp', [(i, i ^ k) for i in range(experts)])  29 us
    ppermute x4, starting transfers between devices, passed(): arrived.append(lax.ppermute(kept, 'seq', pairs))  12.4 us
    ppermute x4, waiting for transfers between devices, passed(): arrived.append(lax.ppermute(kept, 'seq', pairs))  12.1 us
    ppermute x4, starting transfers between devices, passed(): arrived = [lax.ppermute(states, 'seq', pairs)]  11 us
    ppermute x4, waiting for transfers between devices, passed(): arrived = [lax.ppermute(states, 'seq', pairs)]  10.8 us
    pallas_call x4, Pallas kernels, placed(): pl.pallas_call(kernel, grid=(1,), in_specs=in_specs + [anywhere] * len(mo...  8.35 us
    unnamed x54, local copies, waits for them, and re-layouts  7.87 us
  transfers between devices with their start and end apart: 42, of which 23 were waited for; matrix products, arithmetic and copies ran while one was open for 0% of the time, Pallas kernels for 22%

profile of v2, /device:TPU:0, one launch (start us, length us, event | category | flops | bytes accessed | tf_op | source)
XLA Modules:
  0.0 228.5 jit_solution(12917706065164207792)
XLA Ops:
  5.3 5.0 %collective-permute-start.8 = (bf16[128,2048]{1,0:T(8,128)(2,1)S(1)}, bf16[128,2048]{1,0:T(8,128)(2,1)S(1)}, u32[]{:S(2)}, u32[]{:S(2)}) collective-permute-start(bf16[128,2048]{1,0:T(8,128)(2,1)S(1)} %local_states.3), channel_id=1, source_target_pairs={{0,8},{8,16},{16,24},{1,9},{9,17},{17,25},{2,10},{10,18},{18,26},{... | collective-permute-start | bytes 1572872 | tf_op jit(solution)/shard_map/ppermute | solution.py:394
  11.5 3.5 %collective-permute-start.2 = (bf16[128,2048]{1,0:T(8,128)(2,1)S(1)}, bf16[128,2048]{1,0:T(8,128)(2,1)S(1)}, u32[]{:S(2)}, u32[]{:S(2)}) collective-permute-start(bf16[128,2048]{1,0:T(8,128)(2,1)S(1)} %local_states.2), channel_id=1, source_target_pairs={{0,8},{8,16},{16,24},{1,9},{9,17},{17,25},{2,10},{10,18},{18,26},{... | collective-permute-start | bytes 1572872 | tf_op jit(solution)/shard_map/ppermute | solution.py:394
  15.0 7.5 %collective-permute-done.8.state_ref.refs_0_ = bf16[128,2048]{1,0:T(8,128)(2,1)S(1)} collective-permute-done((bf16[128,2048]{1,0:T(8,128)(2,1)S(1)}, bf16[128,2048]{1,0:T(8,128)(2,1)S(1)}, u32[]{:S(2)}, u32[]{:S(2)}) %collective-permute-start.8) | collective-permute-done | bytes 524320 | tf_op jit(solution)/shard_map/ppermute | solution.py:394
  23.5 4.4 %collective-permute-start.9 = (bf16[128,2048]{1,0:T(8,128)(2,1)S(1)}, bf16[128,2048]{1,0:T(8,128)(2,1)S(1)}, u32[]{:S(2)}, u32[]{:S(2)}) collective-permute-start(bf16[128,2048]{1,0:T(8,128)(2,1)S(1)} %keep_states.5), channel_id=1, source_target_pairs={{0,8},{8,16},{16,24},{1,9},{9,17},{17,25},{2,10},{10,18},{18,26},{... | collective-permute-start | bytes 1572872 | tf_op jit(solution)/shard_map/ppermute | solution.py:399
  30.5 3.3 %collective-permute-done.2.state_ref.refs_0_ = bf16[128,2048]{1,0:T(8,128)(2,1)S(1)} collective-permute-done((bf16[128,2048]{1,0:T(8,128)(2,1)S(1)}, bf16[128,2048]{1,0:T(8,128)(2,1)S(1)}, u32[]{:S(2)}, u32[]{:S(2)}) %collective-permute-start.2) | collective-permute-done | bytes 524320 | tf_op jit(solution)/shard_map/ppermute | solution.py:394
  35.5 5.2 %collective-permute-start.3 = (bf16[128,2048]{1,0:T(8,128)(2,1)}, bf16[128,2048]{1,0:T(8,128)(2,1)}, u32[]{:S(2)}, u32[]{:S(2)}) collective-permute-start(bf16[128,2048]{1,0:T(8,128)(2,1)} %keep_states.4), channel_id=1, source_target_pairs={{0,8},{8,16},{16,24},{1,9},{9,17},{17,25},{2,10},{10,18},{18,26},{... | collective-permute-start | bytes 1572872 | tf_op jit(solution)/shard_map/ppermute | solution.py:399
  52.8 10.9 %collective-permute-done.refs_0_ = f32[4,128]{1,0:T(4,128)S(1)} collective-permute-done((f32[4,128]{1,0:T(4,128)S(1)}, f32[4,128]{1,0:T(4,128)S(1)}, u32[]{:S(2)}, u32[]{:S(2)}) %collective-permute-start) | collective-permute-done | bytes 2080 | tf_op jit(solution)/shard_map/ppermute | solution.py:390
  79.1 7.0 %collective-permute-done.21.refs_7_ = bf16[96,2048]{1,0:T(8,128)(2,1)S(1)} collective-permute-done((bf16[96,2048]{1,0:T(8,128)(2,1)S(1)}, bf16[96,2048]{1,0:T(8,128)(2,1)S(1)}, u32[]{:S(2)}, u32[]{:S(2)}) %collective-permute-start.21) | collective-permute-done | bytes 393248 | tf_op jit(solution)/shard_map/ppermute | solution.py:390
  88.9 5.9 %collective-permute-done.16.refs_2_ = bf16[96,2048]{1,0:T(8,128)(2,1)S(1)} collective-permute-done((bf16[96,2048]{1,0:T(8,128)(2,1)S(1)}, bf16[96,2048]{1,0:T(8,128)(2,1)S(1)}, u32[]{:S(2)}, u32[]{:S(2)}) %collective-permute-start.16) | collective-permute-done | bytes 393248 | tf_op jit(solution)/shard_map/ppermute | solution.py:390
  94.8 7.5 %collective-permute-done.17.refs_3_ = bf16[96,2048]{1,0:T(8,128)(2,1)S(1)} collective-permute-done((bf16[96,2048]{1,0:T(8,128)(2,1)S(1)}, bf16[96,2048]{1,0:T(8,128)(2,1)S(1)}, u32[]{:S(2)}, u32[]{:S(2)}) %collective-permute-start.17) | collective-permute-done | bytes 393248 | tf_op jit(solution)/shard_map/ppermute | solution.py:390
  104.4 3.4 %copy-done = bf16[1,1024,4096]{2,1,0:T(8,128)(2,1)S(1)} copy-done((bf16[1,1024,4096]{2,1,0:T(8,128)(2,1)S(1)}, bf16[1,1024,4096]{2,1,0:T(8,128)(2,1)}, u32[]{:S(2)}) %copy-start) | copy-done | bytes 8388632
  107.8 5.8 %back.1.refs_7_ = f32[384,1024]{1,0:T(8,128)S(1)} custom-call(bf16[96,2048]{1,0:T(8,128)(2,1)S(1)} %get-tuple-element.72.refs_0_, bf16[96,2048]{1,0:T(8,128)(2,1)S(1)} %collective-permute-done.15.refs_1_, bf16[96,2048]{1,0:T(8,128)(2,1)S(1)} %collective-permute-done.16.refs_2_, bf16[96,2048]{1,0:T(8,128)(2,1)S(1)} %collective-permute-done.17.refs_3_, ...), custom_call_target="tpu_custom_call" | custom-call | flops 3221225472 | bytes 11534336 | tf_op jit(solution)/shard_map/back/pallas_call | solution.py:551
  113.6 5.4 %collective-permute-done.13.refs_3_ = bf16[96,2048]{1,0:T(8,128)(2,1)S(1)} collective-permute-done((bf16[96,2048]{1,0:T(8,128)(2,1)S(1)}, bf16[96,2048]{1,0:T(8,128)(2,1)S(1)}, u32[]{:S(2)}, u32[]{:S(2)}) %collective-permute-start.13) | collective-permute-done | bytes 393248 | tf_op jit(solution)/shard_map/ppermute | solution.py:390
  122.3 3.4 %up_last.1 = (bf16[384,1024]{1,0:T(8,128)(2,1)S(1)}, bf16[384,1024]{1,0:T(8,128)(2,1)S(1)}, f32[384,128]{1,0:T(8,128)S(1)}) custom-call(bf16[96,2048]{1,0:T(8,128)(2,1)S(1)} %get-tuple-element.59.refs_0_, bf16[96,2048]{1,0:T(8,128)(2,1)S(1)} %collective-permute-done.5.refs_1_, bf16[96,2048]{1,0:T(8,128)(2,1)S(1)} %collective-permute-done.6.refs_2_, ...), custom_call_target="tpu_custom_call" | custom-call | flops 1610612736 | bytes 5767168 | tf_op jit(solution)/shard_map/up_last/pallas_call | solution.py:578
  125.8 2.5 %expert_grad.3 = (bf16[96,2048]{1,0:T(8,128)(2,1)S(1)}, bf16[96,2048]{1,0:T(8,128)(2,1)S(1)}, bf16[96,2048]{1,0:T(8,128)(2,1)S(1)}, bf16[96,2048]{1,0:T(8,128)(2,1)S(1)}) custom-call(bf16[384,1024]{1,0:T(8,128)(2,1)S(1)} %get-tuple-element.94.pre_grad_ref, bf16[4096,1024]{1,0:T(8,128)(2,1)S(1)} %bitcast.23, f32[384,128]{1,0:T(8,128)S(1)} %get-tuple-element.95.along_ref, ...), custom_call_target="tpu_custom_call" | custom-call | flops 1610612736 | bytes 5767168 | tf_op jit(solution)/shard_map/expert_grad/pallas_call | solution.py:593
  134.6 5.8 %collective-permute-done.37.refs_2_.refs_4_ = bf16[96,2048]{1,0:T(8,128)(2,1)S(1)} collective-permute-done((bf16[96,2048]{1,0:T(8,128)(2,1)S(1)}, bf16[96,2048]{1,0:T(8,128)(2,1)S(1)}, u32[]{:S(2)}, u32[]{:S(2)}) %collective-permute-start.37) | collective-permute-done | bytes 393248 | tf_op jit(solution)/shard_map/ppermute | solution.py:390
  140.4 7.5 %collective-permute-done.38.refs_3_.refs_5_ = bf16[96,2048]{1,0:T(8,128)(2,1)S(1)} collective-permute-done((bf16[96,2048]{1,0:T(8,128)(2,1)S(1)}, bf16[96,2048]{1,0:T(8,128)(2,1)S(1)}, u32[]{:S(2)}, u32[]{:S(2)}) %collective-permute-start.38) | collective-permute-done | bytes 393248 | tf_op jit(solution)/shard_map/ppermute | solution.py:390
  159.5 4.5 %collective-permute-done.39.refs_6_ = bf16[128,2048]{1,0:T(8,128)(2,1)S(1)} collective-permute-done((bf16[128,2048]{1,0:T(8,128)(2,1)S(1)}, bf16[128,2048]{1,0:T(8,128)(2,1)S(1)}, u32[]{:S(2)}, u32[]{:S(2)}) %collective-permute-start.39) | collective-permute-done | bytes 524320 | tf_op jit(solution)/shard_map/ppermute | solution.py:390
  173.5 3.0 %collective-permute-done.27.refs_2_ = bf16[96,2048]{1,0:T(8,128)(2,1)S(1)} collective-permute-done((bf16[96,2048]{1,0:T(8,128)(2,1)S(1)}, bf16[96,2048]{1,0:T(8,128)(2,1)S(1)}, u32[]{:S(2)}, u32[]{:S(2)}) %collective-permute-start.27) | collective-permute-done | bytes 393248 | tf_op jit(solution)/shard_map/ppermute | solution.py:390
  177.0 7.6 %collective-permute-done.28.refs_3_ = bf16[96,2048]{1,0:T(8,128)(2,1)S(1)} collective-permute-done((bf16[96,2048]{1,0:T(8,128)(2,1)S(1)}, bf16[96,2048]{1,0:T(8,128)(2,1)S(1)}, u32[]{:S(2)}, u32[]{:S(2)}) %collective-permute-start.28) | collective-permute-done | bytes 393248 | tf_op jit(solution)/shard_map/ppermute | solution.py:390
  187.3 8.3 %collective-permute-done.24.refs_3_ = bf16[96,2048]{1,0:T(8,128)(2,1)S(1)} collective-permute-done((bf16[96,2048]{1,0:T(8,128)(2,1)S(1)}, bf16[96,2048]{1,0:T(8,128)(2,1)S(1)}, u32[]{:S(2)}, u32[]{:S(2)}) %collective-permute-start.24) | collective-permute-done | bytes 393248 | tf_op jit(solution)/shard_map/ppermute | solution.py:390
  207.2 2.5 %output.2.refs_5_ = bf16[128,4096]{1,0:T(8,128)(2,1)} custom-call(bf16[4,128,96]{2,1,0:T(8,128)(2,1)S(1)} %copy-done.20, bf16[128,2048]{1,0:T(8,128)(2,1)} %get-tuple-element.64.own_ref.resid_ref, bf16[96,2048]{1,0:T(8,128)(2,1)S(1)} %get-tuple-element.87.refs_0_, bf16[96,2048]{1,0:T(8,128)(2,1)S(1)} %collective-permute-done.26.refs_1_, ...), custom_call_target="tpu_custom_call" | custom-call | flops 201326592 | bytes 2621440 | tf_op jit(solution)/shard_map/output/pallas_call | solution.py:645
  212.3 3.2 %collective-permute-done.41.refs_1_ = bf16[128,2048]{1,0:T(8,128)(2,1)S(1)} collective-permute-done((bf16[128,2048]{1,0:T(8,128)(2,1)S(1)}, bf16[128,2048]{1,0:T(8,128)(2,1)S(1)}, u32[]{:S(2)}, u32[]{:S(2)}) %collective-permute-start.41) | collective-permute-done | bytes 524320 | tf_op jit(solution)/shard_map/ppermute | solution.py:399
  217.7 8.6 %collective-permute-done.35.refs_1_ = bf16[128,2048]{1,0:T(8,128)(2,1)S(1)} collective-permute-done((bf16[128,2048]{1,0:T(8,128)(2,1)S(1)}, bf16[128,2048]{1,0:T(8,128)(2,1)S(1)}, u32[]{:S(2)}, u32[]{:S(2)}) %collective-permute-start.35) | collective-permute-done | bytes 524320 | tf_op jit(solution)/shard_map/ppermute | solution.py:399
  (153 shorter events, 95.7 us)
Async XLA Ops:
  11.5 22.3 %collective-permute-start.2 = (bf16[128,2048]{1,0:T(8,128)(2,1)S(1)}, bf16[128,2048]{1,0:T(8,128)(2,1)S(1)}, u32[]{:S(2)}, u32[]{:S(2)}) collective-permute-start(bf16[128,2048]{1,0:T(8,128)(2,1)S(1)} %local_states.2), channel_id=1, source_target_pairs={{0,8},{8,16},{16,24},{1,9},{9,17},{17,25},{2,10},{10,18},{18,26},{... | collective-permute-start | bytes 1572872 | tf_op jit(solution)/shard_map/ppermute | solution.py:394
  23.5 21.5 %collective-permute-start.9 = (bf16[128,2048]{1,0:T(8,128)(2,1)S(1)}, bf16[128,2048]{1,0:T(8,128)(2,1)S(1)}, u32[]{:S(2)}, u32[]{:S(2)}) collective-permute-start(bf16[128,2048]{1,0:T(8,128)(2,1)S(1)} %keep_states.5), channel_id=1, source_target_pairs={{0,8},{8,16},{16,24},{1,9},{9,17},{17,25},{2,10},{10,18},{18,26},{... | collective-permute-start | bytes 1572872 | tf_op jit(solution)/shard_map/ppermute | solution.py:399
  29.0 35.6 %collective-permute-start.18 = (bf16[128,2048]{1,0:T(8,128)(2,1)}, bf16[128,2048]{1,0:T(8,128)(2,1)}, u32[]{:S(2)}, u32[]{:S(2)}) collective-permute-start(bf16[128,2048]{1,0:T(8,128)(2,1)} %get-tuple-element.108.own_ref), channel_id=1, source_target_pairs={{0,4},{1,5},{2,6},{3,7},{4,0},{5,1},{6,2},{7,3},{8,12},{9,13},{10,... | collective-permute-start | bytes 1572872 | tf_op jit(solution)/shard_map/ppermute | solution.py:390
  35.5 32.6 %collective-permute-start.3 = (bf16[128,2048]{1,0:T(8,128)(2,1)}, bf16[128,2048]{1,0:T(8,128)(2,1)}, u32[]{:S(2)}, u32[]{:S(2)}) collective-permute-start(bf16[128,2048]{1,0:T(8,128)(2,1)} %keep_states.4), channel_id=1, source_target_pairs={{0,8},{8,16},{16,24},{1,9},{9,17},{17,25},{2,10},{10,18},{18,26},{... | collective-permute-start | bytes 1572872 | tf_op jit(solution)/shard_map/ppermute | solution.py:399
  40.7 30.8 %collective-permute-start.14 = (bf16[128,2048]{1,0:T(8,128)(2,1)}, bf16[128,2048]{1,0:T(8,128)(2,1)}, u32[]{:S(2)}, u32[]{:S(2)}) collective-permute-start(bf16[128,2048]{1,0:T(8,128)(2,1)} %get-tuple-element.109.own_ref), channel_id=1, source_target_pairs={{0,2},{1,3},{2,0},{3,1},{4,6},{5,7},{6,4},{7,5},{8,10},{9,11},{10,... | collective-permute-start | bytes 1572872 | tf_op jit(solution)/shard_map/ppermute | solution.py:390
  47.2 27.9 %collective-permute-start.10 = (bf16[128,2048]{1,0:T(8,128)(2,1)}, bf16[128,2048]{1,0:T(8,128)(2,1)}, u32[]{:S(2)}, u32[]{:S(2)}) collective-permute-start(bf16[128,2048]{1,0:T(8,128)(2,1)} %get-tuple-element.64.own_ref.resid_ref), channel_id=1, source_target_pairs={{0,2},{1,3},{2,0},{3,1},{4,6},{5,7},{6,4},{7,5},{8,10},{9,11},{10,... | collective-permute-start | bytes 1572872 | tf_op jit(solution)/shard_map/ppermute | solution.py:390
  68.2 17.9 %collective-permute-start.21 = (bf16[96,2048]{1,0:T(8,128)(2,1)S(1)}, bf16[96,2048]{1,0:T(8,128)(2,1)S(1)}, u32[]{:S(2)}, u32[]{:S(2)}) collective-permute-start(bf16[96,2048]{1,0:T(8,128)(2,1)S(1)} %get-tuple-element.79), channel_id=1, source_target_pairs={{0,3},{1,2},{2,1},{3,0},{4,7},{5,6},{6,5},{7,4},{8,11},{9,10},{10,... | collective-permute-start | bytes 1179656 | tf_op jit(solution)/shard_map/ppermute | solution.py:390
  77.2 17.6 %collective-permute-start.16 = (bf16[96,2048]{1,0:T(8,128)(2,1)S(1)}, bf16[96,2048]{1,0:T(8,128)(2,1)S(1)}, u32[]{:S(2)}, u32[]{:S(2)}) collective-permute-start(bf16[96,2048]{1,0:T(8,128)(2,1)S(1)} %get-tuple-element.74), channel_id=1, source_target_pairs={{0,4},{1,5},{2,6},{3,7},{4,0},{5,1},{6,2},{7,3},{8,12},{9,13},{10,... | collective-permute-start | bytes 1179656 | tf_op jit(solution)/shard_map/ppermute | solution.py:390
  78.6 23.7 %collective-permute-start.17 = (bf16[96,2048]{1,0:T(8,128)(2,1)S(1)}, bf16[96,2048]{1,0:T(8,128)(2,1)S(1)}, u32[]{:S(2)}, u32[]{:S(2)}) collective-permute-start(bf16[96,2048]{1,0:T(8,128)(2,1)S(1)} %get-tuple-element.75), channel_id=1, source_target_pairs={{0,5},{1,4},{2,7},{3,6},{4,1},{5,0},{6,3},{7,2},{8,13},{9,12},{10,... | collective-permute-start | bytes 1179656 | tf_op jit(solution)/shard_map/ppermute | solution.py:390
  86.1 17.6 %collective-permute-start.11 = (bf16[96,2048]{1,0:T(8,128)(2,1)S(1)}, bf16[96,2048]{1,0:T(8,128)(2,1)S(1)}, u32[]{:S(2)}, u32[]{:S(2)}) collective-permute-start(bf16[96,2048]{1,0:T(8,128)(2,1)S(1)} %get-tuple-element.66), channel_id=1, source_target_pairs={{0,1},{1,0},{2,3},{3,2},{4,5},{5,4},{6,7},{7,6},{8,9},{9,8},{10,11... | collective-permute-start | bytes 1179656 | tf_op jit(solution)/shard_map/ppermute | solution.py:390
  86.7 26.9 %collective-permute-start.12 = (bf16[96,2048]{1,0:T(8,128)(2,1)S(1)}, bf16[96,2048]{1,0:T(8,128)(2,1)S(1)}, u32[]{:S(2)}, u32[]{:S(2)}) collective-permute-start(bf16[96,2048]{1,0:T(8,128)(2,1)S(1)} %get-tuple-element.67), channel_id=1, source_target_pairs={{0,4},{1,5},{2,6},{3,7},{4,0},{5,1},{6,2},{7,3},{8,12},{9,13},{10,... | collective-permute-start | bytes 1179656 | tf_op jit(solution)/shard_map/ppermute | solution.py:390
  88.2 30.7 %collective-permute-start.13 = (bf16[96,2048]{1,0:T(8,128)(2,1)S(1)}, bf16[96,2048]{1,0:T(8,128)(2,1)S(1)}, u32[]{:S(2)}, u32[]{:S(2)}) collective-permute-start(bf16[96,2048]{1,0:T(8,128)(2,1)S(1)} %get-tuple-element.68), channel_id=1, source_target_pairs={{0,5},{1,4},{2,7},{3,6},{4,1},{5,0},{6,3},{7,2},{8,13},{9,12},{10,... | collective-permute-start | bytes 1179656 | tf_op jit(solution)/shard_map/ppermute | solution.py:390
  94.8 26.6 %collective-permute-start.5 = (bf16[96,2048]{1,0:T(8,128)(2,1)S(1)}, bf16[96,2048]{1,0:T(8,128)(2,1)S(1)}, u32[]{:S(2)}, u32[]{:S(2)}) collective-permute-start(bf16[96,2048]{1,0:T(8,128)(2,1)S(1)} %get-tuple-element.60), channel_id=1, source_target_pairs={{0,1},{1,0},{2,3},{3,2},{4,5},{5,4},{6,7},{7,6},{8,9},{9,8},{10,11... | collective-permute-start | bytes 1179656 | tf_op jit(solution)/shard_map/ppermute | solution.py:390
  102.3 19.1 %collective-permute-start.6 = (bf16[96,2048]{1,0:T(8,128)(2,1)S(1)}, bf16[96,2048]{1,0:T(8,128)(2,1)S(1)}, u32[]{:S(2)}, u32[]{:S(2)}) collective-permute-start(bf16[96,2048]{1,0:T(8,128)(2,1)S(1)} %get-tuple-element.61), channel_id=1, source_target_pairs={{0,2},{1,3},{2,0},{3,1},{4,6},{5,7},{6,4},{7,5},{8,10},{9,11},{10,... | collective-permute-start | bytes 1179656 | tf_op jit(solution)/shard_map/ppermute | solution.py:390
  103.8 18.5 %collective-permute-start.7 = (bf16[96,2048]{1,0:T(8,128)(2,1)S(1)}, bf16[96,2048]{1,0:T(8,128)(2,1)S(1)}, u32[]{:S(2)}, u32[]{:S(2)}) collective-permute-start(bf16[96,2048]{1,0:T(8,128)(2,1)S(1)} %get-tuple-element.62), channel_id=1, source_target_pairs={{0,3},{1,2},{2,1},{3,0},{4,7},{5,6},{6,5},{7,4},{8,11},{9,10},{10,... | collective-permute-start | bytes 1179656 | tf_op jit(solution)/shard_map/ppermute | solution.py:390
  130.2 17.7 %collective-permute-start.38 = (bf16[96,2048]{1,0:T(8,128)(2,1)S(1)}, bf16[96,2048]{1,0:T(8,128)(2,1)S(1)}, u32[]{:S(2)}, u32[]{:S(2)}) collective-permute-start(bf16[96,2048]{1,0:T(8,128)(2,1)S(1)} %get-tuple-element.105), channel_id=1, source_target_pairs={{0,5},{1,4},{2,7},{3,6},{4,1},{5,0},{6,3},{7,2},{8,13},{9,12},{10,... | collective-permute-start | bytes 1179656 | tf_op jit(solution)/shard_map/ppermute | solution.py:390
  132.7 17.5 %collective-permute-start.30 = (bf16[96,2048]{1,0:T(8,128)(2,1)S(1)}, bf16[96,2048]{1,0:T(8,128)(2,1)S(1)}, u32[]{:S(2)}, u32[]{:S(2)}) collective-permute-start(bf16[96,2048]{1,0:T(8,128)(2,1)S(1)} %get-tuple-element.97), channel_id=1, source_target_pairs={{0,1},{1,0},{2,3},{3,2},{4,5},{5,4},{6,7},{7,6},{8,9},{9,8},{10,11... | collective-permute-start | bytes 1179656 | tf_op jit(solution)/shard_map/ppermute | solution.py:390
  134.6 17.9 %collective-permute-start.32 = (bf16[96,2048]{1,0:T(8,128)(2,1)S(1)}, bf16[96,2048]{1,0:T(8,128)(2,1)S(1)}, u32[]{:S(2)}, u32[]{:S(2)}) collective-permute-start(bf16[96,2048]{1,0:T(8,128)(2,1)S(1)} %get-tuple-element.99), channel_id=1, source_target_pairs={{0,3},{1,2},{2,1},{3,0},{4,7},{5,6},{6,5},{7,4},{8,11},{9,10},{10,... | collective-permute-start | bytes 1179656 | tf_op jit(solution)/shard_map/ppermute | solution.py:390
  158.0 18.5 %collective-permute-start.27 = (bf16[96,2048]{1,0:T(8,128)(2,1)S(1)}, bf16[96,2048]{1,0:T(8,128)(2,1)S(1)}, u32[]{:S(2)}, u32[]{:S(2)}) collective-permute-start(bf16[96,2048]{1,0:T(8,128)(2,1)S(1)} %get-tuple-element.89), channel_id=1, source_target_pairs={{0,4},{1,5},{2,6},{3,7},{4,0},{5,1},{6,2},{7,3},{8,12},{9,13},{10,... | collective-permute-start | bytes 1179656 | tf_op jit(solution)/shard_map/ppermute | solution.py:390
  158.4 26.2 %collective-permute-start.28 = (bf16[96,2048]{1,0:T(8,128)(2,1)S(1)}, bf16[96,2048]{1,0:T(8,128)(2,1)S(1)}, u32[]{:S(2)}, u32[]{:S(2)}) collective-permute-start(bf16[96,2048]{1,0:T(8,128)(2,1)S(1)} %get-tuple-element.90), channel_id=1, source_target_pairs={{0,5},{1,4},{2,7},{3,6},{4,1},{5,0},{6,3},{7,2},{8,13},{9,12},{10,... | collective-permute-start | bytes 1179656 | tf_op jit(solution)/shard_map/ppermute | solution.py:390
  165.6 32.4 %collective-permute-start.40 = (bf16[128,2048]{1,0:T(8,128)(2,1)S(1)}, bf16[128,2048]{1,0:T(8,128)(2,1)S(1)}, u32[]{:S(2)}, u32[]{:S(2)}) collective-permute-start(bf16[128,2048]{1,0:T(8,128)(2,1)S(1)} %get-tuple-element.107), channel_id=1, source_target_pairs={{8,0},{16,8},{24,16},{9,1},{17,9},{25,17},{10,2},{18,10},{26,18},{... | collective-permute-start | bytes 1572872 | tf_op jit(solution)/shard_map/ppermute | solution.py:394
  169.7 30.6 %collective-permute-start.34 = (bf16[128,2048]{1,0:T(8,128)(2,1)S(1)}, bf16[128,2048]{1,0:T(8,128)(2,1)S(1)}, u32[]{:S(2)}, u32[]{:S(2)}) collective-permute-start(bf16[128,2048]{1,0:T(8,128)(2,1)S(1)} %get-tuple-element.101), channel_id=1, source_target_pairs={{8,0},{16,8},{24,16},{9,1},{17,9},{25,17},{10,2},{18,10},{26,18},{... | collective-permute-start | bytes 1572872 | tf_op jit(solution)/shard_map/ppermute | solution.py:394
  185.9 21.4 %collective-permute-start.29 = (bf16[128,2048]{1,0:T(8,128)(2,1)S(1)}, bf16[128,2048]{1,0:T(8,128)(2,1)S(1)}, u32[]{:S(2)}, u32[]{:S(2)}) collective-permute-start(bf16[128,2048]{1,0:T(8,128)(2,1)S(1)} %relay.5), channel_id=1, source_target_pairs={{0,2},{1,3},{2,0},{3,1},{4,6},{5,7},{6,4},{7,5},{8,10},{9,11},{10,... | collective-permute-start | bytes 1572872 | tf_op jit(solution)/shard_map/ppermute | solution.py:390
  201.2 25.1 %collective-permute-start.35 = (bf16[128,2048]{1,0:T(8,128)(2,1)S(1)}, bf16[128,2048]{1,0:T(8,128)(2,1)S(1)}, u32[]{:S(2)}, u32[]{:S(2)}) collective-permute-start(bf16[128,2048]{1,0:T(8,128)(2,1)S(1)} %keep_states.6), channel_id=1, source_target_pairs={{8,0},{16,8},{24,16},{9,1},{17,9},{25,17},{10,2},{18,10},{26,18},{... | collective-permute-start | bytes 1572872 | tf_op jit(solution)/shard_map/ppermute | solution.py:399
  (45 other events, 598.1 us)

commit v3 on v2

--- a/solution.py
+++ b/solution.py
@@ -23,18 +23,25 @@
     return lax.dot_general(a, b, NT, preferred_element_type=F32)
 
 
-def call(kernel, grid, in_specs, out_specs, out_shape, flops, nbytes, name, scratch=()):
-    return pl.pallas_call(
-        kernel,
+def call(kernel, grid, in_specs, out_specs, out_shape, flops, nbytes, name, scratch=(), after=(), aliases=None):
+    count, more = len(in_specs), len(after)
+
+    def body(*refs):
+        kernel(*refs[:count], *refs[count + more :])
+
+    called = pl.pallas_call(
+        body,
         grid=grid,
-        in_specs=in_specs,
+        in_specs=list(in_specs) + [pl.BlockSpec(memory_space=pl.ANY)] * more,
         out_specs=out_specs,
         out_shape=out_shape,
         scratch_shapes=scratch,
+        input_output_aliases=aliases or {},
         name=name,
         cost_estimate=pl.CostEstimate(flops=flops, bytes_accessed=nbytes, transcendentals=0),
         compiler_params=pltpu.CompilerParams(vmem_limit_bytes=VMEM_BYTES),
     )
+    return lambda *operands: called(*operands, *after)
 
 
 def whole(shape):
@@ -80,7 +87,8 @@
     return slice(h * size, (h + 1) * size)
 
 
-def local_kernel(meta, log_ref, b_ref, x_ref, state_ref):
+def local_kernel(meta, log_ref, b_ref, x_ref, cot_ref, state_ref, chunk_ref):
+    chunk_ref[...] = cot_ref[...]
     size = log_ref.shape[1]
     cum = running(log_ref)
     row, _, _, last = documents(meta, cum.shape[0], size)
@@ -389,32 +397,41 @@
     def offset(a, k):
         return lax.ppermute(a, "exp", [(i, i ^ k) for i in range(experts)])
 
-    def passed(states, step, k):
-        pairs = [(i, i + step) for i in range(blocks) if 0 <= i + step < blocks]
-        arrived = [lax.ppermute(states, "seq", pairs)]
+    def hop(states, step):
+        return lax.ppermute(states, "seq", [(i, i + step) for i in range(blocks) if 0 <= i + step < blocks])
+
+    def hop_on(arrived, step, k, after):
         for _ in range(hops - 1):
             kept = call(
-                keep_kernel, (1,), [SMEM, log_spec(k), part], part, shape(tokens, width), unit, 4 * unit, "keep_states"
+                keep_kernel,
+                (1,),
+                [SMEM, log_spec(k), part],
+                part,
+                shape(tokens, width),
+                unit,
+                4 * unit,
+                "keep_states",
+                after=after,
             )(meta, log, arrived[-1])
-            arrived.append(lax.ppermute(kept, "seq", pairs))
-        return arrived
-
-    states_in, local = [], None
+            arrived = arrived + [hop(kept, step)]
+        return arrived, kept
+
+    states_in, cots = [], []
     for k in range(CHUNKS):
-        local = call(
+        local, cot_chunk = call(
             local_kernel,
             (1,),
-            [SMEM, log_spec(k), small, chunk(k)],
-            part,
-            shape(tokens, width),
+            [SMEM, log_spec(k), small, chunk(k), chunk(k)],
+            [part, part],
+            [shape(tokens, width)] * 2,
             head_flops,
-            4 * unit,
+            8 * unit,
             "local_states",
-        )(meta, log, b, x)
-        states_in.append(passed(local, 1, k))
+        )(meta, log, b, x, cot)
+        states_in.append([hop(local, 1)])
+        cots.append(cot_chunk)
 
     table = jnp.concatenate([expert_ids[0].T.astype(F32), gate_weights[0].T], axis=0)
-    table, cot, _ = lax.optimization_barrier((table, cot, local))
     if relayed:
         plans = [
             [
@@ -465,17 +482,22 @@
         parts = pieces[0].reshape(experts, capacity, width)
         return [lax.all_to_all(parts, "exp", split_axis=0, concat_axis=0, tiled=True).reshape(slots, width)]
 
-    def to_experts(rows, k, spec):
+    def to_experts(rows, k, other, after=()):
         kind = k % 2
         cost = (2 * slots * unit, 2 * (unit + slots * width))
         if not relayed:
             sent = call(
-                direct_gather_kernel, (1,), [whole((slots, tokens)), spec], piece_specs(kind), piece_shapes(kind), *cost, "gather"
+                direct_gather_kernel,
+                (1,),
+                [whole((slots, tokens)), part],
+                piece_specs(kind),
+                piece_shapes(kind),
+                *cost,
+                "gather",
+                after=after,
             )(picks[kind], rows)
-            return switch(sent)
-        by, offsets = kinds[kind]
-        chunk_rows = rows if rows.shape[1] == width else rows[:, k * width : (k + 1) * width]
-        other = offset(chunk_rows, by)
+            return sent, switch(sent)
+        _, offsets = kinds[kind]
         sent = call(
             gather_kernel,
             (1,),
@@ -484,13 +506,18 @@
             piece_shapes(kind),
             *cost,
             "gather",
-        )(picks[kind], chunk_rows, other)
-        return [piece if o == 0 else offset(piece, o) for piece, o in zip(sent, offsets)]
-
-    def to_positions(pieces, k):
+            after=after,
+        )(picks[kind], rows, other)
+        return sent, [piece if o == 0 else offset(piece, o) for piece, o in zip(sent, offsets)]
+
+    def other_of(rows, k):
+        return offset(rows, kinds[k % 2][0]) if relayed else None
+
+    def to_positions(pieces, k, after=()):
         kind = k % 2
         if not relayed:
-            return switch(pieces)
+            arrived = switch(pieces)
+            return arrived[0], arrived
         by, offsets = kinds[kind]
         pieces = [piece if o == 0 else offset(piece, o) for piece, o in zip(pieces, offsets)]
         relay = call(
@@ -502,14 +529,14 @@
             2 * slots * unit,
             2 * (unit + slots * width),
             "relay",
+            after=after,
         )(relay_weights[kind], *pieces)
-        return pieces + [offset(relay, by)]
+        return relay, pieces + [offset(relay, by)]
 
     def moved_specs(kind):
         return piece_specs(kind) + ([part] if relayed else [])
 
-    got_cot = [to_experts(cot, k, chunk(k)) for k in range(CHUNKS)]
-
+    other_cots = [other_of(cots[k], k) for k in range(CHUNKS)]
     inner = call(
         inner_kernel,
         (CHUNKS,),
@@ -520,8 +547,14 @@
         6 * CHUNKS * unit,
         "inner",
     )(meta, log, b, c, x)
-
-    resid, squares, got_in = [], [], []
+    states_in[0], kept = hop_on(states_in[0], 1, 0, [inner, picks[0]])
+    got_cot, sent = [], kept
+    for k in range(CHUNKS):
+        (sent, *_), pieces = to_experts(cots[k], k, other_cots[k], [sent])
+        got_cot.append(pieces)
+    states_in[1], kept = hop_on(states_in[1], 1, 1, [sent])
+
+    resid, squares, others = [], [], []
     for k in range(CHUNKS):
         rows, square = call(
             functools.partial(resid_kernel, hops),
@@ -535,7 +568,9 @@
         )(meta, log, c, inner, *states_in[k])
         resid.append(rows)
         squares.append(square)
-        got_in.append(to_experts(rows, k, part))
+        others.append(other_of(rows, k))
+    (sent, *_), pieces = to_experts(resid[0], 0, others[0], [resid[1]])
+    got_in = [pieces]
 
     each = 2
     step = width // each
@@ -558,7 +593,10 @@
         CHUNKS * chunk_bytes,
         "back",
         [pltpu.VMEM((slots, step), BF16)],
+        after=[sent],
     )(*[piece for pieces in got_cot for piece in pieces], down)
+    _, pieces = to_experts(resid[1], 1, others[1], [back])
+    got_in.append(pieces)
 
     def up_spec(k):
         return pl.BlockSpec((step, hidden), lambda i: (each * k + i, 0))
@@ -600,8 +638,9 @@
             chunk_bytes,
             "expert_grad",
         )(pre_grad, up, along, *got_in[k])
-        got_grad.append(to_positions(expert_grad, k))
-    got_out = []
+        relay, pieces = to_positions(expert_grad, k)
+        got_grad.append(pieces)
+    outs, last = [], relay
     for k in range(CHUNKS):
         kind = k % 2
         expert_out = call(
@@ -613,8 +652,10 @@
             chunk_flops,
             chunk_bytes,
             "expert_out",
+            after=[last],
         )(act, down)
-        got_out.append(to_positions(expert_out, k))
+        outs.append(expert_out)
+        last = expert_out[0]
 
     def weights_spec(kind):
         return whole(own_weights[kind].shape)
@@ -633,30 +674,14 @@
             head_flops + 2 * slots * unit,
             6 * unit + 2 * slots * width,
             "dresid",
-        )(meta, log, c, own_weights[kind], cotangent[0], *squares, *got_grad[k])
+            after=[last],
+        )(meta, log, c, own_weights[kind], cot, *squares, *got_grad[k])
         dresid.append(grad)
-        states_after.append(passed(source, -1, k))
-
-    into = chunk
-    anywhere = pl.BlockSpec(memory_space=pl.ANY)
-
-    def placed(kernel, k, in_specs, operands, earlier, flops, nbytes, name):
-        more = [] if earlier is None else [earlier]
-        return pl.pallas_call(
-            kernel,
-            grid=(1,),
-            in_specs=in_specs + [anywhere] * len(more),
-            out_specs=into(k),
-            out_shape=shape(tokens, features),
-            input_output_aliases={len(operands): 0} if more else {},
-            name=name,
-            cost_estimate=pl.CostEstimate(flops=flops, bytes_accessed=nbytes, transcendentals=0),
-            compiler_params=pltpu.CompilerParams(vmem_limit_bytes=VMEM_BYTES),
-        )(*operands, *more)
-
-    input_grad = output = None
-    for k in range(CHUNKS):
-        inner_back = call(
+        states_after.append([hop(source, -1)])
+        last = grad
+
+    inner_back = [
+        call(
             inner_back_kernel,
             (1,),
             [SMEM, log_spec(k), small, small, part],
@@ -665,17 +690,46 @@
             2 * head_flops,
             6 * unit,
             "inner_back",
+            after=[last],
         )(meta, log, b, c, dresid[k])
-        input_grad = placed(
+        for k in range(CHUNKS)
+    ]
+    states_after[0], last = hop_on(states_after[0], -1, 0, inner_back)
+    got_out = []
+    for k in range(CHUNKS):
+        last, pieces = to_positions(outs[k], k, [last])
+        got_out.append(pieces)
+    states_after[1], last = hop_on(states_after[1], -1, 1, [last])
+
+    def placed(kernel, k, in_specs, operands, earlier, after, flops, nbytes, name):
+        more = [] if earlier is None else [earlier]
+        return call(
+            kernel,
+            (1,),
+            in_specs + [pl.BlockSpec(memory_space=pl.ANY)] * len(more),
+            chunk(k),
+            shape(tokens, features),
+            flops,
+            nbytes,
+            name,
+            after=after,
+            aliases={len(operands): 0} if more else {},
+        )(*operands, *more)
+
+    def input_grads(k, earlier, after):
+        return placed(
             functools.partial(grad_kernel, hops),
             k,
             [SMEM, log_spec(k), small, part] + [part] * hops,
-            [meta, log, b, inner_back, *states_after[k]],
-            input_grad,
+            [meta, log, b, inner_back[k], *states_after[k]],
+            earlier,
+            after,
             hops * head_flops,
             (6 + 2 * hops) * unit,
             "input_grad",
         )
+
+    input_grad, output = input_grads(0, None, [last]), None
     for k in range(CHUNKS):
         kind = k % 2
         output = placed(
@@ -684,10 +738,12 @@
             [weights_spec(kind), part] + moved_specs(kind),
             [own_weights[kind], resid[k], *got_out[k]],
             output,
+            [input_grad] if output is None else [],
             2 * slots * unit,
             4 * unit + 2 * slots * width,
             "output",
         )
+    input_grad = input_grads(1, input_grad, [output])
     return (output[None], input_grad[None])
 
 

time: 229 us -> 204 us (0.89)
  waiting for transfers between devices: 106 us -> 86.9 us
  Pallas kernels: 59 us -> 56.4 us
  local copies, waits for them, and re-layouts: 8.93 us -> 6.45 us
    ppermute x8, waiting for transfers between devices: 22.9 us -> 10.7 us  [hop(): lax.ppermute(states, 'seq', [(i, i + step) for i in range(blocks) if 0 <=...]
    ppermute x34, waiting for transfers between devices: 83.2 us -> 76.2 us  [offset(): return lax.ppermute(a, 'exp', [(i, i ^ k) for i in range(experts)])]
    pallas_call x33, Pallas kernels: 59 us -> 56.4 us  [call(): return lambda *operands: called(*operands, *after)]
    ppermute x8, starting transfers between devices: 23.4 us -> 20.9 us  [hop(): lax.ppermute(states, 'seq', [(i, i + step) for i in range(blocks) if 0 <=...]
    unnamed x54 -> x46, local copies, waits for them, and re-layouts: 7.87 us -> 6.45 us
  transfers between devices with their start and end apart: 42 -> 42, of which waited for: 23 -> 22; matrix products, arithmetic and copies ran while one was open for 0% -> 0% of each run, Pallas kernels for 22% -> 23%
where the time goes in v3:
time: 204 us; the launch traced here: 203 us
  waiting for transfers between devices  86.9 us (43%)
  Pallas kernels  56.4 us (28%)
  starting transfers between devices  51.4 us (25%)
  local copies, waits for them, and re-layouts  6.45 us (3%)
    ppermute x34, waiting for transfers between devices, offset(): return lax.ppermute(a, 'exp', [(i, i ^ k) for i in range(experts)])  76.2 us
    pallas_call x33, Pallas kernels, call(): return lambda *operands: called(*operands, *after)  56.4 us
    ppermute x34, starting transfers between devices, offset(): return lax.ppermute(a, 'exp', [(i, i ^ k) for i in range(experts)])  30.5 us
    ppermute x8, starting transfers between devices, hop(): lax.ppermute(states, 'seq', [(i, i + step) for i in range(blocks) if 0 <=...  20.9 us
    ppermute x8, waiting for transfers between devices, hop(): lax.ppermute(states, 'seq', [(i, i + step) for i in range(blocks) if 0 <=...  10.7 us
    unnamed x46, local copies, waits for them, and re-layouts  6.45 us
  transfers between devices with their start and end apart: 42, of which 22 were waited for; matrix products, arithmetic and copies ran while one was open for 0% of the time, Pallas kernels for 23%

profile of v3, /device:TPU:0, one launch (start us, length us, event | category | flops | bytes accessed | tf_op | source)
XLA Modules:
  0.0 203.0 jit_solution(6483968055005854044)
XLA Ops:
  7.3 4.9 %collective-permute-start.5 = (bf16[128,2048]{1,0:T(8,128)(2,1)}, bf16[128,2048]{1,0:T(8,128)(2,1)S(1)}, u32[]{:S(2)}, u32[]{:S(2)}) collective-permute-start(bf16[128,2048]{1,0:T(8,128)(2,1)} %get-tuple-element.63), channel_id=1, source_target_pairs={{0,8},{8,16},{16,24},{1,9},{9,17},{17,25},{2,10},{10,18},{18,26},{... | collective-permute-start | bytes 1572872 | tf_op jit(solution)/shard_map/ppermute | solution.py:401
  17.4 3.5 %collective-permute-start.2 = (bf16[128,2048]{1,0:T(8,128)(2,1)}, bf16[128,2048]{1,0:T(8,128)(2,1)S(1)}, u32[]{:S(2)}, u32[]{:S(2)}) collective-permute-start(bf16[128,2048]{1,0:T(8,128)(2,1)} %get-tuple-element.58), channel_id=1, source_target_pairs={{0,8},{8,16},{16,24},{1,9},{9,17},{17,25},{2,10},{10,18},{18,26},{... | collective-permute-start | bytes 1572872 | tf_op jit(solution)/shard_map/ppermute | solution.py:401
  21.5 4.6 %collective-permute-done.refs_2_ = f32[4,128]{1,0:T(4,128)S(1)} collective-permute-done((f32[4,128]{1,0:T(4,128)S(1)}, f32[4,128]{1,0:T(4,128)S(1)}, u32[]{:S(2)}, u32[]{:S(2)}) %collective-permute-start) | collective-permute-done | bytes 2080 | tf_op jit(solution)/shard_map/ppermute | solution.py:398
  27.6 2.5 %inner.1.refs_3_ = f32[128,4096]{1,0:T(8,128)S(1)} custom-call(s32[7]{0:T(128)S(1)} %pad_add_fusion.refs_0_, f32[32,128]{1,0:T(8,128)S(1)} %bitcast.41, bf16[128,128]{1,0:T(8,128)(2,1)S(1)} %bitcast.63, bf16[128,128]{1,0:T(8,128)(2,1)S(1)} %bitcast.54, bf16[128,4096]{1,0:T(8,128)(2,1)S(1)} %bitcast.36), custom_call_target="tpu_custom_call" | custom-call | flops 268435456 | bytes 3145728 | tf_op jit(solution)/shard_map/inner/pallas_call | solution.py:44
  31.5 3.6 %collective-permute-start.14 = (bf16[128,2048]{1,0:T(8,128)(2,1)S(1)}, bf16[128,2048]{1,0:T(8,128)(2,1)S(1)}, u32[]{:S(2)}, u32[]{:S(2)}) collective-permute-start(bf16[128,2048]{1,0:T(8,128)(2,1)S(1)} %keep_states.4.refs_3_), channel_id=1, source_target_pairs={{0,8},{8,16},{16,24},{1,9},{9,17},{17,25},{2,10},{10,18},{18,26},{... | collective-permute-start | bytes 1572872 | tf_op jit(solution)/shard_map/ppermute | solution.py:401
  40.1 3.5 %collective-permute-start.6 = (bf16[128,2048]{1,0:T(8,128)(2,1)S(1)}, bf16[128,2048]{1,0:T(8,128)(2,1)S(1)}, u32[]{:S(2)}, u32[]{:S(2)}) collective-permute-start(bf16[128,2048]{1,0:T(8,128)(2,1)S(1)} %keep_states.5), channel_id=1, source_target_pairs={{0,8},{8,16},{16,24},{1,9},{9,17},{17,25},{2,10},{10,18},{18,26},{... | collective-permute-start | bytes 1572872 | tf_op jit(solution)/shard_map/ppermute | solution.py:401
  52.0 3.6 %collective-permute-done.12.refs_6_ = bf16[96,2048]{1,0:T(8,128)(2,1)S(1)} collective-permute-done((bf16[96,2048]{1,0:T(8,128)(2,1)S(1)}, bf16[96,2048]{1,0:T(8,128)(2,1)S(1)}, u32[]{:S(2)}, u32[]{:S(2)}) %collective-permute-start.12) | collective-permute-done | bytes 393248 | tf_op jit(solution)/shard_map/ppermute | solution.py:398
  60.3 6.6 %collective-permute-done.15.refs_2_ = bf16[128,2048]{1,0:T(8,128)(2,1)S(1)} collective-permute-done((bf16[128,2048]{1,0:T(8,128)(2,1)S(1)}, bf16[128,2048]{1,0:T(8,128)(2,1)S(1)}, u32[]{:S(2)}, u32[]{:S(2)}) %collective-permute-start.15) | collective-permute-done | bytes 524320 | tf_op jit(solution)/shard_map/ppermute | solution.py:398
  68.6 5.7 %collective-permute-done.13.refs_7_ = bf16[96,2048]{1,0:T(8,128)(2,1)S(1)} collective-permute-done((bf16[96,2048]{1,0:T(8,128)(2,1)S(1)}, bf16[96,2048]{1,0:T(8,128)(2,1)S(1)}, u32[]{:S(2)}, u32[]{:S(2)}) %collective-permute-start.13) | collective-permute-done | bytes 393248 | tf_op jit(solution)/shard_map/ppermute | solution.py:398
  76.3 6.0 %back.1.refs_3_.refs_7_ = f32[384,1024]{1,0:T(8,128)S(1)} custom-call(bf16[96,2048]{1,0:T(8,128)(2,1)S(1)} %get-tuple-element.64.refs_3_.refs_0_, bf16[96,2048]{1,0:T(8,128)(2,1)S(1)} %collective-permute-done.8.refs_1_, bf16[96,2048]{1,0:T(8,128)(2,1)S(1)} %collective-permute-done.9.refs_2_, bf16[96,2048]{1,0:T(8,128)(2,1)S(1)} %collective-permute-done.10.refs_3_, ...), custom_call_target="tpu_custom_call" | custom-call | flops 3221225472 | bytes 11534336 | tf_op jit(solution)/shard_map/back/pallas_call | solution.py:44
  85.4 5.4 %collective-permute-done.20.refs_2_.refs_5_ = bf16[96,2048]{1,0:T(8,128)(2,1)S(1)} collective-permute-done((bf16[96,2048]{1,0:T(8,128)(2,1)S(1)}, bf16[96,2048]{1,0:T(8,128)(2,1)S(1)}, u32[]{:S(2)}, u32[]{:S(2)}) %collective-permute-start.20) | collective-permute-done | bytes 393248 | tf_op jit(solution)/shard_map/ppermute | solution.py:398
  90.7 6.8 %collective-permute-done.21.refs_3_.refs_6_ = bf16[96,2048]{1,0:T(8,128)(2,1)S(1)} collective-permute-done((bf16[96,2048]{1,0:T(8,128)(2,1)S(1)}, bf16[96,2048]{1,0:T(8,128)(2,1)S(1)}, u32[]{:S(2)}, u32[]{:S(2)}) %collective-permute-start.21) | collective-permute-done | bytes 393248 | tf_op jit(solution)/shard_map/ppermute | solution.py:398
  100.0 2.5 %collective-permute-done.18.refs_3_.refs_6_ = bf16[96,2048]{1,0:T(8,128)(2,1)S(1)} collective-permute-done((bf16[96,2048]{1,0:T(8,128)(2,1)S(1)}, bf16[96,2048]{1,0:T(8,128)(2,1)S(1)}, u32[]{:S(2)}, u32[]{:S(2)}) %collective-permute-start.18) | collective-permute-done | bytes 393248 | tf_op jit(solution)/shard_map/ppermute | solution.py:398
  102.5 3.4 %up_last.1 = (bf16[384,1024]{1,0:T(8,128)(2,1)S(1)}, bf16[384,1024]{1,0:T(8,128)(2,1)S(1)}, f32[384,128]{1,0:T(8,128)S(1)}) custom-call(bf16[96,2048]{1,0:T(8,128)(2,1)S(1)} %get-tuple-element.75.refs_0_.refs_3_, bf16[96,2048]{1,0:T(8,128)(2,1)S(1)} %collective-permute-done.16.refs_1_.refs_4_, bf16[96,2048]{1,0:T(8,128)(2,1)S(1)} %collective-permute-done.17.refs_2_.refs_5_, ...), custom_call_target="tpu_custom_call" | custom-call | flops 1610612736 | bytes 5767168 | tf_op jit(solution)/shard_map/up_last/pallas_call | solution.py:44
  115.1 5.9 %collective-permute-done.32.refs_3_.refs_9_ = bf16[96,2048]{1,0:T(8,128)(2,1)S(1)} collective-permute-done((bf16[96,2048]{1,0:T(8,128)(2,1)S(1)}, bf16[96,2048]{1,0:T(8,128)(2,1)S(1)}, u32[]{:S(2)}, u32[]{:S(2)}) %collective-permute-start.32) | collective-permute-done | bytes 393248 | tf_op jit(solution)/shard_map/ppermute | solution.py:398
  121.0 6.7 %collective-permute-done.33.refs_4_.refs_10_ = bf16[96,2048]{1,0:T(8,128)(2,1)S(1)} collective-permute-done((bf16[96,2048]{1,0:T(8,128)(2,1)S(1)}, bf16[96,2048]{1,0:T(8,128)(2,1)S(1)}, u32[]{:S(2)}, u32[]{:S(2)}) %collective-permute-start.33) | collective-permute-done | bytes 393248 | tf_op jit(solution)/shard_map/ppermute | solution.py:398
  130.0 3.1 %collective-permute-done.24.refs_4_.refs_10_ = bf16[96,2048]{1,0:T(8,128)(2,1)S(1)} collective-permute-done((bf16[96,2048]{1,0:T(8,128)(2,1)S(1)}, bf16[96,2048]{1,0:T(8,128)(2,1)S(1)}, u32[]{:S(2)}, u32[]{:S(2)}) %collective-permute-start.24) | collective-permute-done | bytes 393248 | tf_op jit(solution)/shard_map/ppermute | solution.py:398
  134.9 2.4 %expert_out.2 = (bf16[96,2048]{1,0:T(8,128)(2,1)S(1)}, bf16[96,2048]{1,0:T(8,128)(2,1)S(1)}, bf16[96,2048]{1,0:T(8,128)(2,1)S(1)}, bf16[96,2048]{1,0:T(8,128)(2,1)S(1)}) custom-call(bf16[384,1024]{1,0:T(8,128)(2,1)S(1)} %get-tuple-element.84.refs_0_, bf16[1024,4096]{1,0:T(8,128)(2,1)S(1)} %bitcast.28, bf16[128,2048]{1,0:T(8,128)(2,1)S(1)} %relay.4.refs_2_), custom_call_target="tpu_custom_call" | custom-call | flops 1610612736 | bytes 5767168 | tf_op jit(solution)/shard_map/expert_out/pallas_call | solution.py:44
  137.3 2.5 %expert_out.3 = (bf16[96,2048]{1,0:T(8,128)(2,1)S(1)}, bf16[96,2048]{1,0:T(8,128)(2,1)S(1)}, bf16[96,2048]{1,0:T(8,128)(2,1)S(1)}, bf16[96,2048]{1,0:T(8,128)(2,1)S(1)}) custom-call(bf16[384,1024]{1,0:T(8,128)(2,1)S(1)} %get-tuple-element.84.refs_0_, bf16[1024,4096]{1,0:T(8,128)(2,1)S(1)} %bitcast.29, bf16[96,2048]{1,0:T(8,128)(2,1)S(1)} %get-tuple-element.92.refs_2_.refs_1_), custom_call_target="tpu_custom_call" | custom-call | flops 1610612736 | bytes 5767168 | tf_op jit(solution)/shard_map/expert_out/pallas_call | solution.py:44
  139.8 4.6 %collective-permute-done.34.refs_11_ = bf16[128,2048]{1,0:T(8,128)(2,1)S(1)} collective-permute-done((bf16[128,2048]{1,0:T(8,128)(2,1)S(1)}, bf16[128,2048]{1,0:T(8,128)(2,1)S(1)}, u32[]{:S(2)}, u32[]{:S(2)}) %collective-permute-start.34) | collective-permute-done | bytes 524320 | tf_op jit(solution)/shard_map/ppermute | solution.py:398
  152.8 6.8 %collective-permute-done.29.refs_3_.refs_4_ = bf16[96,2048]{1,0:T(8,128)(2,1)S(1)} collective-permute-done((bf16[96,2048]{1,0:T(8,128)(2,1)S(1)}, bf16[96,2048]{1,0:T(8,128)(2,1)S(1)}, u32[]{:S(2)}, u32[]{:S(2)}) %collective-permute-start.29) | collective-permute-done | bytes 393248 | tf_op jit(solution)/shard_map/ppermute | solution.py:398
  171.7 7.4 %collective-permute-done.27.refs_4_.refs_5_ = bf16[96,2048]{1,0:T(8,128)(2,1)S(1)} collective-permute-done((bf16[96,2048]{1,0:T(8,128)(2,1)S(1)}, bf16[96,2048]{1,0:T(8,128)(2,1)S(1)}, u32[]{:S(2)}, u32[]{:S(2)}) %collective-permute-start.27) | collective-permute-done | bytes 393248 | tf_op jit(solution)/shard_map/ppermute | solution.py:398
  186.7 2.8 %collective-permute-done.38.refs_6_ = bf16[128,2048]{1,0:T(8,128)(2,1)S(1)} collective-permute-done((bf16[128,2048]{1,0:T(8,128)(2,1)S(1)}, bf16[128,2048]{1,0:T(8,128)(2,1)S(1)}, u32[]{:S(2)}, u32[]{:S(2)}) %collective-permute-start.38) | collective-permute-done | bytes 524320 | tf_op jit(solution)/shard_map/ppermute | solution.py:398
  196.0 3.6 %collective-permute-done.41.refs_5_ = bf16[128,2048]{1,0:T(8,128)(2,1)S(1)} collective-permute-done((bf16[128,2048]{1,0:T(8,128)(2,1)S(1)}, bf16[128,2048]{1,0:T(8,128)(2,1)S(1)}, u32[]{:S(2)}, u32[]{:S(2)}) %collective-permute-start.41) | collective-permute-done | bytes 524320 | tf_op jit(solution)/shard_map/ppermute | solution.py:401
  (144 shorter events, 93.4 us)
Async XLA Ops:
  7.3 23.2 %collective-permute-start.5 = (bf16[128,2048]{1,0:T(8,128)(2,1)}, bf16[128,2048]{1,0:T(8,128)(2,1)S(1)}, u32[]{:S(2)}, u32[]{:S(2)}) collective-permute-start(bf16[128,2048]{1,0:T(8,128)(2,1)} %get-tuple-element.63), channel_id=1, source_target_pairs={{0,8},{8,16},{16,24},{1,9},{9,17},{17,25},{2,10},{10,18},{18,26},{... | collective-permute-start | bytes 1572872 | tf_op jit(solution)/shard_map/ppermute | solution.py:401
  12.3 22.8 %collective-permute-start.4 = (bf16[128,2048]{1,0:T(8,128)(2,1)}, bf16[128,2048]{1,0:T(8,128)(2,1)}, u32[]{:S(2)}, u32[]{:S(2)}) collective-permute-start(bf16[128,2048]{1,0:T(8,128)(2,1)} %get-tuple-element.62.refs_1_), channel_id=1, source_target_pairs={{0,2},{1,3},{2,0},{3,1},{4,6},{5,7},{6,4},{7,5},{8,10},{9,11},{10,... | collective-permute-start | bytes 1572872 | tf_op jit(solution)/shard_map/ppermute | solution.py:398
  15.9 21.2 %collective-permute-start.3 = (bf16[128,2048]{1,0:T(8,128)(2,1)}, bf16[128,2048]{1,0:T(8,128)(2,1)}, u32[]{:S(2)}, u32[]{:S(2)}) collective-permute-start(bf16[128,2048]{1,0:T(8,128)(2,1)} %get-tuple-element.60.refs_1_), channel_id=1, source_target_pairs={{0,4},{1,5},{2,6},{3,7},{4,0},{5,1},{6,2},{7,3},{8,12},{9,13},{10,... | collective-permute-start | bytes 1572872 | tf_op jit(solution)/shard_map/ppermute | solution.py:398
  17.4 21.7 %collective-permute-start.2 = (bf16[128,2048]{1,0:T(8,128)(2,1)}, bf16[128,2048]{1,0:T(8,128)(2,1)S(1)}, u32[]{:S(2)}, u32[]{:S(2)}) collective-permute-start(bf16[128,2048]{1,0:T(8,128)(2,1)} %get-tuple-element.58), channel_id=1, source_target_pairs={{0,8},{8,16},{16,24},{1,9},{9,17},{17,25},{2,10},{10,18},{18,26},{... | collective-permute-start | bytes 1572872 | tf_op jit(solution)/shard_map/ppermute | solution.py:401
  40.1 17.3 %collective-permute-start.6 = (bf16[128,2048]{1,0:T(8,128)(2,1)S(1)}, bf16[128,2048]{1,0:T(8,128)(2,1)S(1)}, u32[]{:S(2)}, u32[]{:S(2)}) collective-permute-start(bf16[128,2048]{1,0:T(8,128)(2,1)S(1)} %keep_states.5), channel_id=1, source_target_pairs={{0,8},{8,16},{16,24},{1,9},{9,17},{17,25},{2,10},{10,18},{18,26},{... | collective-permute-start | bytes 1572872 | tf_op jit(solution)/shard_map/ppermute | solution.py:401
  48.9 18.0 %collective-permute-start.15 = (bf16[128,2048]{1,0:T(8,128)(2,1)S(1)}, bf16[128,2048]{1,0:T(8,128)(2,1)S(1)}, u32[]{:S(2)}, u32[]{:S(2)}) collective-permute-start(bf16[128,2048]{1,0:T(8,128)(2,1)S(1)} %get-tuple-element.73.refs_1_), channel_id=1, source_target_pairs={{0,2},{1,3},{2,0},{3,1},{4,6},{5,7},{6,4},{7,5},{8,10},{9,11},{10,... | collective-permute-start | bytes 1572872 | tf_op jit(solution)/shard_map/ppermute | solution.py:398
  50.4 23.9 %collective-permute-start.13 = (bf16[96,2048]{1,0:T(8,128)(2,1)S(1)}, bf16[96,2048]{1,0:T(8,128)(2,1)S(1)}, u32[]{:S(2)}, u32[]{:S(2)}) collective-permute-start(bf16[96,2048]{1,0:T(8,128)(2,1)S(1)} %get-tuple-element.72), channel_id=1, source_target_pairs={{0,3},{1,2},{2,1},{3,0},{4,7},{5,6},{6,5},{7,4},{8,11},{9,10},{10,... | collective-permute-start | bytes 1179656 | tf_op jit(solution)/shard_map/ppermute | solution.py:398
  50.4 24.5 %collective-permute-start.10 = (bf16[96,2048]{1,0:T(8,128)(2,1)S(1)}, bf16[96,2048]{1,0:T(8,128)(2,1)S(1)}, u32[]{:S(2)}, u32[]{:S(2)}) collective-permute-start(bf16[96,2048]{1,0:T(8,128)(2,1)S(1)} %get-tuple-element.69), channel_id=1, source_target_pairs={{0,5},{1,4},{2,7},{3,6},{4,1},{5,0},{6,3},{7,2},{8,13},{9,12},{10,... | collective-permute-start | bytes 1179656 | tf_op jit(solution)/shard_map/ppermute | solution.py:398
  55.6 20.4 %collective-permute-start.8 = (bf16[96,2048]{1,0:T(8,128)(2,1)S(1)}, bf16[96,2048]{1,0:T(8,128)(2,1)S(1)}, u32[]{:S(2)}, u32[]{:S(2)}) collective-permute-start(bf16[96,2048]{1,0:T(8,128)(2,1)S(1)} %get-tuple-element.67), channel_id=1, source_target_pairs={{0,1},{1,0},{2,3},{3,2},{4,5},{5,4},{6,7},{7,6},{8,9},{9,8},{10,11... | collective-permute-start | bytes 1179656 | tf_op jit(solution)/shard_map/ppermute | solution.py:398
  57.3 19.0 %collective-permute-start.9 = (bf16[96,2048]{1,0:T(8,128)(2,1)S(1)}, bf16[96,2048]{1,0:T(8,128)(2,1)S(1)}, u32[]{:S(2)}, u32[]{:S(2)}) collective-permute-start(bf16[96,2048]{1,0:T(8,128)(2,1)S(1)} %get-tuple-element.68), channel_id=1, source_target_pairs={{0,4},{1,5},{2,6},{3,7},{4,0},{5,1},{6,2},{7,3},{8,12},{9,13},{10,... | collective-permute-start | bytes 1179656 | tf_op jit(solution)/shard_map/ppermute | solution.py:398
  76.0 21.6 %collective-permute-start.21 = (bf16[96,2048]{1,0:T(8,128)(2,1)S(1)}, bf16[96,2048]{1,0:T(8,128)(2,1)S(1)}, u32[]{:S(2)}, u32[]{:S(2)}) collective-permute-start(bf16[96,2048]{1,0:T(8,128)(2,1)S(1)} %get-tuple-element.81), channel_id=1, source_target_pairs={{0,5},{1,4},{2,7},{3,6},{4,1},{5,0},{6,3},{7,2},{8,13},{9,12},{10,... | collective-permute-start | bytes 1179656 | tf_op jit(solution)/shard_map/ppermute | solution.py:398
  83.0 17.0 %collective-permute-start.16 = (bf16[96,2048]{1,0:T(8,128)(2,1)S(1)}, bf16[96,2048]{1,0:T(8,128)(2,1)S(1)}, u32[]{:S(2)}, u32[]{:S(2)}) collective-permute-start(bf16[96,2048]{1,0:T(8,128)(2,1)S(1)} %get-tuple-element.76), channel_id=1, source_target_pairs={{0,1},{1,0},{2,3},{3,2},{4,5},{5,4},{6,7},{7,6},{8,9},{9,8},{10,11... | collective-permute-start | bytes 1179656 | tf_op jit(solution)/shard_map/ppermute | solution.py:398
  85.4 17.2 %collective-permute-start.18 = (bf16[96,2048]{1,0:T(8,128)(2,1)S(1)}, bf16[96,2048]{1,0:T(8,128)(2,1)S(1)}, u32[]{:S(2)}, u32[]{:S(2)}) collective-permute-start(bf16[96,2048]{1,0:T(8,128)(2,1)S(1)} %get-tuple-element.78), channel_id=1, source_target_pairs={{0,3},{1,2},{2,1},{3,0},{4,7},{5,6},{6,5},{7,4},{8,11},{9,10},{10,... | collective-permute-start | bytes 1179656 | tf_op jit(solution)/shard_map/ppermute | solution.py:398
  110.1 17.6 %collective-permute-start.33 = (bf16[96,2048]{1,0:T(8,128)(2,1)S(1)}, bf16[96,2048]{1,0:T(8,128)(2,1)S(1)}, u32[]{:S(2)}, u32[]{:S(2)}) collective-permute-start(bf16[96,2048]{1,0:T(8,128)(2,1)S(1)} %get-tuple-element.107), channel_id=1, source_target_pairs={{0,5},{1,4},{2,7},{3,6},{4,1},{5,0},{6,3},{7,2},{8,13},{9,12},{10,... | collective-permute-start | bytes 1179656 | tf_op jit(solution)/shard_map/ppermute | solution.py:398
  112.9 17.1 %collective-permute-start.22 = (bf16[96,2048]{1,0:T(8,128)(2,1)S(1)}, bf16[96,2048]{1,0:T(8,128)(2,1)S(1)}, u32[]{:S(2)}, u32[]{:S(2)}) collective-permute-start(bf16[96,2048]{1,0:T(8,128)(2,1)S(1)} %get-tuple-element.89), channel_id=1, source_target_pairs={{0,1},{1,0},{2,3},{3,2},{4,5},{5,4},{6,7},{7,6},{8,9},{9,8},{10,11... | collective-permute-start | bytes 1179656 | tf_op jit(solution)/shard_map/ppermute | solution.py:398
  113.6 16.3 %collective-permute-start.23 = (bf16[96,2048]{1,0:T(8,128)(2,1)S(1)}, bf16[96,2048]{1,0:T(8,128)(2,1)S(1)}, u32[]{:S(2)}, u32[]{:S(2)}) collective-permute-start(bf16[96,2048]{1,0:T(8,128)(2,1)S(1)} %get-tuple-element.90), channel_id=1, source_target_pairs={{0,2},{1,3},{2,0},{3,1},{4,6},{5,7},{6,4},{7,5},{8,10},{9,11},{10,... | collective-permute-start | bytes 1179656 | tf_op jit(solution)/shard_map/ppermute | solution.py:398
  115.1 17.9 %collective-permute-start.24 = (bf16[96,2048]{1,0:T(8,128)(2,1)S(1)}, bf16[96,2048]{1,0:T(8,128)(2,1)S(1)}, u32[]{:S(2)}, u32[]{:S(2)}) collective-permute-start(bf16[96,2048]{1,0:T(8,128)(2,1)S(1)} %get-tuple-element.91), channel_id=1, source_target_pairs={{0,3},{1,2},{2,1},{3,0},{4,7},{5,6},{6,5},{7,4},{8,11},{9,10},{10,... | collective-permute-start | bytes 1179656 | tf_op jit(solution)/shard_map/ppermute | solution.py:398
  146.0 16.9 %collective-permute-start.35 = (bf16[128,2048]{1,0:T(8,128)(2,1)S(1)}, bf16[128,2048]{1,0:T(8,128)(2,1)S(1)}, u32[]{:S(2)}, u32[]{:S(2)}) collective-permute-start(bf16[128,2048]{1,0:T(8,128)(2,1)S(1)} %get-tuple-element.108), channel_id=1, source_target_pairs={{8,0},{16,8},{24,16},{9,1},{17,9},{25,17},{10,2},{18,10},{26,18},{... | collective-permute-start | bytes 1572872 | tf_op jit(solution)/shard_map/ppermute | solution.py:401
  150.4 30.6 %collective-permute-start.40 = (bf16[128,2048]{1,0:T(8,128)(2,1)S(1)}, bf16[128,2048]{1,0:T(8,128)(2,1)S(1)}, u32[]{:S(2)}, u32[]{:S(2)}) collective-permute-start(bf16[128,2048]{1,0:T(8,128)(2,1)S(1)} %get-tuple-element.111), channel_id=1, source_target_pairs={{8,0},{16,8},{24,16},{9,1},{17,9},{25,17},{10,2},{18,10},{26,18},{... | collective-permute-start | bytes 1572872 | tf_op jit(solution)/shard_map/ppermute | solution.py:401
  152.5 16.7 %collective-permute-start.25 = (bf16[96,2048]{1,0:T(8,128)(2,1)S(1)}, bf16[96,2048]{1,0:T(8,128)(2,1)S(1)}, u32[]{:S(2)}, u32[]{:S(2)}) collective-permute-start(bf16[96,2048]{1,0:T(8,128)(2,1)S(1)} %get-tuple-element.94), channel_id=1, source_target_pairs={{0,1},{1,0},{2,3},{3,2},{4,5},{5,4},{6,7},{7,6},{8,9},{9,8},{10,11... | collective-permute-start | bytes 1179656 | tf_op jit(solution)/shard_map/ppermute | solution.py:398
  162.9 16.2 %collective-permute-start.27 = (bf16[96,2048]{1,0:T(8,128)(2,1)S(1)}, bf16[96,2048]{1,0:T(8,128)(2,1)S(1)}, u32[]{:S(2)}, u32[]{:S(2)}) collective-permute-start(bf16[96,2048]{1,0:T(8,128)(2,1)S(1)} %get-tuple-element.96), channel_id=1, source_target_pairs={{0,3},{1,2},{2,1},{3,0},{4,7},{5,6},{6,5},{7,4},{8,11},{9,10},{10,... | collective-permute-start | bytes 1179656 | tf_op jit(solution)/shard_map/ppermute | solution.py:398
  167.1 17.4 %collective-permute-start.39 = (bf16[128,2048]{1,0:T(8,128)(2,1)S(1)}, bf16[128,2048]{1,0:T(8,128)(2,1)S(1)}, u32[]{:S(2)}, u32[]{:S(2)}) collective-permute-start(bf16[128,2048]{1,0:T(8,128)(2,1)S(1)} %keep_states.6.refs_5_), channel_id=1, source_target_pairs={{8,0},{16,8},{24,16},{9,1},{17,9},{25,17},{10,2},{18,10},{26,18},{... | collective-permute-start | bytes 1572872 | tf_op jit(solution)/shard_map/ppermute | solution.py:401
  169.1 20.4 %collective-permute-start.38 = (bf16[128,2048]{1,0:T(8,128)(2,1)S(1)}, bf16[128,2048]{1,0:T(8,128)(2,1)S(1)}, u32[]{:S(2)}, u32[]{:S(2)}) collective-permute-start(bf16[128,2048]{1,0:T(8,128)(2,1)S(1)} %relay.6.refs_5_), channel_id=1, source_target_pairs={{0,2},{1,3},{2,0},{3,1},{4,6},{5,7},{6,4},{7,5},{8,10},{9,11},{10,... | collective-permute-start | bytes 1572872 | tf_op jit(solution)/shard_map/ppermute | solution.py:398
  181.9 17.8 %collective-permute-start.41 = (bf16[128,2048]{1,0:T(8,128)(2,1)S(1)}, bf16[128,2048]{1,0:T(8,128)(2,1)S(1)}, u32[]{:S(2)}, u32[]{:S(2)}) collective-permute-start(bf16[128,2048]{1,0:T(8,128)(2,1)S(1)} %keep_states.7.refs_6_), channel_id=1, source_target_pairs={{8,0},{16,8},{24,16},{9,1},{17,9},{25,17},{10,2},{18,10},{26,18},{... | collective-permute-start | bytes 1572872 | tf_op jit(solution)/shard_map/ppermute | solution.py:401
  (41 other events, 685.2 us)

commit v4 on v3

--- a/solution.py
+++ b/solution.py
@@ -87,8 +87,7 @@
     return slice(h * size, (h + 1) * size)
 
 
-def local_kernel(meta, log_ref, b_ref, x_ref, cot_ref, state_ref, chunk_ref):
-    chunk_ref[...] = cot_ref[...]
+def local_kernel(meta, log_ref, b_ref, x_ref, state_ref):
     size = log_ref.shape[1]
     cum = running(log_ref)
     row, _, _, last = documents(meta, cum.shape[0], size)
@@ -211,14 +210,12 @@
         out_ref[:, head(h, p)] = (inner_ref[:, head(h, p)] + weight[:, h : h + 1] * carried).astype(BF16)
 
 
-def output_kernel(weights_ref, resid_ref, *refs):
-    out_ref = refs[-1]
-    count = weights_ref.shape[0]
-    moved = combined(weights_ref, refs[:count])
-    for arrived in refs[count : len(refs) - 1]:
-        if arrived.shape == out_ref.shape:
-            moved += arrived[...].astype(F32)
-    out_ref[...] = (resid_ref[...].astype(F32) + moved).astype(BF16)
+def output_kernel(weights_ref, got_ref, *refs):
+    resid, out_ref = refs[:-1], refs[-1]
+    width = resid[0].shape[1]
+    for k, rows in enumerate(resid):
+        at = slice(k * width, (k + 1) * width)
+        out_ref[:, at] = (rows[...].astype(F32) + dot(weights_ref[...], got_ref[:, at])).astype(BF16)
 
 
 def picks_of(table, me, experts, capacity):
@@ -238,10 +235,12 @@
     return picks, [pick * gate[e : e + 1, :] for e, pick in enumerate(picks)]
 
 
-def direct_pick_kernel(experts, capacity, table_ref, pick_ref, weights_ref):
+def direct_pick_kernel(experts, capacity, table_ref, cot_ref, pick_ref, weights_ref, sent_ref):
     picks, gated = picks_of(table_ref[...], 0, experts, capacity)
-    pick_ref[...] = jnp.concatenate(picks, axis=0).astype(BF16)
-    weights_ref[0] = jnp.concatenate(gated, axis=0).T.astype(BF16)
+    pick = jnp.concatenate(picks, axis=0).astype(BF16)
+    pick_ref[...] = pick
+    weights_ref[...] = jnp.concatenate(gated, axis=0).T.astype(BF16)
+    sent_ref[...] = dot(pick, cot_ref[...]).astype(BF16)
 
 
 def relay_pick_kernel(experts, capacity, kinds, me_ref, own_ref, *refs):
@@ -276,26 +275,23 @@
         rows[to : to + count, :] = pieces[piece][at : at + count, :]
 
 
-def back_kernel(plans, *refs):
-    counts = [max(b[0] for b in plan) + 1 for plan in plans]
-    pieces, (down_ref, back_ref, rows) = refs[: sum(counts)], refs[sum(counts) :]
-    step, each = pl.program_id(0), pl.num_programs(0) // len(plans)
-    for k, plan in enumerate(plans):
-        mine = pieces[sum(counts[:k]) : sum(counts[: k + 1])]
-
-        @pl.when(step // each == k)
-        def _(plan=plan, mine=mine):
-            assemble(plan, mine, rows)
-
-    part = dot_nt(rows[...], down_ref[...])
+def back_kernel(capacity, me_ref, rows_ref, down_ref, back_ref, total):
+    step = pl.program_id(0)
+    part = dot_nt(rows_ref[...], down_ref[...])
 
     @pl.when(step == 0)
     def _():
-        back_ref[...] = part
+        total[...] = part
 
     @pl.when(step > 0)
     def _():
-        back_ref[...] += part
+        total[...] += part
+
+    @pl.when(step == pl.num_programs(0) - 1)
+    def _():
+        for i in range(total.shape[0] // capacity):
+            to = pl.multiple_of((i ^ me_ref[0]) * capacity, 8)
+            back_ref[pl.ds(to, capacity), :] = total[i * capacity : (i + 1) * capacity, :]
 
 
 def up_first_kernel(plan, *refs):
@@ -358,10 +354,11 @@
         ).astype(BF16)
 
 
-def expert_out_kernel(plan, act_ref, down_ref, *outs):
-    total = dot(act_ref[...], down_ref[...])
-    for piece, at, to, size in plan:
-        outs[piece][at : at + size, :] = total[to : to + size, :].astype(BF16)
+def expert_out_kernel(capacity, me_ref, act_ref, down_ref, out_ref):
+    total = dot(act_ref[...], down_ref[...]).astype(BF16)
+    for i in range(total.shape[0] // capacity):
+        to = pl.multiple_of((i ^ me_ref[0]) * capacity, 8)
+        out_ref[pl.ds(to, capacity), :] = total[i * capacity : (i + 1) * capacity, :]
 
 
 def on_device(inputs, b_proj, c_proj, log_decay, doc_lengths, expert_ids, gate_weights, w_up, w_down, cotangent):
@@ -416,22 +413,41 @@
             arrived = arrived + [hop(kept, step)]
         return arrived, kept
 
-    states_in, cots = [], []
+    states_in, near = [], []
     for k in range(CHUNKS):
-        local, cot_chunk = call(
+        local = call(
             local_kernel,
             (1,),
-            [SMEM, log_spec(k), small, chunk(k), chunk(k)],
-            [part, part],
-            [shape(tokens, width)] * 2,
+            [SMEM, log_spec(k), small, chunk(k)],
+            part,
+            shape(tokens, width),
             head_flops,
-            8 * unit,
+            4 * unit,
             "local_states",
-        )(meta, log, b, x, cot)
+            after=near,
+        )(meta, log, b, x)
         states_in.append([hop(local, 1)])
-        cots.append(cot_chunk)
+        near = [local]
 
     table = jnp.concatenate([expert_ids[0].T.astype(F32), gate_weights[0].T], axis=0)
+    me = (lax.axis_index("exp") if relayed else jnp.zeros((), jnp.int32)).astype(jnp.int32)[None]
+    pick, weights, sent_cot = call(
+        functools.partial(direct_pick_kernel, experts, capacity),
+        (1,),
+        [whole((4, tokens)), whole((tokens, features))],
+        [whole((slots, tokens)), whole((tokens, slots)), whole((slots, features))],
+        [shape(slots, tokens), shape(tokens, slots), shape(slots, features)],
+        2 * slots * tokens * features,
+        2 * (slots + tokens) * features,
+        "pick_rows",
+        after=near,
+    )(table, cot)
+
+    def switch(rows):
+        parts = rows.reshape(experts, capacity, rows.shape[1])
+        return lax.all_to_all(parts, "exp", split_axis=0, concat_axis=0, tiled=True).reshape(rows.shape)
+
+    got_cot = switch(sent_cot)
     if relayed:
         plans = [
             [
@@ -445,7 +461,6 @@
         pick_shape = (4, 2, capacity, tokens)
         weight_shape = (4, tokens, 2 * capacity)
         outs = [pick_shape, weight_shape, weight_shape] * 2
-        me = lax.axis_index("exp").astype(jnp.int32)[None]
         found = call(
             functools.partial(relay_pick_kernel, experts, capacity, kinds),
             (1,),
@@ -454,33 +469,19 @@
             [jax.ShapeDtypeStruct(s, BF16) for s in outs],
             6 * experts * tokens * tokens,
             4 * slots * tokens,
-            "pick_rows",
+            "pick_relayed",
         )(me, table, *[offset(table, by) for by, _ in kinds])
         picks, own_weights, relay_weights = found[0::3], found[1::3], found[2::3]
     else:
         plans = [[(0, 0, 0, slots)]] * 2
         pieces_of = [[slots]] * 2
-        pick, weights = call(
-            functools.partial(direct_pick_kernel, experts, capacity),
-            (1,),
-            [whole((4, tokens))],
-            [whole((slots, tokens)), whole((1, tokens, slots))],
-            [shape(slots, tokens), jax.ShapeDtypeStruct((1, tokens, slots), BF16)],
-            2 * experts * tokens * tokens,
-            4 * slots * tokens,
-            "pick_rows",
-        )(table)
-        picks, own_weights = [pick] * 2, [weights] * 2
+        picks, own_weights = [pick] * 2, [weights[None]] * 2
 
     def piece_specs(kind):
         return [whole((rows, width)) for rows in pieces_of[kind]]
 
     def piece_shapes(kind):
         return [shape(rows, width) for rows in pieces_of[kind]]
-
-    def switch(pieces):
-        parts = pieces[0].reshape(experts, capacity, width)
-        return [lax.all_to_all(parts, "exp", split_axis=0, concat_axis=0, tiled=True).reshape(slots, width)]
 
     def to_experts(rows, k, other, after=()):
         kind = k % 2
@@ -496,7 +497,7 @@
                 "gather",
                 after=after,
             )(picks[kind], rows)
-            return sent, switch(sent)
+            return sent, [switch(sent[0])]
         _, offsets = kinds[kind]
         sent = call(
             gather_kernel,
@@ -516,7 +517,7 @@
     def to_positions(pieces, k, after=()):
         kind = k % 2
         if not relayed:
-            arrived = switch(pieces)
+            arrived = [switch(pieces[0])]
             return arrived[0], arrived
         by, offsets = kinds[kind]
         pieces = [piece if o == 0 else offset(piece, o) for piece, o in zip(pieces, offsets)]
@@ -536,7 +537,6 @@
     def moved_specs(kind):
         return piece_specs(kind) + ([part] if relayed else [])
 
-    other_cots = [other_of(cots[k], k) for k in range(CHUNKS)]
     inner = call(
         inner_kernel,
         (CHUNKS,),
@@ -546,13 +546,10 @@
         2 * CHUNKS * head_flops,
         6 * CHUNKS * unit,
         "inner",
+        after=[sent_cot],
     )(meta, log, b, c, x)
     states_in[0], kept = hop_on(states_in[0], 1, 0, [inner, picks[0]])
-    got_cot, sent = [], kept
-    for k in range(CHUNKS):
-        (sent, *_), pieces = to_experts(cots[k], k, other_cots[k], [sent])
-        got_cot.append(pieces)
-    states_in[1], kept = hop_on(states_in[1], 1, 1, [sent])
+    states_in[1], _ = hop_on(states_in[1], 1, 1, [] if kept is None else [kept])
 
     resid, squares, others = [], [], []
     for k in range(CHUNKS):
@@ -584,17 +581,17 @@
         ]
 
     back = call(
-        functools.partial(back_kernel, [plans[k % 2] for k in range(CHUNKS)]),
-        (each * CHUNKS,),
-        [spec for k in range(CHUNKS) for spec in step_specs(k % 2, each * k)] + [columns(hidden, step)],
+        functools.partial(back_kernel, capacity),
+        (4,),
+        [SMEM, columns(slots, features // 4), columns(hidden, features // 4)],
         slots_hidden,
         shape(slots, hidden, F32),
         CHUNKS * chunk_flops,
         CHUNKS * chunk_bytes,
         "back",
-        [pltpu.VMEM((slots, step), BF16)],
+        [pltpu.VMEM((slots, hidden), F32)],
         after=[sent],
-    )(*[piece for pieces in got_cot for piece in pieces], down)
+    )(me, got_cot, down)
     _, pieces = to_experts(resid[1], 1, others[1], [back])
     got_in.append(pieces)
 
@@ -640,22 +637,19 @@
         )(pre_grad, up, along, *got_in[k])
         relay, pieces = to_positions(expert_grad, k)
         got_grad.append(pieces)
-    outs, last = [], relay
-    for k in range(CHUNKS):
-        kind = k % 2
-        expert_out = call(
-            functools.partial(expert_out_kernel, plans[kind]),
-            (each,),
-            [slots_hidden, pl.BlockSpec((hidden, step), lambda i, k=k: (0, each * k + i))],
-            step_specs(kind),
-            piece_shapes(kind),
-            chunk_flops,
-            chunk_bytes,
-            "expert_out",
-            after=[last],
-        )(act, down)
-        outs.append(expert_out)
-        last = expert_out[0]
+    expert_out = call(
+        functools.partial(expert_out_kernel, capacity),
+        (4,),
+        [SMEM, slots_hidden, columns(hidden, features // 4)],
+        columns(slots, features // 4),
+        shape(slots, features),
+        CHUNKS * chunk_flops,
+        CHUNKS * chunk_bytes,
+        "expert_out",
+        after=[relay],
+    )(me, act, down)
+    got_out = switch(expert_out)
+    last = expert_out
 
     def weights_spec(kind):
         return whole(own_weights[kind].shape)
@@ -695,10 +689,6 @@
         for k in range(CHUNKS)
     ]
     states_after[0], last = hop_on(states_after[0], -1, 0, inner_back)
-    got_out = []
-    for k in range(CHUNKS):
-        last, pieces = to_positions(outs[k], k, [last])
-        got_out.append(pieces)
     states_after[1], last = hop_on(states_after[1], -1, 1, [last])
 
     def placed(kernel, k, in_specs, operands, earlier, after, flops, nbytes, name):
@@ -729,20 +719,18 @@
             "input_grad",
         )
 
-    input_grad, output = input_grads(0, None, [last]), None
-    for k in range(CHUNKS):
-        kind = k % 2
-        output = placed(
-            output_kernel,
-            k,
-            [weights_spec(kind), part] + moved_specs(kind),
-            [own_weights[kind], resid[k], *got_out[k]],
-            output,
-            [input_grad] if output is None else [],
-            2 * slots * unit,
-            4 * unit + 2 * slots * width,
-            "output",
-        )
+    input_grad = input_grads(0, None, [last])
+    output = call(
+        output_kernel,
+        (1,),
+        [whole((tokens, slots)), whole((slots, features))] + [part] * CHUNKS,
+        whole((tokens, features)),
+        shape(tokens, features),
+        2 * slots * tokens * features,
+        2 * (slots + 2 * tokens) * features,
+        "output",
+        after=[input_grad],
+    )(weights, got_out, *resid)
     input_grad = input_grads(1, input_grad, [output])
     return (output[None], input_grad[None])
 

time: 204 us -> 286 us (1.40)
  waiting for transfers between devices: 86.9 us -> 149 us
  local copies, waits for them, and re-layouts: 6.45 us -> 26.1 us
  starting transfers between devices: 51.4 us -> 48.1 us
    ppermute x8, waiting for transfers between devices: 10.7 us -> 43 us  [hop(): lax.ppermute(states, 'seq', [(i, i + step) for i in range(blocks) if 0 <=...]
    ppermute x34 -> x18, waiting for transfers between devices: 76.2 us -> 106 us  [offset(): return lax.ppermute(a, 'exp', [(i, i ^ k) for i in range(experts)])]
    unnamed x46 -> x138, local copies, waits for them, and re-layouts: 6.45 us -> 26.1 us
    ppermute x34 -> x18, starting transfers between devices: 30.5 us -> 17.2 us  [offset(): return lax.ppermute(a, 'exp', [(i, i ^ k) for i in range(experts)])]
    all_to_all x0 -> x2, starting transfers between devices: none -> 9.2 us  [switch(): lax.all_to_all(parts, 'exp', split_axis=0, concat_axis=0, tiled=True)]
    pallas_call x33 -> x28, Pallas kernels: 56.4 us -> 57.7 us  [call(): return lambda *operands: called(*operands, *after)]
  transfers between devices with their start and end apart: 42 -> 28, of which waited for: 22 -> 17; matrix products, arithmetic and copies ran while one was open for 0% -> 0% of each run, Pallas kernels for 23% -> 13%
where the time goes in v4:
time: 286 us; the launch traced here: 284 us
  waiting for transfers between devices  149 us (52%)
  Pallas kernels  57.7 us (20%)
  starting transfers between devices  48.1 us (17%)
  local copies, waits for them, and re-layouts  26.1 us (9%)
    ppermute x18, waiting for transfers between devices, offset(): return lax.ppermute(a, 'exp', [(i, i ^ k) for i in range(experts)])  106 us
    pallas_call x28, Pallas kernels, call(): return lambda *operands: called(*operands, *after)  57.7 us
    ppermute x8, waiting for transfers between devices, hop(): lax.ppermute(states, 'seq', [(i, i + step) for i in range(blocks) if 0 <=...  43 us
    unnamed x138, local copies, waits for them, and re-layouts  26.1 us
    ppermute x8, starting transfers between devices, hop(): lax.ppermute(states, 'seq', [(i, i + step) for i in range(blocks) if 0 <=...  21.7 us
    ppermute x18, starting transfers between devices, offset(): return lax.ppermute(a, 'exp', [(i, i ^ k) for i in range(experts)])  17.2 us
    all_to_all x2, starting transfers between devices, switch(): lax.all_to_all(parts, 'exp', split_axis=0, concat_axis=0, tiled=True)  9.2 us
  transfers between devices with their start and end apart: 28, of which 17 were waited for; matrix products, arithmetic and copies ran while one was open for 0% of the time, Pallas kernels for 13%

profile of v4, /device:TPU:0, one launch (start us, length us, event | category | flops | bytes accessed | tf_op | source)
XLA Modules:
  0.0 284.1 jit_solution(8442671418864740546)
XLA Ops:
  13.6 5.3 %all-to-all-start = ((bf16[8,48,4096]{2,1,0:T(8,128)(2,1)}), bf16[8,48,4096]{2,1,0:T(8,128)(2,1)}, u32[]{:S(2)}, u32[]{:S(2)}) async-start(bf16[8,48,4096]{2,1,0:T(8,128)(2,1)} %bitcast.12), calls=%async_computation | async-start | bytes 6291456 | tf_op jit(solution)/shard_map/all_to_all | solution.py:448
  18.9 5.1 %collective-permute-start.3 = (bf16[128,2048]{1,0:T(8,128)(2,1)}, bf16[128,2048]{1,0:T(8,128)(2,1)}, u32[]{:S(2)}, u32[]{:S(2)}) collective-permute-start(bf16[128,2048]{1,0:T(8,128)(2,1)} %local_states.2.refs_4_), channel_id=1, source_target_pairs={{0,8},{8,16},{16,24},{1,9},{9,17},{17,25},{2,10},{10,18},{18,26},{... | collective-permute-start | bytes 1572872 | tf_op jit(solution)/shard_map/ppermute | solution.py:398
  24.0 3.5 %collective-permute-start.2 = (bf16[128,2048]{1,0:T(8,128)(2,1)}, bf16[128,2048]{1,0:T(8,128)(2,1)}, u32[]{:S(2)}, u32[]{:S(2)}) collective-permute-start(bf16[128,2048]{1,0:T(8,128)(2,1)} %local_states.3.refs_2_), channel_id=1, source_target_pairs={{0,8},{8,16},{16,24},{1,9},{9,17},{17,25},{2,10},{10,18},{18,26},{... | collective-permute-start | bytes 1572872 | tf_op jit(solution)/shard_map/ppermute | solution.py:398
  33.4 14.1 %collective-permute-done.1.refs_3_ = f32[4,128]{1,0:T(4,128)S(1)} collective-permute-done((f32[4,128]{1,0:T(4,128)S(1)}, f32[4,128]{1,0:T(4,128)S(1)}, u32[]{:S(2)}, u32[]{:S(2)}) %collective-permute-start.1) | collective-permute-done | bytes 2080 | tf_op jit(solution)/shard_map/ppermute | solution.py:395
  47.6 8.4 %collective-permute-done.refs_2_ = f32[4,128]{1,0:T(4,128)S(1)} collective-permute-done((f32[4,128]{1,0:T(4,128)S(1)}, f32[4,128]{1,0:T(4,128)S(1)}, u32[]{:S(2)}, u32[]{:S(2)}) %collective-permute-start) | collective-permute-done | bytes 2080 | tf_op jit(solution)/shard_map/ppermute | solution.py:395
  60.4 4.1 %collective-permute-start.6 = (bf16[128,2048]{1,0:T(8,128)(2,1)S(1)}, bf16[128,2048]{1,0:T(8,128)(2,1)S(1)}, u32[]{:S(2)}, u32[]{:S(2)}) collective-permute-start(bf16[128,2048]{1,0:T(8,128)(2,1)S(1)} %keep_states.4.refs_3_), channel_id=1, source_target_pairs={{0,8},{8,16},{16,24},{1,9},{9,17},{17,25},{2,10},{10,18},{18,26},{... | collective-permute-start | bytes 1572872 | tf_op jit(solution)/shard_map/ppermute | solution.py:398
  66.0 3.7 %collective-permute-start.4 = (bf16[128,2048]{1,0:T(8,128)(2,1)S(1)}, bf16[128,2048]{1,0:T(8,128)(2,1)S(1)}, u32[]{:S(2)}, u32[]{:S(2)}) collective-permute-start(bf16[128,2048]{1,0:T(8,128)(2,1)S(1)} %keep_states.5), channel_id=1, source_target_pairs={{0,8},{8,16},{16,24},{1,9},{9,17},{17,25},{2,10},{10,18},{18,26},{... | collective-permute-start | bytes 1572872 | tf_op jit(solution)/shard_map/ppermute | solution.py:398
  69.7 7.1 %collective-permute-done.6.refs_5_ = bf16[128,2048]{1,0:T(8,128)(2,1)S(1)} collective-permute-done((bf16[128,2048]{1,0:T(8,128)(2,1)S(1)}, bf16[128,2048]{1,0:T(8,128)(2,1)S(1)}, u32[]{:S(2)}, u32[]{:S(2)}) %collective-permute-start.6) | collective-permute-done | bytes 524320 | tf_op jit(solution)/shard_map/ppermute | solution.py:398
  80.9 5.9 %collective-permute-done.4.refs_5_ = bf16[128,2048]{1,0:T(8,128)(2,1)S(1)} collective-permute-done((bf16[128,2048]{1,0:T(8,128)(2,1)S(1)}, bf16[128,2048]{1,0:T(8,128)(2,1)S(1)}, u32[]{:S(2)}, u32[]{:S(2)}) %collective-permute-start.4) | collective-permute-done | bytes 524320 | tf_op jit(solution)/shard_map/ppermute | solution.py:398
  94.8 3.5 %copy-done.1 = bf16[1,1024,4096]{2,1,0:T(8,128)(2,1)S(1)} copy-done((bf16[1,1024,4096]{2,1,0:T(8,128)(2,1)S(1)}, bf16[1,1024,4096]{2,1,0:T(8,128)(2,1)}, u32[]{:S(2)}) %copy-start.1) | copy-done | bytes 8388632
  98.3 6.3 %back.1.refs_3_.refs_7_ = f32[384,1024]{1,0:T(8,128)S(1)} custom-call(s32[1]{0:T(128)} %bitcast.10.refs_0_, bf16[384,4096]{1,0:T(8,128)(2,1)} %bitcast.13.refs_1_, bf16[1024,4096]{1,0:T(8,128)(2,1)S(1)} %bitcast.29, bf16[96,2048]{1,0:T(8,128)(2,1)S(1)} %get-tuple-element.45.refs_3_.refs_0_), custom_call_target="tpu_custom_call" | custom-call | flops 3221225472 | bytes 11534336 | tf_op jit(solution)/shard_map/back/pallas_call | solution.py:44
  107.5 5.3 %collective-permute-done.12.refs_2_.refs_5_ = bf16[96,2048]{1,0:T(8,128)(2,1)S(1)} collective-permute-done((bf16[96,2048]{1,0:T(8,128)(2,1)}, bf16[96,2048]{1,0:T(8,128)(2,1)S(1)}, u32[]{:S(2)}, u32[]{:S(2)}) %collective-permute-start.12) | collective-permute-done | bytes 393248 | tf_op jit(solution)/shard_map/ppermute | solution.py:395
  112.8 5.4 %collective-permute-done.13.refs_3_.refs_6_ = bf16[96,2048]{1,0:T(8,128)(2,1)S(1)} collective-permute-done((bf16[96,2048]{1,0:T(8,128)(2,1)}, bf16[96,2048]{1,0:T(8,128)(2,1)S(1)}, u32[]{:S(2)}, u32[]{:S(2)}) %collective-permute-start.13) | collective-permute-done | bytes 393248 | tf_op jit(solution)/shard_map/ppermute | solution.py:395
  120.6 4.1 %collective-permute-done.10.refs_3_.refs_6_ = bf16[96,2048]{1,0:T(8,128)(2,1)S(1)} collective-permute-done((bf16[96,2048]{1,0:T(8,128)(2,1)S(1)}, bf16[96,2048]{1,0:T(8,128)(2,1)S(1)}, u32[]{:S(2)}, u32[]{:S(2)}) %collective-permute-start.10) | collective-permute-done | bytes 393248 | tf_op jit(solution)/shard_map/ppermute | solution.py:395
  132.9 10.2 %collective-permute-done.15.refs_3_.refs_9_ = bf16[96,2048]{1,0:T(8,128)(2,1)S(1)} collective-permute-done((bf16[96,2048]{1,0:T(8,128)(2,1)S(1)}, bf16[96,2048]{1,0:T(8,128)(2,1)S(1)}, u32[]{:S(2)}, u32[]{:S(2)}) %collective-permute-start.15) | collective-permute-done | bytes 393248 | tf_op jit(solution)/shard_map/ppermute | solution.py:395
  143.1 6.8 %collective-permute-done.16.refs_4_.refs_10_ = bf16[96,2048]{1,0:T(8,128)(2,1)S(1)} collective-permute-done((bf16[96,2048]{1,0:T(8,128)(2,1)S(1)}, bf16[96,2048]{1,0:T(8,128)(2,1)S(1)}, u32[]{:S(2)}, u32[]{:S(2)}) %collective-permute-start.16) | collective-permute-done | bytes 393248 | tf_op jit(solution)/shard_map/ppermute | solution.py:395
  151.4 5.5 %expert_out.1.refs_12_ = bf16[384,4096]{1,0:T(8,128)(2,1)} custom-call(s32[1]{0:T(128)} %bitcast.10.refs_0_, bf16[384,1024]{1,0:T(8,128)(2,1)S(1)} %get-tuple-element.55.refs_1_, bf16[1024,4096]{1,0:T(8,128)(2,1)S(1)} %bitcast.32, bf16[128,2048]{1,0:T(8,128)(2,1)S(1)} %relay.2.refs_3_), custom_call_target="tpu_custom_call" | custom-call | flops 3221225472 | bytes 11534336 | tf_op jit(solution)/shard_map/expert_out/pallas_call | solution.py:44
  156.9 3.9 %all-to-all-start.1 = ((bf16[8,48,4096]{2,1,0:T(8,128)(2,1)}), bf16[8,48,4096]{2,1,0:T(8,128)(2,1)S(1)}, u32[]{:S(2)}, u32[]{:S(2)}) async-start(bf16[8,48,4096]{2,1,0:T(8,128)(2,1)} %bitcast.16), calls=%async_computation.1 | async-start | bytes 6291456 | tf_op jit(solution)/shard_map/all_to_all | solution.py:448
  173.7 32.7 %collective-permute-done.18.refs_3_.refs_9_ = bf16[96,2048]{1,0:T(8,128)(2,1)S(1)} collective-permute-done((bf16[96,2048]{1,0:T(8,128)(2,1)S(1)}, bf16[96,2048]{1,0:T(8,128)(2,1)S(1)}, u32[]{:S(2)}, u32[]{:S(2)}) %collective-permute-start.18) | collective-permute-done | bytes 393248 | tf_op jit(solution)/shard_map/ppermute | solution.py:395
  206.3 7.5 %collective-permute-done.19.refs_4_.refs_10_ = bf16[96,2048]{1,0:T(8,128)(2,1)S(1)} collective-permute-done((bf16[96,2048]{1,0:T(8,128)(2,1)S(1)}, bf16[96,2048]{1,0:T(8,128)(2,1)S(1)}, u32[]{:S(2)}, u32[]{:S(2)}) %collective-permute-start.19) | collective-permute-done | bytes 393248 | tf_op jit(solution)/shard_map/ppermute | solution.py:395
  217.1 11.6 %collective-permute-done.20.refs_11_ = bf16[128,2048]{1,0:T(8,128)(2,1)S(1)} collective-permute-done((bf16[128,2048]{1,0:T(8,128)(2,1)S(1)}, bf16[128,2048]{1,0:T(8,128)(2,1)S(1)}, u32[]{:S(2)}, u32[]{:S(2)}) %collective-permute-start.20) | collective-permute-done | bytes 524320 | tf_op jit(solution)/shard_map/ppermute | solution.py:395
  237.6 10.0 %collective-permute-done.22.refs_2_.refs_4_ = bf16[128,2048]{1,0:T(8,128)(2,1)S(1)} collective-permute-done((bf16[128,2048]{1,0:T(8,128)(2,1)S(1)}, bf16[128,2048]{1,0:T(8,128)(2,1)S(1)}, u32[]{:S(2)}, u32[]{:S(2)}) %collective-permute-start.22) | collective-permute-done | bytes 524320 | tf_op jit(solution)/shard_map/ppermute | solution.py:398
  250.0 8.8 %collective-permute-done.24.refs_2_.refs_4_ = bf16[128,2048]{1,0:T(8,128)(2,1)S(1)} collective-permute-done((bf16[128,2048]{1,0:T(8,128)(2,1)S(1)}, bf16[128,2048]{1,0:T(8,128)(2,1)S(1)}, u32[]{:S(2)}, u32[]{:S(2)}) %collective-permute-start.24) | collective-permute-done | bytes 524320 | tf_op jit(solution)/shard_map/ppermute | solution.py:398
  261.9 8.2 %collective-permute-done.23.refs_5_ = bf16[128,2048]{1,0:T(8,128)(2,1)S(1)} collective-permute-done((bf16[128,2048]{1,0:T(8,128)(2,1)S(1)}, bf16[128,2048]{1,0:T(8,128)(2,1)S(1)}, u32[]{:S(2)}, u32[]{:S(2)}) %collective-permute-start.23) | collective-permute-done | bytes 524320 | tf_op jit(solution)/shard_map/ppermute | solution.py:398
  (203 shorter events, 95.9 us)
Async XLA Ops:
  13.6 81.2 %all-to-all-start = ((bf16[8,48,4096]{2,1,0:T(8,128)(2,1)}), bf16[8,48,4096]{2,1,0:T(8,128)(2,1)}, u32[]{:S(2)}, u32[]{:S(2)}) async-start(bf16[8,48,4096]{2,1,0:T(8,128)(2,1)} %bitcast.12), calls=%async_computation | async-start | bytes 6291456 | tf_op jit(solution)/shard_map/all_to_all | solution.py:448
  18.9 40.0 %collective-permute-start.3 = (bf16[128,2048]{1,0:T(8,128)(2,1)}, bf16[128,2048]{1,0:T(8,128)(2,1)}, u32[]{:S(2)}, u32[]{:S(2)}) collective-permute-start(bf16[128,2048]{1,0:T(8,128)(2,1)} %local_states.2.refs_4_), channel_id=1, source_target_pairs={{0,8},{8,16},{16,24},{1,9},{9,17},{17,25},{2,10},{10,18},{18,26},{... | collective-permute-start | bytes 1572872 | tf_op jit(solution)/shard_map/ppermute | solution.py:398
  24.0 40.5 %collective-permute-start.2 = (bf16[128,2048]{1,0:T(8,128)(2,1)}, bf16[128,2048]{1,0:T(8,128)(2,1)}, u32[]{:S(2)}, u32[]{:S(2)}) collective-permute-start(bf16[128,2048]{1,0:T(8,128)(2,1)} %local_states.3.refs_2_), channel_id=1, source_target_pairs={{0,8},{8,16},{16,24},{1,9},{9,17},{17,25},{2,10},{10,18},{18,26},{... | collective-permute-start | bytes 1572872 | tf_op jit(solution)/shard_map/ppermute | solution.py:398
  27.5 20.1 %collective-permute-start.1 = (f32[4,128]{1,0:T(4,128)S(1)}, f32[4,128]{1,0:T(4,128)S(1)}, u32[]{:S(2)}, u32[]{:S(2)}) collective-permute-start(f32[4,128]{1,0:T(4,128)S(1)} %pad_maximum_fusion.refs_0_.refs_1_), channel_id=1, source_target_pairs={{0,4},{1,5},{2,6},{3,7},{4,0},{5,1},{6,2},{7,3},{8,12},{9,13},{10,... | collective-permute-start | bytes 6152 | tf_op jit(solution)/shard_map/ppermute | solution.py:395
  29.4 26.6 %collective-permute-start = (f32[4,128]{1,0:T(4,128)S(1)}, f32[4,128]{1,0:T(4,128)S(1)}, u32[]{:S(2)}, u32[]{:S(2)}) collective-permute-start(f32[4,128]{1,0:T(4,128)S(1)} %pad_maximum_fusion.refs_0_.refs_1_), channel_id=1, source_target_pairs={{0,2},{1,3},{2,0},{3,1},{4,6},{5,7},{6,4},{7,5},{8,10},{9,11},{10,... | collective-permute-start | bytes 6152 | tf_op jit(solution)/shard_map/ppermute | solution.py:395
  60.4 16.4 %collective-permute-start.6 = (bf16[128,2048]{1,0:T(8,128)(2,1)S(1)}, bf16[128,2048]{1,0:T(8,128)(2,1)S(1)}, u32[]{:S(2)}, u32[]{:S(2)}) collective-permute-start(bf16[128,2048]{1,0:T(8,128)(2,1)S(1)} %keep_states.4.refs_3_), channel_id=1, source_target_pairs={{0,8},{8,16},{16,24},{1,9},{9,17},{17,25},{2,10},{10,18},{18,26},{... | collective-permute-start | bytes 1572872 | tf_op jit(solution)/shard_map/ppermute | solution.py:398
  66.0 20.8 %collective-permute-start.4 = (bf16[128,2048]{1,0:T(8,128)(2,1)S(1)}, bf16[128,2048]{1,0:T(8,128)(2,1)S(1)}, u32[]{:S(2)}, u32[]{:S(2)}) collective-permute-start(bf16[128,2048]{1,0:T(8,128)(2,1)S(1)} %keep_states.5), channel_id=1, source_target_pairs={{0,8},{8,16},{16,24},{1,9},{9,17},{17,25},{2,10},{10,18},{18,26},{... | collective-permute-start | bytes 1572872 | tf_op jit(solution)/shard_map/ppermute | solution.py:398
  89.5 15.2 %collective-permute-start.5 = (bf16[128,2048]{1,0:T(8,128)(2,1)S(1)}, bf16[128,2048]{1,0:T(8,128)(2,1)S(1)}, u32[]{:S(2)}, u32[]{:S(2)}) collective-permute-start(bf16[128,2048]{1,0:T(8,128)(2,1)S(1)} %get-tuple-element.43.refs_3_.refs_1_), channel_id=1, source_target_pairs={{0,4},{1,5},{2,6},{3,7},{4,0},{5,1},{6,2},{7,3},{8,12},{9,13},{10,... | collective-permute-start | bytes 1572872 | tf_op jit(solution)/shard_map/ppermute | solution.py:395
  92.9 14.5 %collective-permute-start.11 = (bf16[96,2048]{1,0:T(8,128)(2,1)}, bf16[96,2048]{1,0:T(8,128)(2,1)S(1)}, u32[]{:S(2)}, u32[]{:S(2)}) collective-permute-start(bf16[96,2048]{1,0:T(8,128)(2,1)} %get-tuple-element.50), channel_id=1, source_target_pairs={{0,1},{1,0},{2,3},{3,2},{4,5},{5,4},{6,7},{7,6},{8,9},{9,8},{10,11... | collective-permute-start | bytes 1179656 | tf_op jit(solution)/shard_map/ppermute | solution.py:395
  92.9 19.8 %collective-permute-start.12 = (bf16[96,2048]{1,0:T(8,128)(2,1)}, bf16[96,2048]{1,0:T(8,128)(2,1)S(1)}, u32[]{:S(2)}, u32[]{:S(2)}) collective-permute-start(bf16[96,2048]{1,0:T(8,128)(2,1)} %get-tuple-element.51), channel_id=1, source_target_pairs={{0,4},{1,5},{2,6},{3,7},{4,0},{5,1},{6,2},{7,3},{8,12},{9,13},{10,... | collective-permute-start | bytes 1179656 | tf_op jit(solution)/shard_map/ppermute | solution.py:395
  93.9 24.2 %collective-permute-start.13 = (bf16[96,2048]{1,0:T(8,128)(2,1)}, bf16[96,2048]{1,0:T(8,128)(2,1)S(1)}, u32[]{:S(2)}, u32[]{:S(2)}) collective-permute-start(bf16[96,2048]{1,0:T(8,128)(2,1)} %get-tuple-element.52), channel_id=1, source_target_pairs={{0,5},{1,4},{2,7},{3,6},{4,1},{5,0},{6,3},{7,2},{8,13},{9,12},{10,... | collective-permute-start | bytes 1179656 | tf_op jit(solution)/shard_map/ppermute | solution.py:395
  105.4 15.2 %collective-permute-start.8 = (bf16[96,2048]{1,0:T(8,128)(2,1)S(1)}, bf16[96,2048]{1,0:T(8,128)(2,1)S(1)}, u32[]{:S(2)}, u32[]{:S(2)}) collective-permute-start(bf16[96,2048]{1,0:T(8,128)(2,1)S(1)} %get-tuple-element.47), channel_id=1, source_target_pairs={{0,1},{1,0},{2,3},{3,2},{4,5},{5,4},{6,7},{7,6},{8,9},{9,8},{10,11... | collective-permute-start | bytes 1179656 | tf_op jit(solution)/shard_map/ppermute | solution.py:395
  105.7 14.9 %collective-permute-start.9 = (bf16[96,2048]{1,0:T(8,128)(2,1)S(1)}, bf16[96,2048]{1,0:T(8,128)(2,1)S(1)}, u32[]{:S(2)}, u32[]{:S(2)}) collective-permute-start(bf16[96,2048]{1,0:T(8,128)(2,1)S(1)} %get-tuple-element.48), channel_id=1, source_target_pairs={{0,2},{1,3},{2,0},{3,1},{4,6},{5,7},{6,4},{7,5},{8,10},{9,11},{10,... | collective-permute-start | bytes 1179656 | tf_op jit(solution)/shard_map/ppermute | solution.py:395
  107.5 17.2 %collective-permute-start.10 = (bf16[96,2048]{1,0:T(8,128)(2,1)S(1)}, bf16[96,2048]{1,0:T(8,128)(2,1)S(1)}, u32[]{:S(2)}, u32[]{:S(2)}) collective-permute-start(bf16[96,2048]{1,0:T(8,128)(2,1)S(1)} %get-tuple-element.49), channel_id=1, source_target_pairs={{0,3},{1,2},{2,1},{3,0},{4,7},{5,6},{6,5},{7,4},{8,11},{9,10},{10,... | collective-permute-start | bytes 1179656 | tf_op jit(solution)/shard_map/ppermute | solution.py:395
  132.9 17.0 %collective-permute-start.16 = (bf16[96,2048]{1,0:T(8,128)(2,1)S(1)}, bf16[96,2048]{1,0:T(8,128)(2,1)S(1)}, u32[]{:S(2)}, u32[]{:S(2)}) collective-permute-start(bf16[96,2048]{1,0:T(8,128)(2,1)S(1)} %get-tuple-element.62), channel_id=1, source_target_pairs={{0,3},{1,2},{2,1},{3,0},{4,7},{5,6},{6,5},{7,4},{8,11},{9,10},{10,... | collective-permute-start | bytes 1179656 | tf_op jit(solution)/shard_map/ppermute | solution.py:395
  156.9 115.3 %all-to-all-start.1 = ((bf16[8,48,4096]{2,1,0:T(8,128)(2,1)}), bf16[8,48,4096]{2,1,0:T(8,128)(2,1)S(1)}, u32[]{:S(2)}, u32[]{:S(2)}) async-start(bf16[8,48,4096]{2,1,0:T(8,128)(2,1)} %bitcast.16), calls=%async_computation.1 | async-start | bytes 6291456 | tf_op jit(solution)/shard_map/all_to_all | solution.py:448
  172.2 34.1 %collective-permute-start.18 = (bf16[96,2048]{1,0:T(8,128)(2,1)S(1)}, bf16[96,2048]{1,0:T(8,128)(2,1)S(1)}, u32[]{:S(2)}, u32[]{:S(2)}) collective-permute-start(bf16[96,2048]{1,0:T(8,128)(2,1)S(1)} %get-tuple-element.68), channel_id=1, source_target_pairs={{0,4},{1,5},{2,6},{3,7},{4,0},{5,1},{6,2},{7,3},{8,12},{9,13},{10,... | collective-permute-start | bytes 1179656 | tf_op jit(solution)/shard_map/ppermute | solution.py:395
  173.6 40.2 %collective-permute-start.19 = (bf16[96,2048]{1,0:T(8,128)(2,1)S(1)}, bf16[96,2048]{1,0:T(8,128)(2,1)S(1)}, u32[]{:S(2)}, u32[]{:S(2)}) collective-permute-start(bf16[96,2048]{1,0:T(8,128)(2,1)S(1)} %get-tuple-element.69), channel_id=1, source_target_pairs={{0,5},{1,4},{2,7},{3,6},{4,1},{5,0},{6,3},{7,2},{8,13},{9,12},{10,... | collective-permute-start | bytes 1179656 | tf_op jit(solution)/shard_map/ppermute | solution.py:395
  214.5 14.2 %collective-permute-start.20 = (bf16[128,2048]{1,0:T(8,128)(2,1)S(1)}, bf16[128,2048]{1,0:T(8,128)(2,1)S(1)}, u32[]{:S(2)}, u32[]{:S(2)}) collective-permute-start(bf16[128,2048]{1,0:T(8,128)(2,1)S(1)} %relay.3), channel_id=1, source_target_pairs={{0,2},{1,3},{2,0},{3,1},{4,6},{5,7},{6,4},{7,5},{8,10},{9,11},{10,... | collective-permute-start | bytes 1572872 | tf_op jit(solution)/shard_map/ppermute | solution.py:395
  216.4 15.3 %collective-permute-start.21 = (bf16[128,2048]{1,0:T(8,128)(2,1)S(1)}, bf16[128,2048]{1,0:T(8,128)(2,1)S(1)}, u32[]{:S(2)}, u32[]{:S(2)}) collective-permute-start(bf16[128,2048]{1,0:T(8,128)(2,1)S(1)} %copy-done.20), channel_id=1, source_target_pairs={{0,4},{1,5},{2,6},{3,7},{4,0},{5,1},{6,2},{7,3},{8,12},{9,13},{10,... | collective-permute-start | bytes 1572872 | tf_op jit(solution)/shard_map/ppermute | solution.py:395
  230.4 17.2 %collective-permute-start.22 = (bf16[128,2048]{1,0:T(8,128)(2,1)S(1)}, bf16[128,2048]{1,0:T(8,128)(2,1)S(1)}, u32[]{:S(2)}, u32[]{:S(2)}) collective-permute-start(bf16[128,2048]{1,0:T(8,128)(2,1)S(1)} %get-tuple-element.74), channel_id=1, source_target_pairs={{8,0},{16,8},{24,16},{9,1},{17,9},{25,17},{10,2},{18,10},{26,18},{... | collective-permute-start | bytes 1572872 | tf_op jit(solution)/shard_map/ppermute | solution.py:398
  233.4 25.4 %collective-permute-start.24 = (bf16[128,2048]{1,0:T(8,128)(2,1)S(1)}, bf16[128,2048]{1,0:T(8,128)(2,1)S(1)}, u32[]{:S(2)}, u32[]{:S(2)}) collective-permute-start(bf16[128,2048]{1,0:T(8,128)(2,1)S(1)} %get-tuple-element.75), channel_id=1, source_target_pairs={{8,0},{16,8},{24,16},{9,1},{17,9},{25,17},{10,2},{18,10},{26,18},{... | collective-permute-start | bytes 1572872 | tf_op jit(solution)/shard_map/ppermute | solution.py:398
  248.5 21.5 %collective-permute-start.23 = (bf16[128,2048]{1,0:T(8,128)(2,1)S(1)}, bf16[128,2048]{1,0:T(8,128)(2,1)S(1)}, u32[]{:S(2)}, u32[]{:S(2)}) collective-permute-start(bf16[128,2048]{1,0:T(8,128)(2,1)S(1)} %keep_states.6.refs_3_), channel_id=1, source_target_pairs={{8,0},{16,8},{24,16},{9,1},{17,9},{25,17},{10,2},{18,10},{26,18},{... | collective-permute-start | bytes 1572872 | tf_op jit(solution)/shard_map/ppermute | solution.py:398
  260.6 19.6 %collective-permute-start.25 = (bf16[128,2048]{1,0:T(8,128)(2,1)}, bf16[128,2048]{1,0:T(8,128)(2,1)}, u32[]{:S(2)}, u32[]{:S(2)}) collective-permute-start(bf16[128,2048]{1,0:T(8,128)(2,1)} %keep_states.7.refs_6_), channel_id=1, source_target_pairs={{8,0},{16,8},{24,16},{9,1},{17,9},{25,17},{10,2},{18,10},{26,18},{... | collective-permute-start | bytes 1572872 | tf_op jit(solution)/shard_map/ppermute | solution.py:398
  (73 other events, 1040.6 us)

commit v5 on v3

--- a/solution.py
+++ b/solution.py
@@ -12,6 +12,7 @@
 BF16 = jnp.bfloat16
 CHUNKS = 2
 VMEM_BYTES = 32 * 1024 * 1024
+VMEM_ALL = 60 * 1024 * 1024
 NT = (((1,), (1,)), ((), ()))
 
 
@@ -23,7 +24,7 @@
     return lax.dot_general(a, b, NT, preferred_element_type=F32)
 
 
-def call(kernel, grid, in_specs, out_specs, out_shape, flops, nbytes, name, scratch=(), after=(), aliases=None):
+def call(kernel, grid, in_specs, out_specs, out_shape, flops, nbytes, name, scratch=(), after=(), aliases=None, vmem=VMEM_BYTES):
     count, more = len(in_specs), len(after)
 
     def body(*refs):
@@ -39,7 +40,7 @@
         input_output_aliases=aliases or {},
         name=name,
         cost_estimate=pl.CostEstimate(flops=flops, bytes_accessed=nbytes, transcendentals=0),
-        compiler_params=pltpu.CompilerParams(vmem_limit_bytes=VMEM_BYTES),
+        compiler_params=pltpu.CompilerParams(vmem_limit_bytes=vmem),
     )
     return lambda *operands: called(*operands, *after)
 
@@ -52,12 +53,13 @@
     return pl.BlockSpec((rows, width), lambda i: (0, i))
 
 
+anywhere = pl.BlockSpec(memory_space=pl.ANY)
 SMEM = pl.BlockSpec(memory_space=pltpu.SMEM)
 
 
-def documents(meta, rows, size):
+def documents(meta, size, shift=0):
     count = meta.shape[0] - 1
-    first = meta[count]
+    first = meta[count] + shift * size
     along = first + lax.broadcasted_iota(jnp.int32, (1, size), 1)
     down = first + lax.broadcasted_iota(jnp.int32, (size, 1), 0)
     row = jnp.full((1, size), -1, jnp.int32)
@@ -87,11 +89,10 @@
     return slice(h * size, (h + 1) * size)
 
 
-def local_kernel(meta, log_ref, b_ref, x_ref, cot_ref, state_ref, chunk_ref):
-    chunk_ref[...] = cot_ref[...]
+def local_kernel(meta, log_ref, b_ref, x_ref, state_ref):
     size = log_ref.shape[1]
     cum = running(log_ref)
-    row, _, _, last = documents(meta, cum.shape[0], size)
+    row, _, _, last = documents(meta, size)
     tail = (row == last).astype(F32)
     weight = tail * jnp.exp(cum[:, size - 1 :] - cum)
     b_t = b_ref[...].astype(F32).T
@@ -102,7 +103,7 @@
 
 
 def pair_mask(meta, size):
-    row, col, before, last = documents(meta, size, size)
+    row, col, before, last = documents(meta, size)
     later = lax.broadcasted_iota(jnp.int32, (size, size), 0)
     earlier = lax.broadcasted_iota(jnp.int32, (size, size), 1)
     return row, col, before, last, later, earlier
@@ -137,7 +138,7 @@
 def keep_kernel(meta, log_ref, state_ref, out_ref):
     size = log_ref.shape[1]
     total = jnp.exp(running(log_ref)[:, size - 1 :])
-    _, _, before, last = documents(meta, 1, size)
+    _, _, before, last = documents(meta, size)
     total = jnp.where(before == last, total, 0.0)
     p = state_ref.shape[1] // total.shape[0]
     for h in range(total.shape[0]):
@@ -146,17 +147,96 @@
         ).astype(BF16)
 
 
-def resid_kernel(hops, meta, log_ref, c_ref, inner_ref, *refs):
-    states, (resid_ref, squares_ref) = refs[:hops], refs[hops:]
+def prepare_kernel(b_ref, c_ref, log_ref, cot_ref, ids_ref, gates_ref, b_pack_ref, c_pack_ref, *chunks):
+    chunks, both = chunks[:-1], chunks[-1]
+    size = ids_ref.shape[1]
+    width = chunks[0].shape[1] - size
+    table = jnp.concatenate([ids_ref[...].astype(F32), gates_ref[...], jnp.zeros((size - 4, size), F32)], axis=0)
+    table = table.T.astype(BF16)
+    for k, chunk in enumerate(chunks):
+        for ref, to in ((chunk, 0), (both, k * size)):
+            ref[to : to + size, :width] = cot_ref[:, k * width : (k + 1) * width]
+            ref[to : to + size, width:] = table
+    rest, heads, at = log_ref[...], log_ref.shape[0], b_ref.shape[0]
+    b_pack_ref[:at, :] = b_ref[...]
+    c_pack_ref[:at, :] = c_ref[...]
+    for _ in range(3):
+        term = rest.astype(BF16)
+        rest = rest - term.astype(F32)
+        b_pack_ref[at : at + heads, :] = term
+        c_pack_ref[at : at + heads, :] = term
+        at += heads
+
+
+def pass_kernel(ahead, chunk, meta, log_ref, near_ref, far_ref, rows_ref, state_ref, sent_ref):
+    size, heads = log_ref.shape[1], log_ref.shape[0]
+    half = size // 2
+    _, _, before, last = documents(meta, size)
+    near_row, _, _, _ = documents(meta, size, -1 if ahead else 1)
+    far_row, _, _, _ = documents(meta, size, 1 if ahead else -1)
+    total = jnp.where(before == last, jnp.exp(running(log_ref)[:, size - 1 :]), 0.0)
+    terms = (near_ref.shape[0] - size) // 3
+    near_log = jnp.zeros((heads, size), F32)
+    for i in range(3):
+        at = size + i * terms + chunk * heads
+        near_log += near_ref[at : at + heads, :].astype(F32)
+    cum = running(near_log)
+    if ahead:
+        weight = jnp.where(near_row == before, jnp.exp(cum[:, size - 1 :] - cum), 0.0)
+        count = jnp.sum((far_row == last).astype(F32), axis=1, keepdims=True)
+        rows, wanted = slice(half, size), slice(0, half)
+    else:
+        weight = jnp.where(near_row == last, jnp.exp(cum), 0.0)
+        count = jnp.sum((far_row == before).astype(F32), axis=1, keepdims=True)
+        rows, wanted = slice(0, half), slice(half, size)
+    few = (count <= half).astype(F32)
+    weight_t = weight.T
+    near_t = near_ref[:size, :].astype(F32).T
+    far = far_ref[wanted, :]
+    width = rows_ref.shape[1]
+    p = width // heads
+    for h in range(heads):
+        at = head(h, p)
+        state = dot((near_t * weight[h : h + 1, :]).astype(BF16), rows_ref[:, at]).astype(BF16)
+        state_ref[:, at] = state
+        scale = total[h : h + 1, :]
+        sums = dot(far, state) * (few * scale)
+        scaled = rows_ref[rows, at].astype(F32) * (weight_t[rows, h : h + 1] * ((1.0 - few) * scale))
+        sent_ref[:, at] = (sums + scaled).astype(BF16)
+    sent_ref[:, width:] = near_ref[rows, :]
+
+
+def spread_of(few, shift, mine, theirs):
+    size, half = mine.shape[0], theirs.shape[0]
+    down = lax.broadcasted_iota(jnp.int32, (size, half), 0)
+    along = lax.broadcasted_iota(jnp.int32, (size, half), 1)
+    same = (down == along + shift).astype(F32)
+    return (few * same + (1.0 - few) * dot_nt(mine, theirs)).astype(BF16)
+
+
+def carried_in(mine, spread, states, at):
+    carried = dot(mine, states[0][:, at])
+    if spread is not None:
+        return carried + dot(spread, states[1][:, at])
+    for state in states[1:]:
+        carried += dot(mine, state[:, at])
+    return carried
+
+
+def resid_kernel(relayed, meta, log_ref, c_ref, inner_ref, *refs):
+    states, (resid_ref, squares_ref) = refs[:-2], refs[-2:]
     size = log_ref.shape[1]
-    _, col, before, _ = documents(meta, size, size)
+    row, col, before, _ = documents(meta, size)
     weight = jnp.where(col == before, jnp.exp(running(log_ref).T), 0.0)
-    p = inner_ref.shape[1] // log_ref.shape[0]
+    width = inner_ref.shape[1]
+    p = width // log_ref.shape[0]
+    spread = None
+    if relayed:
+        few = (jnp.sum((row == before).astype(F32), axis=1, keepdims=True) <= size // 2).astype(F32)
+        spread = spread_of(few, 0, c_ref[...], states[2][...])
     squares = jnp.zeros((size, p), F32)
     for h in range(log_ref.shape[0]):
-        carried = dot(c_ref[...], states[0][:, head(h, p)])
-        for state in states[1:]:
-            carried += dot(c_ref[...], state[:, head(h, p)])
+        carried = carried_in(c_ref[...], spread, states, head(h, p))
         rows = (inner_ref[:, head(h, p)] + weight[:, h : h + 1] * carried).astype(BF16)
         resid_ref[:, head(h, p)] = rows
         squares += rows.astype(F32) * rows.astype(F32)
@@ -177,37 +257,44 @@
 
 def dresid_kernel(chunks, features, meta, log_ref, c_ref, weights_ref, cot_ref, *refs):
     squares, refs = refs[:chunks], refs[chunks:]
-    moved_refs, (dresid_ref, source_ref) = refs[:-2], refs[-2:]
+    count = weights_ref.shape[0]
+    relayed = weights_ref.shape[0] > 1
+    moved_refs, outs = (refs[:-1], refs[-1:]) if relayed else (refs[:-2], refs[-2:])
+    dresid_ref = outs[0]
     size = log_ref.shape[1]
-    row, _, before, _ = documents(meta, size, size)
+    row, _, before, _ = documents(meta, size)
     weight = jnp.where(row == before, jnp.exp(running(log_ref)), 0.0)
     c_t = c_ref[...].astype(F32).T
     total = squares[0][...]
     for part in squares[1:]:
         total = total + part[...]
     scale = lax.rsqrt(total[:, :1] / features + EPSILON)
-    count = weights_ref.shape[0]
     moved = combined(weights_ref, moved_refs[:count])
     for arrived in moved_refs[count:]:
         moved += arrived[...].astype(F32)
     dresid_ref[...] = (cot_ref[...].astype(F32) + scale * moved).astype(BF16)
+    if relayed:
+        return
     p = cot_ref.shape[1] // log_ref.shape[0]
     for h in range(log_ref.shape[0]):
         c_weighted = (c_t * weight[h : h + 1, :]).astype(BF16)
-        source_ref[:, head(h, p)] = dot(c_weighted, dresid_ref[:, head(h, p)]).astype(BF16)
-
-
-def grad_kernel(hops, meta, log_ref, b_ref, inner_ref, *refs):
-    states, out_ref = refs[:hops], refs[-1]
+        outs[1][:, head(h, p)] = dot(c_weighted, dresid_ref[:, head(h, p)]).astype(BF16)
+
+
+def grad_kernel(count, relayed, meta, log_ref, b_ref, inner_ref, *refs):
+    states, out_ref = refs[:count], refs[-1]
     size = log_ref.shape[1]
-    _, col, _, last = documents(meta, size, size)
+    row, col, _, last = documents(meta, size)
     cum = running(log_ref)
     weight = jnp.where(col == last, jnp.exp(cum[:, size - 1 :] - cum).T, 0.0)
-    p = inner_ref.shape[1] // log_ref.shape[0]
+    width = inner_ref.shape[1]
+    p = width // log_ref.shape[0]
+    spread = None
+    if relayed:
+        few = (jnp.sum((row == last).astype(F32), axis=1, keepdims=True) <= size // 2).astype(F32)
+        spread = spread_of(few, size // 2, b_ref[...], states[2][...])
     for h in range(log_ref.shape[0]):
-        carried = dot(b_ref[...], states[0][:, head(h, p)])
-        for state in states[1:]:
-            carried += dot(b_ref[...], state[:, head(h, p)])
+        carried = carried_in(b_ref[...], spread, states, head(h, p))
         out_ref[:, head(h, p)] = (inner_ref[:, head(h, p)] + weight[:, h : h + 1] * carried).astype(BF16)
 
 
@@ -247,17 +334,86 @@
 def relay_pick_kernel(experts, capacity, kinds, me_ref, own_ref, *refs):
     tables, outs = refs[: len(kinds)], refs[len(kinds) :]
     me = me_ref[0]
-    picks, gated = picks_of(own_ref[...], me, experts, capacity)
+    picks, gated = picks_of(own_ref[...].astype(F32).T, me, experts, capacity)
     none = jnp.zeros_like(picks[0])
     for (_, offsets), table_ref, (pick_ref, own_weights_ref, relay_weights_ref) in zip(
         kinds, tables, (outs[:3], outs[3:])
     ):
-        other_picks, other_gated = picks_of(table_ref[...], me, experts, capacity)
+        other_picks, other_gated = picks_of(table_ref[...].astype(F32).T, me, experts, capacity)
         for i, o in enumerate(offsets):
             pick_ref[i, 0] = picks[o].astype(BF16)
             pick_ref[i, 1] = other_picks[o].astype(BF16)
             own_weights_ref[i] = jnp.concatenate([gated[o], none], axis=0).T.astype(BF16)
             relay_weights_ref[i] = jnp.concatenate([none, other_gated[o]], axis=0).T.astype(BF16)
+
+
+def side_pick_kernel(experts, capacity, kinds, me_ref, own_ref, sibling_ref, *refs):
+    tables, outs = refs[:4], refs[4:]
+    mine = [picks_of(t[...].astype(F32).T, me_ref[0], experts, capacity) for t in (own_ref, sibling_ref)]
+    for k, (_, partner) in enumerate(kinds):
+        near = [picks_of(t[...].astype(F32).T, me_ref[0], experts, capacity) for t in tables[2 * k : 2 * k + 2]]
+        pick_ref, gated_ref = outs[2 * k : 2 * k + 2]
+        for source, (picks, gated) in enumerate((mine[0], near[0], mine[1], near[1])):
+            for e, to in enumerate((0, partner)):
+                pick_ref[e, source] = picks[to].astype(BF16)
+                gated_ref[e, source] = gated[to]
+
+
+def side_weights_kernel(*refs):
+    for gated_ref, weights_ref in zip(refs[:2], refs[2:]):
+        for e in range(2):
+            for source in range(4):
+                weights_ref[source, e] = gated_ref[e, source].T.astype(BF16)
+
+
+def side_gather_kernel(*refs):
+    picks, rows, outs = refs[:2], (refs[2:6], refs[6:10]), (refs[10:12], refs[12:14])
+    capacity = picks[0].shape[2]
+    for e in (1, 0):
+        for k in range(2):
+            for source in range(4):
+                at = slice(source * capacity, (source + 1) * capacity)
+                outs[k][e][at, :] = dot(picks[k][e, source], rows[k][source][...]).astype(BF16)
+
+
+def partial(weights_ref, pieces, source):
+    slots = weights_ref.shape[3]
+    rows = slice(source * slots, (source + 1) * slots)
+    total = dot(weights_ref[source, 0], pieces[0][rows, :])
+    for e, piece in enumerate(pieces[1:]):
+        total += dot(weights_ref[source, e + 1], piece[rows, :])
+    return total
+
+
+def side_sums_kernel(*refs):
+    weights, pieces, relayed_ref, own_ref = refs[:2], (refs[2:4], refs[4:6]), refs[6], refs[7]
+    size = weights[0].shape[2]
+    for ref, source in ((relayed_ref, 3), (own_ref, 2)):
+        for k in range(2):
+            ref[k * size : (k + 1) * size, :] = partial(weights[k], pieces[k], source).astype(BF16)
+
+
+def side_relay_kernel(*refs):
+    weights, pieces, arrived, outs = refs[:2], (refs[2:4], refs[4:6]), refs[6], refs[7:]
+    size = weights[0].shape[2]
+    for k in range(2):
+        total = partial(weights[k], pieces[k], 1) + arrived[k * size : (k + 1) * size, :].astype(F32)
+        outs[k][...] = total.astype(BF16)
+
+
+def side_output_kernel(first_weights, second_weights, first_resid, second_resid, *refs):
+    out_ref, refs = refs[-1], refs[:-1]
+    count, width = len(refs) // 2, first_resid.shape[1]
+    for k, (weights, resid) in enumerate(((first_weights, first_resid), (second_weights, second_resid))):
+        terms = refs[k * count : (k + 1) * count]
+        sums = partial(weights, terms[:2], 0)
+        for arrived in terms[2:]:
+            sums += arrived[...].astype(F32)
+        out_ref[:, k * width : (k + 1) * width] = (resid[...].astype(F32) + sums).astype(BF16)
+
+
+def hold_kernel(*refs):
+    pass
 
 
 def gather_kernel(pick_ref, own_ref, other_ref, *outs):
@@ -374,7 +530,7 @@
     slots = experts * capacity
     width = features // CHUNKS
     hops = max(1, blocks // 2)
-    relayed = experts == 8
+    relayed = experts == 8 and hops == 2
     kinds = ((2, (0, 1, 4, 5)), (4, (0, 1, 2, 3)))
 
     x, b, c, log, cot = inputs[0], b_proj[0], c_proj[0], log_decay[0], cotangent[0]
@@ -400,7 +556,24 @@
     def hop(states, step):
         return lax.ppermute(states, "seq", [(i, i + step) for i in range(blocks) if 0 <= i + step < blocks])
 
-    def hop_on(arrived, step, k, after):
+    def hop_on(arrived, spec, step, k, after):
+        if relayed:
+            near, far = (b_pack, c_pack) if step > 0 else (c_pack, b_pack)
+            wide = arrived.shape[1]
+            taken, sent = call(
+                functools.partial(pass_kernel, step > 0, k),
+                (1,),
+                [SMEM, whole((heads, tokens)) if wide == features else log_spec(k), whole(near.shape), small, spec],
+                [whole((tokens, wide)), whole((tokens // 2, wide + state))],
+                [shape(tokens, wide), shape(tokens // 2, wide + state)],
+                2 * head_flops,
+                5 * unit,
+                "pass_states",
+                after=after,
+            )(meta, log, near, far, arrived)
+            passed = hop(sent, step)
+            return [taken, passed, passed], sent
+        arrived = [arrived]
         for _ in range(hops - 1):
             kept = call(
                 keep_kernel,
@@ -416,22 +589,37 @@
             arrived = arrived + [hop(kept, step)]
         return arrived, kept
 
-    states_in, cots = [], []
-    for k in range(CHUNKS):
-        local, cot_chunk = call(
-            local_kernel,
-            (1,),
-            [SMEM, log_spec(k), small, chunk(k), chunk(k)],
-            [part, part],
-            [shape(tokens, width)] * 2,
-            head_flops,
-            8 * unit,
-            "local_states",
-        )(meta, log, b, x, cot)
-        states_in.append([hop(local, 1)])
-        cots.append(cot_chunk)
-
-    table = jnp.concatenate([expert_ids[0].T.astype(F32), gate_weights[0].T], axis=0)
+    if relayed:
+        moving = hop(x, 1)
+        pack = (tokens + 3 * heads, state)
+        b_pack, c_pack, *cots, cot_both = call(
+            prepare_kernel,
+            (1,),
+            [small, small, whole((heads, tokens)), whole((tokens, features)), whole((2, tokens)), whole((2, tokens))],
+            [whole(pack)] * 2 + [whole((tokens, width + 128))] * CHUNKS + [whole((2 * tokens, width + 128))],
+            [shape(*pack)] * 2 + [shape(tokens, width + 128)] * CHUNKS + [shape(2 * tokens, width + 128)],
+            0,
+            4 * tokens * features,
+            "prepare",
+            vmem=VMEM_ALL,
+        )(b, c, log, cot, expert_ids[0].T, gate_weights[0].T)
+        b_pack, c_pack = hop(b_pack, 1), hop(c_pack, -1)
+    else:
+        moving = []
+        for k in range(CHUNKS):
+            local = call(
+                local_kernel,
+                (1,),
+                [SMEM, log_spec(k), small, chunk(k)],
+                part,
+                shape(tokens, width),
+                head_flops,
+                4 * unit,
+                "local_states",
+            )(meta, log, b, x)
+            moving.append(hop(local, 1))
+        cots = [cot[:, k * width : (k + 1) * width] for k in range(CHUNKS)]
+
     if relayed:
         plans = [
             [
@@ -446,18 +634,21 @@
         weight_shape = (4, tokens, 2 * capacity)
         outs = [pick_shape, weight_shape, weight_shape] * 2
         me = lax.axis_index("exp").astype(jnp.int32)[None]
+        other_cots = [offset(rows, by) for rows, (by, _) in zip(cots, kinds)]
         found = call(
             functools.partial(relay_pick_kernel, experts, capacity, kinds),
             (1,),
-            [SMEM] + [whole((4, tokens))] * 3,
+            [SMEM] + [pl.BlockSpec((tokens, 128), lambda i: (0, width // 128))] * 3,
             [whole(s) for s in outs],
             [jax.ShapeDtypeStruct(s, BF16) for s in outs],
             6 * experts * tokens * tokens,
             4 * slots * tokens,
             "pick_rows",
-        )(me, table, *[offset(table, by) for by, _ in kinds])
+        )(me, cots[0], *other_cots)
         picks, own_weights, relay_weights = found[0::3], found[1::3], found[2::3]
     else:
+        table = jnp.concatenate([expert_ids[0].T.astype(F32), gate_weights[0].T], axis=0)
+        other_cots = [None] * CHUNKS
         plans = [[(0, 0, 0, slots)]] * 2
         pieces_of = [[slots]] * 2
         pick, weights = call(
@@ -536,7 +727,6 @@
     def moved_specs(kind):
         return piece_specs(kind) + ([part] if relayed else [])
 
-    other_cots = [other_of(cots[k], k) for k in range(CHUNKS)]
     inner = call(
         inner_kernel,
         (CHUNKS,),
@@ -547,30 +737,99 @@
         6 * CHUNKS * unit,
         "inner",
     )(meta, log, b, c, x)
-    states_in[0], kept = hop_on(states_in[0], 1, 0, [inner, picks[0]])
-    got_cot, sent = [], kept
-    for k in range(CHUNKS):
-        (sent, *_), pieces = to_experts(cots[k], k, other_cots[k], [sent])
-        got_cot.append(pieces)
-    states_in[1], kept = hop_on(states_in[1], 1, 1, [sent])
+    if relayed:
+        first_in, kept = hop_on(moving, whole((tokens, features)), 1, 0, [inner, picks[0]])
+        second_in = first_in
+    else:
+        first_in, kept = hop_on(moving[0], part, 1, 0, [inner, picks[0]])
+    if relayed:
+        held = call(
+            hold_kernel,
+            (1,),
+            [anywhere] * 2,
+            [anywhere] * 2,
+            [shape(tokens, width + 128)] * 2,
+            0,
+            0,
+            "hold",
+            after=[kept],
+            aliases={0: 0, 1: 1},
+        )(*other_cots)
+        cot_sibling = offset(cot_both, 1)
+        side_others = [offset(rows, 1) for rows in held]
+        table_spec = pl.BlockSpec((tokens, 128), lambda i: (0, width // 128))
+        side_kinds = ((2, 4), (4, 2))
+        side_plans = [
+            [
+                (e, j * capacity, (to ^ source) * capacity, capacity)
+                for e, to in enumerate((0, partner))
+                for j, source in enumerate((0, by, 1, by ^ 1))
+            ]
+            for by, partner in side_kinds
+        ]
+        side_shape, side_weight_shape = (2, 4, capacity, tokens), (4, 2, tokens, capacity)
+        found = call(
+            functools.partial(side_pick_kernel, experts, capacity, side_kinds),
+            (1,),
+            [SMEM] + [table_spec] * 6,
+            [whole(side_shape)] * 4,
+            [jax.ShapeDtypeStruct(side_shape, kind) for kind in (BF16, F32)] * 2,
+            12 * experts * tokens * tokens,
+            8 * slots * tokens,
+            "side_picks",
+        )(me, cots[0], cot_sibling, held[0], side_others[0], held[1], side_others[1])
+        side_picks, side_gated = found[0::2], found[1::2]
+        side_spec = whole((4 * capacity, width))
+        both = [pl.BlockSpec((tokens, width), lambda i, k=k: (k, 0)) for k in range(2)]
+        sent = call(
+            side_gather_kernel,
+            (1,),
+            [whole(side_shape)] * 2 + [spec for k in range(2) for spec in (part, part, both[k], part)],
+            [side_spec] * 4,
+            [shape(4 * capacity, width)] * 4,
+            4 * slots * unit,
+            8 * slots * width,
+            "side_gather",
+            after=[kept],
+        )(*side_picks, *[r for k in range(2) for r in (cots[k], held[k], cot_sibling, side_others[k])])
+        got_cot = [[sent[2 * k], offset(sent[2 * k + 1], side_kinds[k][1])] for k in range(2)]
+        sent = sent[1]
+        early = [[], [pieces[1] for pieces in got_cot]]
+    else:
+        got_cot, sent, early = [], kept, [[], []]
+        for k in range(CHUNKS):
+            (sent, *_), pieces = to_experts(cots[k], k, other_cots[k], [sent])
+            got_cot.append(pieces)
+    if not relayed:
+        second_in, _ = hop_on(moving[1], part, 1, 1, [sent])
+    states_in = [first_in, second_in]
+
+
+    def states_specs(k, w):
+        if not relayed:
+            return [part] * hops
+        return [
+            chunk(k),
+            chunk(k, tokens // 2),
+            pl.BlockSpec((tokens // 2, state), lambda i: (0, w // state)),
+        ]
 
     resid, squares, others = [], [], []
     for k in range(CHUNKS):
         rows, square = call(
-            functools.partial(resid_kernel, hops),
-            (1,),
-            [SMEM, log_spec(k), small, chunk(k)] + [part] * hops,
+            functools.partial(resid_kernel, relayed),
+            (1,),
+            [SMEM, log_spec(k), small, chunk(k)] + states_specs(k, features),
             [part, whole((tokens, 128))],
             [shape(tokens, width), shape(tokens, 128, F32)],
             hops * head_flops,
             (6 + 2 * hops) * unit,
             "resid",
+            after=early[k],
         )(meta, log, c, inner, *states_in[k])
         resid.append(rows)
         squares.append(square)
         others.append(other_of(rows, k))
-    (sent, *_), pieces = to_experts(resid[0], 0, others[0], [resid[1]])
-    got_in = [pieces]
 
     each = 2
     step = width // each
@@ -583,19 +842,31 @@
             pl.BlockSpec((rows, step), lambda i: (0, jnp.clip(i - first, 0, each - 1))) for rows in pieces_of[kind]
         ]
 
+    if relayed:
+        cot_plans = side_plans
+        cot_specs = [
+            pl.BlockSpec((4 * capacity, step), lambda i, k=k: (0, jnp.clip(i - each * k, 0, each - 1)))
+            for k in range(CHUNKS)
+            for _ in range(2)
+        ]
+    else:
+        cot_plans = [plans[k % 2] for k in range(CHUNKS)]
+        cot_specs = [spec for k in range(CHUNKS) for spec in step_specs(k % 2, each * k)]
     back = call(
-        functools.partial(back_kernel, [plans[k % 2] for k in range(CHUNKS)]),
+        functools.partial(back_kernel, cot_plans),
         (each * CHUNKS,),
-        [spec for k in range(CHUNKS) for spec in step_specs(k % 2, each * k)] + [columns(hidden, step)],
+        cot_specs + [columns(hidden, step)],
         slots_hidden,
         shape(slots, hidden, F32),
         CHUNKS * chunk_flops,
         CHUNKS * chunk_bytes,
         "back",
         [pltpu.VMEM((slots, step), BF16)],
-        after=[sent],
+        after=[resid[1]],
     )(*[piece for pieces in got_cot for piece in pieces], down)
-    _, pieces = to_experts(resid[1], 1, others[1], [back])
+    (sent, *_), pieces = to_experts(resid[0], 0, others[0], [back])
+    got_in = [pieces]
+    _, pieces = to_experts(resid[1], 1, others[1], [sent])
     got_in.append(pieces)
 
     def up_spec(k):
@@ -625,7 +896,7 @@
         [pltpu.VMEM((slots, hidden), F32), pltpu.VMEM((slots, 128), F32), pltpu.VMEM((slots, step), BF16)],
     )(*got_in[1], up, total, total_squares, back)
 
-    got_grad = []
+    got_grad, grads, last = [], [], []
     for k in range(CHUNKS):
         kind = k % 2
         expert_grad = call(
@@ -637,25 +908,32 @@
             chunk_flops,
             chunk_bytes,
             "expert_grad",
+            after=last,
         )(pre_grad, up, along, *got_in[k])
-        relay, pieces = to_positions(expert_grad, k)
-        got_grad.append(pieces)
-    outs, last = [], relay
+        last = expert_grad[:1]
+        grads.append(expert_grad)
+    outs = []
     for k in range(CHUNKS):
         kind = k % 2
         expert_out = call(
-            functools.partial(expert_out_kernel, plans[kind]),
+            functools.partial(expert_out_kernel, side_plans[k] if relayed else plans[kind]),
             (each,),
             [slots_hidden, pl.BlockSpec((hidden, step), lambda i, k=k: (0, each * k + i))],
-            step_specs(kind),
-            piece_shapes(kind),
+            [pl.BlockSpec((4 * capacity, step), lambda i: (0, i))] * 2 if relayed else step_specs(kind),
+            [shape(4 * capacity, width)] * 2 if relayed else piece_shapes(kind),
             chunk_flops,
             chunk_bytes,
             "expert_out",
-            after=[last],
+            after=last,
         )(act, down)
         outs.append(expert_out)
-        last = expert_out[0]
+        last = expert_out[:1]
+
+    for k in range(CHUNKS):
+        relay, pieces = to_positions(grads[k], k, last)
+        got_grad.append(pieces)
+        last = [relay]
+    last = relay
 
     def weights_spec(kind):
         return whole(own_weights[kind].shape)
@@ -663,25 +941,28 @@
     dresid, states_after = [], []
     for k in range(CHUNKS):
         kind = k % 2
-        grad, source = call(
+        grads_here = call(
             functools.partial(dresid_kernel, CHUNKS, features),
             (1,),
             [SMEM, log_spec(k), small, weights_spec(kind), chunk(k)]
             + [whole((tokens, 128))] * CHUNKS
             + moved_specs(kind),
-            [part, part],
-            [shape(tokens, width)] * 2,
+            [part] * (1 if relayed else 2),
+            [shape(tokens, width)] * (1 if relayed else 2),
             head_flops + 2 * slots * unit,
             6 * unit + 2 * slots * width,
             "dresid",
             after=[last],
         )(meta, log, c, own_weights[kind], cot, *squares, *got_grad[k])
-        dresid.append(grad)
-        states_after.append([hop(source, -1)])
-        last = grad
-
-    inner_back = [
-        call(
+        dresid.append(grads_here[0])
+        states_after.append(hop(grads_here[-1], -1))
+        last = dresid[k]
+
+    if relayed:
+        states_after[0], last = hop_on(states_after[0], part, -1, 0, [last])
+    inner_back = []
+    for k in range(CHUNKS):
+        last = call(
             inner_back_kernel,
             (1,),
             [SMEM, log_spec(k), small, small, part],
@@ -692,14 +973,65 @@
             "inner_back",
             after=[last],
         )(meta, log, b, c, dresid[k])
-        for k in range(CHUNKS)
-    ]
-    states_after[0], last = hop_on(states_after[0], -1, 0, inner_back)
+        inner_back.append(last)
     got_out = []
-    for k in range(CHUNKS):
-        last, pieces = to_positions(outs[k], k, [last])
-        got_out.append(pieces)
-    states_after[1], last = hop_on(states_after[1], -1, 1, [last])
+    if relayed:
+        held = call(
+            hold_kernel,
+            (1,),
+            [anywhere] * 2,
+            [anywhere] * 2,
+            [shape(4 * capacity, width)] * 2,
+            0,
+            0,
+            "hold",
+            after=[dresid[0]],
+            aliases={0: 0, 1: 1},
+        )(outs[0][1], outs[1][1])
+        side_weights = call(
+            side_weights_kernel,
+            (1,),
+            [whole(side_shape)] * 2,
+            [whole(side_weight_shape)] * 2,
+            [jax.ShapeDtypeStruct(side_weight_shape, BF16)] * 2,
+            0,
+            16 * slots * tokens,
+            "side_weights",
+            after=outs[0][:1],
+        )(*side_gated)
+        out_pieces = [[outs[k][0], offset(held[k], side_kinds[k][1])] for k in range(2)]
+        states_after[1], last = hop_on(states_after[1], part, -1, 1, [last])
+        operands = [*side_weights, *out_pieces[0], *out_pieces[1]]
+        specs = [whole(side_weight_shape)] * 2 + [side_spec] * 4
+        sums = call(
+            side_sums_kernel,
+            (1,),
+            specs,
+            [whole((2 * tokens, width))] * 2,
+            [shape(2 * tokens, width)] * 2,
+            4 * slots * unit,
+            8 * slots * width,
+            "side_sums",
+            after=[last],
+        )(*operands)
+        sums_here = [offset(rows, 1) for rows in sums]
+        sent = call(
+            side_relay_kernel,
+            (1,),
+            specs + [whole((2 * tokens, width))],
+            [part] * 2,
+            [shape(tokens, width)] * 2,
+            4 * slots * unit,
+            8 * slots * width,
+            "side_relay",
+        )(*operands, sums_here[0])
+        last = sent[0]
+        relayed_sums = [offset(sent[k], side_kinds[k][0]) for k in range(2)]
+    else:
+        for k in range(CHUNKS):
+            states_after[k], last = hop_on(states_after[k], part, -1, k, [last])
+            last, pieces = to_positions(outs[k], k, [last])
+            got_out.append(pieces)
 
     def placed(kernel, k, in_specs, operands, earlier, after, flops, nbytes, name):
         more = [] if earlier is None else [earlier]
@@ -718,9 +1050,9 @@
 
     def input_grads(k, earlier, after):
         return placed(
-            functools.partial(grad_kernel, hops),
+            functools.partial(grad_kernel, 3 if relayed else hops, relayed),
             k,
-            [SMEM, log_spec(k), small, part] + [part] * hops,
+            [SMEM, log_spec(k), small, part] + states_specs(0, width),
             [meta, log, b, inner_back[k], *states_after[k]],
             earlier,
             after,
@@ -730,19 +1062,34 @@
         )
 
     input_grad, output = input_grads(0, None, [last]), None
-    for k in range(CHUNKS):
-        kind = k % 2
-        output = placed(
-            output_kernel,
-            k,
-            [weights_spec(kind), part] + moved_specs(kind),
-            [own_weights[kind], resid[k], *got_out[k]],
-            output,
-            [input_grad] if output is None else [],
+    if relayed:
+        output = call(
+            side_output_kernel,
+            (1,),
+            [whole(side_weight_shape)] * 2
+            + [part] * 2
+            + [spec for k in range(2) for spec in (side_spec, side_spec, both[k], part)],
+            whole((tokens, features)),
+            shape(tokens, features),
             2 * slots * unit,
-            4 * unit + 2 * slots * width,
+            8 * unit + 4 * slots * width,
             "output",
-        )
+            after=[input_grad],
+        )(*side_weights, *resid, *[r for k in range(2) for r in (*out_pieces[k], sums_here[1], relayed_sums[k])])
+    else:
+        for k in range(CHUNKS):
+            kind = k % 2
+            output = placed(
+                output_kernel,
+                k,
+                [weights_spec(kind), part] + moved_specs(kind),
+                [own_weights[kind], resid[k], *got_out[k]],
+                output,
+                [input_grad] if output is None else [],
+                2 * slots * unit,
+                4 * unit + 2 * slots * width,
+                "output",
+            )
     input_grad = input_grads(1, input_grad, [output])
     return (output[None], input_grad[None])
 

time: 204 us -> 194 us (0.951)
  starting transfers between devices: 51.4 us -> 42.9 us
  waiting for transfers between devices: 86.9 us -> 90.6 us
  Pallas kernels: 56.4 us -> 53.5 us
    ppermute x8, waiting for transfers between devices: 10.7 us -> 38.1 us  [hop(): lax.ppermute(states, 'seq', [(i, i + step) for i in range(blocks) if 0 <=...]
    ppermute x34 -> x29, waiting for transfers between devices: 76.2 us -> 52.5 us  [offset(): return lax.ppermute(a, 'exp', [(i, i ^ k) for i in range(experts)])]
    ppermute x34 -> x29, starting transfers between devices: 30.5 us -> 23.1 us  [offset(): return lax.ppermute(a, 'exp', [(i, i ^ k) for i in range(experts)])]
    pallas_call x33, Pallas kernels: 56.4 us -> 53.5 us  [call(): return lambda *operands: called(*operands, *after)]
    unnamed x46 -> x44, local copies, waits for them, and re-layouts: 6.45 us -> 4.77 us
  transfers between devices with their start and end apart: 42 -> 37, of which waited for: 22 -> 15; matrix products, arithmetic and copies ran while one was open for 0% -> 0% of each run, Pallas kernels for 23% -> 22%
where the time goes in v5:
time: 194 us
  waiting for transfers between devices  90.6 us (47%)
  Pallas kernels  53.5 us (28%)
  starting transfers between devices  42.9 us (22%)
  local copies, waits for them, and re-layouts  4.77 us (2%)
    pallas_call x33, Pallas kernels, call(): return lambda *operands: called(*operands, *after)  53.5 us
    ppermute x29, waiting for transfers between devices, offset(): return lax.ppermute(a, 'exp', [(i, i ^ k) for i in range(experts)])  52.5 us
    ppermute x8, waiting for transfers between devices, hop(): lax.ppermute(states, 'seq', [(i, i + step) for i in range(blocks) if 0 <=...  38.1 us
    ppermute x29, starting transfers between devices, offset(): return lax.ppermute(a, 'exp', [(i, i ^ k) for i in range(experts)])  23.1 us
    ppermute x8, starting transfers between devices, hop(): lax.ppermute(states, 'seq', [(i, i + step) for i in range(blocks) if 0 <=...  19.8 us
    unnamed x44, local copies, waits for them, and re-layouts  4.77 us
  transfers between devices with their start and end apart: 37, of which 15 were waited for; matrix products, arithmetic and copies ran while one was open for 0% of the time, Pallas kernels for 22%

profile of v5, /device:TPU:0, one launch (start us, length us, event | category | flops | bytes accessed | tf_op | source)
XLA Modules:
  0.0 193.7 jit_solution(3556578187519129904)
XLA Ops:
  0.6 6.1 %collective-permute-start.5 = (bf16[128,4096]{1,0:T(8,128)(2,1)}, bf16[128,4096]{1,0:T(8,128)(2,1)}, u32[]{:S(2)}, u32[]{:S(2)}) collective-permute-start(bf16[128,4096]{1,0:T(8,128)(2,1)} %bitcast.61), channel_id=1, source_target_pairs={{0,8},{8,16},{16,24},{1,9},{9,17},{17,25},{2,10},{10,18},{18,26},{... | collective-permute-start | bytes 3145736 | tf_op jit(solution)/shard_map/ppermute | solution.py:557
  6.7 2.8 %prepare.1 = (bf16[224,128]{1,0:T(8,128)(2,1)}, bf16[224,128]{1,0:T(8,128)(2,1)}, bf16[128,2176]{1,0:T(8,128)(2,1)}, bf16[128,2176]{1,0:T(8,128)(2,1)}, bf16[256,2176]{1,0:T(8,128)(2,1)}) custom-call(bf16[128,128]{1,0:T(8,128)(2,1)} %bitcast.55, bf16[128,128]{1,0:T(8,128)(2,1)} %bitcast.47, f32[32,128]{1,0:T(8,128)} %bitcast.34, bf16[128,4096]{1,0:T(8,128)(2,1)} %bitcast.29, ...), custom_call_target="tpu_custom_call" | custom-call | bytes 2097152 | tf_op jit(solution)/shard_map/prepare/pallas_call | solution.py:45
  12.5 2.5 %collective-permute-start.3 = (bf16[224,128]{1,0:T(8,128)(2,1)}, bf16[224,128]{1,0:T(8,128)(2,1)S(1)}, u32[]{:S(2)}, u32[]{:S(2)}) collective-permute-start(bf16[224,128]{1,0:T(8,128)(2,1)} %get-tuple-element.69), channel_id=1, source_target_pairs={{0,8},{8,16},{16,24},{1,9},{9,17},{17,25},{2,10},{10,18},{18,26},{... | collective-permute-start | bytes 172040 | tf_op jit(solution)/shard_map/ppermute | solution.py:557
  15.0 8.8 %collective-permute-done.1.refs_2_.refs_0_ = bf16[128,2176]{1,0:T(8,128)(2,1)S(1)} collective-permute-done((bf16[128,2176]{1,0:T(8,128)(2,1)}, bf16[128,2176]{1,0:T(8,128)(2,1)S(1)}, u32[]{:S(2)}, u32[]{:S(2)}) %collective-permute-start.1) | collective-permute-done | bytes 557088 | tf_op jit(solution)/shard_map/ppermute | solution.py:554
  28.0 2.5 %inner.1.refs_5_.refs_3_ = f32[128,4096]{1,0:T(8,128)S(1)} custom-call(s32[7]{0:T(128)S(1)} %pad_add_fusion.refs_0_, f32[32,128]{1,0:T(8,128)S(1)} %bitcast.35, bf16[128,128]{1,0:T(8,128)(2,1)S(1)} %bitcast.56, bf16[128,128]{1,0:T(8,128)(2,1)S(1)} %bitcast.48, bf16[128,4096]{1,0:T(8,128)(2,1)S(1)} %bitcast.62), custom_call_target="tpu_custom_call" | custom-call | flops 268435456 | bytes 3145728 | tf_op jit(solution)/shard_map/inner/pallas_call | solution.py:45
  31.0 2.6 %pass_states.3 = (bf16[128,4096]{1,0:T(8,128)(2,1)S(1)}, bf16[64,4224]{1,0:T(8,128)(2,1)S(1)}) custom-call(s32[7]{0:T(128)S(1)} %pad_add_fusion.refs_0_, f32[32,128]{1,0:T(8,128)S(1)} %bitcast.36, bf16[224,128]{1,0:T(8,128)(2,1)S(1)} %collective-permute-done.3.refs_2_.refs_3_, bf16[224,128]{1,0:T(8,128)(2,1)S(1)} %collective-permute-done.4.refs_3_.refs_2_, ...), custom_call_target="tpu_custom_call" | custom-call | flops 134217728 | bytes 1310720 | tf_op jit(solution)/shard_map/pass_states/pallas_call | solution.py:45
  41.1 4.6 %collective-permute-start.8 = (bf16[64,4224]{1,0:T(8,128)(2,1)S(1)}, bf16[64,4224]{1,0:T(8,128)(2,1)S(1)}, u32[]{:S(2)}, u32[]{:S(2)}) collective-permute-start(bf16[64,4224]{1,0:T(8,128)(2,1)S(1)} %get-tuple-element.72.refs_2_.refs_10_), channel_id=1, source_target_pairs={{0,8},{8,16},{16,24},{1,9},{9,17},{17,25},{2,10},{10,18},{18,26},{... | collective-permute-start | bytes 1622024 | tf_op jit(solution)/shard_map/ppermute | solution.py:557
  45.7 11.2 %collective-permute-done.8.refs_5_.refs_6_ = bf16[64,4224]{1,0:T(8,128)(2,1)S(1)} collective-permute-done((bf16[64,4224]{1,0:T(8,128)(2,1)S(1)}, bf16[64,4224]{1,0:T(8,128)(2,1)S(1)}, u32[]{:S(2)}, u32[]{:S(2)}) %collective-permute-start.8) | collective-permute-done | bytes 540704 | tf_op jit(solution)/shard_map/ppermute | solution.py:557
  62.0 6.0 %back.1.refs_3_.refs_7_ = f32[384,1024]{1,0:T(8,128)S(1)} custom-call(bf16[192,2048]{1,0:T(8,128)(2,1)S(1)} %get-tuple-element.85.refs_0_, bf16[192,2048]{1,0:T(8,128)(2,1)S(1)} %collective-permute-done.9.refs_7_.refs_1_, bf16[192,2048]{1,0:T(8,128)(2,1)S(1)} %get-tuple-element.86.refs_2_, bf16[192,2048]{1,0:T(8,128)(2,1)S(1)} %collective-permute-done.10.refs_8_.refs_3_, ...), custom_call_target="tpu_custom_call" | custom-call | flops 3221225472 | bytes 11534336 | tf_op jit(solution)/shard_map/back/pallas_call | solution.py:45
  68.0 2.9 %collective-permute-done.12.refs_2_ = bf16[128,2048]{1,0:T(8,128)(2,1)S(1)} collective-permute-done((bf16[128,2048]{1,0:T(8,128)(2,1)S(1)}, bf16[128,2048]{1,0:T(8,128)(2,1)S(1)}, u32[]{:S(2)}, u32[]{:S(2)}) %collective-permute-start.12) | collective-permute-done | bytes 524320 | tf_op jit(solution)/shard_map/ppermute | solution.py:554
  76.2 7.5 %collective-permute-done.17.refs_2_.refs_5_ = bf16[96,2048]{1,0:T(8,128)(2,1)S(1)} collective-permute-done((bf16[96,2048]{1,0:T(8,128)(2,1)S(1)}, bf16[96,2048]{1,0:T(8,128)(2,1)S(1)}, u32[]{:S(2)}, u32[]{:S(2)}) %collective-permute-start.17) | collective-permute-done | bytes 393248 | tf_op jit(solution)/shard_map/ppermute | solution.py:554
  83.7 7.5 %collective-permute-done.18.refs_3_.refs_6_ = bf16[96,2048]{1,0:T(8,128)(2,1)S(1)} collective-permute-done((bf16[96,2048]{1,0:T(8,128)(2,1)S(1)}, bf16[96,2048]{1,0:T(8,128)(2,1)S(1)}, u32[]{:S(2)}, u32[]{:S(2)}) %collective-permute-start.18) | collective-permute-done | bytes 393248 | tf_op jit(solution)/shard_map/ppermute | solution.py:554
  91.3 2.5 %up_first.1 = (f32[384,1024]{1,0:T(8,128)S(1)}, f32[384,128]{1,0:T(8,128)S(1)}) custom-call(bf16[96,2048]{1,0:T(8,128)(2,1)S(1)} %get-tuple-element.87.refs_3_.refs_0_, bf16[96,2048]{1,0:T(8,128)(2,1)S(1)} %collective-permute-done.16.refs_1_.refs_4_, bf16[96,2048]{1,0:T(8,128)(2,1)S(1)} %collective-permute-done.17.refs_2_.refs_5_, ...), custom_call_target="tpu_custom_call" | custom-call | flops 1610612736 | bytes 5767168 | tf_op jit(solution)/shard_map/up_first/pallas_call | solution.py:45
  93.8 3.5 %up_last.1 = (bf16[384,1024]{1,0:T(8,128)(2,1)S(1)}, bf16[384,1024]{1,0:T(8,128)(2,1)S(1)}, f32[384,128]{1,0:T(8,128)S(1)}) custom-call(bf16[96,2048]{1,0:T(8,128)(2,1)S(1)} %get-tuple-element.88.refs_0_.refs_3_, bf16[96,2048]{1,0:T(8,128)(2,1)S(1)} %collective-permute-done.13.refs_1_.refs_4_, bf16[96,2048]{1,0:T(8,128)(2,1)S(1)} %collective-permute-done.14.refs_2_.refs_5_, ...), custom_call_target="tpu_custom_call" | custom-call | flops 1610612736 | bytes 5767168 | tf_op jit(solution)/shard_map/up_last/pallas_call | solution.py:45
  97.3 2.4 %expert_grad.2 = (bf16[96,2048]{1,0:T(8,128)(2,1)S(1)}, bf16[96,2048]{1,0:T(8,128)(2,1)S(1)}, bf16[96,2048]{1,0:T(8,128)(2,1)S(1)}, bf16[96,2048]{1,0:T(8,128)(2,1)S(1)}) custom-call(bf16[384,1024]{1,0:T(8,128)(2,1)S(1)} %get-tuple-element.98.refs_0_, bf16[4096,1024]{1,0:T(8,128)(2,1)S(1)} %bitcast.22, f32[384,128]{1,0:T(8,128)S(1)} %get-tuple-element.99.refs_2_, ...), custom_call_target="tpu_custom_call" | custom-call | flops 1610612736 | bytes 5767168 | tf_op jit(solution)/shard_map/expert_grad/pallas_call | solution.py:45
  101.8 2.4 %expert_grad.3 = (bf16[96,2048]{1,0:T(8,128)(2,1)S(1)}, bf16[96,2048]{1,0:T(8,128)(2,1)S(1)}, bf16[96,2048]{1,0:T(8,128)(2,1)S(1)}, bf16[96,2048]{1,0:T(8,128)(2,1)S(1)}) custom-call(bf16[384,1024]{1,0:T(8,128)(2,1)S(1)} %get-tuple-element.98.refs_0_, bf16[4096,1024]{1,0:T(8,128)(2,1)S(1)} %bitcast.23, f32[384,128]{1,0:T(8,128)S(1)} %get-tuple-element.99.refs_2_, ...), custom_call_target="tpu_custom_call" | custom-call | flops 1610612736 | bytes 5767168 | tf_op jit(solution)/shard_map/expert_grad/pallas_call | solution.py:45
  105.4 2.4 %expert_out.2 = (bf16[192,2048]{1,0:T(8,128)(2,1)S(1)}, bf16[192,2048]{1,0:T(8,128)(2,1)S(1)}) custom-call(bf16[384,1024]{1,0:T(8,128)(2,1)S(1)} %get-tuple-element.97.refs_0_, bf16[1024,4096]{1,0:T(8,128)(2,1)S(1)} %bitcast.27, bf16[96,2048]{1,0:T(8,128)(2,1)S(1)} %get-tuple-element.101.refs_2_.refs_1_.refs_7_), custom_call_target="tpu_custom_call" | custom-call | flops 1610612736 | bytes 5767168 | tf_op jit(solution)/shard_map/expert_out/pallas_call | solution.py:45
  108.8 2.4 %expert_out.3 = (bf16[192,2048]{1,0:T(8,128)(2,1)S(1)}, bf16[192,2048]{1,0:T(8,128)(2,1)S(1)}) custom-call(bf16[384,1024]{1,0:T(8,128)(2,1)S(1)} %get-tuple-element.97.refs_0_, bf16[1024,4096]{1,0:T(8,128)(2,1)S(1)} %bitcast.28, bf16[192,2048]{1,0:T(8,128)(2,1)S(1)} %get-tuple-element.102.refs_2_.refs_4_), custom_call_target="tpu_custom_call" | custom-call | flops 1610612736 | bytes 5767168 | tf_op jit(solution)/shard_map/expert_out/pallas_call | solution.py:45
  112.3 6.7 %collective-permute-done.21.refs_4_.refs_10_ = bf16[96,2048]{1,0:T(8,128)(2,1)S(1)} collective-permute-done((bf16[96,2048]{1,0:T(8,128)(2,1)S(1)}, bf16[96,2048]{1,0:T(8,128)(2,1)S(1)}, u32[]{:S(2)}, u32[]{:S(2)}) %collective-permute-start.21) | collective-permute-done | bytes 393248 | tf_op jit(solution)/shard_map/ppermute | solution.py:554
  120.3 3.2 %collective-permute-done.25.refs_4_.refs_10_ = bf16[96,2048]{1,0:T(8,128)(2,1)S(1)} collective-permute-done((bf16[96,2048]{1,0:T(8,128)(2,1)S(1)}, bf16[96,2048]{1,0:T(8,128)(2,1)S(1)}, u32[]{:S(2)}, u32[]{:S(2)}) %collective-permute-start.25) | collective-permute-done | bytes 393248 | tf_op jit(solution)/shard_map/ppermute | solution.py:554
  125.3 10.4 %collective-permute-done.22.refs_11_ = bf16[128,2048]{1,0:T(8,128)(2,1)S(1)} collective-permute-done((bf16[128,2048]{1,0:T(8,128)(2,1)S(1)}, bf16[128,2048]{1,0:T(8,128)(2,1)S(1)}, u32[]{:S(2)}, u32[]{:S(2)}) %collective-permute-start.22) | collective-permute-done | bytes 524320 | tf_op jit(solution)/shard_map/ppermute | solution.py:554
  143.0 13.0 %collective-permute-done.30.refs_4_ = bf16[128,2048]{1,0:T(8,128)(2,1)S(1)} collective-permute-done((bf16[128,2048]{1,0:T(8,128)(2,1)S(1)}, bf16[128,2048]{1,0:T(8,128)(2,1)S(1)}, u32[]{:S(2)}, u32[]{:S(2)}) %collective-permute-start.30) | collective-permute-done | bytes 524320 | tf_op jit(solution)/shard_map/ppermute | solution.py:557
  160.2 4.9 %collective-permute-done.29.refs_4_ = bf16[128,2048]{1,0:T(8,128)(2,1)S(1)} collective-permute-done((bf16[128,2048]{1,0:T(8,128)(2,1)S(1)}, bf16[128,2048]{1,0:T(8,128)(2,1)S(1)}, u32[]{:S(2)}, u32[]{:S(2)}) %collective-permute-start.29) | collective-permute-done | bytes 524320 | tf_op jit(solution)/shard_map/ppermute | solution.py:557
  176.1 8.9 %collective-permute-done.35.refs_5_.refs_6_ = bf16[64,2176]{1,0:T(8,128)(2,1)S(1)} collective-permute-done((bf16[64,2176]{1,0:T(8,128)(2,1)S(1)}, bf16[64,2176]{1,0:T(8,128)(2,1)S(1)}, u32[]{:S(2)}, u32[]{:S(2)}) %collective-permute-start.35) | collective-permute-done | bytes 278560 | tf_op jit(solution)/shard_map/ppermute | solution.py:557
  (130 shorter events, 64.9 us)
Async XLA Ops:
  0.6 30.4 %collective-permute-start.5 = (bf16[128,4096]{1,0:T(8,128)(2,1)}, bf16[128,4096]{1,0:T(8,128)(2,1)}, u32[]{:S(2)}, u32[]{:S(2)}) collective-permute-start(bf16[128,4096]{1,0:T(8,128)(2,1)} %bitcast.61), channel_id=1, source_target_pairs={{0,8},{8,16},{16,24},{1,9},{9,17},{17,25},{2,10},{10,18},{18,26},{... | collective-permute-start | bytes 3145736 | tf_op jit(solution)/shard_map/ppermute | solution.py:557
  11.0 19.6 %collective-permute-start.2 = (bf16[128,2176]{1,0:T(8,128)(2,1)}, bf16[128,2176]{1,0:T(8,128)(2,1)S(1)}, u32[]{:S(2)}, u32[]{:S(2)}) collective-permute-start(bf16[128,2176]{1,0:T(8,128)(2,1)} %get-tuple-element.68.refs_6_), channel_id=1, source_target_pairs={{0,4},{1,5},{2,6},{3,7},{4,0},{5,1},{6,2},{7,3},{8,12},{9,13},{10,... | collective-permute-start | bytes 1671176 | tf_op jit(solution)/shard_map/ppermute | solution.py:554
  12.5 21.8 %collective-permute-start = (bf16[256,2176]{1,0:T(8,128)(2,1)}, bf16[256,2176]{1,0:T(8,128)(2,1)S(1)}, u32[]{:S(2)}, u32[]{:S(2)}) collective-permute-start(bf16[256,2176]{1,0:T(8,128)(2,1)} %get-tuple-element.67), channel_id=1, source_target_pairs={{0,1},{1,0},{2,3},{3,2},{4,5},{5,4},{6,7},{7,6},{8,9},{9,8},{10,11... | collective-permute-start | bytes 3342344 | tf_op jit(solution)/shard_map/ppermute | solution.py:554
  12.5 18.5 %collective-permute-start.3 = (bf16[224,128]{1,0:T(8,128)(2,1)}, bf16[224,128]{1,0:T(8,128)(2,1)S(1)}, u32[]{:S(2)}, u32[]{:S(2)}) collective-permute-start(bf16[224,128]{1,0:T(8,128)(2,1)} %get-tuple-element.69), channel_id=1, source_target_pairs={{0,8},{8,16},{16,24},{1,9},{9,17},{17,25},{2,10},{10,18},{18,26},{... | collective-permute-start | bytes 172040 | tf_op jit(solution)/shard_map/ppermute | solution.py:557
  38.0 21.0 %collective-permute-start.10 = (bf16[192,2048]{1,0:T(8,128)(2,1)S(1)}, bf16[192,2048]{1,0:T(8,128)(2,1)S(1)}, u32[]{:S(2)}, u32[]{:S(2)}) collective-permute-start(bf16[192,2048]{1,0:T(8,128)(2,1)S(1)} %get-tuple-element.82), channel_id=1, source_target_pairs={{0,2},{1,3},{2,0},{3,1},{4,6},{5,7},{6,4},{7,5},{8,10},{9,11},{10,... | collective-permute-start | bytes 2359304 | tf_op jit(solution)/shard_map/ppermute | solution.py:554
  39.6 19.4 %collective-permute-start.9 = (bf16[192,2048]{1,0:T(8,128)(2,1)S(1)}, bf16[192,2048]{1,0:T(8,128)(2,1)S(1)}, u32[]{:S(2)}, u32[]{:S(2)}) collective-permute-start(bf16[192,2048]{1,0:T(8,128)(2,1)S(1)} %get-tuple-element.81), channel_id=1, source_target_pairs={{0,4},{1,5},{2,6},{3,7},{4,0},{5,1},{6,2},{7,3},{8,12},{9,13},{10,... | collective-permute-start | bytes 2359304 | tf_op jit(solution)/shard_map/ppermute | solution.py:554
  41.1 15.8 %collective-permute-start.8 = (bf16[64,4224]{1,0:T(8,128)(2,1)S(1)}, bf16[64,4224]{1,0:T(8,128)(2,1)S(1)}, u32[]{:S(2)}, u32[]{:S(2)}) collective-permute-start(bf16[64,4224]{1,0:T(8,128)(2,1)S(1)} %get-tuple-element.72.refs_2_.refs_10_), channel_id=1, source_target_pairs={{0,8},{8,16},{16,24},{1,9},{9,17},{17,25},{2,10},{10,18},{18,26},{... | collective-permute-start | bytes 1622024 | tf_op jit(solution)/shard_map/ppermute | solution.py:557
  72.3 18.9 %collective-permute-start.18 = (bf16[96,2048]{1,0:T(8,128)(2,1)S(1)}, bf16[96,2048]{1,0:T(8,128)(2,1)S(1)}, u32[]{:S(2)}, u32[]{:S(2)}) collective-permute-start(bf16[96,2048]{1,0:T(8,128)(2,1)S(1)} %get-tuple-element.94), channel_id=1, source_target_pairs={{0,5},{1,4},{2,7},{3,6},{4,1},{5,0},{6,3},{7,2},{8,13},{9,12},{10,... | collective-permute-start | bytes 1179656 | tf_op jit(solution)/shard_map/ppermute | solution.py:554
  74.3 19.5 %collective-permute-start.13 = (bf16[96,2048]{1,0:T(8,128)(2,1)S(1)}, bf16[96,2048]{1,0:T(8,128)(2,1)S(1)}, u32[]{:S(2)}, u32[]{:S(2)}) collective-permute-start(bf16[96,2048]{1,0:T(8,128)(2,1)S(1)} %get-tuple-element.89), channel_id=1, source_target_pairs={{0,1},{1,0},{2,3},{3,2},{4,5},{5,4},{6,7},{7,6},{8,9},{9,8},{10,11... | collective-permute-start | bytes 1179656 | tf_op jit(solution)/shard_map/ppermute | solution.py:554
  74.7 19.1 %collective-permute-start.14 = (bf16[96,2048]{1,0:T(8,128)(2,1)S(1)}, bf16[96,2048]{1,0:T(8,128)(2,1)S(1)}, u32[]{:S(2)}, u32[]{:S(2)}) collective-permute-start(bf16[96,2048]{1,0:T(8,128)(2,1)S(1)} %get-tuple-element.90), channel_id=1, source_target_pairs={{0,2},{1,3},{2,0},{3,1},{4,6},{5,7},{6,4},{7,5},{8,10},{9,11},{10,... | collective-permute-start | bytes 1179656 | tf_op jit(solution)/shard_map/ppermute | solution.py:554
  75.3 18.5 %collective-permute-start.15 = (bf16[96,2048]{1,0:T(8,128)(2,1)S(1)}, bf16[96,2048]{1,0:T(8,128)(2,1)S(1)}, u32[]{:S(2)}, u32[]{:S(2)}) collective-permute-start(bf16[96,2048]{1,0:T(8,128)(2,1)S(1)} %get-tuple-element.91), channel_id=1, source_target_pairs={{0,3},{1,2},{2,1},{3,0},{4,7},{5,6},{6,5},{7,4},{8,11},{9,10},{10,... | collective-permute-start | bytes 1179656 | tf_op jit(solution)/shard_map/ppermute | solution.py:554
  101.3 17.7 %collective-permute-start.21 = (bf16[96,2048]{1,0:T(8,128)(2,1)S(1)}, bf16[96,2048]{1,0:T(8,128)(2,1)S(1)}, u32[]{:S(2)}, u32[]{:S(2)}) collective-permute-start(bf16[96,2048]{1,0:T(8,128)(2,1)S(1)} %get-tuple-element.112), channel_id=1, source_target_pairs={{0,5},{1,4},{2,7},{3,6},{4,1},{5,0},{6,3},{7,2},{8,13},{9,12},{10,... | collective-permute-start | bytes 1179656 | tf_op jit(solution)/shard_map/ppermute | solution.py:554
  104.1 16.2 %collective-permute-start.23 = (bf16[96,2048]{1,0:T(8,128)(2,1)S(1)}, bf16[96,2048]{1,0:T(8,128)(2,1)S(1)}, u32[]{:S(2)}, u32[]{:S(2)}) collective-permute-start(bf16[96,2048]{1,0:T(8,128)(2,1)S(1)} %get-tuple-element.116), channel_id=1, source_target_pairs={{0,1},{1,0},{2,3},{3,2},{4,5},{5,4},{6,7},{7,6},{8,9},{9,8},{10,11... | collective-permute-start | bytes 1179656 | tf_op jit(solution)/shard_map/ppermute | solution.py:554
  104.9 15.4 %collective-permute-start.24 = (bf16[96,2048]{1,0:T(8,128)(2,1)S(1)}, bf16[96,2048]{1,0:T(8,128)(2,1)S(1)}, u32[]{:S(2)}, u32[]{:S(2)}) collective-permute-start(bf16[96,2048]{1,0:T(8,128)(2,1)S(1)} %get-tuple-element.117), channel_id=1, source_target_pairs={{0,2},{1,3},{2,0},{3,1},{4,6},{5,7},{6,4},{7,5},{8,10},{9,11},{10,... | collective-permute-start | bytes 1179656 | tf_op jit(solution)/shard_map/ppermute | solution.py:554
  107.8 15.7 %collective-permute-start.25 = (bf16[96,2048]{1,0:T(8,128)(2,1)S(1)}, bf16[96,2048]{1,0:T(8,128)(2,1)S(1)}, u32[]{:S(2)}, u32[]{:S(2)}) collective-permute-start(bf16[96,2048]{1,0:T(8,128)(2,1)S(1)} %get-tuple-element.118), channel_id=1, source_target_pairs={{0,3},{1,2},{2,1},{3,0},{4,7},{5,6},{6,5},{7,4},{8,11},{9,10},{10,... | collective-permute-start | bytes 1179656 | tf_op jit(solution)/shard_map/ppermute | solution.py:554
  119.7 16.0 %collective-permute-start.22 = (bf16[128,2048]{1,0:T(8,128)(2,1)S(1)}, bf16[128,2048]{1,0:T(8,128)(2,1)S(1)}, u32[]{:S(2)}, u32[]{:S(2)}) collective-permute-start(bf16[128,2048]{1,0:T(8,128)(2,1)S(1)} %relay.2.refs_5_), channel_id=1, source_target_pairs={{0,2},{1,3},{2,0},{3,1},{4,6},{5,7},{6,4},{7,5},{8,10},{9,11},{10,... | collective-permute-start | bytes 1572872 | tf_op jit(solution)/shard_map/ppermute | solution.py:554
  124.2 15.9 %collective-permute-start.28 = (bf16[128,2048]{1,0:T(8,128)(2,1)S(1)}, bf16[128,2048]{1,0:T(8,128)(2,1)S(1)}, u32[]{:S(2)}, u32[]{:S(2)}) collective-permute-start(bf16[128,2048]{1,0:T(8,128)(2,1)S(1)} %relay.3.refs_12_), channel_id=1, source_target_pairs={{0,4},{1,5},{2,6},{3,7},{4,0},{5,1},{6,2},{7,3},{8,12},{9,13},{10,... | collective-permute-start | bytes 1572872 | tf_op jit(solution)/shard_map/ppermute | solution.py:554
  137.0 29.5 %collective-permute-start.26 = (bf16[192,2048]{1,0:T(8,128)(2,1)S(1)}, bf16[192,2048]{1,0:T(8,128)(2,1)S(1)}, u32[]{:S(2)}, u32[]{:S(2)}) collective-permute-start(bf16[192,2048]{1,0:T(8,128)(2,1)S(1)} %get-tuple-element.119), channel_id=1, source_target_pairs={{0,4},{1,5},{2,6},{3,7},{4,0},{5,1},{6,2},{7,3},{8,12},{9,13},{10,... | collective-permute-start | bytes 2359304 | tf_op jit(solution)/shard_map/ppermute | solution.py:554
  138.0 28.5 %collective-permute-start.27 = (bf16[192,2048]{1,0:T(8,128)(2,1)S(1)}, bf16[192,2048]{1,0:T(8,128)(2,1)S(1)}, u32[]{:S(2)}, u32[]{:S(2)}) collective-permute-start(bf16[192,2048]{1,0:T(8,128)(2,1)S(1)} %get-tuple-element.120), channel_id=1, source_target_pairs={{0,2},{1,3},{2,0},{3,1},{4,6},{5,7},{6,4},{7,5},{8,10},{9,11},{10,... | collective-permute-start | bytes 2359304 | tf_op jit(solution)/shard_map/ppermute | solution.py:554
  138.6 17.4 %collective-permute-start.30 = (bf16[128,2048]{1,0:T(8,128)(2,1)S(1)}, bf16[128,2048]{1,0:T(8,128)(2,1)S(1)}, u32[]{:S(2)}, u32[]{:S(2)}) collective-permute-start(bf16[128,2048]{1,0:T(8,128)(2,1)S(1)} %dresid.2.refs_2_.refs_12_.refs_4_), channel_id=1, source_target_pairs={{8,0},{16,8},{24,16},{9,1},{17,9},{25,17},{10,2},{18,10},{26,18},{... | collective-permute-start | bytes 1572872 | tf_op jit(solution)/shard_map/ppermute | solution.py:557
  141.4 23.7 %collective-permute-start.29 = (bf16[128,2048]{1,0:T(8,128)(2,1)S(1)}, bf16[128,2048]{1,0:T(8,128)(2,1)S(1)}, u32[]{:S(2)}, u32[]{:S(2)}) collective-permute-start(bf16[128,2048]{1,0:T(8,128)(2,1)S(1)} %dresid.3.refs_5_.refs_4_), channel_id=1, source_target_pairs={{8,0},{16,8},{24,16},{9,1},{17,9},{25,17},{10,2},{18,10},{26,18},{... | collective-permute-start | bytes 1572872 | tf_op jit(solution)/shard_map/ppermute | solution.py:557
  167.8 19.4 %collective-permute-start.31 = (bf16[256,2048]{1,0:T(8,128)(2,1)S(1)}, bf16[256,2048]{1,0:T(8,128)(2,1)S(1)}, u32[]{:S(2)}, u32[]{:S(2)}) collective-permute-start(bf16[256,2048]{1,0:T(8,128)(2,1)S(1)} %get-tuple-element.124), channel_id=1, source_target_pairs={{0,1},{1,0},{2,3},{3,2},{4,5},{5,4},{6,7},{7,6},{8,9},{9,8},{10,11... | collective-permute-start | bytes 3145736 | tf_op jit(solution)/shard_map/ppermute | solution.py:554
  171.1 16.1 %collective-permute-start.33 = (bf16[128,2048]{1,0:T(8,128)(2,1)S(1)}, bf16[128,2048]{1,0:T(8,128)(2,1)S(1)}, u32[]{:S(2)}, u32[]{:S(2)}) collective-permute-start(bf16[128,2048]{1,0:T(8,128)(2,1)S(1)} %get-tuple-element.126.refs_7_), channel_id=1, source_target_pairs={{0,2},{1,3},{2,0},{3,1},{4,6},{5,7},{6,4},{7,5},{8,10},{9,11},{10,... | collective-permute-start | bytes 1572872 | tf_op jit(solution)/shard_map/ppermute | solution.py:554
  174.8 15.5 %collective-permute-start.36 = (bf16[64,2176]{1,0:T(8,128)(2,1)S(1)}, bf16[64,2176]{1,0:T(8,128)(2,1)S(1)}, u32[]{:S(2)}, u32[]{:S(2)}) collective-permute-start(bf16[64,2176]{1,0:T(8,128)(2,1)S(1)} %get-tuple-element.123.refs_6_), channel_id=1, source_target_pairs={{8,0},{16,8},{24,16},{9,1},{17,9},{25,17},{10,2},{18,10},{26,18},{... | collective-permute-start | bytes 835592 | tf_op jit(solution)/shard_map/ppermute | solution.py:557
  (35 other events, 359.2 us)

commit v6 on v5

--- a/solution.py
+++ b/solution.py
@@ -386,18 +386,20 @@
 
 
 def side_sums_kernel(*refs):
-    weights, pieces, relayed_ref, own_ref = refs[:2], (refs[2:4], refs[4:6]), refs[6], refs[7]
-    size = weights[0].shape[2]
-    for ref, source in ((relayed_ref, 3), (own_ref, 2)):
+    weights, pieces, outs = refs[:2], (refs[2:4], refs[4:6]), refs[6:]
+    for i, source in enumerate((3, 2)):
         for k in range(2):
-            ref[k * size : (k + 1) * size, :] = partial(weights[k], pieces[k], source).astype(BF16)
+            outs[2 * i + k][...] = partial(weights[k], pieces[k], source).astype(BF16)
+
+
+def tick_kernel(out_ref):
+    out_ref[...] = jnp.zeros_like(out_ref)
 
 
 def side_relay_kernel(*refs):
-    weights, pieces, arrived, outs = refs[:2], (refs[2:4], refs[4:6]), refs[6], refs[7:]
-    size = weights[0].shape[2]
+    weights, pieces, arrived, outs = refs[:2], (refs[2:4], refs[4:6]), refs[6:8], refs[8:]
     for k in range(2):
-        total = partial(weights[k], pieces[k], 1) + arrived[k * size : (k + 1) * size, :].astype(F32)
+        total = partial(weights[k], pieces[k], 1) + arrived[k][...].astype(F32)
         outs[k][...] = total.astype(BF16)
 
 
@@ -620,6 +622,12 @@
             moving.append(hop(local, 1))
         cots = [cot[:, k * width : (k + 1) * width] for k in range(CHUNKS)]
 
+    def tick(arrived):
+        mark = call(
+            tick_kernel, (1,), [], whole((16, 128)), shape(16, 128), 0, 0, "tick", after=[arrived]
+        )()
+        return offset(mark, 1)
+
     if relayed:
         plans = [
             [
@@ -746,17 +754,17 @@
         held = call(
             hold_kernel,
             (1,),
-            [anywhere] * 2,
-            [anywhere] * 2,
-            [shape(tokens, width + 128)] * 2,
+            [anywhere] * 3,
+            [anywhere] * 3,
+            [shape(tokens, width + 128)] * 2 + [shape(2 * tokens, width + 128)],
             0,
             0,
             "hold",
-            after=[kept],
-            aliases={0: 0, 1: 1},
-        )(*other_cots)
-        cot_sibling = offset(cot_both, 1)
-        side_others = [offset(rows, 1) for rows in held]
+            after=[moving, inner, b_pack, c_pack],
+            aliases={0: 0, 1: 1, 2: 2},
+        )(*other_cots, cot_both)
+        cot_sibling = offset(held[2], 1)
+        side_others = [offset(rows, 1) for rows in held[:2]]
         table_spec = pl.BlockSpec((tokens, 128), lambda i: (0, width // 128))
         side_kinds = ((2, 4), (4, 2))
         side_plans = [
@@ -985,7 +993,7 @@
             0,
             0,
             "hold",
-            after=[dresid[0]],
+            after=[dresid[1]],
             aliases={0: 0, 1: 1},
         )(outs[0][1], outs[1][1])
         side_weights = call(
@@ -1000,31 +1008,32 @@
             after=outs[0][:1],
         )(*side_gated)
         out_pieces = [[outs[k][0], offset(held[k], side_kinds[k][1])] for k in range(2)]
-        states_after[1], last = hop_on(states_after[1], part, -1, 1, [last])
         operands = [*side_weights, *out_pieces[0], *out_pieces[1]]
         specs = [whole(side_weight_shape)] * 2 + [side_spec] * 4
         sums = call(
             side_sums_kernel,
             (1,),
             specs,
-            [whole((2 * tokens, width))] * 2,
-            [shape(2 * tokens, width)] * 2,
+            [part] * 4,
+            [shape(tokens, width)] * 4,
             4 * slots * unit,
             8 * slots * width,
             "side_sums",
             after=[last],
         )(*operands)
         sums_here = [offset(rows, 1) for rows in sums]
+        states_after[1], last = hop_on(states_after[1], part, -1, 1, [sums[0]])
         sent = call(
             side_relay_kernel,
             (1,),
-            specs + [whole((2 * tokens, width))],
+            specs + [part] * 2,
             [part] * 2,
             [shape(tokens, width)] * 2,
             4 * slots * unit,
             8 * slots * width,
             "side_relay",
-        )(*operands, sums_here[0])
+            after=[last],
+        )(*operands, *sums_here[:2])
         last = sent[0]
         relayed_sums = [offset(sent[k], side_kinds[k][0]) for k in range(2)]
     else:
@@ -1063,19 +1072,21 @@
 
     input_grad, output = input_grads(0, None, [last]), None
     if relayed:
+        input_grad = input_grads(1, input_grad, [])
+    if relayed:
         output = call(
             side_output_kernel,
             (1,),
             [whole(side_weight_shape)] * 2
             + [part] * 2
-            + [spec for k in range(2) for spec in (side_spec, side_spec, both[k], part)],
+            + [spec for k in range(2) for spec in (side_spec, side_spec, part, part)],
             whole((tokens, features)),
             shape(tokens, features),
             2 * slots * unit,
             8 * unit + 4 * slots * width,
             "output",
             after=[input_grad],
-        )(*side_weights, *resid, *[r for k in range(2) for r in (*out_pieces[k], sums_here[1], relayed_sums[k])])
+        )(*side_weights, *resid, *[r for k in range(2) for r in (*out_pieces[k], sums_here[2 + k], relayed_sums[k])])
     else:
         for k in range(CHUNKS):
             kind = k % 2
@@ -1090,7 +1101,8 @@
                 4 * unit + 2 * slots * width,
                 "output",
             )
-    input_grad = input_grads(1, input_grad, [output])
+    if not relayed:
+        input_grad = input_grads(1, input_grad, [output])
     return (output[None], input_grad[None])
 
 

time: 194 us -> 190 us (0.979)
  waiting for transfers between devices: 90.6 us -> 87.8 us
    ppermute x29 -> x31, waiting for transfers between devices: 52.5 us -> 44.8 us  [offset(): return lax.ppermute(a, 'exp', [(i, i ^ k) for i in range(experts)])]
    ppermute x8, waiting for transfers between devices: 38.1 us -> 43 us  [hop(): lax.ppermute(states, 'seq', [(i, i + step) for i in range(blocks) if 0 <=...]
    ppermute x29 -> x31, starting transfers between devices: 23.1 us -> 24.4 us  [offset(): return lax.ppermute(a, 'exp', [(i, i ^ k) for i in range(experts)])]
    unnamed x44 -> x48, local copies, waits for them, and re-layouts: 4.77 us -> 3.56 us
  transfers between devices with their start and end apart: 37 -> 39, of which waited for: 15 -> 19; matrix products, arithmetic and copies ran while one was open for 0% -> 0% of each run, Pallas kernels for 22% -> 22%
where the time goes in v6:
time: 190 us; the launch traced here: 189 us
  waiting for transfers between devices  87.8 us (46%)
  Pallas kernels  52.5 us (28%)
  starting transfers between devices  43.6 us (23%)
  local copies, waits for them, and re-layouts  3.56 us (2%)
    pallas_call x33, Pallas kernels, call(): return lambda *operands: called(*operands, *after)  52.5 us
    ppermute x31, waiting for transfers between devices, offset(): return lax.ppermute(a, 'exp', [(i, i ^ k) for i in range(experts)])  44.8 us
    ppermute x8, waiting for transfers between devices, hop(): lax.ppermute(states, 'seq', [(i, i + step) for i in range(blocks) if 0 <=...  43 us
    ppermute x31, starting transfers between devices, offset(): return lax.ppermute(a, 'exp', [(i, i ^ k) for i in range(experts)])  24.4 us
    ppermute x8, starting transfers between devices, hop(): lax.ppermute(states, 'seq', [(i, i + step) for i in range(blocks) if 0 <=...  19.3 us
  transfers between devices with their start and end apart: 39, of which 19 were waited for; matrix products, arithmetic and copies ran while one was open for 0% of the time, Pallas kernels for 22%

profile of v6, /device:TPU:0, one launch (start us, length us, event | category | flops | bytes accessed | tf_op | source)
XLA Modules:
  0.0 189.5 jit_solution(11094667853693120127)
XLA Ops:
  0.6 5.1 %collective-permute-start.2 = (bf16[128,4096]{1,0:T(8,128)(2,1)}, bf16[128,4096]{1,0:T(8,128)(2,1)S(1)}, u32[]{:S(2)}, u32[]{:S(2)}) collective-permute-start(bf16[128,4096]{1,0:T(8,128)(2,1)} %bitcast.60), channel_id=1, source_target_pairs={{0,8},{8,16},{16,24},{1,9},{9,17},{17,25},{2,10},{10,18},{18,26},{... | collective-permute-start | bytes 3145736 | tf_op jit(solution)/shard_map/ppermute | solution.py:559
  5.8 2.8 %prepare.1 = (bf16[224,128]{1,0:T(8,128)(2,1)}, bf16[224,128]{1,0:T(8,128)(2,1)}, bf16[128,2176]{1,0:T(8,128)(2,1)}, bf16[128,2176]{1,0:T(8,128)(2,1)}, bf16[256,2176]{1,0:T(8,128)(2,1)}) custom-call(bf16[128,128]{1,0:T(8,128)(2,1)} %bitcast.54, bf16[128,128]{1,0:T(8,128)(2,1)} %bitcast.46, f32[32,128]{1,0:T(8,128)} %bitcast.33, bf16[128,4096]{1,0:T(8,128)(2,1)} %bitcast.29, ...), custom_call_target="tpu_custom_call" | custom-call | bytes 2097152 | tf_op jit(solution)/shard_map/prepare/pallas_call | solution.py:45
  11.6 3.4 %collective-permute-start.3 = (bf16[224,128]{1,0:T(8,128)(2,1)}, bf16[224,128]{1,0:T(8,128)(2,1)S(1)}, u32[]{:S(2)}, u32[]{:S(2)}) collective-permute-start(bf16[224,128]{1,0:T(8,128)(2,1)} %get-tuple-element.72), channel_id=1, source_target_pairs={{0,8},{8,16},{16,24},{1,9},{9,17},{17,25},{2,10},{10,18},{18,26},{... | collective-permute-start | bytes 172040 | tf_op jit(solution)/shard_map/ppermute | solution.py:559
  19.2 2.5 %inner.1.refs_4_.refs_5_.refs_3_ = f32[128,4096]{1,0:T(8,128)S(1)} custom-call(s32[7]{0:T(128)S(1)} %pad_add_fusion.refs_0_, f32[32,128]{1,0:T(8,128)S(1)} %bitcast.34, bf16[128,128]{1,0:T(8,128)(2,1)S(1)} %bitcast.55, bf16[128,128]{1,0:T(8,128)(2,1)S(1)} %bitcast.47, bf16[128,4096]{1,0:T(8,128)(2,1)S(1)} %bitcast.61), custom_call_target="tpu_custom_call" | custom-call | flops 268435456 | bytes 3145728 | tf_op jit(solution)/shard_map/inner/pallas_call | solution.py:45
  24.5 5.2 %collective-permute-done.3.refs_5_.refs_2_.refs_3_ = bf16[224,128]{1,0:T(8,128)(2,1)S(1)} collective-permute-done((bf16[224,128]{1,0:T(8,128)(2,1)}, bf16[224,128]{1,0:T(8,128)(2,1)S(1)}, u32[]{:S(2)}, u32[]{:S(2)}) %collective-permute-start.3) | collective-permute-done | bytes 57376 | tf_op jit(solution)/shard_map/ppermute | solution.py:559
  38.8 4.3 %collective-permute-start.8 = (bf16[64,4224]{1,0:T(8,128)(2,1)S(1)}, bf16[64,4224]{1,0:T(8,128)(2,1)S(1)}, u32[]{:S(2)}, u32[]{:S(2)}) collective-permute-start(bf16[64,4224]{1,0:T(8,128)(2,1)S(1)} %get-tuple-element.82.refs_10_), channel_id=1, source_target_pairs={{0,8},{8,16},{16,24},{1,9},{9,17},{17,25},{2,10},{10,18},{18,26},{... | collective-permute-start | bytes 1622024 | tf_op jit(solution)/shard_map/ppermute | solution.py:559
  43.1 11.2 %collective-permute-done.8.refs_5_.refs_6_ = bf16[64,4224]{1,0:T(8,128)(2,1)S(1)} collective-permute-done((bf16[64,4224]{1,0:T(8,128)(2,1)S(1)}, bf16[64,4224]{1,0:T(8,128)(2,1)S(1)}, u32[]{:S(2)}, u32[]{:S(2)}) %collective-permute-start.8) | collective-permute-done | bytes 540704 | tf_op jit(solution)/shard_map/ppermute | solution.py:559
  59.6 5.9 %back.1.refs_3_.refs_7_ = f32[384,1024]{1,0:T(8,128)S(1)} custom-call(bf16[192,2048]{1,0:T(8,128)(2,1)S(1)} %get-tuple-element.89.refs_0_, bf16[192,2048]{1,0:T(8,128)(2,1)S(1)} %collective-permute-done.9.refs_7_.refs_1_, bf16[192,2048]{1,0:T(8,128)(2,1)S(1)} %get-tuple-element.90.refs_2_, bf16[192,2048]{1,0:T(8,128)(2,1)S(1)} %collective-permute-done.10.refs_8_.refs_3_, ...), custom_call_target="tpu_custom_call" | custom-call | flops 3221225472 | bytes 11534336 | tf_op jit(solution)/shard_map/back/pallas_call | solution.py:45
  65.6 2.8 %collective-permute-done.12.refs_2_ = bf16[128,2048]{1,0:T(8,128)(2,1)S(1)} collective-permute-done((bf16[128,2048]{1,0:T(8,128)(2,1)S(1)}, bf16[128,2048]{1,0:T(8,128)(2,1)S(1)}, u32[]{:S(2)}, u32[]{:S(2)}) %collective-permute-start.12) | collective-permute-done | bytes 524320 | tf_op jit(solution)/shard_map/ppermute | solution.py:556
  73.6 7.5 %collective-permute-done.17.refs_2_.refs_5_ = bf16[96,2048]{1,0:T(8,128)(2,1)S(1)} collective-permute-done((bf16[96,2048]{1,0:T(8,128)(2,1)S(1)}, bf16[96,2048]{1,0:T(8,128)(2,1)S(1)}, u32[]{:S(2)}, u32[]{:S(2)}) %collective-permute-start.17) | collective-permute-done | bytes 393248 | tf_op jit(solution)/shard_map/ppermute | solution.py:556
  81.1 7.5 %collective-permute-done.18.refs_3_.refs_6_ = bf16[96,2048]{1,0:T(8,128)(2,1)S(1)} collective-permute-done((bf16[96,2048]{1,0:T(8,128)(2,1)S(1)}, bf16[96,2048]{1,0:T(8,128)(2,1)S(1)}, u32[]{:S(2)}, u32[]{:S(2)}) %collective-permute-start.18) | collective-permute-done | bytes 393248 | tf_op jit(solution)/shard_map/ppermute | solution.py:556
  88.6 2.4 %up_first.1 = (f32[384,1024]{1,0:T(8,128)S(1)}, f32[384,128]{1,0:T(8,128)S(1)}) custom-call(bf16[96,2048]{1,0:T(8,128)(2,1)S(1)} %get-tuple-element.91.refs_3_.refs_0_, bf16[96,2048]{1,0:T(8,128)(2,1)S(1)} %collective-permute-done.16.refs_1_.refs_4_, bf16[96,2048]{1,0:T(8,128)(2,1)S(1)} %collective-permute-done.17.refs_2_.refs_5_, ...), custom_call_target="tpu_custom_call" | custom-call | flops 1610612736 | bytes 5767168 | tf_op jit(solution)/shard_map/up_first/pallas_call | solution.py:45
  91.1 3.4 %up_last.1 = (bf16[384,1024]{1,0:T(8,128)(2,1)S(1)}, bf16[384,1024]{1,0:T(8,128)(2,1)S(1)}, f32[384,128]{1,0:T(8,128)S(1)}) custom-call(bf16[96,2048]{1,0:T(8,128)(2,1)S(1)} %get-tuple-element.92.refs_0_.refs_3_, bf16[96,2048]{1,0:T(8,128)(2,1)S(1)} %collective-permute-done.13.refs_1_.refs_4_, bf16[96,2048]{1,0:T(8,128)(2,1)S(1)} %collective-permute-done.14.refs_2_.refs_5_, ...), custom_call_target="tpu_custom_call" | custom-call | flops 1610612736 | bytes 5767168 | tf_op jit(solution)/shard_map/up_last/pallas_call | solution.py:45
  94.5 2.4 %expert_grad.2 = (bf16[96,2048]{1,0:T(8,128)(2,1)S(1)}, bf16[96,2048]{1,0:T(8,128)(2,1)S(1)}, bf16[96,2048]{1,0:T(8,128)(2,1)S(1)}, bf16[96,2048]{1,0:T(8,128)(2,1)S(1)}) custom-call(bf16[384,1024]{1,0:T(8,128)(2,1)S(1)} %get-tuple-element.102.refs_0_, bf16[4096,1024]{1,0:T(8,128)(2,1)S(1)} %bitcast.22, f32[384,128]{1,0:T(8,128)S(1)} %get-tuple-element.103.refs_2_, ...), custom_call_target="tpu_custom_call" | custom-call | flops 1610612736 | bytes 5767168 | tf_op jit(solution)/shard_map/expert_grad/pallas_call | solution.py:45
  99.0 2.4 %expert_grad.3 = (bf16[96,2048]{1,0:T(8,128)(2,1)S(1)}, bf16[96,2048]{1,0:T(8,128)(2,1)S(1)}, bf16[96,2048]{1,0:T(8,128)(2,1)S(1)}, bf16[96,2048]{1,0:T(8,128)(2,1)S(1)}) custom-call(bf16[384,1024]{1,0:T(8,128)(2,1)S(1)} %get-tuple-element.102.refs_0_, bf16[4096,1024]{1,0:T(8,128)(2,1)S(1)} %bitcast.23, f32[384,128]{1,0:T(8,128)S(1)} %get-tuple-element.103.refs_2_, ...), custom_call_target="tpu_custom_call" | custom-call | flops 1610612736 | bytes 5767168 | tf_op jit(solution)/shard_map/expert_grad/pallas_call | solution.py:45
  103.6 2.4 %expert_out.2 = (bf16[192,2048]{1,0:T(8,128)(2,1)S(1)}, bf16[192,2048]{1,0:T(8,128)(2,1)S(1)}) custom-call(bf16[384,1024]{1,0:T(8,128)(2,1)S(1)} %get-tuple-element.101.refs_0_, bf16[1024,4096]{1,0:T(8,128)(2,1)S(1)} %bitcast.27, bf16[96,2048]{1,0:T(8,128)(2,1)S(1)} %get-tuple-element.105.refs_2_.refs_1_.refs_7_), custom_call_target="tpu_custom_call" | custom-call | flops 1610612736 | bytes 5767168 | tf_op jit(solution)/shard_map/expert_out/pallas_call | solution.py:45
  105.9 2.6 %expert_out.3 = (bf16[192,2048]{1,0:T(8,128)(2,1)S(1)}, bf16[192,2048]{1,0:T(8,128)(2,1)S(1)}) custom-call(bf16[384,1024]{1,0:T(8,128)(2,1)S(1)} %get-tuple-element.101.refs_0_, bf16[1024,4096]{1,0:T(8,128)(2,1)S(1)} %bitcast.28, bf16[192,2048]{1,0:T(8,128)(2,1)S(1)} %get-tuple-element.106.refs_2_.refs_4_), custom_call_target="tpu_custom_call" | custom-call | flops 1610612736 | bytes 5767168 | tf_op jit(solution)/shard_map/expert_out/pallas_call | solution.py:45
  109.5 6.7 %collective-permute-done.24.refs_4_.refs_10_ = bf16[96,2048]{1,0:T(8,128)(2,1)S(1)} collective-permute-done((bf16[96,2048]{1,0:T(8,128)(2,1)S(1)}, bf16[96,2048]{1,0:T(8,128)(2,1)S(1)}, u32[]{:S(2)}, u32[]{:S(2)}) %collective-permute-start.24) | collective-permute-done | bytes 393248 | tf_op jit(solution)/shard_map/ppermute | solution.py:556
  117.5 3.2 %collective-permute-done.21.refs_4_.refs_10_ = bf16[96,2048]{1,0:T(8,128)(2,1)S(1)} collective-permute-done((bf16[96,2048]{1,0:T(8,128)(2,1)S(1)}, bf16[96,2048]{1,0:T(8,128)(2,1)S(1)}, u32[]{:S(2)}, u32[]{:S(2)}) %collective-permute-start.21) | collective-permute-done | bytes 393248 | tf_op jit(solution)/shard_map/ppermute | solution.py:556
  122.8 10.1 %collective-permute-done.26.refs_11_ = bf16[128,2048]{1,0:T(8,128)(2,1)S(1)} collective-permute-done((bf16[128,2048]{1,0:T(8,128)(2,1)S(1)}, bf16[128,2048]{1,0:T(8,128)(2,1)S(1)}, u32[]{:S(2)}, u32[]{:S(2)}) %collective-permute-start.26) | collective-permute-done | bytes 524320 | tf_op jit(solution)/shard_map/ppermute | solution.py:556
  143.0 14.3 %collective-permute-done.29.refs_4_ = bf16[128,2048]{1,0:T(8,128)(2,1)S(1)} collective-permute-done((bf16[128,2048]{1,0:T(8,128)(2,1)S(1)}, bf16[128,2048]{1,0:T(8,128)(2,1)S(1)}, u32[]{:S(2)}, u32[]{:S(2)}) %collective-permute-start.29) | collective-permute-done | bytes 524320 | tf_op jit(solution)/shard_map/ppermute | solution.py:559
  164.7 2.5 %collective-permute-done.33.refs_4_ = bf16[128,2048]{1,0:T(8,128)(2,1)S(1)} collective-permute-done((bf16[128,2048]{1,0:T(8,128)(2,1)S(1)}, bf16[128,2048]{1,0:T(8,128)(2,1)S(1)}, u32[]{:S(2)}, u32[]{:S(2)}) %collective-permute-start.33) | collective-permute-done | bytes 524320 | tf_op jit(solution)/shard_map/ppermute | solution.py:559
  170.8 3.3 %collective-permute-done.38.refs_5_.refs_6_ = bf16[64,2176]{1,0:T(8,128)(2,1)S(1)} collective-permute-done((bf16[64,2176]{1,0:T(8,128)(2,1)S(1)}, bf16[64,2176]{1,0:T(8,128)(2,1)S(1)}, u32[]{:S(2)}, u32[]{:S(2)}) %collective-permute-start.38) | collective-permute-done | bytes 278560 | tf_op jit(solution)/shard_map/ppermute | solution.py:559
  177.7 6.5 %collective-permute-done.37.refs_5_.refs_6_ = bf16[64,2176]{1,0:T(8,128)(2,1)S(1)} collective-permute-done((bf16[64,2176]{1,0:T(8,128)(2,1)S(1)}, bf16[64,2176]{1,0:T(8,128)(2,1)S(1)}, u32[]{:S(2)}, u32[]{:S(2)}) %collective-permute-start.37) | collective-permute-done | bytes 278560 | tf_op jit(solution)/shard_map/ppermute | solution.py:559
  (138 shorter events, 67.9 us)
Async XLA Ops:
  0.6 29.0 %collective-permute-start.2 = (bf16[128,4096]{1,0:T(8,128)(2,1)}, bf16[128,4096]{1,0:T(8,128)(2,1)S(1)}, u32[]{:S(2)}, u32[]{:S(2)}) collective-permute-start(bf16[128,4096]{1,0:T(8,128)(2,1)} %bitcast.60), channel_id=1, source_target_pairs={{0,8},{8,16},{16,24},{1,9},{9,17},{17,25},{2,10},{10,18},{18,26},{... | collective-permute-start | bytes 3145736 | tf_op jit(solution)/shard_map/ppermute | solution.py:559
  11.6 18.1 %collective-permute-start.3 = (bf16[224,128]{1,0:T(8,128)(2,1)}, bf16[224,128]{1,0:T(8,128)(2,1)S(1)}, u32[]{:S(2)}, u32[]{:S(2)}) collective-permute-start(bf16[224,128]{1,0:T(8,128)(2,1)} %get-tuple-element.72), channel_id=1, source_target_pairs={{0,8},{8,16},{16,24},{1,9},{9,17},{17,25},{2,10},{10,18},{18,26},{... | collective-permute-start | bytes 172040 | tf_op jit(solution)/shard_map/ppermute | solution.py:559
  15.0 14.7 %collective-permute-start.4 = (bf16[224,128]{1,0:T(8,128)(2,1)}, bf16[224,128]{1,0:T(8,128)(2,1)S(1)}, u32[]{:S(2)}, u32[]{:S(2)}) collective-permute-start(bf16[224,128]{1,0:T(8,128)(2,1)} %get-tuple-element.73), channel_id=1, source_target_pairs={{8,0},{16,8},{24,16},{9,1},{17,9},{25,17},{10,2},{18,10},{26,18},{... | collective-permute-start | bytes 172040 | tf_op jit(solution)/shard_map/ppermute | solution.py:559
  35.7 20.7 %collective-permute-start.10 = (bf16[192,2048]{1,0:T(8,128)(2,1)S(1)}, bf16[192,2048]{1,0:T(8,128)(2,1)S(1)}, u32[]{:S(2)}, u32[]{:S(2)}) collective-permute-start(bf16[192,2048]{1,0:T(8,128)(2,1)S(1)} %get-tuple-element.86), channel_id=1, source_target_pairs={{0,2},{1,3},{2,0},{3,1},{4,6},{5,7},{6,4},{7,5},{8,10},{9,11},{10,... | collective-permute-start | bytes 2359304 | tf_op jit(solution)/shard_map/ppermute | solution.py:556
  37.3 19.3 %collective-permute-start.9 = (bf16[192,2048]{1,0:T(8,128)(2,1)S(1)}, bf16[192,2048]{1,0:T(8,128)(2,1)S(1)}, u32[]{:S(2)}, u32[]{:S(2)}) collective-permute-start(bf16[192,2048]{1,0:T(8,128)(2,1)S(1)} %get-tuple-element.85), channel_id=1, source_target_pairs={{0,4},{1,5},{2,6},{3,7},{4,0},{5,1},{6,2},{7,3},{8,12},{9,13},{10,... | collective-permute-start | bytes 2359304 | tf_op jit(solution)/shard_map/ppermute | solution.py:556
  38.8 15.5 %collective-permute-start.8 = (bf16[64,4224]{1,0:T(8,128)(2,1)S(1)}, bf16[64,4224]{1,0:T(8,128)(2,1)S(1)}, u32[]{:S(2)}, u32[]{:S(2)}) collective-permute-start(bf16[64,4224]{1,0:T(8,128)(2,1)S(1)} %get-tuple-element.82.refs_10_), channel_id=1, source_target_pairs={{0,8},{8,16},{16,24},{1,9},{9,17},{17,25},{2,10},{10,18},{18,26},{... | collective-permute-start | bytes 1622024 | tf_op jit(solution)/shard_map/ppermute | solution.py:559
  69.7 18.9 %collective-permute-start.18 = (bf16[96,2048]{1,0:T(8,128)(2,1)S(1)}, bf16[96,2048]{1,0:T(8,128)(2,1)S(1)}, u32[]{:S(2)}, u32[]{:S(2)}) collective-permute-start(bf16[96,2048]{1,0:T(8,128)(2,1)S(1)} %get-tuple-element.98), channel_id=1, source_target_pairs={{0,5},{1,4},{2,7},{3,6},{4,1},{5,0},{6,3},{7,2},{8,13},{9,12},{10,... | collective-permute-start | bytes 1179656 | tf_op jit(solution)/shard_map/ppermute | solution.py:556
  71.7 19.4 %collective-permute-start.13 = (bf16[96,2048]{1,0:T(8,128)(2,1)S(1)}, bf16[96,2048]{1,0:T(8,128)(2,1)S(1)}, u32[]{:S(2)}, u32[]{:S(2)}) collective-permute-start(bf16[96,2048]{1,0:T(8,128)(2,1)S(1)} %get-tuple-element.93), channel_id=1, source_target_pairs={{0,1},{1,0},{2,3},{3,2},{4,5},{5,4},{6,7},{7,6},{8,9},{9,8},{10,11... | collective-permute-start | bytes 1179656 | tf_op jit(solution)/shard_map/ppermute | solution.py:556
  72.1 19.0 %collective-permute-start.14 = (bf16[96,2048]{1,0:T(8,128)(2,1)S(1)}, bf16[96,2048]{1,0:T(8,128)(2,1)S(1)}, u32[]{:S(2)}, u32[]{:S(2)}) collective-permute-start(bf16[96,2048]{1,0:T(8,128)(2,1)S(1)} %get-tuple-element.94), channel_id=1, source_target_pairs={{0,2},{1,3},{2,0},{3,1},{4,6},{5,7},{6,4},{7,5},{8,10},{9,11},{10,... | collective-permute-start | bytes 1179656 | tf_op jit(solution)/shard_map/ppermute | solution.py:556
  72.6 18.5 %collective-permute-start.15 = (bf16[96,2048]{1,0:T(8,128)(2,1)S(1)}, bf16[96,2048]{1,0:T(8,128)(2,1)S(1)}, u32[]{:S(2)}, u32[]{:S(2)}) collective-permute-start(bf16[96,2048]{1,0:T(8,128)(2,1)S(1)} %get-tuple-element.95), channel_id=1, source_target_pairs={{0,3},{1,2},{2,1},{3,0},{4,7},{5,6},{6,5},{7,4},{8,11},{9,10},{10,... | collective-permute-start | bytes 1179656 | tf_op jit(solution)/shard_map/ppermute | solution.py:556
  98.8 17.4 %collective-permute-start.24 = (bf16[96,2048]{1,0:T(8,128)(2,1)S(1)}, bf16[96,2048]{1,0:T(8,128)(2,1)S(1)}, u32[]{:S(2)}, u32[]{:S(2)}) collective-permute-start(bf16[96,2048]{1,0:T(8,128)(2,1)S(1)} %get-tuple-element.121), channel_id=1, source_target_pairs={{0,5},{1,4},{2,7},{3,6},{4,1},{5,0},{6,3},{7,2},{8,13},{9,12},{10,... | collective-permute-start | bytes 1179656 | tf_op jit(solution)/shard_map/ppermute | solution.py:556
  101.3 16.2 %collective-permute-start.19 = (bf16[96,2048]{1,0:T(8,128)(2,1)S(1)}, bf16[96,2048]{1,0:T(8,128)(2,1)S(1)}, u32[]{:S(2)}, u32[]{:S(2)}) collective-permute-start(bf16[96,2048]{1,0:T(8,128)(2,1)S(1)} %get-tuple-element.114), channel_id=1, source_target_pairs={{0,1},{1,0},{2,3},{3,2},{4,5},{5,4},{6,7},{7,6},{8,9},{9,8},{10,11... | collective-permute-start | bytes 1179656 | tf_op jit(solution)/shard_map/ppermute | solution.py:556
  102.1 15.4 %collective-permute-start.20 = (bf16[96,2048]{1,0:T(8,128)(2,1)S(1)}, bf16[96,2048]{1,0:T(8,128)(2,1)S(1)}, u32[]{:S(2)}, u32[]{:S(2)}) collective-permute-start(bf16[96,2048]{1,0:T(8,128)(2,1)S(1)} %get-tuple-element.115), channel_id=1, source_target_pairs={{0,2},{1,3},{2,0},{3,1},{4,6},{5,7},{6,4},{7,5},{8,10},{9,11},{10,... | collective-permute-start | bytes 1179656 | tf_op jit(solution)/shard_map/ppermute | solution.py:556
  102.7 18.1 %collective-permute-start.21 = (bf16[96,2048]{1,0:T(8,128)(2,1)S(1)}, bf16[96,2048]{1,0:T(8,128)(2,1)S(1)}, u32[]{:S(2)}, u32[]{:S(2)}) collective-permute-start(bf16[96,2048]{1,0:T(8,128)(2,1)S(1)} %get-tuple-element.116), channel_id=1, source_target_pairs={{0,3},{1,2},{2,1},{3,0},{4,7},{5,6},{6,5},{7,4},{8,11},{9,10},{10,... | collective-permute-start | bytes 1179656 | tf_op jit(solution)/shard_map/ppermute | solution.py:556
  116.9 16.0 %collective-permute-start.26 = (bf16[128,2048]{1,0:T(8,128)(2,1)S(1)}, bf16[128,2048]{1,0:T(8,128)(2,1)S(1)}, u32[]{:S(2)}, u32[]{:S(2)}) collective-permute-start(bf16[128,2048]{1,0:T(8,128)(2,1)S(1)} %relay.2.refs_5_), channel_id=1, source_target_pairs={{0,2},{1,3},{2,0},{3,1},{4,6},{5,7},{6,4},{7,5},{8,10},{9,11},{10,... | collective-permute-start | bytes 1572872 | tf_op jit(solution)/shard_map/ppermute | solution.py:556
  121.5 14.3 %collective-permute-start.25 = (bf16[128,2048]{1,0:T(8,128)(2,1)S(1)}, bf16[128,2048]{1,0:T(8,128)(2,1)S(1)}, u32[]{:S(2)}, u32[]{:S(2)}) collective-permute-start(bf16[128,2048]{1,0:T(8,128)(2,1)S(1)} %relay.3.refs_12_), channel_id=1, source_target_pairs={{0,4},{1,5},{2,6},{3,7},{4,0},{5,1},{6,2},{7,3},{8,12},{9,13},{10,... | collective-permute-start | bytes 1572872 | tf_op jit(solution)/shard_map/ppermute | solution.py:556
  137.1 24.4 %collective-permute-start.27 = (bf16[192,2048]{1,0:T(8,128)(2,1)S(1)}, bf16[192,2048]{1,0:T(8,128)(2,1)S(1)}, u32[]{:S(2)}, u32[]{:S(2)}) collective-permute-start(bf16[192,2048]{1,0:T(8,128)(2,1)S(1)} %get-tuple-element.124), channel_id=1, source_target_pairs={{0,4},{1,5},{2,6},{3,7},{4,0},{5,1},{6,2},{7,3},{8,12},{9,13},{10,... | collective-permute-start | bytes 2359304 | tf_op jit(solution)/shard_map/ppermute | solution.py:556
  138.5 23.0 %collective-permute-start.28 = (bf16[192,2048]{1,0:T(8,128)(2,1)S(1)}, bf16[192,2048]{1,0:T(8,128)(2,1)S(1)}, u32[]{:S(2)}, u32[]{:S(2)}) collective-permute-start(bf16[192,2048]{1,0:T(8,128)(2,1)S(1)} %get-tuple-element.125), channel_id=1, source_target_pairs={{0,2},{1,3},{2,0},{3,1},{4,6},{5,7},{6,4},{7,5},{8,10},{9,11},{10,... | collective-permute-start | bytes 2359304 | tf_op jit(solution)/shard_map/ppermute | solution.py:556
  140.2 17.1 %collective-permute-start.29 = (bf16[128,2048]{1,0:T(8,128)(2,1)S(1)}, bf16[128,2048]{1,0:T(8,128)(2,1)S(1)}, u32[]{:S(2)}, u32[]{:S(2)}) collective-permute-start(bf16[128,2048]{1,0:T(8,128)(2,1)S(1)} %dresid.2.refs_12_.refs_4_), channel_id=1, source_target_pairs={{8,0},{16,8},{24,16},{9,1},{17,9},{25,17},{10,2},{18,10},{26,18},{... | collective-permute-start | bytes 1572872 | tf_op jit(solution)/shard_map/ppermute | solution.py:559
  141.7 25.5 %collective-permute-start.33 = (bf16[128,2048]{1,0:T(8,128)(2,1)S(1)}, bf16[128,2048]{1,0:T(8,128)(2,1)S(1)}, u32[]{:S(2)}, u32[]{:S(2)}) collective-permute-start(bf16[128,2048]{1,0:T(8,128)(2,1)S(1)} %dresid.3.refs_2_.refs_5_.refs_4_), channel_id=1, source_target_pairs={{8,0},{16,8},{24,16},{9,1},{17,9},{25,17},{10,2},{18,10},{26,18},{... | collective-permute-start | bytes 1572872 | tf_op jit(solution)/shard_map/ppermute | solution.py:559
  164.6 21.8 %collective-permute-start.30 = (bf16[128,2048]{1,0:T(8,128)(2,1)S(1)}, bf16[128,2048]{1,0:T(8,128)(2,1)S(1)}, u32[]{:S(2)}, u32[]{:S(2)}) collective-permute-start(bf16[128,2048]{1,0:T(8,128)(2,1)S(1)} %get-tuple-element.127), channel_id=1, source_target_pairs={{0,1},{1,0},{2,3},{3,2},{4,5},{5,4},{6,7},{7,6},{8,9},{9,8},{10,11... | collective-permute-start | bytes 1572872 | tf_op jit(solution)/shard_map/ppermute | solution.py:556
  167.3 19.1 %collective-permute-start.35 = (bf16[128,2048]{1,0:T(8,128)(2,1)S(1)}, bf16[128,2048]{1,0:T(8,128)(2,1)S(1)}, u32[]{:S(2)}, u32[]{:S(2)}) collective-permute-start(bf16[128,2048]{1,0:T(8,128)(2,1)S(1)} %get-tuple-element.132), channel_id=1, source_target_pairs={{0,1},{1,0},{2,3},{3,2},{4,5},{5,4},{6,7},{7,6},{8,9},{9,8},{10,11... | collective-permute-start | bytes 1572872 | tf_op jit(solution)/shard_map/ppermute | solution.py:556
  169.3 17.1 %collective-permute-start.34 = (bf16[128,2048]{1,0:T(8,128)(2,1)S(1)}, bf16[128,2048]{1,0:T(8,128)(2,1)S(1)}, u32[]{:S(2)}, u32[]{:S(2)}) collective-permute-start(bf16[128,2048]{1,0:T(8,128)(2,1)S(1)} %get-tuple-element.131.refs_7_), channel_id=1, source_target_pairs={{0,2},{1,3},{2,0},{3,1},{4,6},{5,7},{6,4},{7,5},{8,10},{9,11},{10,... | collective-permute-start | bytes 1572872 | tf_op jit(solution)/shard_map/ppermute | solution.py:556
  170.0 16.4 %collective-permute-start.36 = (bf16[128,2048]{1,0:T(8,128)(2,1)S(1)}, bf16[128,2048]{1,0:T(8,128)(2,1)S(1)}, u32[]{:S(2)}, u32[]{:S(2)}) collective-permute-start(bf16[128,2048]{1,0:T(8,128)(2,1)S(1)} %get-tuple-element.133), channel_id=1, source_target_pairs={{0,4},{1,5},{2,6},{3,7},{4,0},{5,1},{6,2},{7,3},{8,12},{9,13},{10,... | collective-permute-start | bytes 1572872 | tf_op jit(solution)/shard_map/ppermute | solution.py:556
  (39 other events, 372.7 us)

commit v7 on v6

--- a/solution.py
+++ b/solution.py
@@ -168,7 +168,7 @@
         at += heads
 
 
-def pass_kernel(ahead, chunk, meta, log_ref, near_ref, far_ref, rows_ref, state_ref, sent_ref):
+def pass_kernel(ahead, chunk, meta, log_ref, near_ref, far_ref, rows_ref, state_ref, *sent_refs):
     size, heads = log_ref.shape[1], log_ref.shape[0]
     half = size // 2
     _, _, before, last = documents(meta, size)
@@ -202,8 +202,11 @@
         scale = total[h : h + 1, :]
         sums = dot(far, state) * (few * scale)
         scaled = rows_ref[rows, at].astype(F32) * (weight_t[rows, h : h + 1] * ((1.0 - few) * scale))
-        sent_ref[:, at] = (sums + scaled).astype(BF16)
-    sent_ref[:, width:] = near_ref[rows, :]
+        sent_ref = sent_refs[h * len(sent_refs) // heads]
+        to = head(h % (heads // len(sent_refs)), p)
+        sent_ref[:, to] = (sums + scaled).astype(BF16)
+    for sent_ref in sent_refs:
+        sent_ref[:, width // len(sent_refs) :] = near_ref[rows, :]
 
 
 def spread_of(few, shift, mine, theirs):
@@ -281,6 +284,19 @@
         outs[1][:, head(h, p)] = dot(c_weighted, dresid_ref[:, head(h, p)]).astype(BF16)
 
 
+def dresid_all_kernel(features, first_weights, second_weights, cot_ref, *refs):
+    squares, refs, dresid_ref = refs[:2], refs[2:-1], refs[-1]
+    scale = lax.rsqrt((squares[0][:, :1] + squares[1][:, :1]) / features + EPSILON)
+    count, width = len(refs) // 2, cot_ref.shape[1] // 2
+    for k, weights in enumerate((first_weights, second_weights)):
+        terms = refs[k * count : (k + 1) * count]
+        moved = combined(weights, terms[: weights.shape[0]])
+        for arrived in terms[weights.shape[0] :]:
+            moved += arrived[...].astype(F32)
+        at = slice(k * width, (k + 1) * width)
+        dresid_ref[:, at] = (cot_ref[:, at].astype(F32) + scale * moved).astype(BF16)
+
+
 def grad_kernel(count, relayed, meta, log_ref, b_ref, inner_ref, *refs):
     states, out_ref = refs[:count], refs[-1]
     size = log_ref.shape[1]
@@ -558,23 +574,23 @@
     def hop(states, step):
         return lax.ppermute(states, "seq", [(i, i + step) for i in range(blocks) if 0 <= i + step < blocks])
 
-    def hop_on(arrived, spec, step, k, after):
+    def hop_on(arrived, spec, step, k, after, parts=1):
         if relayed:
             near, far = (b_pack, c_pack) if step > 0 else (c_pack, b_pack)
             wide = arrived.shape[1]
-            taken, sent = call(
+            taken, *sent = call(
                 functools.partial(pass_kernel, step > 0, k),
                 (1,),
                 [SMEM, whole((heads, tokens)) if wide == features else log_spec(k), whole(near.shape), small, spec],
-                [whole((tokens, wide)), whole((tokens // 2, wide + state))],
-                [shape(tokens, wide), shape(tokens // 2, wide + state)],
+                [whole((tokens, wide))] + [whole((tokens // 2, wide // parts + state))] * parts,
+                [shape(tokens, wide)] + [shape(tokens // 2, wide // parts + state)] * parts,
                 2 * head_flops,
                 5 * unit,
                 "pass_states",
                 after=after,
             )(meta, log, near, far, arrived)
-            passed = hop(sent, step)
-            return [taken, passed, passed], sent
+            passed = [hop(rows, step) for rows in sent]
+            return [[taken, rows, rows] for rows in passed], sent[0]
         arrived = [arrived]
         for _ in range(hops - 1):
             kept = call(
@@ -746,7 +762,7 @@
         "inner",
     )(meta, log, b, c, x)
     if relayed:
-        first_in, kept = hop_on(moving, whole((tokens, features)), 1, 0, [inner, picks[0]])
+        [first_in], kept = hop_on(moving, whole((tokens, features)), 1, 0, [inner, picks[0]])
         second_in = first_in
     else:
         first_in, kept = hop_on(moving[0], part, 1, 0, [inner, picks[0]])
@@ -947,41 +963,69 @@
         return whole(own_weights[kind].shape)
 
     dresid, states_after = [], []
-    for k in range(CHUNKS):
-        kind = k % 2
-        grads_here = call(
-            functools.partial(dresid_kernel, CHUNKS, features),
-            (1,),
-            [SMEM, log_spec(k), small, weights_spec(kind), chunk(k)]
-            + [whole((tokens, 128))] * CHUNKS
-            + moved_specs(kind),
-            [part] * (1 if relayed else 2),
-            [shape(tokens, width)] * (1 if relayed else 2),
-            head_flops + 2 * slots * unit,
-            6 * unit + 2 * slots * width,
+    if relayed:
+        dresid_whole = call(
+            functools.partial(dresid_all_kernel, features),
+            (1,),
+            [weights_spec(k) for k in range(2)]
+            + [whole((tokens, features))]
+            + [whole((tokens, 128))] * 2
+            + [spec for k in range(2) for spec in moved_specs(k)],
+            whole((tokens, features)),
+            shape(tokens, features),
+            4 * slots * unit,
+            8 * unit + 4 * slots * width,
             "dresid",
             after=[last],
-        )(meta, log, c, own_weights[kind], cot, *squares, *got_grad[k])
-        dresid.append(grads_here[0])
-        states_after.append(hop(grads_here[-1], -1))
-        last = dresid[k]
-
-    if relayed:
-        states_after[0], last = hop_on(states_after[0], part, -1, 0, [last])
+        )(*own_weights, cot, *squares, *got_grad[0], *got_grad[1])
+        moving_back = hop(dresid_whole, -1)
+        last = dresid_whole
+    else:
+        for k in range(CHUNKS):
+            kind = k % 2
+            grads_here = call(
+                functools.partial(dresid_kernel, CHUNKS, features),
+                (1,),
+                [SMEM, log_spec(k), small, weights_spec(kind), chunk(k)]
+                + [whole((tokens, 128))] * CHUNKS
+                + moved_specs(kind),
+                [part] * (1 if relayed else 2),
+                [shape(tokens, width)] * (1 if relayed else 2),
+                head_flops + 2 * slots * unit,
+                6 * unit + 2 * slots * width,
+                "dresid",
+                after=[last],
+            )(meta, log, c, own_weights[kind], cot, *squares, *got_grad[k])
+            dresid.append(grads_here[0])
+            states_after.append(hop(grads_here[-1], -1))
+            last = dresid[k]
     inner_back = []
-    for k in range(CHUNKS):
-        last = call(
+    if relayed:
+        last = inner_back_whole = call(
             inner_back_kernel,
-            (1,),
-            [SMEM, log_spec(k), small, small, part],
-            part,
-            shape(tokens, width, F32),
-            2 * head_flops,
-            6 * unit,
+            (CHUNKS,),
+            [SMEM, pl.BlockSpec((heads // CHUNKS, tokens), lambda i: (i, 0)), small, small, columns(tokens, width)],
+            columns(tokens, width),
+            shape(tokens, features, F32),
+            2 * CHUNKS * head_flops,
+            6 * CHUNKS * unit,
             "inner_back",
             after=[last],
-        )(meta, log, b, c, dresid[k])
-        inner_back.append(last)
+        )(meta, log, b, c, dresid_whole)
+    else:
+        for k in range(CHUNKS):
+            last = call(
+                inner_back_kernel,
+                (1,),
+                [SMEM, log_spec(k), small, small, part],
+                part,
+                shape(tokens, width, F32),
+                2 * head_flops,
+                6 * unit,
+                "inner_back",
+                after=[last],
+            )(meta, log, b, c, dresid[k])
+            inner_back.append(last)
     got_out = []
     if relayed:
         held = call(
@@ -993,7 +1037,7 @@
             0,
             0,
             "hold",
-            after=[dresid[1]],
+            after=[dresid_whole],
             aliases={0: 0, 1: 1},
         )(outs[0][1], outs[1][1])
         side_weights = call(
@@ -1022,7 +1066,6 @@
             after=[last],
         )(*operands)
         sums_here = [offset(rows, 1) for rows in sums]
-        states_after[1], last = hop_on(states_after[1], part, -1, 1, [sums[0]])
         sent = call(
             side_relay_kernel,
             (1,),
@@ -1032,9 +1075,8 @@
             4 * slots * unit,
             8 * slots * width,
             "side_relay",
-            after=[last],
         )(*operands, *sums_here[:2])
-        last = sent[0]
+        after_whole, last = hop_on(moving_back, whole((tokens, features)), -1, 0, [sent[0]], CHUNKS)
         relayed_sums = [offset(sent[k], side_kinds[k][0]) for k in range(2)]
     else:
         for k in range(CHUNKS):
@@ -1070,9 +1112,10 @@
             "input_grad",
         )
 
-    input_grad, output = input_grads(0, None, [last]), None
-    if relayed:
-        input_grad = input_grads(1, input_grad, [])
+    if relayed:
+        pass
+    else:
+        input_grad, output = input_grads(0, None, [last]), None
     if relayed:
         output = call(
             side_output_kernel,
@@ -1085,8 +1128,26 @@
             2 * slots * unit,
             8 * unit + 4 * slots * width,
             "output",
-            after=[input_grad],
+            after=[last],
         )(*side_weights, *resid, *[r for k in range(2) for r in (*out_pieces[k], sums_here[2 + k], relayed_sums[k])])
+        input_grad = None
+        for k in range(CHUNKS):
+            more = [] if input_grad is None else [input_grad]
+            input_grad = call(
+                functools.partial(grad_kernel, 3, relayed),
+                (1,),
+                [SMEM, log_spec(k), small, chunk(k), chunk(k)]
+                + [whole((tokens // 2, width)), pl.BlockSpec((tokens // 2, state), lambda i: (0, width // state))]
+                + [anywhere] * len(more),
+                chunk(k),
+                shape(tokens, features),
+                hops * head_flops,
+                (6 + 2 * hops) * unit,
+                "input_grad",
+                after=[output] if k == 0 else [],
+                aliases={7: 0} if more else {},
+                vmem=VMEM_BYTES,
+            )(meta, log, b, inner_back_whole, *after_whole[k], *more)
     else:
         for k in range(CHUNKS):
             kind = k % 2

time: 190 us -> 186 us (0.979)
  Pallas kernels: 52.5 us -> 50.3 us
  starting transfers between devices: 43.6 us -> 41.4 us
    ppermute x31, waiting for transfers between devices: 44.8 us -> 69.2 us  [offset(): return lax.ppermute(a, 'exp', [(i, i ^ k) for i in range(experts)])]
    ppermute x8 -> x7, waiting for transfers between devices: 43 us -> 19.3 us  [hop(): lax.ppermute(states, 'seq', [(i, i + step) for i in range(blocks) if 0 <=...]
    pallas_call x33 -> x30, Pallas kernels: 52.5 us -> 50.3 us  [call(): return lambda *operands: called(*operands, *after)]
    ppermute x8 -> x7, starting transfers between devices: 19.3 us -> 18 us  [hop(): lax.ppermute(states, 'seq', [(i, i + step) for i in range(blocks) if 0 <=...]
  transfers between devices with their start and end apart: 39 -> 38, of which waited for: 19 -> 23; matrix products, arithmetic and copies ran while one was open for 0% -> 0% of each run, Pallas kernels for 22% -> 21%
where the time goes in v7:
time: 186 us
  waiting for transfers between devices  88.5 us (48%)
  Pallas kernels  50.3 us (27%)
  starting transfers between devices  41.4 us (22%)
  local copies, waits for them, and re-layouts  3.56 us (2%)
    ppermute x31, waiting for transfers between devices, offset(): return lax.ppermute(a, 'exp', [(i, i ^ k) for i in range(experts)])  69.2 us
    pallas_call x30, Pallas kernels, call(): return lambda *operands: called(*operands, *after)  50.3 us
    ppermute x31, starting transfers between devices, offset(): return lax.ppermute(a, 'exp', [(i, i ^ k) for i in range(experts)])  23.4 us
    ppermute x7, waiting for transfers between devices, hop(): lax.ppermute(states, 'seq', [(i, i + step) for i in range(blocks) if 0 <=...  19.3 us
    ppermute x7, starting transfers between devices, hop(): lax.ppermute(states, 'seq', [(i, i + step) for i in range(blocks) if 0 <=...  18 us
  transfers between devices with their start and end apart: 38, of which 23 were waited for; matrix products, arithmetic and copies ran while one was open for 0% of the time, Pallas kernels for 21%

profile of v7, /device:TPU:0, one launch (start us, length us, event | category | flops | bytes accessed | tf_op | source)
XLA Modules:
  0.0 185.6 jit_solution(12569610342712074041)
XLA Ops:
  0.6 5.1 %collective-permute-start.2 = (bf16[128,4096]{1,0:T(8,128)(2,1)}, bf16[128,4096]{1,0:T(8,128)(2,1)S(1)}, u32[]{:S(2)}, u32[]{:S(2)}) collective-permute-start(bf16[128,4096]{1,0:T(8,128)(2,1)} %bitcast.41), channel_id=1, source_target_pairs={{0,8},{8,16},{16,24},{1,9},{9,17},{17,25},{2,10},{10,18},{18,26},{... | collective-permute-start | bytes 3145736 | tf_op jit(solution)/shard_map/ppermute | solution.py:575
  5.8 2.8 %prepare.1 = (bf16[224,128]{1,0:T(8,128)(2,1)}, bf16[224,128]{1,0:T(8,128)(2,1)}, bf16[128,2176]{1,0:T(8,128)(2,1)}, bf16[128,2176]{1,0:T(8,128)(2,1)}, bf16[256,2176]{1,0:T(8,128)(2,1)}) custom-call(bf16[128,128]{1,0:T(8,128)(2,1)} %bitcast.48, bf16[128,128]{1,0:T(8,128)(2,1)} %bitcast.43, f32[32,128]{1,0:T(8,128)} %bitcast.32, bf16[128,4096]{1,0:T(8,128)(2,1)} %bitcast.29, ...), custom_call_target="tpu_custom_call" | custom-call | bytes 2097152 | tf_op jit(solution)/shard_map/prepare/pallas_call | solution.py:45
  11.5 3.4 %collective-permute-start.3 = (bf16[224,128]{1,0:T(8,128)(2,1)}, bf16[224,128]{1,0:T(8,128)(2,1)S(1)}, u32[]{:S(2)}, u32[]{:S(2)}) collective-permute-start(bf16[224,128]{1,0:T(8,128)(2,1)} %get-tuple-element.71), channel_id=1, source_target_pairs={{0,8},{8,16},{16,24},{1,9},{9,17},{17,25},{2,10},{10,18},{18,26},{... | collective-permute-start | bytes 172040 | tf_op jit(solution)/shard_map/ppermute | solution.py:575
  19.2 2.5 %inner.1.refs_4_.refs_5_.refs_3_ = f32[128,4096]{1,0:T(8,128)S(1)} custom-call(s32[7]{0:T(128)S(1)} %pad_add_fusion.refs_0_, f32[32,128]{1,0:T(8,128)S(1)} %bitcast.33, bf16[128,128]{1,0:T(8,128)(2,1)S(1)} %bitcast.49, bf16[128,128]{1,0:T(8,128)(2,1)S(1)} %bitcast.44, bf16[128,4096]{1,0:T(8,128)(2,1)S(1)} %bitcast.42), custom_call_target="tpu_custom_call" | custom-call | flops 268435456 | bytes 3145728 | tf_op jit(solution)/shard_map/inner/pallas_call | solution.py:45
  24.5 5.2 %collective-permute-done.3.refs_5_.refs_2_.refs_3_ = bf16[224,128]{1,0:T(8,128)(2,1)S(1)} collective-permute-done((bf16[224,128]{1,0:T(8,128)(2,1)}, bf16[224,128]{1,0:T(8,128)(2,1)S(1)}, u32[]{:S(2)}, u32[]{:S(2)}) %collective-permute-start.3) | collective-permute-done | bytes 57376 | tf_op jit(solution)/shard_map/ppermute | solution.py:575
  38.8 4.3 %collective-permute-start.8 = (bf16[64,4224]{1,0:T(8,128)(2,1)S(1)}, bf16[64,4224]{1,0:T(8,128)(2,1)S(1)}, u32[]{:S(2)}, u32[]{:S(2)}) collective-permute-start(bf16[64,4224]{1,0:T(8,128)(2,1)S(1)} %get-tuple-element.81.refs_10_), channel_id=1, source_target_pairs={{0,8},{8,16},{16,24},{1,9},{9,17},{17,25},{2,10},{10,18},{18,26},{... | collective-permute-start | bytes 1622024 | tf_op jit(solution)/shard_map/ppermute | solution.py:575
  43.1 11.2 %collective-permute-done.8.refs_5_.refs_6_ = bf16[64,4224]{1,0:T(8,128)(2,1)S(1)} collective-permute-done((bf16[64,4224]{1,0:T(8,128)(2,1)S(1)}, bf16[64,4224]{1,0:T(8,128)(2,1)S(1)}, u32[]{:S(2)}, u32[]{:S(2)}) %collective-permute-start.8) | collective-permute-done | bytes 540704 | tf_op jit(solution)/shard_map/ppermute | solution.py:575
  59.7 5.9 %back.1.refs_3_.refs_7_ = f32[384,1024]{1,0:T(8,128)S(1)} custom-call(bf16[192,2048]{1,0:T(8,128)(2,1)S(1)} %get-tuple-element.88.refs_0_, bf16[192,2048]{1,0:T(8,128)(2,1)S(1)} %collective-permute-done.9.refs_7_.refs_1_, bf16[192,2048]{1,0:T(8,128)(2,1)S(1)} %get-tuple-element.89.refs_2_, bf16[192,2048]{1,0:T(8,128)(2,1)S(1)} %collective-permute-done.10.refs_8_.refs_3_, ...), custom_call_target="tpu_custom_call" | custom-call | flops 3221225472 | bytes 11534336 | tf_op jit(solution)/shard_map/back/pallas_call | solution.py:45
  65.6 2.8 %collective-permute-done.12.refs_2_ = bf16[128,2048]{1,0:T(8,128)(2,1)S(1)} collective-permute-done((bf16[128,2048]{1,0:T(8,128)(2,1)S(1)}, bf16[128,2048]{1,0:T(8,128)(2,1)S(1)}, u32[]{:S(2)}, u32[]{:S(2)}) %collective-permute-start.12) | collective-permute-done | bytes 524320 | tf_op jit(solution)/shard_map/ppermute | solution.py:572
  73.6 7.5 %collective-permute-done.17.refs_2_.refs_5_ = bf16[96,2048]{1,0:T(8,128)(2,1)S(1)} collective-permute-done((bf16[96,2048]{1,0:T(8,128)(2,1)S(1)}, bf16[96,2048]{1,0:T(8,128)(2,1)S(1)}, u32[]{:S(2)}, u32[]{:S(2)}) %collective-permute-start.17) | collective-permute-done | bytes 393248 | tf_op jit(solution)/shard_map/ppermute | solution.py:572
  81.1 7.5 %collective-permute-done.18.refs_3_.refs_6_ = bf16[96,2048]{1,0:T(8,128)(2,1)S(1)} collective-permute-done((bf16[96,2048]{1,0:T(8,128)(2,1)S(1)}, bf16[96,2048]{1,0:T(8,128)(2,1)S(1)}, u32[]{:S(2)}, u32[]{:S(2)}) %collective-permute-start.18) | collective-permute-done | bytes 393248 | tf_op jit(solution)/shard_map/ppermute | solution.py:572
  88.6 2.4 %up_first.1 = (f32[384,1024]{1,0:T(8,128)S(1)}, f32[384,128]{1,0:T(8,128)S(1)}) custom-call(bf16[96,2048]{1,0:T(8,128)(2,1)S(1)} %get-tuple-element.90.refs_3_.refs_0_, bf16[96,2048]{1,0:T(8,128)(2,1)S(1)} %collective-permute-done.16.refs_1_.refs_4_, bf16[96,2048]{1,0:T(8,128)(2,1)S(1)} %collective-permute-done.17.refs_2_.refs_5_, ...), custom_call_target="tpu_custom_call" | custom-call | flops 1610612736 | bytes 5767168 | tf_op jit(solution)/shard_map/up_first/pallas_call | solution.py:45
  91.1 3.4 %up_last.1 = (bf16[384,1024]{1,0:T(8,128)(2,1)S(1)}, bf16[384,1024]{1,0:T(8,128)(2,1)S(1)}, f32[384,128]{1,0:T(8,128)S(1)}) custom-call(bf16[96,2048]{1,0:T(8,128)(2,1)S(1)} %get-tuple-element.91.refs_0_.refs_3_, bf16[96,2048]{1,0:T(8,128)(2,1)S(1)} %collective-permute-done.13.refs_1_.refs_4_, bf16[96,2048]{1,0:T(8,128)(2,1)S(1)} %collective-permute-done.14.refs_2_.refs_5_, ...), custom_call_target="tpu_custom_call" | custom-call | flops 1610612736 | bytes 5767168 | tf_op jit(solution)/shard_map/up_last/pallas_call | solution.py:45
  94.5 2.4 %expert_grad.2 = (bf16[96,2048]{1,0:T(8,128)(2,1)S(1)}, bf16[96,2048]{1,0:T(8,128)(2,1)S(1)}, bf16[96,2048]{1,0:T(8,128)(2,1)S(1)}, bf16[96,2048]{1,0:T(8,128)(2,1)S(1)}) custom-call(bf16[384,1024]{1,0:T(8,128)(2,1)S(1)} %get-tuple-element.101.refs_0_, bf16[4096,1024]{1,0:T(8,128)(2,1)S(1)} %bitcast.22, f32[384,128]{1,0:T(8,128)S(1)} %get-tuple-element.102.refs_2_, ...), custom_call_target="tpu_custom_call" | custom-call | flops 1610612736 | bytes 5767168 | tf_op jit(solution)/shard_map/expert_grad/pallas_call | solution.py:45
  99.0 2.4 %expert_grad.3 = (bf16[96,2048]{1,0:T(8,128)(2,1)S(1)}, bf16[96,2048]{1,0:T(8,128)(2,1)S(1)}, bf16[96,2048]{1,0:T(8,128)(2,1)S(1)}, bf16[96,2048]{1,0:T(8,128)(2,1)S(1)}) custom-call(bf16[384,1024]{1,0:T(8,128)(2,1)S(1)} %get-tuple-element.101.refs_0_, bf16[4096,1024]{1,0:T(8,128)(2,1)S(1)} %bitcast.23, f32[384,128]{1,0:T(8,128)S(1)} %get-tuple-element.102.refs_2_, ...), custom_call_target="tpu_custom_call" | custom-call | flops 1610612736 | bytes 5767168 | tf_op jit(solution)/shard_map/expert_grad/pallas_call | solution.py:45
  103.6 2.4 %expert_out.2 = (bf16[192,2048]{1,0:T(8,128)(2,1)S(1)}, bf16[192,2048]{1,0:T(8,128)(2,1)S(1)}) custom-call(bf16[384,1024]{1,0:T(8,128)(2,1)S(1)} %get-tuple-element.100.refs_0_, bf16[1024,4096]{1,0:T(8,128)(2,1)S(1)} %bitcast.27, bf16[96,2048]{1,0:T(8,128)(2,1)S(1)} %get-tuple-element.104.refs_2_.refs_1_.refs_10_), custom_call_target="tpu_custom_call" | custom-call | flops 1610612736 | bytes 5767168 | tf_op jit(solution)/shard_map/expert_out/pallas_call | solution.py:45
  105.9 2.6 %expert_out.3 = (bf16[192,2048]{1,0:T(8,128)(2,1)S(1)}, bf16[192,2048]{1,0:T(8,128)(2,1)S(1)}) custom-call(bf16[384,1024]{1,0:T(8,128)(2,1)S(1)} %get-tuple-element.100.refs_0_, bf16[1024,4096]{1,0:T(8,128)(2,1)S(1)} %bitcast.28, bf16[192,2048]{1,0:T(8,128)(2,1)S(1)} %get-tuple-element.105.refs_2_.refs_4_), custom_call_target="tpu_custom_call" | custom-call | flops 1610612736 | bytes 5767168 | tf_op jit(solution)/shard_map/expert_out/pallas_call | solution.py:45
  109.5 6.7 %collective-permute-done.21.refs_4_.refs_8_ = bf16[96,2048]{1,0:T(8,128)(2,1)S(1)} collective-permute-done((bf16[96,2048]{1,0:T(8,128)(2,1)S(1)}, bf16[96,2048]{1,0:T(8,128)(2,1)S(1)}, u32[]{:S(2)}, u32[]{:S(2)}) %collective-permute-start.21) | collective-permute-done | bytes 393248 | tf_op jit(solution)/shard_map/ppermute | solution.py:572
  116.9 3.8 %collective-permute-done.25.refs_4_.refs_13_ = bf16[96,2048]{1,0:T(8,128)(2,1)S(1)} collective-permute-done((bf16[96,2048]{1,0:T(8,128)(2,1)S(1)}, bf16[96,2048]{1,0:T(8,128)(2,1)S(1)}, u32[]{:S(2)}, u32[]{:S(2)}) %collective-permute-start.25) | collective-permute-done | bytes 393248 | tf_op jit(solution)/shard_map/ppermute | solution.py:572
  123.4 12.6 %collective-permute-done.26.refs_14_ = bf16[128,2048]{1,0:T(8,128)(2,1)S(1)} collective-permute-done((bf16[128,2048]{1,0:T(8,128)(2,1)S(1)}, bf16[128,2048]{1,0:T(8,128)(2,1)S(1)}, u32[]{:S(2)}, u32[]{:S(2)}) %collective-permute-start.26) | collective-permute-done | bytes 524320 | tf_op jit(solution)/shard_map/ppermute | solution.py:572
  141.4 2.5 %inner_back.1.refs_6_.refs_3_ = f32[128,4096]{1,0:T(8,128)S(1)} custom-call(s32[7]{0:T(128)S(1)} %pad_add_fusion.refs_0_, f32[32,128]{1,0:T(8,128)S(1)} %bitcast.37, bf16[128,128]{1,0:T(8,128)(2,1)S(1)} %bitcast.50, bf16[128,128]{1,0:T(8,128)(2,1)S(1)} %bitcast.47, bf16[128,4096]{1,0:T(8,128)(2,1)S(1)} %dresid.1.refs_2_.refs_4_.refs_5_, ...), custom_call_target="tpu_custom_call" | custom-call | flops 268435456 | bytes 3145728 | tf_op jit(solution)/shard_map/inner_back/pallas_call | solution.py:45
  143.9 13.8 %collective-permute-done.27.refs_3_.refs_5_ = bf16[192,2048]{1,0:T(8,128)(2,1)S(1)} collective-permute-done((bf16[192,2048]{1,0:T(8,128)(2,1)S(1)}, bf16[192,2048]{1,0:T(8,128)(2,1)S(1)}, u32[]{:S(2)}, u32[]{:S(2)}) %collective-permute-start.27) | collective-permute-done | bytes 786464 | tf_op jit(solution)/shard_map/ppermute | solution.py:572
  171.1 5.7 %collective-permute-done.32.refs_7_ = bf16[128,2048]{1,0:T(8,128)(2,1)S(1)} collective-permute-done((bf16[128,2048]{1,0:T(8,128)(2,1)S(1)}, bf16[128,2048]{1,0:T(8,128)(2,1)S(1)}, u32[]{:S(2)}, u32[]{:S(2)}) %collective-permute-start.32) | collective-permute-done | bytes 524320 | tf_op jit(solution)/shard_map/ppermute | solution.py:572
  183.4 2.2 %input_grad.3 = bf16[128,4096]{1,0:T(8,128)(2,1)} custom-call(s32[7]{0:T(128)S(1)} %pad_add_fusion.refs_0_, f32[32,128]{1,0:T(8,128)S(1)} %bitcast.40, bf16[128,128]{1,0:T(8,128)(2,1)S(1)} %bitcast.52, f32[128,4096]{1,0:T(8,128)S(1)} %inner_back.1.refs_6_.refs_3_, bf16[128,4096]{1,0:T(8,128)(2,1)S(1)} %get-tuple-element.132.refs_4_, ...), custom_call_target="tpu_custom_call", output_to_operand_aliasing={{}: (7, {})} | custom-call | flops 134217728 | bytes 2621440 | tf_op jit(solution)/shard_map/input_grad/pallas_call | solution.py:45
  (133 shorter events, 63.4 us)
Async XLA Ops:
  0.6 29.0 %collective-permute-start.2 = (bf16[128,4096]{1,0:T(8,128)(2,1)}, bf16[128,4096]{1,0:T(8,128)(2,1)S(1)}, u32[]{:S(2)}, u32[]{:S(2)}) collective-permute-start(bf16[128,4096]{1,0:T(8,128)(2,1)} %bitcast.41), channel_id=1, source_target_pairs={{0,8},{8,16},{16,24},{1,9},{9,17},{17,25},{2,10},{10,18},{18,26},{... | collective-permute-start | bytes 3145736 | tf_op jit(solution)/shard_map/ppermute | solution.py:575
  8.5 14.3 %collective-permute-start = (bf16[128,2176]{1,0:T(8,128)(2,1)}, bf16[128,2176]{1,0:T(8,128)(2,1)S(1)}, u32[]{:S(2)}, u32[]{:S(2)}) collective-permute-start(bf16[128,2176]{1,0:T(8,128)(2,1)} %get-tuple-element.68.refs_1_.refs_2_), channel_id=1, source_target_pairs={{0,2},{1,3},{2,0},{3,1},{4,6},{5,7},{6,4},{7,5},{8,10},{9,11},{10,... | collective-permute-start | bytes 1671176 | tf_op jit(solution)/shard_map/ppermute | solution.py:572
  10.0 14.0 %collective-permute-start.1 = (bf16[128,2176]{1,0:T(8,128)(2,1)}, bf16[128,2176]{1,0:T(8,128)(2,1)S(1)}, u32[]{:S(2)}, u32[]{:S(2)}) collective-permute-start(bf16[128,2176]{1,0:T(8,128)(2,1)} %get-tuple-element.69.refs_6_), channel_id=1, source_target_pairs={{0,4},{1,5},{2,6},{3,7},{4,0},{5,1},{6,2},{7,3},{8,12},{9,13},{10,... | collective-permute-start | bytes 1671176 | tf_op jit(solution)/shard_map/ppermute | solution.py:572
  11.5 18.1 %collective-permute-start.3 = (bf16[224,128]{1,0:T(8,128)(2,1)}, bf16[224,128]{1,0:T(8,128)(2,1)S(1)}, u32[]{:S(2)}, u32[]{:S(2)}) collective-permute-start(bf16[224,128]{1,0:T(8,128)(2,1)} %get-tuple-element.71), channel_id=1, source_target_pairs={{0,8},{8,16},{16,24},{1,9},{9,17},{17,25},{2,10},{10,18},{18,26},{... | collective-permute-start | bytes 172040 | tf_op jit(solution)/shard_map/ppermute | solution.py:575
  15.0 14.7 %collective-permute-start.4 = (bf16[224,128]{1,0:T(8,128)(2,1)}, bf16[224,128]{1,0:T(8,128)(2,1)S(1)}, u32[]{:S(2)}, u32[]{:S(2)}) collective-permute-start(bf16[224,128]{1,0:T(8,128)(2,1)} %get-tuple-element.72), channel_id=1, source_target_pairs={{8,0},{16,8},{24,16},{9,1},{17,9},{25,17},{10,2},{18,10},{26,18},{... | collective-permute-start | bytes 172040 | tf_op jit(solution)/shard_map/ppermute | solution.py:575
  35.7 20.7 %collective-permute-start.10 = (bf16[192,2048]{1,0:T(8,128)(2,1)S(1)}, bf16[192,2048]{1,0:T(8,128)(2,1)S(1)}, u32[]{:S(2)}, u32[]{:S(2)}) collective-permute-start(bf16[192,2048]{1,0:T(8,128)(2,1)S(1)} %get-tuple-element.85), channel_id=1, source_target_pairs={{0,2},{1,3},{2,0},{3,1},{4,6},{5,7},{6,4},{7,5},{8,10},{9,11},{10,... | collective-permute-start | bytes 2359304 | tf_op jit(solution)/shard_map/ppermute | solution.py:572
  37.3 19.3 %collective-permute-start.9 = (bf16[192,2048]{1,0:T(8,128)(2,1)S(1)}, bf16[192,2048]{1,0:T(8,128)(2,1)S(1)}, u32[]{:S(2)}, u32[]{:S(2)}) collective-permute-start(bf16[192,2048]{1,0:T(8,128)(2,1)S(1)} %get-tuple-element.84), channel_id=1, source_target_pairs={{0,4},{1,5},{2,6},{3,7},{4,0},{5,1},{6,2},{7,3},{8,12},{9,13},{10,... | collective-permute-start | bytes 2359304 | tf_op jit(solution)/shard_map/ppermute | solution.py:572
  38.8 15.5 %collective-permute-start.8 = (bf16[64,4224]{1,0:T(8,128)(2,1)S(1)}, bf16[64,4224]{1,0:T(8,128)(2,1)S(1)}, u32[]{:S(2)}, u32[]{:S(2)}) collective-permute-start(bf16[64,4224]{1,0:T(8,128)(2,1)S(1)} %get-tuple-element.81.refs_10_), channel_id=1, source_target_pairs={{0,8},{8,16},{16,24},{1,9},{9,17},{17,25},{2,10},{10,18},{18,26},{... | collective-permute-start | bytes 1622024 | tf_op jit(solution)/shard_map/ppermute | solution.py:575
  69.7 18.9 %collective-permute-start.18 = (bf16[96,2048]{1,0:T(8,128)(2,1)S(1)}, bf16[96,2048]{1,0:T(8,128)(2,1)S(1)}, u32[]{:S(2)}, u32[]{:S(2)}) collective-permute-start(bf16[96,2048]{1,0:T(8,128)(2,1)S(1)} %get-tuple-element.97), channel_id=1, source_target_pairs={{0,5},{1,4},{2,7},{3,6},{4,1},{5,0},{6,3},{7,2},{8,13},{9,12},{10,... | collective-permute-start | bytes 1179656 | tf_op jit(solution)/shard_map/ppermute | solution.py:572
  71.7 19.4 %collective-permute-start.13 = (bf16[96,2048]{1,0:T(8,128)(2,1)S(1)}, bf16[96,2048]{1,0:T(8,128)(2,1)S(1)}, u32[]{:S(2)}, u32[]{:S(2)}) collective-permute-start(bf16[96,2048]{1,0:T(8,128)(2,1)S(1)} %get-tuple-element.92), channel_id=1, source_target_pairs={{0,1},{1,0},{2,3},{3,2},{4,5},{5,4},{6,7},{7,6},{8,9},{9,8},{10,11... | collective-permute-start | bytes 1179656 | tf_op jit(solution)/shard_map/ppermute | solution.py:572
  72.1 19.0 %collective-permute-start.14 = (bf16[96,2048]{1,0:T(8,128)(2,1)S(1)}, bf16[96,2048]{1,0:T(8,128)(2,1)S(1)}, u32[]{:S(2)}, u32[]{:S(2)}) collective-permute-start(bf16[96,2048]{1,0:T(8,128)(2,1)S(1)} %get-tuple-element.93), channel_id=1, source_target_pairs={{0,2},{1,3},{2,0},{3,1},{4,6},{5,7},{6,4},{7,5},{8,10},{9,11},{10,... | collective-permute-start | bytes 1179656 | tf_op jit(solution)/shard_map/ppermute | solution.py:572
  72.6 18.5 %collective-permute-start.15 = (bf16[96,2048]{1,0:T(8,128)(2,1)S(1)}, bf16[96,2048]{1,0:T(8,128)(2,1)S(1)}, u32[]{:S(2)}, u32[]{:S(2)}) collective-permute-start(bf16[96,2048]{1,0:T(8,128)(2,1)S(1)} %get-tuple-element.94), channel_id=1, source_target_pairs={{0,3},{1,2},{2,1},{3,0},{4,7},{5,6},{6,5},{7,4},{8,11},{9,10},{10,... | collective-permute-start | bytes 1179656 | tf_op jit(solution)/shard_map/ppermute | solution.py:572
  98.8 17.4 %collective-permute-start.21 = (bf16[96,2048]{1,0:T(8,128)(2,1)S(1)}, bf16[96,2048]{1,0:T(8,128)(2,1)S(1)}, u32[]{:S(2)}, u32[]{:S(2)}) collective-permute-start(bf16[96,2048]{1,0:T(8,128)(2,1)S(1)} %get-tuple-element.116), channel_id=1, source_target_pairs={{0,5},{1,4},{2,7},{3,6},{4,1},{5,0},{6,3},{7,2},{8,13},{9,12},{10,... | collective-permute-start | bytes 1179656 | tf_op jit(solution)/shard_map/ppermute | solution.py:572
  101.3 15.6 %collective-permute-start.23 = (bf16[96,2048]{1,0:T(8,128)(2,1)S(1)}, bf16[96,2048]{1,0:T(8,128)(2,1)S(1)}, u32[]{:S(2)}, u32[]{:S(2)}) collective-permute-start(bf16[96,2048]{1,0:T(8,128)(2,1)S(1)} %get-tuple-element.119), channel_id=1, source_target_pairs={{0,1},{1,0},{2,3},{3,2},{4,5},{5,4},{6,7},{7,6},{8,9},{9,8},{10,11... | collective-permute-start | bytes 1179656 | tf_op jit(solution)/shard_map/ppermute | solution.py:572
  102.1 14.8 %collective-permute-start.24 = (bf16[96,2048]{1,0:T(8,128)(2,1)S(1)}, bf16[96,2048]{1,0:T(8,128)(2,1)S(1)}, u32[]{:S(2)}, u32[]{:S(2)}) collective-permute-start(bf16[96,2048]{1,0:T(8,128)(2,1)S(1)} %get-tuple-element.120), channel_id=1, source_target_pairs={{0,2},{1,3},{2,0},{3,1},{4,6},{5,7},{6,4},{7,5},{8,10},{9,11},{10,... | collective-permute-start | bytes 1179656 | tf_op jit(solution)/shard_map/ppermute | solution.py:572
  102.7 18.1 %collective-permute-start.25 = (bf16[96,2048]{1,0:T(8,128)(2,1)S(1)}, bf16[96,2048]{1,0:T(8,128)(2,1)S(1)}, u32[]{:S(2)}, u32[]{:S(2)}) collective-permute-start(bf16[96,2048]{1,0:T(8,128)(2,1)S(1)} %get-tuple-element.121), channel_id=1, source_target_pairs={{0,3},{1,2},{2,1},{3,0},{4,7},{5,6},{6,5},{7,4},{8,11},{9,10},{10,... | collective-permute-start | bytes 1179656 | tf_op jit(solution)/shard_map/ppermute | solution.py:572
  121.5 14.6 %collective-permute-start.26 = (bf16[128,2048]{1,0:T(8,128)(2,1)S(1)}, bf16[128,2048]{1,0:T(8,128)(2,1)S(1)}, u32[]{:S(2)}, u32[]{:S(2)}) collective-permute-start(bf16[128,2048]{1,0:T(8,128)(2,1)S(1)} %relay.3.refs_15_), channel_id=1, source_target_pairs={{0,4},{1,5},{2,6},{3,7},{4,0},{5,1},{6,2},{7,3},{8,12},{9,13},{10,... | collective-permute-start | bytes 1572872 | tf_op jit(solution)/shard_map/ppermute | solution.py:572
  122.8 14.3 %collective-permute-start.22 = (bf16[128,2048]{1,0:T(8,128)(2,1)S(1)}, bf16[128,2048]{1,0:T(8,128)(2,1)S(1)}, u32[]{:S(2)}, u32[]{:S(2)}) collective-permute-start(bf16[128,2048]{1,0:T(8,128)(2,1)S(1)} %relay.2.refs_5_), channel_id=1, source_target_pairs={{0,2},{1,3},{2,0},{3,1},{4,6},{5,7},{6,4},{7,5},{8,10},{9,11},{10,... | collective-permute-start | bytes 1572872 | tf_op jit(solution)/shard_map/ppermute | solution.py:572
  138.5 19.2 %collective-permute-start.27 = (bf16[192,2048]{1,0:T(8,128)(2,1)S(1)}, bf16[192,2048]{1,0:T(8,128)(2,1)S(1)}, u32[]{:S(2)}, u32[]{:S(2)}) collective-permute-start(bf16[192,2048]{1,0:T(8,128)(2,1)S(1)} %get-tuple-element.123), channel_id=1, source_target_pairs={{0,4},{1,5},{2,6},{3,7},{4,0},{5,1},{6,2},{7,3},{8,12},{9,13},{10,... | collective-permute-start | bytes 2359304 | tf_op jit(solution)/shard_map/ppermute | solution.py:572
  139.3 18.8 %collective-permute-start.28 = (bf16[192,2048]{1,0:T(8,128)(2,1)S(1)}, bf16[192,2048]{1,0:T(8,128)(2,1)S(1)}, u32[]{:S(2)}, u32[]{:S(2)}) collective-permute-start(bf16[192,2048]{1,0:T(8,128)(2,1)S(1)} %get-tuple-element.124), channel_id=1, source_target_pairs={{0,2},{1,3},{2,0},{3,1},{4,6},{5,7},{6,4},{7,5},{8,10},{9,11},{10,... | collective-permute-start | bytes 2359304 | tf_op jit(solution)/shard_map/ppermute | solution.py:572
  139.9 26.8 %collective-permute-start.35 = (bf16[128,4096]{1,0:T(8,128)(2,1)S(1)}, bf16[128,4096]{1,0:T(8,128)(2,1)S(1)}, u32[]{:S(2)}, u32[]{:S(2)}) collective-permute-start(bf16[128,4096]{1,0:T(8,128)(2,1)S(1)} %dresid.1.refs_2_.refs_4_.refs_5_), channel_id=1, source_target_pairs={{8,0},{16,8},{24,16},{9,1},{17,9},{25,17},{10,2},{18,10},{26,18},{... | collective-permute-start | bytes 3145736 | tf_op jit(solution)/shard_map/ppermute | solution.py:575
  162.8 14.0 %collective-permute-start.32 = (bf16[128,2048]{1,0:T(8,128)(2,1)S(1)}, bf16[128,2048]{1,0:T(8,128)(2,1)S(1)}, u32[]{:S(2)}, u32[]{:S(2)}) collective-permute-start(bf16[128,2048]{1,0:T(8,128)(2,1)S(1)} %get-tuple-element.128.refs_5_), channel_id=1, source_target_pairs={{0,2},{1,3},{2,0},{3,1},{4,6},{5,7},{6,4},{7,5},{8,10},{9,11},{10,... | collective-permute-start | bytes 1572872 | tf_op jit(solution)/shard_map/ppermute | solution.py:572
  163.4 13.7 %collective-permute-start.34 = (bf16[128,2048]{1,0:T(8,128)(2,1)S(1)}, bf16[128,2048]{1,0:T(8,128)(2,1)S(1)}, u32[]{:S(2)}, u32[]{:S(2)}) collective-permute-start(bf16[128,2048]{1,0:T(8,128)(2,1)S(1)} %get-tuple-element.130), channel_id=1, source_target_pairs={{0,4},{1,5},{2,6},{3,7},{4,0},{5,1},{6,2},{7,3},{8,12},{9,13},{10,... | collective-permute-start | bytes 1572872 | tf_op jit(solution)/shard_map/ppermute | solution.py:572
  169.8 13.6 %collective-permute-start.36 = (bf16[64,2176]{1,0:T(8,128)(2,1)S(1)}, bf16[64,2176]{1,0:T(8,128)(2,1)S(1)}, u32[]{:S(2)}, u32[]{:S(2)}) collective-permute-start(bf16[64,2176]{1,0:T(8,128)(2,1)S(1)} %get-tuple-element.133), channel_id=1, source_target_pairs={{8,0},{16,8},{24,16},{9,1},{17,9},{25,17},{10,2},{18,10},{26,18},{... | collective-permute-start | bytes 835592 | tf_op jit(solution)/shard_map/ppermute | solution.py:575
  (38 other events, 337.0 us)

commit v8 on v7

--- a/solution.py
+++ b/solution.py
@@ -11,7 +11,7 @@
 F32 = jnp.float32
 BF16 = jnp.bfloat16
 CHUNKS = 2
-VMEM_BYTES = 32 * 1024 * 1024
+VMEM_BYTES = 26 * 1024 * 1024
 VMEM_ALL = 60 * 1024 * 1024
 NT = (((1,), (1,)), ((), ()))
 
@@ -420,7 +420,8 @@
 
 
 def side_output_kernel(first_weights, second_weights, first_resid, second_resid, *refs):
-    out_ref, refs = refs[-1], refs[:-1]
+    out_ref, mark_ref, refs = refs[-2], refs[-1], refs[:-2]
+    mark_ref[...] = jnp.zeros_like(mark_ref)
     count, width = len(refs) // 2, first_resid.shape[1]
     for k, (weights, resid) in enumerate(((first_weights, first_resid), (second_weights, second_resid))):
         terms = refs[k * count : (k + 1) * count]
@@ -1117,14 +1118,14 @@
     else:
         input_grad, output = input_grads(0, None, [last]), None
     if relayed:
-        output = call(
+        output, mark = call(
             side_output_kernel,
             (1,),
             [whole(side_weight_shape)] * 2
             + [part] * 2
             + [spec for k in range(2) for spec in (side_spec, side_spec, part, part)],
-            whole((tokens, features)),
-            shape(tokens, features),
+            [whole((tokens, features)), whole((16, 128))],
+            [shape(tokens, features), shape(16, 128)],
             2 * slots * unit,
             8 * unit + 4 * slots * width,
             "output",
@@ -1144,7 +1145,7 @@
                 hops * head_flops,
                 (6 + 2 * hops) * unit,
                 "input_grad",
-                after=[output] if k == 0 else [],
+                after=[mark] if k == 0 else [],
                 aliases={7: 0} if more else {},
                 vmem=VMEM_BYTES,
             )(meta, log, b, inner_back_whole, *after_whole[k], *more)

time: 186 us -> 186 us (level)
  transfers between devices with their start and end apart: 38 -> 38, of which waited for: 23 -> 24; matrix products, arithmetic and copies ran while one was open for 0% -> 0% of each run, Pallas kernels for 21% -> 21%
where the time goes in v8:
time: 186 us; the launch traced here: 185 us
  waiting for transfers between devices  89.6 us (48%)
  Pallas kernels  50.3 us (27%)
  starting transfers between devices  41.4 us (22%)
  local copies, waits for them, and re-layouts  2.33 us (1%)
    ppermute x31, waiting for transfers between devices, offset(): return lax.ppermute(a, 'exp', [(i, i ^ k) for i in range(experts)])  69.1 us
    pallas_call x30, Pallas kernels, call(): return lambda *operands: called(*operands, *after)  50.3 us
    ppermute x31, starting transfers between devices, offset(): return lax.ppermute(a, 'exp', [(i, i ^ k) for i in range(experts)])  23.4 us
    ppermute x7, waiting for transfers between devices, hop(): lax.ppermute(states, 'seq', [(i, i + step) for i in range(blocks) if 0 <=...  20.5 us
    ppermute x7, starting transfers between devices, hop(): lax.ppermute(states, 'seq', [(i, i + step) for i in range(blocks) if 0 <=...  18 us
  transfers between devices with their start and end apart: 38, of which 24 were waited for; matrix products, arithmetic and copies ran while one was open for 0% of the time, Pallas kernels for 21%

profile of v8, /device:TPU:0, one launch (start us, length us, event | category | flops | bytes accessed | tf_op | source)
XLA Modules:
  0.0 185.5 jit_solution(16833341062763579201)
XLA Ops:
  0.6 5.1 %collective-permute-start.2 = (bf16[128,4096]{1,0:T(8,128)(2,1)}, bf16[128,4096]{1,0:T(8,128)(2,1)S(1)}, u32[]{:S(2)}, u32[]{:S(2)}) collective-permute-start(bf16[128,4096]{1,0:T(8,128)(2,1)} %bitcast.40), channel_id=1, source_target_pairs={{0,8},{8,16},{16,24},{1,9},{9,17},{17,25},{2,10},{10,18},{18,26},{... | collective-permute-start | bytes 3145736 | tf_op jit(solution)/shard_map/ppermute | solution.py:576
  5.8 2.8 %prepare.1 = (bf16[224,128]{1,0:T(8,128)(2,1)}, bf16[224,128]{1,0:T(8,128)(2,1)}, bf16[128,2176]{1,0:T(8,128)(2,1)}, bf16[128,2176]{1,0:T(8,128)(2,1)}, bf16[256,2176]{1,0:T(8,128)(2,1)}) custom-call(bf16[128,128]{1,0:T(8,128)(2,1)} %bitcast.47, bf16[128,128]{1,0:T(8,128)(2,1)} %bitcast.42, f32[32,128]{1,0:T(8,128)} %bitcast.31, bf16[128,4096]{1,0:T(8,128)(2,1)} %bitcast.29, ...), custom_call_target="tpu_custom_call" | custom-call | bytes 2097152 | tf_op jit(solution)/shard_map/prepare/pallas_call | solution.py:45
  11.6 3.4 %collective-permute-start.3 = (bf16[224,128]{1,0:T(8,128)(2,1)}, bf16[224,128]{1,0:T(8,128)(2,1)S(1)}, u32[]{:S(2)}, u32[]{:S(2)}) collective-permute-start(bf16[224,128]{1,0:T(8,128)(2,1)} %get-tuple-element.73), channel_id=1, source_target_pairs={{0,8},{8,16},{16,24},{1,9},{9,17},{17,25},{2,10},{10,18},{18,26},{... | collective-permute-start | bytes 172040 | tf_op jit(solution)/shard_map/ppermute | solution.py:576
  19.3 2.5 %inner.1.refs_4_.refs_5_.refs_3_ = f32[128,4096]{1,0:T(8,128)S(1)} custom-call(s32[7]{0:T(128)S(1)} %pad_add_fusion.refs_0_, f32[32,128]{1,0:T(8,128)S(1)} %bitcast.32, bf16[128,128]{1,0:T(8,128)(2,1)S(1)} %bitcast.48, bf16[128,128]{1,0:T(8,128)(2,1)S(1)} %bitcast.43, bf16[128,4096]{1,0:T(8,128)(2,1)S(1)} %bitcast.41), custom_call_target="tpu_custom_call" | custom-call | flops 268435456 | bytes 3145728 | tf_op jit(solution)/shard_map/inner/pallas_call | solution.py:45
  24.5 5.2 %collective-permute-done.3.refs_5_.refs_2_.refs_3_ = bf16[224,128]{1,0:T(8,128)(2,1)S(1)} collective-permute-done((bf16[224,128]{1,0:T(8,128)(2,1)}, bf16[224,128]{1,0:T(8,128)(2,1)S(1)}, u32[]{:S(2)}, u32[]{:S(2)}) %collective-permute-start.3) | collective-permute-done | bytes 57376 | tf_op jit(solution)/shard_map/ppermute | solution.py:576
  38.7 4.3 %collective-permute-start.8 = (bf16[64,4224]{1,0:T(8,128)(2,1)S(1)}, bf16[64,4224]{1,0:T(8,128)(2,1)S(1)}, u32[]{:S(2)}, u32[]{:S(2)}) collective-permute-start(bf16[64,4224]{1,0:T(8,128)(2,1)S(1)} %get-tuple-element.83.refs_10_), channel_id=1, source_target_pairs={{0,8},{8,16},{16,24},{1,9},{9,17},{17,25},{2,10},{10,18},{18,26},{... | collective-permute-start | bytes 1622024 | tf_op jit(solution)/shard_map/ppermute | solution.py:576
  43.0 11.2 %collective-permute-done.8.refs_5_.refs_6_ = bf16[64,4224]{1,0:T(8,128)(2,1)S(1)} collective-permute-done((bf16[64,4224]{1,0:T(8,128)(2,1)S(1)}, bf16[64,4224]{1,0:T(8,128)(2,1)S(1)}, u32[]{:S(2)}, u32[]{:S(2)}) %collective-permute-start.8) | collective-permute-done | bytes 540704 | tf_op jit(solution)/shard_map/ppermute | solution.py:576
  59.6 5.9 %back.1.refs_3_.refs_7_ = f32[384,1024]{1,0:T(8,128)S(1)} custom-call(bf16[192,2048]{1,0:T(8,128)(2,1)S(1)} %get-tuple-element.90.refs_0_, bf16[192,2048]{1,0:T(8,128)(2,1)S(1)} %collective-permute-done.9.refs_7_.refs_1_, bf16[192,2048]{1,0:T(8,128)(2,1)S(1)} %get-tuple-element.91.refs_2_, bf16[192,2048]{1,0:T(8,128)(2,1)S(1)} %collective-permute-done.10.refs_8_.refs_3_, ...), custom_call_target="tpu_custom_call" | custom-call | flops 3221225472 | bytes 11534336 | tf_op jit(solution)/shard_map/back/pallas_call | solution.py:45
  65.5 2.8 %collective-permute-done.12.refs_2_ = bf16[128,2048]{1,0:T(8,128)(2,1)S(1)} collective-permute-done((bf16[128,2048]{1,0:T(8,128)(2,1)S(1)}, bf16[128,2048]{1,0:T(8,128)(2,1)S(1)}, u32[]{:S(2)}, u32[]{:S(2)}) %collective-permute-start.12) | collective-permute-done | bytes 524320 | tf_op jit(solution)/shard_map/ppermute | solution.py:573
  73.6 7.5 %collective-permute-done.17.refs_2_.refs_5_ = bf16[96,2048]{1,0:T(8,128)(2,1)S(1)} collective-permute-done((bf16[96,2048]{1,0:T(8,128)(2,1)S(1)}, bf16[96,2048]{1,0:T(8,128)(2,1)S(1)}, u32[]{:S(2)}, u32[]{:S(2)}) %collective-permute-start.17) | collective-permute-done | bytes 393248 | tf_op jit(solution)/shard_map/ppermute | solution.py:573
  81.1 7.5 %collective-permute-done.18.refs_3_.refs_6_ = bf16[96,2048]{1,0:T(8,128)(2,1)S(1)} collective-permute-done((bf16[96,2048]{1,0:T(8,128)(2,1)S(1)}, bf16[96,2048]{1,0:T(8,128)(2,1)S(1)}, u32[]{:S(2)}, u32[]{:S(2)}) %collective-permute-start.18) | collective-permute-done | bytes 393248 | tf_op jit(solution)/shard_map/ppermute | solution.py:573
  88.6 2.4 %up_first.1 = (f32[384,1024]{1,0:T(8,128)S(1)}, f32[384,128]{1,0:T(8,128)S(1)}) custom-call(bf16[96,2048]{1,0:T(8,128)(2,1)S(1)} %get-tuple-element.92.refs_3_.refs_0_, bf16[96,2048]{1,0:T(8,128)(2,1)S(1)} %collective-permute-done.16.refs_1_.refs_4_, bf16[96,2048]{1,0:T(8,128)(2,1)S(1)} %collective-permute-done.17.refs_2_.refs_5_, ...), custom_call_target="tpu_custom_call" | custom-call | flops 1610612736 | bytes 5767168 | tf_op jit(solution)/shard_map/up_first/pallas_call | solution.py:45
  91.1 3.4 %up_last.1 = (bf16[384,1024]{1,0:T(8,128)(2,1)S(1)}, bf16[384,1024]{1,0:T(8,128)(2,1)S(1)}, f32[384,128]{1,0:T(8,128)S(1)}) custom-call(bf16[96,2048]{1,0:T(8,128)(2,1)S(1)} %get-tuple-element.93.refs_0_.refs_3_, bf16[96,2048]{1,0:T(8,128)(2,1)S(1)} %collective-permute-done.13.refs_1_.refs_4_, bf16[96,2048]{1,0:T(8,128)(2,1)S(1)} %collective-permute-done.14.refs_2_.refs_5_, ...), custom_call_target="tpu_custom_call" | custom-call | flops 1610612736 | bytes 5767168 | tf_op jit(solution)/shard_map/up_last/pallas_call | solution.py:45
  94.5 2.4 %expert_grad.2 = (bf16[96,2048]{1,0:T(8,128)(2,1)S(1)}, bf16[96,2048]{1,0:T(8,128)(2,1)S(1)}, bf16[96,2048]{1,0:T(8,128)(2,1)S(1)}, bf16[96,2048]{1,0:T(8,128)(2,1)S(1)}) custom-call(bf16[384,1024]{1,0:T(8,128)(2,1)S(1)} %get-tuple-element.103.refs_0_, bf16[4096,1024]{1,0:T(8,128)(2,1)S(1)} %bitcast.22, f32[384,128]{1,0:T(8,128)S(1)} %get-tuple-element.104.refs_2_, ...), custom_call_target="tpu_custom_call" | custom-call | flops 1610612736 | bytes 5767168 | tf_op jit(solution)/shard_map/expert_grad/pallas_call | solution.py:45
  98.9 2.4 %expert_grad.3 = (bf16[96,2048]{1,0:T(8,128)(2,1)S(1)}, bf16[96,2048]{1,0:T(8,128)(2,1)S(1)}, bf16[96,2048]{1,0:T(8,128)(2,1)S(1)}, bf16[96,2048]{1,0:T(8,128)(2,1)S(1)}) custom-call(bf16[384,1024]{1,0:T(8,128)(2,1)S(1)} %get-tuple-element.103.refs_0_, bf16[4096,1024]{1,0:T(8,128)(2,1)S(1)} %bitcast.23, f32[384,128]{1,0:T(8,128)S(1)} %get-tuple-element.104.refs_2_, ...), custom_call_target="tpu_custom_call" | custom-call | flops 1610612736 | bytes 5767168 | tf_op jit(solution)/shard_map/expert_grad/pallas_call | solution.py:45
  103.5 2.4 %expert_out.2 = (bf16[192,2048]{1,0:T(8,128)(2,1)S(1)}, bf16[192,2048]{1,0:T(8,128)(2,1)S(1)}) custom-call(bf16[384,1024]{1,0:T(8,128)(2,1)S(1)} %get-tuple-element.102.refs_0_, bf16[1024,4096]{1,0:T(8,128)(2,1)S(1)} %bitcast.27, bf16[96,2048]{1,0:T(8,128)(2,1)S(1)} %get-tuple-element.106.refs_2_.refs_1_.refs_10_), custom_call_target="tpu_custom_call" | custom-call | flops 1610612736 | bytes 5767168 | tf_op jit(solution)/shard_map/expert_out/pallas_call | solution.py:45
  105.9 2.6 %expert_out.3 = (bf16[192,2048]{1,0:T(8,128)(2,1)S(1)}, bf16[192,2048]{1,0:T(8,128)(2,1)S(1)}) custom-call(bf16[384,1024]{1,0:T(8,128)(2,1)S(1)} %get-tuple-element.102.refs_0_, bf16[1024,4096]{1,0:T(8,128)(2,1)S(1)} %bitcast.28, bf16[192,2048]{1,0:T(8,128)(2,1)S(1)} %get-tuple-element.107.refs_2_.refs_4_), custom_call_target="tpu_custom_call" | custom-call | flops 1610612736 | bytes 5767168 | tf_op jit(solution)/shard_map/expert_out/pallas_call | solution.py:45
  109.5 6.7 %collective-permute-done.21.refs_4_.refs_8_ = bf16[96,2048]{1,0:T(8,128)(2,1)S(1)} collective-permute-done((bf16[96,2048]{1,0:T(8,128)(2,1)S(1)}, bf16[96,2048]{1,0:T(8,128)(2,1)S(1)}, u32[]{:S(2)}, u32[]{:S(2)}) %collective-permute-start.21) | collective-permute-done | bytes 393248 | tf_op jit(solution)/shard_map/ppermute | solution.py:573
  116.9 3.8 %collective-permute-done.25.refs_4_.refs_13_ = bf16[96,2048]{1,0:T(8,128)(2,1)S(1)} collective-permute-done((bf16[96,2048]{1,0:T(8,128)(2,1)S(1)}, bf16[96,2048]{1,0:T(8,128)(2,1)S(1)}, u32[]{:S(2)}, u32[]{:S(2)}) %collective-permute-start.25) | collective-permute-done | bytes 393248 | tf_op jit(solution)/shard_map/ppermute | solution.py:573
  123.4 12.6 %collective-permute-done.26.refs_14_ = bf16[128,2048]{1,0:T(8,128)(2,1)S(1)} collective-permute-done((bf16[128,2048]{1,0:T(8,128)(2,1)S(1)}, bf16[128,2048]{1,0:T(8,128)(2,1)S(1)}, u32[]{:S(2)}, u32[]{:S(2)}) %collective-permute-start.26) | collective-permute-done | bytes 524320 | tf_op jit(solution)/shard_map/ppermute | solution.py:573
  141.3 2.5 %inner_back.1.refs_6_.refs_3_ = f32[128,4096]{1,0:T(8,128)S(1)} custom-call(s32[7]{0:T(128)S(1)} %pad_add_fusion.refs_0_, f32[32,128]{1,0:T(8,128)S(1)} %bitcast.36, bf16[128,128]{1,0:T(8,128)(2,1)S(1)} %bitcast.49, bf16[128,128]{1,0:T(8,128)(2,1)S(1)} %bitcast.46, bf16[128,4096]{1,0:T(8,128)(2,1)S(1)} %dresid.1.refs_2_.refs_4_.refs_5_, ...), custom_call_target="tpu_custom_call" | custom-call | flops 268435456 | bytes 3145728 | tf_op jit(solution)/shard_map/inner_back/pallas_call | solution.py:45
  143.8 13.8 %collective-permute-done.27.refs_3_.refs_5_ = bf16[192,2048]{1,0:T(8,128)(2,1)S(1)} collective-permute-done((bf16[192,2048]{1,0:T(8,128)(2,1)S(1)}, bf16[192,2048]{1,0:T(8,128)(2,1)S(1)}, u32[]{:S(2)}, u32[]{:S(2)}) %collective-permute-start.27) | collective-permute-done | bytes 786464 | tf_op jit(solution)/shard_map/ppermute | solution.py:573
  171.0 5.7 %collective-permute-done.32.refs_7_ = bf16[128,2048]{1,0:T(8,128)(2,1)S(1)} collective-permute-done((bf16[128,2048]{1,0:T(8,128)(2,1)S(1)}, bf16[128,2048]{1,0:T(8,128)(2,1)S(1)}, u32[]{:S(2)}, u32[]{:S(2)}) %collective-permute-start.32) | collective-permute-done | bytes 524320 | tf_op jit(solution)/shard_map/ppermute | solution.py:573
  179.9 2.2 %input_grad.2.refs_7_ = bf16[128,4096]{1,0:T(8,128)(2,1)} custom-call(s32[7]{0:T(128)S(1)} %pad_add_fusion.refs_0_, f32[32,128]{1,0:T(8,128)S(1)} %bitcast.38, bf16[128,128]{1,0:T(8,128)(2,1)S(1)} %bitcast.50, f32[128,4096]{1,0:T(8,128)S(1)} %inner_back.1.refs_6_.refs_3_, bf16[128,4096]{1,0:T(8,128)(2,1)S(1)} %get-tuple-element.135.refs_4_, ...), custom_call_target="tpu_custom_call" | custom-call | flops 134217728 | bytes 2621440 | tf_op jit(solution)/shard_map/input_grad/pallas_call | solution.py:45
  (115 shorter events, 63.4 us)
Async XLA Ops:
  0.6 29.0 %collective-permute-start.2 = (bf16[128,4096]{1,0:T(8,128)(2,1)}, bf16[128,4096]{1,0:T(8,128)(2,1)S(1)}, u32[]{:S(2)}, u32[]{:S(2)}) collective-permute-start(bf16[128,4096]{1,0:T(8,128)(2,1)} %bitcast.40), channel_id=1, source_target_pairs={{0,8},{8,16},{16,24},{1,9},{9,17},{17,25},{2,10},{10,18},{18,26},{... | collective-permute-start | bytes 3145736 | tf_op jit(solution)/shard_map/ppermute | solution.py:576
  8.6 14.3 %collective-permute-start = (bf16[128,2176]{1,0:T(8,128)(2,1)}, bf16[128,2176]{1,0:T(8,128)(2,1)S(1)}, u32[]{:S(2)}, u32[]{:S(2)}) collective-permute-start(bf16[128,2176]{1,0:T(8,128)(2,1)} %get-tuple-element.70.refs_1_.refs_2_), channel_id=1, source_target_pairs={{0,2},{1,3},{2,0},{3,1},{4,6},{5,7},{6,4},{7,5},{8,10},{9,11},{10,... | collective-permute-start | bytes 1671176 | tf_op jit(solution)/shard_map/ppermute | solution.py:573
  10.1 14.0 %collective-permute-start.1 = (bf16[128,2176]{1,0:T(8,128)(2,1)}, bf16[128,2176]{1,0:T(8,128)(2,1)S(1)}, u32[]{:S(2)}, u32[]{:S(2)}) collective-permute-start(bf16[128,2176]{1,0:T(8,128)(2,1)} %get-tuple-element.71.refs_6_), channel_id=1, source_target_pairs={{0,4},{1,5},{2,6},{3,7},{4,0},{5,1},{6,2},{7,3},{8,12},{9,13},{10,... | collective-permute-start | bytes 1671176 | tf_op jit(solution)/shard_map/ppermute | solution.py:573
  11.6 18.1 %collective-permute-start.3 = (bf16[224,128]{1,0:T(8,128)(2,1)}, bf16[224,128]{1,0:T(8,128)(2,1)S(1)}, u32[]{:S(2)}, u32[]{:S(2)}) collective-permute-start(bf16[224,128]{1,0:T(8,128)(2,1)} %get-tuple-element.73), channel_id=1, source_target_pairs={{0,8},{8,16},{16,24},{1,9},{9,17},{17,25},{2,10},{10,18},{18,26},{... | collective-permute-start | bytes 172040 | tf_op jit(solution)/shard_map/ppermute | solution.py:576
  15.0 14.7 %collective-permute-start.4 = (bf16[224,128]{1,0:T(8,128)(2,1)}, bf16[224,128]{1,0:T(8,128)(2,1)S(1)}, u32[]{:S(2)}, u32[]{:S(2)}) collective-permute-start(bf16[224,128]{1,0:T(8,128)(2,1)} %get-tuple-element.74), channel_id=1, source_target_pairs={{8,0},{16,8},{24,16},{9,1},{17,9},{25,17},{10,2},{18,10},{26,18},{... | collective-permute-start | bytes 172040 | tf_op jit(solution)/shard_map/ppermute | solution.py:576
  35.6 20.7 %collective-permute-start.10 = (bf16[192,2048]{1,0:T(8,128)(2,1)S(1)}, bf16[192,2048]{1,0:T(8,128)(2,1)S(1)}, u32[]{:S(2)}, u32[]{:S(2)}) collective-permute-start(bf16[192,2048]{1,0:T(8,128)(2,1)S(1)} %get-tuple-element.87), channel_id=1, source_target_pairs={{0,2},{1,3},{2,0},{3,1},{4,6},{5,7},{6,4},{7,5},{8,10},{9,11},{10,... | collective-permute-start | bytes 2359304 | tf_op jit(solution)/shard_map/ppermute | solution.py:573
  37.2 19.3 %collective-permute-start.9 = (bf16[192,2048]{1,0:T(8,128)(2,1)S(1)}, bf16[192,2048]{1,0:T(8,128)(2,1)S(1)}, u32[]{:S(2)}, u32[]{:S(2)}) collective-permute-start(bf16[192,2048]{1,0:T(8,128)(2,1)S(1)} %get-tuple-element.86), channel_id=1, source_target_pairs={{0,4},{1,5},{2,6},{3,7},{4,0},{5,1},{6,2},{7,3},{8,12},{9,13},{10,... | collective-permute-start | bytes 2359304 | tf_op jit(solution)/shard_map/ppermute | solution.py:573
  38.7 15.5 %collective-permute-start.8 = (bf16[64,4224]{1,0:T(8,128)(2,1)S(1)}, bf16[64,4224]{1,0:T(8,128)(2,1)S(1)}, u32[]{:S(2)}, u32[]{:S(2)}) collective-permute-start(bf16[64,4224]{1,0:T(8,128)(2,1)S(1)} %get-tuple-element.83.refs_10_), channel_id=1, source_target_pairs={{0,8},{8,16},{16,24},{1,9},{9,17},{17,25},{2,10},{10,18},{18,26},{... | collective-permute-start | bytes 1622024 | tf_op jit(solution)/shard_map/ppermute | solution.py:576
  69.6 18.9 %collective-permute-start.18 = (bf16[96,2048]{1,0:T(8,128)(2,1)S(1)}, bf16[96,2048]{1,0:T(8,128)(2,1)S(1)}, u32[]{:S(2)}, u32[]{:S(2)}) collective-permute-start(bf16[96,2048]{1,0:T(8,128)(2,1)S(1)} %get-tuple-element.99), channel_id=1, source_target_pairs={{0,5},{1,4},{2,7},{3,6},{4,1},{5,0},{6,3},{7,2},{8,13},{9,12},{10,... | collective-permute-start | bytes 1179656 | tf_op jit(solution)/shard_map/ppermute | solution.py:573
  71.6 19.4 %collective-permute-start.13 = (bf16[96,2048]{1,0:T(8,128)(2,1)S(1)}, bf16[96,2048]{1,0:T(8,128)(2,1)S(1)}, u32[]{:S(2)}, u32[]{:S(2)}) collective-permute-start(bf16[96,2048]{1,0:T(8,128)(2,1)S(1)} %get-tuple-element.94), channel_id=1, source_target_pairs={{0,1},{1,0},{2,3},{3,2},{4,5},{5,4},{6,7},{7,6},{8,9},{9,8},{10,11... | collective-permute-start | bytes 1179656 | tf_op jit(solution)/shard_map/ppermute | solution.py:573
  72.0 19.0 %collective-permute-start.14 = (bf16[96,2048]{1,0:T(8,128)(2,1)S(1)}, bf16[96,2048]{1,0:T(8,128)(2,1)S(1)}, u32[]{:S(2)}, u32[]{:S(2)}) collective-permute-start(bf16[96,2048]{1,0:T(8,128)(2,1)S(1)} %get-tuple-element.95), channel_id=1, source_target_pairs={{0,2},{1,3},{2,0},{3,1},{4,6},{5,7},{6,4},{7,5},{8,10},{9,11},{10,... | collective-permute-start | bytes 1179656 | tf_op jit(solution)/shard_map/ppermute | solution.py:573
  72.6 18.5 %collective-permute-start.15 = (bf16[96,2048]{1,0:T(8,128)(2,1)S(1)}, bf16[96,2048]{1,0:T(8,128)(2,1)S(1)}, u32[]{:S(2)}, u32[]{:S(2)}) collective-permute-start(bf16[96,2048]{1,0:T(8,128)(2,1)S(1)} %get-tuple-element.96), channel_id=1, source_target_pairs={{0,3},{1,2},{2,1},{3,0},{4,7},{5,6},{6,5},{7,4},{8,11},{9,10},{10,... | collective-permute-start | bytes 1179656 | tf_op jit(solution)/shard_map/ppermute | solution.py:573
  98.8 17.4 %collective-permute-start.21 = (bf16[96,2048]{1,0:T(8,128)(2,1)S(1)}, bf16[96,2048]{1,0:T(8,128)(2,1)S(1)}, u32[]{:S(2)}, u32[]{:S(2)}) collective-permute-start(bf16[96,2048]{1,0:T(8,128)(2,1)S(1)} %get-tuple-element.118), channel_id=1, source_target_pairs={{0,5},{1,4},{2,7},{3,6},{4,1},{5,0},{6,3},{7,2},{8,13},{9,12},{10,... | collective-permute-start | bytes 1179656 | tf_op jit(solution)/shard_map/ppermute | solution.py:573
  101.3 15.6 %collective-permute-start.23 = (bf16[96,2048]{1,0:T(8,128)(2,1)S(1)}, bf16[96,2048]{1,0:T(8,128)(2,1)S(1)}, u32[]{:S(2)}, u32[]{:S(2)}) collective-permute-start(bf16[96,2048]{1,0:T(8,128)(2,1)S(1)} %get-tuple-element.121), channel_id=1, source_target_pairs={{0,1},{1,0},{2,3},{3,2},{4,5},{5,4},{6,7},{7,6},{8,9},{9,8},{10,11... | collective-permute-start | bytes 1179656 | tf_op jit(solution)/shard_map/ppermute | solution.py:573
  102.1 14.8 %collective-permute-start.24 = (bf16[96,2048]{1,0:T(8,128)(2,1)S(1)}, bf16[96,2048]{1,0:T(8,128)(2,1)S(1)}, u32[]{:S(2)}, u32[]{:S(2)}) collective-permute-start(bf16[96,2048]{1,0:T(8,128)(2,1)S(1)} %get-tuple-element.122), channel_id=1, source_target_pairs={{0,2},{1,3},{2,0},{3,1},{4,6},{5,7},{6,4},{7,5},{8,10},{9,11},{10,... | collective-permute-start | bytes 1179656 | tf_op jit(solution)/shard_map/ppermute | solution.py:573
  102.6 18.1 %collective-permute-start.25 = (bf16[96,2048]{1,0:T(8,128)(2,1)S(1)}, bf16[96,2048]{1,0:T(8,128)(2,1)S(1)}, u32[]{:S(2)}, u32[]{:S(2)}) collective-permute-start(bf16[96,2048]{1,0:T(8,128)(2,1)S(1)} %get-tuple-element.123), channel_id=1, source_target_pairs={{0,3},{1,2},{2,1},{3,0},{4,7},{5,6},{6,5},{7,4},{8,11},{9,10},{10,... | collective-permute-start | bytes 1179656 | tf_op jit(solution)/shard_map/ppermute | solution.py:573
  121.4 14.6 %collective-permute-start.26 = (bf16[128,2048]{1,0:T(8,128)(2,1)S(1)}, bf16[128,2048]{1,0:T(8,128)(2,1)S(1)}, u32[]{:S(2)}, u32[]{:S(2)}) collective-permute-start(bf16[128,2048]{1,0:T(8,128)(2,1)S(1)} %relay.3.refs_15_), channel_id=1, source_target_pairs={{0,4},{1,5},{2,6},{3,7},{4,0},{5,1},{6,2},{7,3},{8,12},{9,13},{10,... | collective-permute-start | bytes 1572872 | tf_op jit(solution)/shard_map/ppermute | solution.py:573
  122.8 14.3 %collective-permute-start.22 = (bf16[128,2048]{1,0:T(8,128)(2,1)S(1)}, bf16[128,2048]{1,0:T(8,128)(2,1)S(1)}, u32[]{:S(2)}, u32[]{:S(2)}) collective-permute-start(bf16[128,2048]{1,0:T(8,128)(2,1)S(1)} %relay.2.refs_5_), channel_id=1, source_target_pairs={{0,2},{1,3},{2,0},{3,1},{4,6},{5,7},{6,4},{7,5},{8,10},{9,11},{10,... | collective-permute-start | bytes 1572872 | tf_op jit(solution)/shard_map/ppermute | solution.py:573
  138.4 19.1 %collective-permute-start.27 = (bf16[192,2048]{1,0:T(8,128)(2,1)S(1)}, bf16[192,2048]{1,0:T(8,128)(2,1)S(1)}, u32[]{:S(2)}, u32[]{:S(2)}) collective-permute-start(bf16[192,2048]{1,0:T(8,128)(2,1)S(1)} %get-tuple-element.125), channel_id=1, source_target_pairs={{0,4},{1,5},{2,6},{3,7},{4,0},{5,1},{6,2},{7,3},{8,12},{9,13},{10,... | collective-permute-start | bytes 2359304 | tf_op jit(solution)/shard_map/ppermute | solution.py:573
  139.2 18.8 %collective-permute-start.28 = (bf16[192,2048]{1,0:T(8,128)(2,1)S(1)}, bf16[192,2048]{1,0:T(8,128)(2,1)S(1)}, u32[]{:S(2)}, u32[]{:S(2)}) collective-permute-start(bf16[192,2048]{1,0:T(8,128)(2,1)S(1)} %get-tuple-element.126), channel_id=1, source_target_pairs={{0,2},{1,3},{2,0},{3,1},{4,6},{5,7},{6,4},{7,5},{8,10},{9,11},{10,... | collective-permute-start | bytes 2359304 | tf_op jit(solution)/shard_map/ppermute | solution.py:573
  139.8 26.8 %collective-permute-start.35 = (bf16[128,4096]{1,0:T(8,128)(2,1)S(1)}, bf16[128,4096]{1,0:T(8,128)(2,1)S(1)}, u32[]{:S(2)}, u32[]{:S(2)}) collective-permute-start(bf16[128,4096]{1,0:T(8,128)(2,1)S(1)} %dresid.1.refs_2_.refs_4_.refs_5_), channel_id=1, source_target_pairs={{8,0},{16,8},{24,16},{9,1},{17,9},{25,17},{10,2},{18,10},{26,18},{... | collective-permute-start | bytes 3145736 | tf_op jit(solution)/shard_map/ppermute | solution.py:576
  162.7 14.0 %collective-permute-start.32 = (bf16[128,2048]{1,0:T(8,128)(2,1)S(1)}, bf16[128,2048]{1,0:T(8,128)(2,1)S(1)}, u32[]{:S(2)}, u32[]{:S(2)}) collective-permute-start(bf16[128,2048]{1,0:T(8,128)(2,1)S(1)} %get-tuple-element.130.refs_5_), channel_id=1, source_target_pairs={{0,2},{1,3},{2,0},{3,1},{4,6},{5,7},{6,4},{7,5},{8,10},{9,11},{10,... | collective-permute-start | bytes 1572872 | tf_op jit(solution)/shard_map/ppermute | solution.py:573
  163.3 13.7 %collective-permute-start.34 = (bf16[128,2048]{1,0:T(8,128)(2,1)S(1)}, bf16[128,2048]{1,0:T(8,128)(2,1)S(1)}, u32[]{:S(2)}, u32[]{:S(2)}) collective-permute-start(bf16[128,2048]{1,0:T(8,128)(2,1)S(1)} %get-tuple-element.132), channel_id=1, source_target_pairs={{0,4},{1,5},{2,6},{3,7},{4,0},{5,1},{6,2},{7,3},{8,12},{9,13},{10,... | collective-permute-start | bytes 1572872 | tf_op jit(solution)/shard_map/ppermute | solution.py:573
  169.7 13.6 %collective-permute-start.36 = (bf16[64,2176]{1,0:T(8,128)(2,1)S(1)}, bf16[64,2176]{1,0:T(8,128)(2,1)S(1)}, u32[]{:S(2)}, u32[]{:S(2)}) collective-permute-start(bf16[64,2176]{1,0:T(8,128)(2,1)S(1)} %get-tuple-element.136), channel_id=1, source_target_pairs={{8,0},{16,8},{24,16},{9,1},{17,9},{25,17},{10,2},{18,10},{26,18},{... | collective-permute-start | bytes 835592 | tf_op jit(solution)/shard_map/ppermute | solution.py:576
  (29 other events, 273.4 us)
